TPU v7x, 128 devices: a whole 4x4x4 slice. The times are simulated.
128 devices in a mesh: rep: 16 (over y_lo, x, core), shard: 8 (over z, y_hi).
Axes of the slice: x: 4, y: 4 (y_hi: 2, y_lo: 2; y = y_hi * 2 + y_lo), z: 4, core: 2. Of those that a mesh axis runs over, the one named last changes fastest.
Arguments:
- tokens: bfloat16 [16, 1024, 1536], P('rep', 'shard'), may hold values from -6 to 6
- lengths: int32 [16], P('rep'), may hold values from 256 to 1024, as said below
- grad_output: bfloat16 [16, 1024, 1536], P('rep', 'shard'), may hold values from -6 to 6
- norm_attn_one: bfloat16 [1536], P('shard'), may hold values from 0.099609375 to 1.8984375
- w_query_one: bfloat16 [1536, 1536], P('shard'), may hold values from -0.15625 to 0.15625
- w_key_one: bfloat16 [1536, 768], P('shard'), may hold values from -0.15625 to 0.15625
- w_value_one: bfloat16 [1536, 768], P('shard'), may hold values from -0.15625 to 0.15625
- w_out_one: bfloat16 [1536, 1536], P('shard'), may hold values from -0.4375 to 0.4375
- norm_mlp_one: bfloat16 [1536], P('shard'), may hold values from 0.099609375 to 1.8984375
- w_gate_one: bfloat16 [1536, 4096], P('shard'), may hold values from -0.15625 to 0.15625
- w_up_one: bfloat16 [1536, 4096], P('shard'), may hold values from -0.15625 to 0.15625
- w_down_one: bfloat16 [4096, 1536], P('shard'), may hold values from -0.09375 to 0.09375
- norm_attn_two: bfloat16 [1536], P('shard'), may hold values from 0.099609375 to 1.8984375
- w_query_two: bfloat16 [1536, 1536], P('shard'), may hold values from -0.15625 to 0.15625
- w_key_two: bfloat16 [1536, 768], P('shard'), may hold values from -0.15625 to 0.15625
- w_value_two: bfloat16 [1536, 768], P('shard'), may hold values from -0.15625 to 0.15625
- w_out_two: bfloat16 [1536, 1536], P('shard'), may hold values from -0.4375 to 0.4375
- norm_mlp_two: bfloat16 [1536], P('shard'), may hold values from 0.099609375 to 1.8984375
- w_gate_two: bfloat16 [1536, 4096], P('shard'), may hold values from -0.15625 to 0.15625
- w_up_two: bfloat16 [1536, 4096], P('shard'), may hold values from -0.15625 to 0.15625
- w_down_two: bfloat16 [4096, 1536], P('shard'), may hold values from -0.09375 to 0.09375
Outputs:
- output: bfloat16 [16, 1024, 1536], P('rep', 'shard')
- input_grad: float32 [16, 1024, 1536], P('rep', 'shard')
- grad_norm_attn_one: float32 [1536], P('shard')
- grad_query_one: float32 [1536, 1536], P('shard')
- grad_key_one: float32 [1536, 768], P('shard')
- grad_value_one: float32 [1536, 768], P('shard')
- grad_out_one: float32 [1536, 1536], P('shard')
- grad_norm_mlp_one: float32 [1536], P('shard')
- grad_gate_one: float32 [1536, 4096], P('shard')
- grad_up_one: float32 [1536, 4096], P('shard')
- grad_down_one: float32 [4096, 1536], P('shard')
- grad_norm_attn_two: float32 [1536], P('shard')
- grad_query_two: float32 [1536, 1536], P('shard')
- grad_key_two: float32 [1536, 768], P('shard')
- grad_value_two: float32 [1536, 768], P('shard')
- grad_out_two: float32 [1536, 1536], P('shard')
- grad_norm_mlp_two: float32 [1536], P('shard')
- grad_gate_two: float32 [1536, 4096], P('shard')
- grad_up_two: float32 [1536, 4096], P('shard')
- grad_down_two: float32 [4096, 1536], P('shard')
Inputs may be any that keep to these rules, and one draw needn't show every extreme that they name: `lengths`: every draw has slots of length exactly 1024 and one of length exactly 256.
All inputs are finite; a program needn't handle non-finite values.
Results may differ from a plain program's by a relative error of at most 0.028.
Values may be sent and summed in bfloat16 or wider, within the bound.
No kernel may reach another device: no remote copies, remote signals or barrier semaphores. Data moves between devices by JAX's collectives and lax.ppermute only.
A program may use at most 256 MiB of HBM per device.

v0:
```python
import jax
import jax.numpy as jnp
from jax import lax
from jax.sharding import PartitionSpec as P

HEAD_DIM = 96
WINDOW = 512


EPSILON = 1e-05
ROPE_BASE = 100000.0
NEGATIVE = -1e30


def rms_norm(values, gain):
    return values * lax.rsqrt(jnp.mean(values * values, axis=-1, keepdims=True) + EPSILON) * gain


def rotate(tensor, places):
    half = tensor.shape[-1] // 2
    freq = ROPE_BASE ** (-jnp.arange(half, dtype=jnp.float32) * (2.0 / tensor.shape[-1]))
    angle = places.astype(jnp.float32)[:, None] * freq[None, :]
    cosine = jnp.cos(angle)[:, None, :]
    sine = jnp.sin(angle)[:, None, :]
    first = tensor[..., :half]
    second = tensor[..., half:]
    return jnp.concatenate(
        [first * cosine - second * sine, second * cosine + first * sine], axis=-1
    )


def unrotate(tensor, places):

    def turned(inner):
        return rotate(inner, places)

    return jax.vjp(turned, jnp.zeros_like(tensor))[1](tensor)[0]


def scores_of(query_group, key_group, places, lengths, window):
    raw = jnp.einsum(
        "sqkgd,spkd->skgqp", query_group, key_group, preferred_element_type=jnp.float32
    )
    key_places = jnp.arange(key_group.shape[1], dtype=jnp.int32)
    gap = places[:, None] - key_places[None, :]
    inside = (key_places[None, None, :] < lengths[:, None, None]) & ((gap >= 0) & (gap < window))[
        None
    ]
    allowed = inside | (gap == 0)[None]
    return (raw * HEAD_DIM ** (-0.5), allowed[:, None, None])


def gather_rows(block):
    return lax.all_gather(block, "shard", axis=1, tiled=True)


def sum_rows(block):
    return lax.psum_scatter(block, "shard", scatter_dimension=1, tiled=True)


def replica_every(parts):
    return lax.psum(
        (
            parts[0],
            parts[1],
            parts[2],
            parts[3],
            parts[4],
            parts[5],
            parts[6],
            parts[7],
            parts[8],
            parts[9],
            parts[10],
            parts[11],
            parts[12],
            parts[13],
            parts[14],
            parts[15],
            parts[16],
            parts[17],
        ),
        "rep",
    )


def attention_columns(state, weights, lengths, window, stretch):
    gain, w_query, w_key, w_value, w_out = weights
    slots = lengths.shape[0]
    width = state.shape[1]
    normed = rms_norm(state, gain.astype(jnp.float32)).astype(jnp.bfloat16)
    normed_all = gather_rows(normed.reshape(slots, stretch, width))
    total = normed_all.shape[1]
    flat = normed_all.reshape(slots * total, width)
    places = jnp.arange(total, dtype=jnp.int32)
    heads_here = w_query.shape[1] // HEAD_DIM
    groups_here = w_key.shape[1] // HEAD_DIM
    query_raw = jnp.dot(flat, w_query, preferred_element_type=jnp.float32)
    key_raw = jnp.dot(flat, w_key, preferred_element_type=jnp.float32)
    value_raw = jnp.dot(flat, w_value, preferred_element_type=jnp.float32)
    queries = rotate(query_raw.reshape(slots, total, heads_here, HEAD_DIM), places).astype(
        jnp.bfloat16
    )
    key_group = rotate(key_raw.reshape(slots, total, groups_here, HEAD_DIM), places).astype(
        jnp.bfloat16
    )
    value_group = value_raw.astype(jnp.bfloat16).reshape(slots, total, groups_here, HEAD_DIM)
    query_group = queries.reshape(slots, total, groups_here, heads_here // groups_here, HEAD_DIM)
    scores, allowed = scores_of(query_group, key_group, places, lengths, window)
    masked = jnp.where(allowed, scores, NEGATIVE)
    peak = jnp.max(masked, axis=-1, keepdims=True)
    shifted = jnp.where(allowed, jnp.exp(masked - peak), 0.0)
    totals = jnp.sum(shifted, axis=-1, keepdims=True)
    probs = (shifted / totals).astype(jnp.bfloat16)
    mixed = jnp.einsum("skgqp,spkd->sqkgd", probs, value_group, preferred_element_type=jnp.float32)
    mixed = mixed.reshape(slots * total, heads_here * HEAD_DIM).astype(jnp.bfloat16)
    partial_out = jnp.dot(mixed, w_out, preferred_element_type=jnp.float32).reshape(
        slots, total, width
    )
    result = state + sum_rows(partial_out).reshape(slots * stretch, width)
    return (
        result,
        (state, flat, query_group, key_group, value_group, peak + jnp.log(totals), mixed),
    )


def attention_columns_back(grad, saved, weights, lengths, window, stretch):
    gain, w_query, w_key, w_value, w_out = weights
    state, flat, query_group, key_group, value_group, log_total, mixed = saved
    slots = lengths.shape[0]
    width = state.shape[1]
    total = key_group.shape[1]
    rows = slots * total
    places = jnp.arange(total, dtype=jnp.int32)
    grad_low = gather_rows(grad.astype(jnp.bfloat16).reshape(slots, stretch, width)).reshape(
        rows, width
    )
    grad_wout = jnp.einsum("rq,rd->qd", mixed, grad_low, preferred_element_type=jnp.float32)
    grad_mixed = jnp.einsum("rd,qd->rq", grad_low, w_out, preferred_element_type=jnp.float32)
    grad_mixed = grad_mixed.astype(jnp.bfloat16).reshape(query_group.shape)
    scores, allowed = scores_of(query_group, key_group, places, lengths, window)
    probs = jnp.where(allowed, jnp.exp(jnp.where(allowed, scores - log_total, NEGATIVE)), 0.0)
    grad_probs = jnp.einsum(
        "sqkgd,spkd->skgqp", grad_mixed, value_group, preferred_element_type=jnp.float32
    )
    inner = jnp.sum(grad_probs * probs, axis=-1, keepdims=True)
    grad_raw = (probs * (grad_probs - inner) * HEAD_DIM ** (-0.5)).astype(jnp.bfloat16)
    grad_query = jnp.einsum(
        "skgqp,spkd->sqkgd", grad_raw, key_group, preferred_element_type=jnp.float32
    )
    grad_keys = jnp.einsum(
        "skgqp,sqkgd->spkd", grad_raw, query_group, preferred_element_type=jnp.float32
    )
    grad_values = jnp.einsum(
        "skgqp,sqkgd->spkd",
        probs.astype(jnp.bfloat16),
        grad_mixed,
        preferred_element_type=jnp.float32,
    )
    heads_here = query_group.shape[2] * query_group.shape[3]
    groups_here = key_group.shape[2]
    query_low = (
        unrotate(grad_query.reshape(slots, total, heads_here, HEAD_DIM), places)
        .reshape(rows, heads_here * HEAD_DIM)
        .astype(jnp.bfloat16)
    )
    keys_low = (
        unrotate(grad_keys, places).reshape(rows, groups_here * HEAD_DIM).astype(jnp.bfloat16)
    )
    values_low = grad_values.reshape(rows, groups_here * HEAD_DIM).astype(jnp.bfloat16)
    grad_wq = jnp.einsum("rd,rq->dq", flat, query_low, preferred_element_type=jnp.float32)
    grad_wk = jnp.einsum("rd,rq->dq", flat, keys_low, preferred_element_type=jnp.float32)
    grad_wv = jnp.einsum("rd,rq->dq", flat, values_low, preferred_element_type=jnp.float32)
    grad_normed = jnp.einsum("rq,dq->rd", query_low, w_query, preferred_element_type=jnp.float32)
    grad_normed = grad_normed + jnp.einsum(
        "rq,dq->rd", keys_low, w_key, preferred_element_type=jnp.float32
    )
    grad_normed = grad_normed + jnp.einsum(
        "rq,dq->rd", values_low, w_value, preferred_element_type=jnp.float32
    )
    own_normed = sum_rows(grad_normed.reshape(slots, total, width)).reshape(slots * stretch, width)
    grad_state, grad_gain = jax.vjp(rms_norm, state, gain.astype(jnp.float32))[1](own_normed)
    return (grad + grad_state, (grad_gain, grad_wq, grad_wk, grad_wv, grad_wout))


def feed_columns(state, weights, slots, stretch):
    gain, w_gate, w_up, w_down = weights
    width = state.shape[1]
    normed = rms_norm(state, gain.astype(jnp.float32)).astype(jnp.bfloat16)
    normed_all = gather_rows(normed.reshape(slots, stretch, width))
    total = normed_all.shape[1]
    flat = normed_all.reshape(slots * total, width)
    gate = jnp.dot(flat, w_gate, preferred_element_type=jnp.float32)
    lifted = jnp.dot(flat, w_up, preferred_element_type=jnp.float32)
    hidden = (jax.nn.silu(gate) * lifted).astype(jnp.bfloat16)
    partial_out = jnp.dot(hidden, w_down, preferred_element_type=jnp.float32).reshape(
        slots, total, width
    )
    result = state + sum_rows(partial_out).reshape(slots * stretch, width)
    return (result, (state, flat, gate, lifted, hidden))


def feed_columns_back(grad, saved, weights, slots, stretch):
    gain, w_gate, w_up, w_down = weights
    state, flat, gate, lifted, hidden = saved
    width = state.shape[1]
    total = flat.shape[0] // slots
    grad_low = gather_rows(grad.astype(jnp.bfloat16).reshape(slots, stretch, width)).reshape(
        slots * total, width
    )
    grad_down = jnp.einsum("rf,rd->fd", hidden, grad_low, preferred_element_type=jnp.float32)
    grad_hidden = jnp.einsum("rd,fd->rf", grad_low, w_down, preferred_element_type=jnp.float32)
    sigma = jax.nn.sigmoid(gate)
    grad_gate = (grad_hidden * lifted * sigma * (1.0 + gate * (1.0 - sigma))).astype(jnp.bfloat16)
    grad_lift = (grad_hidden * gate * sigma).astype(jnp.bfloat16)
    grad_wg = jnp.einsum("rd,rf->df", flat, grad_gate, preferred_element_type=jnp.float32)
    grad_wu = jnp.einsum("rd,rf->df", flat, grad_lift, preferred_element_type=jnp.float32)
    grad_normed = jnp.einsum("rf,df->rd", grad_gate, w_gate, preferred_element_type=jnp.float32)
    grad_normed = grad_normed + jnp.einsum(
        "rf,df->rd", grad_lift, w_up, preferred_element_type=jnp.float32
    )
    own_normed = sum_rows(grad_normed.reshape(slots, total, width)).reshape(slots * stretch, width)
    grad_state, grad_gain = jax.vjp(rms_norm, state, gain.astype(jnp.float32))[1](own_normed)
    return (grad + grad_state, (grad_gain, grad_wg, grad_wu, grad_down))


def body(
    tokens,
    lengths,
    grad_output,
    norm_attn_one,
    w_query_one,
    w_key_one,
    w_value_one,
    w_out_one,
    norm_mlp_one,
    w_gate_one,
    w_up_one,
    w_down_one,
    norm_attn_two,
    w_query_two,
    w_key_two,
    w_value_two,
    w_out_two,
    norm_mlp_two,
    w_gate_two,
    w_up_two,
    w_down_two,
):
    slots, stretch, width = tokens.shape
    rows = slots * stretch
    group = lax.axis_size("shard")
    places = lax.axis_index("shard") * stretch + jnp.arange(stretch, dtype=jnp.int32)
    valid = (places[None, :] < lengths[:, None]).astype(jnp.float32)
    span = stretch * group
    state = tokens.astype(jnp.float32).reshape(rows, width)
    grad_start = (grad_output.astype(jnp.float32) * valid[:, :, None]).reshape(rows, width)

    def tiled(gain):
        return jnp.broadcast_to(gain[:, None], (gain.shape[0], group))

    relaid = (
        lax.all_to_all(tiled(norm_attn_one), "shard", split_axis=1, concat_axis=0, tiled=True),
        lax.all_to_all(tiled(norm_mlp_one), "shard", split_axis=1, concat_axis=0, tiled=True),
        lax.all_to_all(tiled(norm_attn_two), "shard", split_axis=1, concat_axis=0, tiled=True),
        lax.all_to_all(tiled(norm_mlp_two), "shard", split_axis=1, concat_axis=0, tiled=True),
        lax.all_to_all(w_query_one, "shard", split_axis=1, concat_axis=0, tiled=True),
        lax.all_to_all(w_key_one, "shard", split_axis=1, concat_axis=0, tiled=True),
        lax.all_to_all(w_value_one, "shard", split_axis=1, concat_axis=0, tiled=True),
        lax.all_to_all(w_gate_one, "shard", split_axis=1, concat_axis=0, tiled=True),
        lax.all_to_all(w_up_one, "shard", split_axis=1, concat_axis=0, tiled=True),
        lax.all_to_all(w_query_two, "shard", split_axis=1, concat_axis=0, tiled=True),
        lax.all_to_all(w_key_two, "shard", split_axis=1, concat_axis=0, tiled=True),
        lax.all_to_all(w_value_two, "shard", split_axis=1, concat_axis=0, tiled=True),
        lax.all_to_all(w_gate_two, "shard", split_axis=1, concat_axis=0, tiled=True),
        lax.all_to_all(w_up_two, "shard", split_axis=1, concat_axis=0, tiled=True),
    )
    layers = (
        (
            (relaid[0].reshape(-1), relaid[4], relaid[5], relaid[6], w_out_one),
            (relaid[1].reshape(-1), relaid[7], relaid[8], w_down_one),
            WINDOW,
        ),
        (
            (relaid[2].reshape(-1), relaid[9], relaid[10], relaid[11], w_out_two),
            (relaid[3].reshape(-1), relaid[12], relaid[13], w_down_two),
            span,
        ),
    )
    records = []
    for attention_cols, feed_cols, window in layers:
        state, attention_saved = attention_columns(state, attention_cols, lengths, window, stretch)
        state, feed_saved = feed_columns(state, feed_cols, slots, stretch)
        records.append((attention_saved, feed_saved))
    output = state.reshape(slots, stretch, width).astype(jnp.bfloat16)
    grad = grad_start
    terms = [None, None]
    for layer_index in (1, 0):
        attention_cols, feed_cols, window = layers[layer_index]
        attention_saved, feed_saved = records[layer_index]
        grad, feed_terms = feed_columns_back(grad, feed_saved, feed_cols, slots, stretch)
        grad, attention_terms = attention_columns_back(
            grad, attention_saved, attention_cols, lengths, window, stretch
        )
        terms[layer_index] = (attention_terms, feed_terms)
    first_attn, first_feed = terms[0]
    second_attn, second_feed = terms[1]
    returned = (
        lax.all_to_all(
            first_attn[0].reshape(-1, 1), "shard", split_axis=0, concat_axis=1, tiled=True
        ),
        lax.all_to_all(
            first_feed[0].reshape(-1, 1), "shard", split_axis=0, concat_axis=1, tiled=True
        ),
        lax.all_to_all(
            second_attn[0].reshape(-1, 1), "shard", split_axis=0, concat_axis=1, tiled=True
        ),
        lax.all_to_all(
            second_feed[0].reshape(-1, 1), "shard", split_axis=0, concat_axis=1, tiled=True
        ),
        lax.all_to_all(first_attn[1], "shard", split_axis=0, concat_axis=1, tiled=True),
        lax.all_to_all(first_attn[2], "shard", split_axis=0, concat_axis=1, tiled=True),
        lax.all_to_all(first_attn[3], "shard", split_axis=0, concat_axis=1, tiled=True),
        lax.all_to_all(first_feed[1], "shard", split_axis=0, concat_axis=1, tiled=True),
        lax.all_to_all(first_feed[2], "shard", split_axis=0, concat_axis=1, tiled=True),
        lax.all_to_all(second_attn[1], "shard", split_axis=0, concat_axis=1, tiled=True),
        lax.all_to_all(second_attn[2], "shard", split_axis=0, concat_axis=1, tiled=True),
        lax.all_to_all(second_attn[3], "shard", split_axis=0, concat_axis=1, tiled=True),
        lax.all_to_all(second_feed[1], "shard", split_axis=0, concat_axis=1, tiled=True),
        lax.all_to_all(second_feed[2], "shard", split_axis=0, concat_axis=1, tiled=True),
    )
    gain_sums = [jnp.sum(returned[index], axis=1) for index in range(4)]
    shards = [
        gain_sums[0],
        returned[4],
        returned[5],
        returned[6],
        first_attn[4],
        gain_sums[1],
        returned[7],
        returned[8],
        first_feed[3],
        gain_sums[2],
        returned[9],
        returned[10],
        returned[11],
        second_attn[4],
        gain_sums[3],
        returned[12],
        returned[13],
        second_feed[3],
    ]
    shards = list(replica_every(shards))
    input_grad = grad.reshape(slots, stretch, width)
    return (
        output,
        input_grad,
        shards[0],
        shards[1],
        shards[2],
        shards[3],
        shards[4],
        shards[5],
        shards[6],
        shards[7],
        shards[8],
        shards[9],
        shards[10],
        shards[11],
        shards[12],
        shards[13],
        shards[14],
        shards[15],
        shards[16],
        shards[17],
    )


def solution(mesh):
    placed = (
        P("rep", "shard", None),
        P("rep"),
        P("rep", "shard", None),
        P("shard"),
        P("shard", None),
        P("shard", None),
        P("shard", None),
        P("shard", None),
        P("shard"),
        P("shard", None),
        P("shard", None),
        P("shard", None),
        P("shard"),
        P("shard", None),
        P("shard", None),
        P("shard", None),
        P("shard", None),
        P("shard"),
        P("shard", None),
        P("shard", None),
        P("shard", None),
    )
    return jax.shard_map(
        body,
        mesh=mesh,
        in_specs=placed,
        out_specs=(
            P("rep", "shard", None),
            P("rep", "shard", None),
            P("shard"),
            P("shard", None),
            P("shard", None),
            P("shard", None),
            P("shard", None),
            P("shard"),
            P("shard", None),
            P("shard", None),
            P("shard", None),
            P("shard"),
            P("shard", None),
            P("shard", None),
            P("shard", None),
            P("shard", None),
            P("shard"),
            P("shard", None),
            P("shard", None),
            P("shard", None),
        ),
        check_vma=False,
    )
```

profile of v0, /device:TPU:1, one launch (start us, length us, event | category | flops | bytes accessed | tf_op | source)
XLA Modules:
  0.0 2073.8 jit_solution(4195342095310137266)
XLA Ops:
  8.6 8.5 all-to-all-start
  72.2 21.9 %all-gather.9.cloned.1.call-done = bf16[1,1024,1536]{2,1,0:T(8,128)(2,1)} async-done(((bf16[1,128,1536]{2,1,0:T(8,128)(2,1)}), bf16[1,1024,1536]{2,1,0:T(8,128)(2,1)}) %all-gather.9.cloned.1.call-update) | async-done | bytes 3145744 | tf_op jit(solution)/shard_map/all_gather | solution.py:54
  113.2 8.9 all_to_all.446
  123.5 85.1 %reduce-scatter.9.cloned.1.call-done = f32[1,128,1536]{2,1,0:T(8,128)} async-done(((f32[1,1024,1536]{2,1,0:T(8,128)}), f32[1,128,1536]{2,1,0:T(8,128)}) %reduce-scatter.9.cloned.1.call-update) | async-done | bytes 786448 | tf_op jit(solution)/shard_map/reduce_scatter | solution.py:58
  220.6 24.5 %all-to-all-done.5 = bf16[192,8,512]{2,0,1:T(8,128)(2,1)} async-done(((bf16[192,8,512]{2,0,1:T(8,128)(2,1)}), bf16[192,8,512]{2,0,1:T(8,128)(2,1)}, u32[]{:S(2)}, u32[]{:S(2)}) %all-to-all-start.5) | async-done | bytes 1572896 | tf_op jit(solution)/shard_map/all_to_all | solution.py:270
  251.3 46.4 %all-gather.11.cloned.1.call-done = bf16[1,1024,1536]{2,1,0:T(8,128)(2,1)} async-done(((bf16[1,128,1536]{2,1,0:T(8,128)(2,1)}), bf16[1,1024,1536]{2,1,0:T(8,128)(2,1)}) %all-gather.11.cloned.1.call-update) | async-done | bytes 3145744 | tf_op jit(solution)/shard_map/all_gather | solution.py:54
  315.6 8.9 all_to_all.447
  325.2 85.4 %reduce-scatter.11.cloned.1.call-done = f32[1,128,1536]{2,1,0:T(8,128)} async-done(((f32[1,1024,1536]{2,1,0:T(8,128)}), f32[1,128,1536]{2,1,0:T(8,128)}) %reduce-scatter.11.cloned.1.call-update) | async-done | bytes 786448 | tf_op jit(solution)/shard_map/reduce_scatter | solution.py:58
  463.5 20.3 all-gather.13.cloned.1.call-done
  503.0 8.9 all_to_all.448
  513.9 83.9 %reduce-scatter.13.cloned.1.call-done = f32[1,128,1536]{2,1,0:T(8,128)} async-done(((f32[1,1024,1536]{2,1,0:T(8,128)}), f32[1,128,1536]{2,1,0:T(8,128)}) %reduce-scatter.13.cloned.1.call-update) | async-done | bytes 786448 | tf_op jit(solution)/shard_map/reduce_scatter | solution.py:58
  615.1 24.1 %all-to-all-done.13 = bf16[192,8,512]{2,0,1:T(8,128)(2,1)} async-done(((bf16[192,8,512]{2,0,1:T(8,128)(2,1)}), bf16[192,8,512]{2,0,1:T(8,128)(2,1)}, u32[]{:S(2)}, u32[]{:S(2)}) %all-to-all-start.13) | async-done | bytes 1572896 | tf_op jit(solution)/shard_map/all_to_all | solution.py:276
  644.3 46.2 %all-gather.15.cloned.1.call-done = bf16[1,1024,1536]{2,1,0:T(8,128)(2,1)} async-done(((bf16[1,128,1536]{2,1,0:T(8,128)(2,1)}), bf16[1,1024,1536]{2,1,0:T(8,128)(2,1)}) %all-gather.15.cloned.1.call-update) | async-done | bytes 3145744 | tf_op jit(solution)/shard_map/all_gather | solution.py:54
  701.5 51.8 %all-gather.17.cloned.1.call-done = bf16[1,1024,1536]{2,1,0:T(8,128)(2,1)} async-done(((bf16[1,128,1536]{2,1,0:T(8,128)(2,1)}), bf16[1,1024,1536]{2,1,0:T(8,128)(2,1)}) %all-gather.17.cloned.1.call-update) | async-done | bytes 3145744 | tf_op jit(solution)/shard_map/all_gather | solution.py:54
  775.8 90.3 %reduce-scatter.17.cloned.1.call-done = f32[1,128,1536]{2,1,0:T(8,128)} async-done(((f32[1,1024,1536]{2,1,0:T(8,128)}), f32[1,128,1536]{2,1,0:T(8,128)}) %reduce-scatter.17.cloned.1.call-update) | async-done | bytes 786448 | tf_op jit(solution)/shard_map/reduce_scatter | solution.py:58
  868.7 97.9 %reduce-scatter.15.cloned.1.call-done = f32[1,128,1536]{2,1,0:T(8,128)} async-done(((f32[1,1024,1536]{2,1,0:T(8,128)}), f32[1,128,1536]{2,1,0:T(8,128)}) %reduce-scatter.15.cloned.1.call-update) | async-done | bytes 786448 | tf_op jit(solution)/shard_map/reduce_scatter | solution.py:58
  970.7 60.4 %all-gather.19.cloned.1.call-done = bf16[1,1024,1536]{2,1,0:T(8,128)(2,1)} async-done(((bf16[1,128,1536]{2,1,0:T(8,128)(2,1)}), bf16[1,1024,1536]{2,1,0:T(8,128)(2,1)}) %all-gather.19.cloned.1.call-update) | async-done | bytes 3145744 | tf_op jit(solution)/shard_map/all_gather | solution.py:54
  1056.8 96.2 %reduce-scatter.19.cloned.1.call-done = f32[1,128,1536]{2,1,0:T(8,128)} async-done(((f32[1,1024,1536]{2,1,0:T(8,128)}), f32[1,128,1536]{2,1,0:T(8,128)}) %reduce-scatter.19.cloned.1.call-update) | async-done | bytes 786448 | tf_op jit(solution)/shard_map/reduce_scatter | solution.py:58
  1157.8 61.0 %all-gather.21.cloned.1.call-done = bf16[1,1024,1536]{2,1,0:T(8,128)(2,1)} async-done(((bf16[1,128,1536]{2,1,0:T(8,128)(2,1)}), bf16[1,1024,1536]{2,1,0:T(8,128)(2,1)}) %all-gather.21.cloned.1.call-update) | async-done | bytes 3145744 | tf_op jit(solution)/shard_map/all_gather | solution.py:54
  1233.5 96.3 %reduce-scatter.21.cloned.1.call-done = f32[1,128,1536]{2,1,0:T(8,128)} async-done(((f32[1,1024,1536]{2,1,0:T(8,128)}), f32[1,128,1536]{2,1,0:T(8,128)}) %reduce-scatter.21.cloned.1.call-update) | async-done | bytes 786448 | tf_op jit(solution)/shard_map/reduce_scatter | solution.py:58
  1354.6 62.0 %all-gather.23.cloned.1.call-done = bf16[1,1024,1536]{2,1,0:T(8,128)(2,1)} async-done(((bf16[1,128,1536]{2,1,0:T(8,128)(2,1)}), bf16[1,1024,1536]{2,1,0:T(8,128)(2,1)}) %all-gather.23.cloned.1.call-update) | async-done | bytes 3145744 | tf_op jit(solution)/shard_map/all_gather | solution.py:54
  1447.3 8.4 add_bitcast_fusion
  1464.2 29.9 %all-to-all-done.27 = f32[8,192,512]{2,1,0:T(8,128)} async-done(((f32[8,192,512]{2,1,0:T(8,128)}), f32[8,192,512]{2,1,0:T(8,128)}, u32[]{:S(2)}, u32[]{:S(2)}) %all-to-all-start.27) | async-done | bytes 3145760 | tf_op jit(solution)/shard_map/all_to_all | solution.py:330
  1501.6 14.1 all-to-all-done.23
  1524.3 17.1 all-to-all-done.24
  1556.2 9.6 all-to-all-done.22
  1578.1 39.6 %all-to-all-done.19 = f32[8,192,512]{2,1,0:T(8,128)} async-done(((f32[8,192,512]{2,1,0:T(8,128)}), f32[8,192,512]{2,1,0:T(8,128)}, u32[]{:S(2)}, u32[]{:S(2)}) %all-to-all-start.19) | async-done | bytes 3145760 | tf_op jit(solution)/shard_map/all_to_all | solution.py:324
  1630.6 29.6 %all-to-all-done.20 = f32[8,192,512]{2,1,0:T(8,128)} async-done(((f32[8,192,512]{2,1,0:T(8,128)}), f32[8,192,512]{2,1,0:T(8,128)}, u32[]{:S(2)}, u32[]{:S(2)}) %all-to-all-start.20) | async-done | bytes 3145760 | tf_op jit(solution)/shard_map/all_to_all | solution.py:325
  1668.5 9.1 all-to-all-done.16
  1773.0 123.7 %all-to-all-done.18 = f32[8,192,1]{1,2,0:T(1,128)S(1)} async-done(((f32[8,192,1]{1,2,0:T(1,128)}), f32[8,192,1]{1,2,0:T(1,128)S(1)}, u32[]{:S(2)}, u32[]{:S(2)}) %all-to-all-start.18) | async-done | bytes 6176 | tf_op jit(solution)/shard_map/all_to_all | solution.py:312
  1908.5 29.1 %all-reduce.8 = (f32[192]{0:T(256)}, f32[192]{0:T(256)}, f32[192]{0:T(256)}, f32[192]{0:T(256)}) all-reduce(f32[192]{0:T(256)S(1)} %reduce_sum.197, f32[192]{0:T(256)S(1)} %reduce_sum.202, f32[192]{0:T(256)S(1)} %reduce_sum.204, f32[192]{0:T(256)S(1)} %reduce_sum.209), channel_id=1, replica_groups=mesh['rep'=16,'shard'=8] {'rep'}, use_global_device_ids=true, to_apply=%region_24.25 | all-reduce | flops 768 | bytes 6144 | tf_op jit(solution)/shard_map/psum | solution.py:62
  1937.6 103.7 %all-reduce.12.cloned.1.call-done = (f32[192,1536]{1,0:T(8,128)}, f32[192,768]{1,0:T(8,128)}, f32[192,768]{1,0:T(8,128)}, f32[192,1536]{1,0:T(8,128)}, f32[192,4...) async-done(((f32[192,1536]{1,0:T(8,128)}, ...) | async-done | bytes 25952272 | tf_op jit(solution)/shard_map/psum | solution.py:62
  (530 shorter events, 554.6 us)
Async XLA Ops:
  17.1 77.0 %all-gather.9.cloned.1.call-start = ((), (), s32[]{:S(2)}) async-start(), calls=%async_computation.36 | async-start | bytes 3538944 | tf_op jit(solution)/shard_map/all_gather | solution.py:54
  56.1 152.5 %reduce-scatter.9.cloned.1.call-start = ((), (), s32[]{:S(2)}) async-start(), calls=%async_computation.37 | async-start | bytes 7077888 | tf_op jit(solution)/shard_map/reduce_scatter | solution.py:58
  112.6 185.1 %all-gather.11.cloned.1.call-start = ((), (), s32[]{:S(2)}) async-start(), calls=%async_computation.38 | async-start | bytes 3538944 | tf_op jit(solution)/shard_map/all_gather | solution.py:54
  214.3 30.8 %all-to-all-start.5 = ((bf16[192,8,512]{2,0,1:T(8,128)(2,1)}), bf16[192,8,512]{2,0,1:T(8,128)(2,1)}, u32[]{:S(2)}, u32[]{:S(2)}) async-start(bf16[192,8,512]{2,0,1:T(8,128)(2,1)} %bitcast.595), calls=%async_computation.6 | async-start | bytes 3145728 | tf_op jit(solution)/shard_map/all_to_all | solution.py:270
  245.1 58.0 %all-to-all-start.6 = ((bf16[192,8,512]{2,0,1:T(8,128)(2,1)}), bf16[192,8,512]{2,0,1:T(8,128)(2,1)S(1)}, u32[]{:S(2)}, u32[]{:S(2)}) async-start(bf16[192,8,512]{2,0,1:T(8,128)(2,1)} %bitcast.594), calls=%async_computation.7 | async-start | bytes 3145728 | tf_op jit(solution)/shard_map/all_to_all | solution.py:271
  251.2 159.4 %reduce-scatter.11.cloned.1.call-start = ((), (), s32[]{:S(2)}) async-start(), calls=%async_computation.39 | async-start | bytes 7077888 | tf_op jit(solution)/shard_map/reduce_scatter | solution.py:58
  315.0 168.8 %all-gather.13.cloned.1.call-start = ((), (), s32[]{:S(2)}) async-start(), calls=%async_computation.40 | async-start | bytes 3538944 | tf_op jit(solution)/shard_map/all_gather | solution.py:54
  441.6 19.7 all-to-all-start.10
  445.8 152.1 %reduce-scatter.13.cloned.1.call-start = ((), (), s32[]{:S(2)}) async-start(), calls=%async_computation.41 | async-start | bytes 7077888 | tf_op jit(solution)/shard_map/reduce_scatter | solution.py:58
  502.3 188.2 %all-gather.15.cloned.1.call-start = ((), (), s32[]{:S(2)}) async-start(), calls=%async_computation.42 | async-start | bytes 3538944 | tf_op jit(solution)/shard_map/all_gather | solution.py:54
  602.7 150.5 %all-gather.17.cloned.1.call-start = ((), (), s32[]{:S(2)}) async-start(), calls=%async_computation.44 | async-start | bytes 3538944 | tf_op jit(solution)/shard_map/all_gather | solution.py:54
  607.9 31.3 %all-to-all-start.13 = ((bf16[192,8,512]{2,0,1:T(8,128)(2,1)}), bf16[192,8,512]{2,0,1:T(8,128)(2,1)}, u32[]{:S(2)}, u32[]{:S(2)}) async-start(bf16[192,8,512]{2,0,1:T(8,128)(2,1)} %bitcast.619), calls=%async_computation.16 | async-start | bytes 3145728 | tf_op jit(solution)/shard_map/all_to_all | solution.py:276
  639.2 56.8 %all-to-all-start.12 = ((bf16[192,8,512]{2,0,1:T(8,128)(2,1)}), bf16[192,8,512]{2,0,1:T(8,128)(2,1)}, u32[]{:S(2)}, u32[]{:S(2)}) async-start(bf16[192,8,512]{2,0,1:T(8,128)(2,1)} %bitcast.618), calls=%async_computation.15 | async-start | bytes 3145728 | tf_op jit(solution)/shard_map/all_to_all | solution.py:275
  644.1 222.0 %reduce-scatter.17.cloned.1.call-start = ((), (), s32[]{:S(2)}) async-start(), calls=%async_computation.45 | async-start | bytes 7077888 | tf_op jit(solution)/shard_map/reduce_scatter | solution.py:58
  770.0 196.7 %reduce-scatter.15.cloned.1.call-start = ((), (), s32[]{:S(2)}) async-start(), calls=%async_computation.43 | async-start | bytes 7077888 | tf_op jit(solution)/shard_map/reduce_scatter | solution.py:58
  775.8 255.3 %all-gather.19.cloned.1.call-start = ((), (), s32[]{:S(2)}) async-start(), calls=%async_computation.46 | async-start | bytes 3538944 | tf_op jit(solution)/shard_map/all_gather | solution.py:54
  969.6 183.4 %reduce-scatter.19.cloned.1.call-start = ((), (), s32[]{:S(2)}) async-start(), calls=%async_computation.47 | async-start | bytes 7077888 | tf_op jit(solution)/shard_map/reduce_scatter | solution.py:58
  1056.7 162.0 %all-gather.21.cloned.1.call-start = ((), (), s32[]{:S(2)}) async-start(), calls=%async_computation.48 | async-start | bytes 3538944 | tf_op jit(solution)/shard_map/all_gather | solution.py:54
  1157.3 172.4 %reduce-scatter.21.cloned.1.call-start = ((), (), s32[]{:S(2)}) async-start(), calls=%async_computation.49 | async-start | bytes 7077888 | tf_op jit(solution)/shard_map/reduce_scatter | solution.py:58
  1233.4 183.2 %all-gather.23.cloned.1.call-start = ((), (), s32[]{:S(2)}) async-start(), calls=%async_computation.50 | async-start | bytes 3538944 | tf_op jit(solution)/shard_map/all_gather | solution.py:54
  1344.3 98.1 %all-to-all-start.26 = ((f32[8,192,512]{2,1,0:T(8,128)}), f32[8,192,512]{2,1,0:T(8,128)}, u32[]{:S(2)}, u32[]{:S(2)}) async-start(f32[8,192,512]{2,1,0:T(8,128)} %fusion.132), calls=%async_computation.34 | async-start | bytes 6291456 | tf_op jit(solution)/shard_map/all_to_all | solution.py:329
  1442.4 51.7 %all-to-all-start.27 = ((f32[8,192,512]{2,1,0:T(8,128)}), f32[8,192,512]{2,1,0:T(8,128)}, u32[]{:S(2)}, u32[]{:S(2)}) async-start(f32[8,192,512]{2,1,0:T(8,128)} %fusion.130), calls=%async_computation.35 | async-start | bytes 6291456 | tf_op jit(solution)/shard_map/all_to_all | solution.py:330
  1447.0 449.8 %reduce-scatter.23.cloned.1.call-start = ((), (), s32[]{:S(2)}) async-start(), calls=%async_computation.51 | async-start | bytes 7077888 | tf_op jit(solution)/shard_map/reduce_scatter | solution.py:58
  1494.1 21.6 %all-to-all-start.23 = ((f32[8,192,96]{2,1,0:T(8,128)}), f32[8,192,96]{2,1,0:T(8,128)S(1)}, u32[]{:S(2)}, u32[]{:S(2)}) async-start(f32[8,192,96]{2,1,0:T(8,128)} %fusion.195), calls=%async_computation.31 | async-start | bytes 1572864 | tf_op jit(solution)/shard_map/all_to_all | solution.py:327
  1515.6 25.7 %all-to-all-start.24 = ((f32[8,192,96]{2,1,0:T(8,128)}), f32[8,192,96]{2,1,0:T(8,128)S(1)}, u32[]{:S(2)}, u32[]{:S(2)}) async-start(f32[8,192,96]{2,1,0:T(8,128)} %fusion.193), calls=%async_computation.32 | async-start | bytes 1572864 | tf_op jit(solution)/shard_map/all_to_all | solution.py:328
  1542.3 23.6 %all-to-all-start.22 = ((f32[8,192,192]{2,1,0:T(8,128)}), f32[8,192,192]{2,1,0:T(8,128)S(1)}, u32[]{:S(2)}, u32[]{:S(2)}) async-start(f32[8,192,192]{2,1,0:T(8,128)} %fusion.249), calls=%async_computation.30 | async-start | bytes 3145728 | tf_op jit(solution)/shard_map/all_to_all | solution.py:326
  1565.8 51.9 %all-to-all-start.19 = ((f32[8,192,512]{2,1,0:T(8,128)}), f32[8,192,512]{2,1,0:T(8,128)}, u32[]{:S(2)}, u32[]{:S(2)}) async-start(f32[8,192,512]{2,1,0:T(8,128)} %fusion.136), calls=%async_computation.27 | async-start | bytes 6291456 | tf_op jit(solution)/shard_map/all_to_all | solution.py:324
  1617.7 42.4 %all-to-all-start.20 = ((f32[8,192,512]{2,1,0:T(8,128)}), f32[8,192,512]{2,1,0:T(8,128)}, u32[]{:S(2)}, u32[]{:S(2)}) async-start(f32[8,192,512]{2,1,0:T(8,128)} %fusion.134), calls=%async_computation.28 | async-start | bytes 6291456 | tf_op jit(solution)/shard_map/all_to_all | solution.py:325
  1677.6 19.6 all-to-all-start.17
  1698.1 44.7 %all-to-all-start.15 = ((f32[8,192,192]{2,1,0:T(8,128)}), f32[8,192,192]{2,1,0:T(8,128)S(1)}, u32[]{:S(2)}, u32[]{:S(2)}) async-start(f32[8,192,192]{2,1,0:T(8,128)} %fusion.248), calls=%async_computation.23 | async-start | bytes 3145728 | tf_op jit(solution)/shard_map/all_to_all | solution.py:321
  1704.6 336.7 %all-reduce.12.cloned.1.call-start = ((), (), s32[]{:S(2)}) async-start(), calls=%async_computation.52 | async-start | bytes 51904512 | tf_op jit(solution)/shard_map/psum | solution.py:62
  1769.6 127.1 %all-to-all-start.18 = ((f32[8,192,1]{1,2,0:T(1,128)}), f32[8,192,1]{1,2,0:T(1,128)S(1)}, u32[]{:S(2)}, u32[]{:S(2)}) async-start(f32[8,192,1]{1,2,0:T(1,128)} %all_to_all.415), calls=%async_computation.26 | async-start | bytes 16384 | tf_op jit(solution)/shard_map/all_to_all | solution.py:312
  (149 other events, 3753.1 us)
Sparse Core Ops, SparseCore 0:
  25.8 68.2 all-gather.8
  112.7 95.8 reduce-scatter.8
  213.2 84.4 all-gather.10
  315.1 95.4 reduce-scatter.10
  414.6 69.1 all-gather.12
  502.5 95.3 reduce-scatter.12
  602.9 87.6 all-gather.14
  693.4 59.8 all-gather.16
  770.1 95.9 reduce-scatter.16
  869.8 96.7 reduce-scatter.14
  969.8 61.2 all-gather.18
  1056.8 96.0 reduce-scatter.18
  1157.4 61.2 all-gather.20
  1233.5 96.1 reduce-scatter.20
  1334.3 82.2 all-gather.22
  1455.8 155.3 reduce-scatter.22
  1745.4 295.9 all-reduce.11
where the time goes:
time: 2080 us; the launch traced here: 2070 us
  waiting for transfers between devices  1480 us (71%)
  matrix products  204 us (10%)
  local copies, waits for them, and re-layouts  141 us (7%)
  starting transfers between devices  118 us (6%)
  blocking collectives  55.8 us (3%)
  other arithmetic  55.7 us (3%)
    reduce_scatter x8, waiting for transfers between devices, sum_rows(): return lax.psum_scatter(block, 'shard', scatter_dimension=1, tiled=True)  635 us
    all_gather x8, waiting for transfers between devices, gather_rows(): return lax.all_gather(block, 'shard', axis=1, tiled=True)  370 us
    all_to_all x1, waiting for transfers between devices, body(): lax.all_to_all(first_feed[0].reshape(-1, 1), 'shard', split_axis=0, conca...  124 us
    psum x1, waiting for transfers between devices, replica_every(): lax.psum((parts[0], parts[1], parts[2], parts[3], parts[4], parts[5], par...  104 us
    unnamed x296, local copies, waits for them, and re-layouts  43.8 us
  transfers between devices with their start and end apart: 42, of which 36 were waited for; matrix products, arithmetic and copies ran while one was open for 10% of the time, Pallas kernels for 0%

commit v1 on v0

v1 whole, which is shorter than its diff:
```python
import jax
import jax.numpy as jnp
from jax import lax
from jax.sharding import Mesh
from jax.sharding import PartitionSpec as P

HEAD_DIM = 96
WINDOW = 512
EPSILON = 1e-05
ROPE_BASE = 100000.0
NEGATIVE = -1e30

F32 = jnp.float32
BF16 = jnp.bfloat16

AXES = ("ylo", "x", "core", "z", "yhi")
SIZES = (2, 4, 2, 4, 2)
REP = ("ylo", "x", "core")
SHARD = ("z", "yhi")
SPREAD = ("z", "yhi", "core")

RIGHT = [(i, (i + 1) % 4) for i in range(4)]
LEFT = [(i, (i - 1) % 4) for i in range(4)]
SWAP = [(0, 1), (1, 0)]


def number(ylo, x, core, z, yhi):
    return (((ylo * 4 + x) * 2 + core) * 4 + z) * 2 + yhi


def permutation(place):
    pairs = []
    for ylo in range(2):
        for x in range(4):
            for core in range(2):
                for z in range(4):
                    for yhi in range(2):
                        pairs.append(
                            (number(ylo, x, core, z, yhi), number(ylo, *place(x, core, z, yhi)))
                        )
    return pairs


def inverse(pairs):
    return [(there, here) for here, there in pairs]


LINES = [permutation(lambda x, c, z, h, k=k: ((z + k) % 4, h, x, c)) for k in range(4)]
ROWS = permutation(lambda x, c, z, h: (z, c, 2 * h + x // 2, x % 2))


def to_lines(block, z):
    part = block.shape[0] // 4
    out = []
    for k in range(4):
        piece = lax.dynamic_slice_in_dim(block, ((z + k) % 4) * part, part, axis=0)
        out.append(lax.ppermute(piece, AXES, LINES[k]))
    return jnp.concatenate(out, axis=0)


def from_lines(block, z):
    part = block.shape[0] // 4
    out = jnp.zeros_like(block)
    for k in range(4):
        piece = lax.ppermute(block[part * k : part * (k + 1)], AXES, inverse(LINES[k]))
        out = lax.dynamic_update_slice_in_dim(out, piece, ((z + k) % 4) * part, axis=0)
    return out


def ring_gather(block):
    half = block.shape[0] // 2
    from_left = lax.ppermute(block, "x", RIGHT)
    from_right = lax.ppermute(block, "x", LEFT)
    far_first = lax.ppermute(from_left[:half], "x", RIGHT)
    far_second = lax.ppermute(from_right[half:], "x", LEFT)
    return jnp.concatenate([block, from_left, from_right, far_first, far_second], axis=0)


def ring_scatter(partial):
    rows = partial.shape[0] // 4
    half = rows // 2
    own = partial[:rows]
    left = partial[rows : 2 * rows]
    right = partial[2 * rows : 3 * rows]
    far = partial[3 * rows :].astype(BF16)
    first = lax.ppermute(far[:half], "x", RIGHT).astype(F32)
    second = lax.ppermute(far[half:], "x", LEFT).astype(F32)
    right = jnp.concatenate([right[:half] + first, right[half:]], axis=0).astype(BF16)
    left = jnp.concatenate([left[:half], left[half:] + second], axis=0).astype(BF16)
    from_left = lax.ppermute(right, "x", RIGHT).astype(F32)
    from_right = lax.ppermute(left, "x", LEFT).astype(F32)
    return own + from_left + from_right


def rms_norm(values, gain):
    return values * lax.rsqrt(jnp.mean(values * values, axis=-1, keepdims=True) + EPSILON) * gain


def turn(tensor, cosine, sine):
    half = tensor.shape[-1] // 2
    first = tensor[..., :half]
    second = tensor[..., half:]
    return jnp.concatenate(
        [first * cosine - second * sine, second * cosine + first * sine], axis=-1
    )


def masked_scores(queries, keys, context, window):
    places, key_places, length = context[0], context[1], context[2]
    raw = jnp.einsum("qkgd,pkd->kgqp", queries, keys, preferred_element_type=F32)
    gap = places[:, None] - key_places[None, :]
    allowed = ((key_places[None, :] < length) & (gap >= 0) & (gap < window)) | (gap == 0)
    return raw * HEAD_DIM ** (-0.5), allowed[None, None]


def attention_forward(state, weights, context, window):
    gain, w_qkv, w_out = weights
    cosine, sine = context[3], context[4]
    normed = rms_norm(state, gain).astype(BF16)
    flat = ring_gather(normed)
    rows = flat.shape[0]
    raw = jnp.dot(flat, w_qkv, preferred_element_type=F32)
    kv_here = w_qkv.shape[1] // (4 * HEAD_DIM)
    span = kv_here * HEAD_DIM
    queries = turn(raw[:, : 2 * span].reshape(rows, 2 * kv_here, HEAD_DIM), cosine, sine)
    queries = queries.astype(BF16).reshape(rows, kv_here, 2, HEAD_DIM)
    keys = turn(raw[:, 2 * span : 3 * span].reshape(rows, kv_here, HEAD_DIM), cosine, sine)
    both = jnp.concatenate([keys.reshape(rows, span), raw[:, 3 * span :]], axis=1).astype(BF16)
    both = jnp.concatenate([both, lax.ppermute(both, "core", SWAP)], axis=0)
    keys = both[:, :span].reshape(2 * rows, kv_here, HEAD_DIM)
    values = both[:, span:].reshape(2 * rows, kv_here, HEAD_DIM)
    scores, allowed = masked_scores(queries, keys, context, window)
    masked = jnp.where(allowed, scores, NEGATIVE)
    peak = jnp.max(masked, axis=-1, keepdims=True)
    shifted = jnp.where(allowed, jnp.exp(masked - peak), 0.0)
    totals = jnp.sum(shifted, axis=-1, keepdims=True)
    probs = (shifted / totals).astype(BF16)
    mixed = jnp.einsum("kgqp,pkd->qkgd", probs, values, preferred_element_type=F32)
    mixed = mixed.reshape(rows, 2 * span).astype(BF16)
    partial = jnp.dot(mixed, w_out, preferred_element_type=F32)
    result = state + ring_scatter(partial)
    return result, (state, flat, queries, keys, values, peak + jnp.log(totals), mixed)


def attention_backward(grad, saved, weights, context, window):
    gain, w_qkv, w_out = weights
    cosine, sine = context[3], context[4]
    state, flat, queries, keys, values, log_total, mixed = saved
    rows = flat.shape[0]
    kv_here = keys.shape[1]
    span = kv_here * HEAD_DIM
    grad_low = ring_gather(grad.astype(BF16))
    grad_mixed = jnp.einsum("rd,qd->rq", grad_low, w_out, preferred_element_type=F32)
    grad_mixed = grad_mixed.astype(BF16).reshape(queries.shape)
    scores, allowed = masked_scores(queries, keys, context, window)
    probs = jnp.where(allowed, jnp.exp(jnp.where(allowed, scores - log_total, NEGATIVE)), 0.0)
    grad_probs = jnp.einsum("qkgd,pkd->kgqp", grad_mixed, values, preferred_element_type=F32)
    inner = jnp.sum(grad_probs * probs, axis=-1, keepdims=True)
    grad_raw = (probs * (grad_probs - inner) * HEAD_DIM ** (-0.5)).astype(BF16)
    grad_keys = jnp.einsum("kgqp,qkgd->pkd", grad_raw, queries, preferred_element_type=F32)
    grad_values = jnp.einsum(
        "kgqp,qkgd->pkd", probs.astype(BF16), grad_mixed, preferred_element_type=F32
    )
    both = jnp.concatenate(
        [grad_keys.reshape(2 * rows, span), grad_values.reshape(2 * rows, span)], axis=1
    )
    other = lax.ppermute(both[rows:].astype(BF16), "core", SWAP)
    grad_query = jnp.einsum("kgqp,pkd->qkgd", grad_raw, keys, preferred_element_type=F32)
    query_low = turn(grad_query.reshape(rows, 2 * kv_here, HEAD_DIM), cosine, -sine)
    query_low = query_low.reshape(rows, 2 * span).astype(BF16)
    both = both[:rows] + other.astype(F32)
    keys_low = turn(both[:, :span].reshape(rows, kv_here, HEAD_DIM), cosine, -sine)
    low = jnp.concatenate(
        [query_low, keys_low.reshape(rows, span).astype(BF16), both[:, span:].astype(BF16)], axis=1
    )
    partial = jnp.einsum("rq,dq->rd", low, w_qkv, preferred_element_type=F32)
    own_normed = ring_scatter(partial)
    grad_wout = jnp.einsum("rq,rd->qd", mixed, grad_low, preferred_element_type=F32)
    grad_wqkv = jnp.einsum("rd,rq->dq", flat, low, preferred_element_type=F32)
    grad_state, grad_gain = jax.vjp(rms_norm, state, gain)[1](own_normed)
    return grad + grad_state, grad_gain, grad_wqkv.astype(BF16), grad_wout.astype(BF16)


def feed_forward(state, weights):
    gain, w_pair, w_down = weights
    hidden_here = w_down.shape[0]
    normed = rms_norm(state, gain).astype(BF16)
    flat = ring_gather(normed)
    gate = jnp.dot(flat, w_pair[:, :hidden_here], preferred_element_type=F32)
    lifted = jnp.dot(flat, w_pair[:, hidden_here:], preferred_element_type=F32)
    hidden = (jax.nn.silu(gate) * lifted).astype(BF16)
    partial = jnp.dot(hidden, w_down, preferred_element_type=F32)
    return state + ring_scatter(partial), (state, flat, gate, lifted, hidden)


def feed_backward(grad, saved, weights):
    gain, w_pair, w_down = weights
    state, flat, gate, lifted, hidden = saved
    grad_low = ring_gather(grad.astype(BF16))
    grad_hidden = jnp.einsum("rd,fd->rf", grad_low, w_down, preferred_element_type=F32)
    sigma = jax.nn.sigmoid(gate)
    grad_gate = (grad_hidden * lifted * sigma * (1.0 + gate * (1.0 - sigma))).astype(BF16)
    grad_lift = (grad_hidden * gate * sigma).astype(BF16)
    low = jnp.concatenate([grad_gate, grad_lift], axis=1)
    partial = jnp.einsum("rf,df->rd", low, w_pair, preferred_element_type=F32)
    own_normed = ring_scatter(partial)
    grad_pair = jnp.einsum("rd,rf->df", flat, low, preferred_element_type=F32)
    grad_down = jnp.einsum("rf,rd->fd", hidden, grad_low, preferred_element_type=F32)
    grad_state, grad_gain = jax.vjp(rms_norm, state, gain)[1](own_normed)
    return grad + grad_state, grad_gain, grad_pair.astype(BF16), grad_down.astype(BF16)


def spread_sum(parts):
    sums = lax.psum_scatter(parts, SPREAD, scatter_dimension=0, tiled=True)
    return tuple(
        (item.astype(F32) + lax.ppermute(item, "ylo", SWAP).astype(F32)).astype(BF16)
        for item in sums
    )


def home_columns(pieces, widths):
    every = lax.all_gather(pieces, ("x", "core"), axis=0, tiled=False)
    out = []
    start = 0
    for width in widths:
        part = every[:, :, start : start + width]
        rows = part.shape[1]
        part = part.reshape(4, 2, rows, width).transpose(1, 2, 0, 3)
        out.append(part.reshape(2 * rows, 4 * width).astype(F32))
        start += width
    return out


def home_rows(piece):
    piece = lax.ppermute(piece, AXES, inverse(ROWS))
    return lax.all_gather(piece, ("x", "core"), axis=0, tiled=True).astype(F32)


def body(tokens, lengths, grad_output, *weights):
    slots, stretch, width = tokens.shape
    x = lax.axis_index("x")
    core = lax.axis_index("core")
    z = lax.axis_index("z")
    yhi = lax.axis_index("yhi")
    piece = 2 * x + core
    here = (2 * z + yhi) * stretch + jnp.arange(stretch, dtype=jnp.int32)
    valid = (here < lengths[0])[:, None]
    grad_start = jnp.where(valid, grad_output[0], 0).astype(BF16)

    def rows_piece(weight):
        part = weight.shape[0] // 8
        return lax.dynamic_slice_in_dim(weight, piece * part, part, axis=0)

    def columns_piece(weight):
        rows, columns = weight.shape
        return lax.dynamic_slice(
            weight, (core * (rows // 2), x * (columns // 4)), (rows // 2, columns // 4)
        )

    layers = []
    gains = jnp.stack([weights[0], weights[5], weights[9], weights[14]])
    gains = lax.dynamic_slice_in_dim(gains, core * 96, 96, axis=1)[None]
    gathered_gains = None
    for index, base in enumerate((0, 9)):
        w_q, w_k, w_v, w_out = weights[base + 1 : base + 5]
        w_gate, w_up, w_down = weights[base + 6 : base + 9]
        w_qkv = jnp.concatenate([columns_piece(w) for w in (w_q, w_k, w_v)], axis=1)
        pair = jnp.concatenate([columns_piece(w_gate), columns_piece(w_up)], axis=1)
        out_piece = lax.ppermute(rows_piece(w_out), AXES, ROWS)
        down_piece = lax.ppermute(rows_piece(w_down), AXES, ROWS)
        attn = (w_qkv, out_piece) + ((gains,) if index == 0 else ())
        attn = lax.all_gather(attn, SPREAD, axis=0, tiled=True)
        feed = lax.all_gather((pair, down_piece), SPREAD, axis=0, tiled=True)
        if index == 0:
            gathered_gains = attn[2].transpose(1, 0, 2).reshape(4, width).astype(F32)
        layers.append((attn[0], attn[1], feed[0], feed[1]))

    state = to_lines(tokens[0], z).astype(F32)
    length = lax.ppermute(lengths, AXES, LINES_LENGTH)[0]
    grad = to_lines(grad_start, z).astype(F32)

    part = stretch // 4

    def member_places(member, side):
        block = jnp.arange(4, dtype=jnp.int32)
        inner = jnp.arange(part, dtype=jnp.int32)
        home = (member - block + 4) % 4
        return (
            home[:, None] * (2 * stretch) + side * stretch + member * part + inner[None, :]
        ).reshape(-1)

    def line_places(side):
        return jnp.concatenate(
            [member_places((x + step) % 4, side) for step in (0, 3, 1, 2)]
        )

    places = line_places(core)
    key_places = jnp.concatenate([places, line_places(1 - core)])
    half = HEAD_DIM // 2
    freq = ROPE_BASE ** (-jnp.arange(half, dtype=F32) * (2.0 / HEAD_DIM))
    angle = places.astype(F32)[:, None] * freq[None, :]
    context = (places, key_places, length, jnp.cos(angle)[:, None, :], jnp.sin(angle)[:, None, :])
    span = 8 * stretch

    records = []
    for index, window in enumerate((WINDOW, span)):
        w_qkv, w_out, pair, down = layers[index]
        attn = (gathered_gains[2 * index], w_qkv, w_out)
        feed = (gathered_gains[2 * index + 1], pair, down)
        state, attn_saved = attention_forward(state, attn, context, window)
        state, feed_saved = feed_forward(state, feed)
        records.append((attn, feed, attn_saved, feed_saved, window))
    output = from_lines(state.astype(BF16), z)[None]

    results = [None] * 18
    gain_grads = [None] * 4
    for index in (1, 0):
        attn, feed, attn_saved, feed_saved, window = records[index]
        base = 9 * index
        grad, gain_grads[2 * index + 1], g_pair, g_down = feed_backward(grad, feed_saved, feed)
        g_pair, g_down = spread_sum((g_pair, g_down))
        results[base + 6], results[base + 7] = home_columns(g_pair, (1024, 1024))
        results[base + 8] = home_rows(g_down)
        grad, gain_grads[2 * index], g_qkv, g_out = attention_backward(
            grad, attn_saved, attn, context, window
        )
        if index:
            g_qkv, g_out = spread_sum((g_qkv, g_out))
        else:
            g_gain = jnp.stack(gain_grads).astype(BF16).reshape(4, 16, 96).transpose(1, 0, 2)
            g_qkv, g_out, g_gain = spread_sum((g_qkv, g_out, g_gain))
            g_gain = lax.all_gather(g_gain[0], ("x", "core"), axis=0, tiled=False).astype(F32)
            g_gain = g_gain.reshape(4, 2, 4, 96).sum(axis=0).transpose(1, 0, 2).reshape(4, 192)
        results[base + 1 : base + 4] = home_columns(g_qkv, (384, 192, 192))
        results[base + 4] = home_rows(g_out)
    for index, slot in enumerate((0, 5, 9, 14)):
        results[slot] = g_gain[index]
    input_grad = from_lines(grad.astype(BF16), z).astype(F32)[None]
    return (output, input_grad, *results)


LINES_LENGTH = permutation(lambda x, c, z, h: (z, h, x, c))


def solution(mesh):
    fine = Mesh(mesh.devices.reshape(SIZES), AXES)
    token = P(REP, SHARD, None)
    vector = P(SHARD)
    matrix = P(SHARD, None)
    layer = (vector, matrix, matrix, matrix, matrix, vector, matrix, matrix, matrix)
    return jax.shard_map(
        body,
        mesh=fine,
        in_specs=(token, P(REP), token) + layer + layer,
        out_specs=(token, token) + layer + layer,
        check_vma=False,
    )
```

time: 2080 us -> 1430 us (0.69)
  waiting for transfers between devices: 1480 us -> 683 us
  blocking collectives: 55.8 us -> 150 us
  starting transfers between devices: 118 us -> 207 us
  local copies, waits for them, and re-layouts: 141 us -> 114 us
    all_to_all x25 -> x0, waiting for transfers between devices: 374 us -> none  [the longest x1 124 us: body(): lax.all_to_all(first_feed[0].reshape(-1, 1), 'shard', split_axis=0, conca...]
    reduce_scatter x8, waiting for transfers between devices: 635 us -> 317 us  [spread_sum(): sums = lax.psum_scatter(parts, SPREAD, scatter_dimension=0, tiled=True)]
    ppermute x0 -> x102, starting transfers between devices: none -> 206 us  [the longest x8 54.3 us: to_lines(): out.append(lax.ppermute(piece, AXES, LINES[k]))]
    all_gather x8 -> x14, waiting for transfers between devices: 370 us -> 197 us  [the longest x4 111 us: body(): feed = lax.all_gather((pair, down_piece), SPREAD, axis=0, tiled=True)]
    ppermute x0 -> x102, waiting for transfers between devices: none -> 169 us  [the longest x9 39.4 us: spread_sum(): lax.ppermute(item, 'ylo', SWAP).astype(F32)]
    all_to_all x25 -> x0, starting transfers between devices: 115 us -> none  [the longest x1 8.49 us: body(): lax.all_to_all(tiled(norm_attn_one), 'shard', split_axis=1, concat_axis=0...]
    psum x1 -> x0, waiting for transfers between devices: 104 us -> none  [replica_every(): lax.psum((parts[0], parts[1], parts[2], parts[3], parts[4], parts[5], par...]
    all_gather x0 -> x4, blocking collectives: none -> 88 us  [the longest x2 40.2 us: home_rows(): return lax.all_gather(piece, ('x', 'core'), axis=0, tiled=True).astype(F32)]
  transfers between devices with their start and end apart: 42 -> 124, of which waited for: 36 -> 58; matrix products, arithmetic and copies ran while one was open for 10% -> 20% of each run, Pallas kernels for 0% -> 0%
where the time goes in v1:
time: 1430 us
  waiting for transfers between devices  683 us (48%)
  starting transfers between devices  207 us (14%)
  matrix products  187 us (13%)
  blocking collectives  150 us (10%)
  local copies, waits for them, and re-layouts  114 us (8%)
  other arithmetic  65.8 us (5%)
  between operations  18.1 us (1%)
    reduce_scatter x8, waiting for transfers between devices, spread_sum(): sums = lax.psum_scatter(parts, SPREAD, scatter_dimension=0, tiled=True)  317 us
    all_gather x4, waiting for transfers between devices, body(): feed = lax.all_gather((pair, down_piece), SPREAD, axis=0, tiled=True)  111 us
    unnamed x1, blocking collectives  62.5 us
    unnamed x234, local copies, waits for them, and re-layouts  59.2 us
    ppermute x8, starting transfers between devices, to_lines(): out.append(lax.ppermute(piece, AXES, LINES[k]))  54.3 us
    all_gather x4, waiting for transfers between devices, home_columns(): every = lax.all_gather(pieces, ('x', 'core'), axis=0, tiled=False)  48.2 us
    all_gather x2, blocking collectives, home_rows(): return lax.all_gather(piece, ('x', 'core'), axis=0, tiled=True).astype(F32)  40.2 us
    ppermute x9, waiting for transfers between devices, spread_sum(): lax.ppermute(item, 'ylo', SWAP).astype(F32)  39.4 us
  transfers between devices with their start and end apart: 124, of which 58 were waited for; matrix products, arithmetic and copies ran while one was open for 20% of the time, Pallas kernels for 0%

profile of v1, /device:TPU:1, one launch (start us, length us, event | category | flops | bytes accessed | tf_op | source)
XLA Modules:
  0.0 1425.8 jit_solution(9899318982019181134)
XLA Ops:
  17.8 31.8 %collective-permute-start.3 = (bf16[32,1536]{1,0:T(8,128)(2,1)S(1)}, bf16[32,1536]{1,0:T(8,128)(2,1)S(1)}, u32[]{:S(2)}, u32[]{:S(2)}) collective-permute-start(bf16[32,1536]{1,0:T(8,128)(2,1)S(1)} %get-tuple-element.155), channel_id=1, source_target_pairs={{0,48},{1,56},{2,0},{3,8},{4,16},{5,24},{6,32},{7,40},{8,49},{9,57... | collective-permute-start | bytes 294920 | tf_op jit(solution)/shard_map/ppermute | solution.py:57
  63.0 28.7 %all-gather.5 = bf16[16,4,96]{2,1,0:T(4,128)(2,1)S(1)} all-gather(bf16[1,4,96]{2,1,0:T(4,128)(2,1)S(1)} %fusion.108), channel_id=2, replica_groups=mesh['ylo'=2,'x'=4,'core'=2,'z'=4,'yhi'=2] {'z','yhi','core'}, dimensions={0}, use_global_device_ids=true | all-gather | bytes 13056 | tf_op jit(solution)/shard_map/all_gather | solution.py:272
  104.4 14.4 %collective-permute-done.4 = bf16[128,1536]{1,0:T(8,128)(2,1)S(1)} collective-permute-done((bf16[128,1536]{1,0:T(8,128)(2,1)S(1)}, bf16[128,1536]{1,0:T(8,128)(2,1)S(1)}, u32[]{:S(2)}, u32[]{:S(2)}) %collective-permute-start.4) | collective-permute-done | bytes 393248 | tf_op jit(solution)/shard_map/ppermute | solution.py:72
  211.1 34.5 %all-gather.27.cloned.1.call-done = bf16[1024,1536]{1,0:T(8,128)(2,1)} async-done(((bf16[64,1536]{1,0:T(8,128)(2,1)}), bf16[1024,1536]{1,0:T(8,128)(2,1)}) %all-gather.27.cloned.1.call-update) | async-done | bytes 3145744 | tf_op jit(solution)/shard_map/all_gather | solution.py:273
  325.3 16.8 %all-gather.31.cloned.1.call-done = bf16[384,1536]{1,0:T(8,128)(2,1)} async-done(((bf16[24,1536]{1,0:T(8,128)(2,1)}), bf16[384,1536]{1,0:T(8,128)(2,1)}) %all-gather.31.cloned.1.call-update) | async-done | bytes 1179664 | tf_op jit(solution)/shard_map/all_gather | solution.py:272
  368.9 25.3 %all-gather.35.cloned.1.call-done = bf16[1024,1536]{1,0:T(8,128)(2,1)} async-done(((bf16[64,1536]{1,0:T(8,128)(2,1)}), bf16[1024,1536]{1,0:T(8,128)(2,1)}) %all-gather.35.cloned.1.call-update) | async-done | bytes 3145744 | tf_op jit(solution)/shard_map/all_gather | solution.py:273
  408.6 51.6 %all-gather.33.cloned.1.call-done = bf16[1536,2048]{1,0:T(8,128)(2,1)} async-done(((bf16[96,2048]{1,0:T(8,128)(2,1)}), bf16[1536,2048]{1,0:T(8,128)(2,1)}) %all-gather.33.cloned.1.call-update) | async-done | bytes 6291472 | tf_op jit(solution)/shard_map/all_gather | solution.py:273
  493.2 8.1 collective-permute-done.42
  505.9 6.5 collective-permute-done.59
  528.4 15.0 %fusion.25 = f32[2,96,1024,1]{2,1,3,0:T(8,128)} fusion(f32[2,1024,512,2]{2,1,3,0:T(8,128)} %fusion.206, bf16[512,2,2,48]{0,3,2,1:T(8,128)(2,1)} %bitcast.429, bf16[512,2,2,48]{0,3,2,1:T(8,128)(2,1)} %bitcast.428, f32[2,1024,512,2]{2,1,3,0:T(8,128)} %copy-done.3, f32[2,2,512]{2,1,0:T(2,128)S(1)} %log_add_fusion.1, pred[512,1024]{0,1:T(8,128)(4,1)} %get-tuple-element.165), kind=kOutput, calls=%fused_computation.45 | convolution fusion | flops 430705664 | bytes 18489344 | tf_op jit(solution)/shard_map/kgqp,qkgd->pkd/dot_general | solution.py:160
  550.4 14.8 %fusion.26 = f32[2,96,2,512]{3,1,2,0:T(8,128)} fusion(bf16[1024,2,96,1]{0,2,3,1:T(8,128)(2,1)} %bitcast.414, f32[2,1024,512,2]{2,1,3,0:T(8,128)} %fusion.206, f32[2,1024,512,2]{2,1,3,0:T(8,128)} %copy-done.3, f32[2,2,512]{2,1,0:T(2,128)S(1)} %log_add_fusion.1, pred[512,1024]{0,1:T(8,128)(4,1)} %get-tuple-element.165), kind=kOutput, calls=%fused_computation.46 | convolution fusion | flops 429919232 | bytes 18489344 | tf_op jit(solution)/shard_map/kgqp,pkd->qkgd/dot_general | solution.py:168
  581.3 7.5 collective-permute-done.67
  616.6 6.4 fusion.201
  667.3 13.4 fusion.28
  680.8 6.5 fusion.18
  688.1 9.3 collective-permute-start.80
  697.4 14.9 %fusion.29 = f32[2,96,2,512]{3,1,2,0:T(8,128)} fusion(bf16[1024,2,96,1]{0,2,3,1:T(8,128)(2,1)} %bitcast.410, f32[2,1024,512,2]{2,1,3,0:T(8,128)} %fusion.207, f32[2,1024,512,2]{2,1,3,0:T(8,128)} %copy-done.2, f32[2,2,512]{2,1,0:T(2,128)S(1)} %log_add_fusion, pred[512,1024]{0,1:T(8,128)(4,1)S(1)} %copy-done.19), kind=kOutput, calls=%fused_computation.49 | convolution fusion | flops 429919232 | bytes 18489344 | tf_op jit(solution)/shard_map/kgqp,pkd->qkgd/dot_general | solution.py:168
  725.5 7.8 convolution_convert_fusion
  736.7 8.1 convolution_convert_fusion.1
  764.0 59.7 %reduce-scatter.9.cloned.1.call-done = bf16[96,768]{1,0:T(8,128)(2,1)} async-done(((bf16[1536,768]{1,0:T(8,128)(2,1)}), bf16[96,768]{1,0:T(8,128)(2,1)}) %reduce-scatter.9.cloned.1.call-update) | async-done | bytes 147472 | tf_op jit(solution)/shard_map/reduce_scatter | solution.py:214
  829.5 73.7 %reduce-scatter.15.cloned.1.call-done = bf16[64,1536]{1,0:T(8,128)(2,1)} async-done(((bf16[1024,1536]{1,0:T(8,128)(2,1)}), bf16[64,1536]{1,0:T(8,128)(2,1)}) %reduce-scatter.15.cloned.1.call-update) | async-done | bytes 196624 | tf_op jit(solution)/shard_map/reduce_scatter | solution.py:214
  910.5 85.5 %reduce-scatter.21.cloned.1.call-done = bf16[96,2048]{1,0:T(8,128)(2,1)} async-done(((bf16[1536,2048]{1,0:T(8,128)(2,1)}), bf16[96,2048]{1,0:T(8,128)(2,1)}) %reduce-scatter.21.cloned.1.call-update) | async-done | bytes 393232 | tf_op jit(solution)/shard_map/reduce_scatter | solution.py:214
  996.4 8.7 collective-permute-done.99
  1027.6 39.0 %reduce-scatter.19.cloned.1.call-done = bf16[24,1536]{1,0:T(8,128)(2,1)} async-done(((bf16[384,1536]{1,0:T(8,128)(2,1)}), bf16[24,1536]{1,0:T(8,128)(2,1)}) %reduce-scatter.19.cloned.1.call-update) | async-done | bytes 73744 | tf_op jit(solution)/shard_map/reduce_scatter | solution.py:214
  1082.3 17.3 %all_gather.84 = bf16[192,1536]{1,0:T(8,128)(2,1)S(1)} all-gather(bf16[24,1536]{1,0:T(8,128)(2,1)S(1)} %collective-permute-done.98), channel_id=1, replica_groups=mesh['ylo'=2,'x'=4,'core'=2,'z'=4,'yhi'=2] {'x','core'}, dimensions={0}, use_global_device_ids=true | all-gather | bytes 663552 | tf_op jit(solution)/shard_map/all_gather | solution.py:236
  1102.2 58.5 %reduce-scatter.13.cloned.1.call-done = bf16[96,2048]{1,0:T(8,128)(2,1)} async-done(((bf16[1536,2048]{1,0:T(8,128)(2,1)}), bf16[96,2048]{1,0:T(8,128)(2,1)}) %reduce-scatter.13.cloned.1.call-update) | async-done | bytes 393232 | tf_op jit(solution)/shard_map/reduce_scatter | solution.py:214
  1174.7 62.5 %all-reduce = bf16[16,4,96]{2,1,0:T(4,128)(2,1)S(1)} all-reduce(bf16[16,4,96]{2,1,0:T(4,128)(2,1)S(1)} %copy.153), channel_id=7, replica_groups=mesh['ylo'=2,'x'=4,'core'=2,'z'=4,'yhi'=2] {'z','yhi','core'}, use_global_device_ids=true, to_apply=%region_18.19.clone | all-reduce | flops 6144 | bytes 24576
  1251.2 19.1 %all_gather.75 = bf16[8,4,96]{2,1,0:T(4,128)(2,1)S(1)} all-gather(bf16[1,4,96]{2,1,0:T(4,128)(2,1)S(1)} %add_convert_fusion.16), channel_id=1, replica_groups=mesh['ylo'=2,'x'=4,'core'=2,'z'=4,'yhi'=2] {'x','core'}, dimensions={0}, use_global_device_ids=true | all-gather | bytes 6912 | tf_op jit(solution)/shard_map/all_gather | solution.py:332
  1279.4 22.9 %all_gather.78 = bf16[192,1536]{1,0:T(8,128)(2,1)S(1)} all-gather(bf16[24,1536]{1,0:T(8,128)(2,1)S(1)} %collective-permute-done.92), channel_id=1, replica_groups=mesh['ylo'=2,'x'=4,'core'=2,'z'=4,'yhi'=2] {'x','core'}, dimensions={0}, use_global_device_ids=true | all-gather | bytes 663552 | tf_op jit(solution)/shard_map/all_gather | solution.py:236
  1324.2 20.6 %all-gather.37.cloned.1.call-done = bf16[512,1536]{1,0:T(8,128)(2,1)} async-done(((bf16[64,1536]{1,0:T(8,128)(2,1)}), bf16[512,1536]{1,0:T(8,128)(2,1)}) %all-gather.37.cloned.1.call-update) | async-done | bytes 1572880 | tf_op jit(solution)/shard_map/all_gather | solution.py:236
  1348.2 26.8 %all-gather.47.cloned.1.call-done = bf16[768,2048]{1,0:T(8,128)(2,1)} async-done(((bf16[96,2048]{1,0:T(8,128)(2,1)}), bf16[768,2048]{1,0:T(8,128)(2,1)}) %all-gather.47.cloned.1.call-update) | async-done | bytes 3145744 | tf_op jit(solution)/shard_map/all_gather | solution.py:222
  1388.7 16.4 %all-gather.43.cloned.1.call-done = bf16[768,2048]{1,0:T(8,128)(2,1)} async-done(((bf16[96,2048]{1,0:T(8,128)(2,1)}), bf16[768,2048]{1,0:T(8,128)(2,1)}) %all-gather.43.cloned.1.call-update) | async-done | bytes 3145744 | tf_op jit(solution)/shard_map/all_gather | solution.py:222
  (768 shorter events, 575.6 us)
Async XLA Ops:
  7.2 119.3 %all-gather.21.cloned.1.call-start = ((), (), s32[]{:S(2)}) async-start(), calls=%async_computation.8 | async-start | bytes 2506752 | tf_op jit(solution)/shard_map/all_gather | solution.py:272
  11.1 140.8 %all-gather.23.cloned.1.call-start = ((), (), s32[]{:S(2)}) async-start(), calls=%async_computation.9 | async-start | bytes 1253376 | tf_op jit(solution)/shard_map/all_gather | solution.py:272
  13.3 188.5 %all-gather.25.cloned.1.call-start = ((), (), s32[]{:S(2)}) async-start(), calls=%async_computation.10 | async-start | bytes 6684672 | tf_op jit(solution)/shard_map/all_gather | solution.py:273
  16.2 229.5 %all-gather.27.cloned.1.call-start = ((), (), s32[]{:S(2)}) async-start(), calls=%async_computation.11 | async-start | bytes 3342336 | tf_op jit(solution)/shard_map/all_gather | solution.py:273
  17.6 279.1 %all-gather.29.cloned.1.call-start = ((), (), s32[]{:S(2)}) async-start(), calls=%async_computation.12 | async-start | bytes 2506752 | tf_op jit(solution)/shard_map/all_gather | solution.py:272
  17.8 77.8 %collective-permute-start.3 = (bf16[32,1536]{1,0:T(8,128)(2,1)S(1)}, bf16[32,1536]{1,0:T(8,128)(2,1)S(1)}, u32[]{:S(2)}, u32[]{:S(2)}) collective-permute-start(bf16[32,1536]{1,0:T(8,128)(2,1)S(1)} %get-tuple-element.155), channel_id=1, source_target_pairs={{0,48},{1,56},{2,0},{3,8},{4,16},{5,24},{6,32},{7,40},{8,49},{9,57... | collective-permute-start | bytes 294920 | tf_op jit(solution)/shard_map/ppermute | solution.py:57
  49.6 46.8 %collective-permute-start.2 = (bf16[32,1536]{1,0:T(8,128)(2,1)S(1)}, bf16[32,1536]{1,0:T(8,128)(2,1)S(1)}, u32[]{:S(2)}, u32[]{:S(2)}) collective-permute-start(bf16[32,1536]{1,0:T(8,128)(2,1)S(1)} %get-tuple-element.156), channel_id=1, source_target_pairs={{0,32},{1,40},{2,48},{3,56},{4,0},{5,8},{6,16},{7,24},{8,33},{9,41... | collective-permute-start | bytes 294920 | tf_op jit(solution)/shard_map/ppermute | solution.py:57
  52.9 44.2 %collective-permute-start = (bf16[32,1536]{1,0:T(8,128)(2,1)S(1)}, bf16[32,1536]{1,0:T(8,128)(2,1)S(1)}, u32[]{:S(2)}, u32[]{:S(2)}) collective-permute-start(bf16[32,1536]{1,0:T(8,128)(2,1)S(1)} %get-tuple-element.153), channel_id=1, source_target_pairs={{0,0},{1,8},{2,16},{3,24},{4,32},{5,40},{6,48},{7,56},{8,1},{9,9},... | collective-permute-start | bytes 294920 | tf_op jit(solution)/shard_map/ppermute | solution.py:57
  57.3 45.7 %collective-permute-start.9 = (s32[1]{0:T(128)}, s32[1]{0:T(128)}, u32[]{:S(2)}, u32[]{:S(2)}) collective-permute-start(s32[1]{0:T(128)} %param.22), channel_id=1, source_target_pairs={{0,0},{1,8},{2,16},{3,24},{4,32},{5,40},{6,48},{7,56},{8,1},{9,9},... | collective-permute-start | bytes 20 | tf_op jit(solution)/shard_map/ppermute | solution.py:279
  62.8 279.4 %all-gather.31.cloned.1.call-start = ((), (), s32[]{:S(2)}) async-start(), calls=%async_computation.13 | async-start | bytes 1253376 | tf_op jit(solution)/shard_map/all_gather | solution.py:272
  104.3 289.8 %all-gather.35.cloned.1.call-start = ((), (), s32[]{:S(2)}) async-start(), calls=%async_computation.15 | async-start | bytes 3342336 | tf_op jit(solution)/shard_map/all_gather | solution.py:273
  137.7 322.4 %all-gather.33.cloned.1.call-start = ((), (), s32[]{:S(2)}) async-start(), calls=%async_computation.14 | async-start | bytes 6684672 | tf_op jit(solution)/shard_map/all_gather | solution.py:273
  173.6 78.8 %collective-permute-start.48 = (bf16[32,1536]{1,0:T(8,128)(2,1)}, bf16[32,1536]{1,0:T(8,128)(2,1)S(1)}, u32[]{:S(2)}, u32[]{:S(2)}) collective-permute-start(bf16[32,1536]{1,0:T(8,128)(2,1)} %get-tuple-element.147), channel_id=1, source_target_pairs={{0,16},{1,24},{2,32},{3,40},{4,48},{5,56},{6,0},{7,8},{8,17},{9,25... | collective-permute-start | bytes 294920 | tf_op jit(solution)/shard_map/ppermute | solution.py:57
  173.7 86.2 %collective-permute-start.49 = (bf16[32,1536]{1,0:T(8,128)(2,1)}, bf16[32,1536]{1,0:T(8,128)(2,1)}, u32[]{:S(2)}, u32[]{:S(2)}) collective-permute-start(bf16[32,1536]{1,0:T(8,128)(2,1)} %get-tuple-element.146), channel_id=1, source_target_pairs={{0,32},{1,40},{2,48},{3,56},{4,0},{5,8},{6,16},{7,24},{8,33},{9,41... | collective-permute-start | bytes 294920 | tf_op jit(solution)/shard_map/ppermute | solution.py:57
  186.4 561.8 %reduce-scatter.17.cloned.1.call-start = ((), (), s32[]{:S(2)}) async-start(), calls=%async_computation.21 | async-start | bytes 2506752 | tf_op jit(solution)/shard_map/reduce_scatter | solution.py:214
  186.5 74.9 %collective-permute-start.50 = (bf16[32,1536]{1,0:T(8,128)(2,1)}, bf16[32,1536]{1,0:T(8,128)(2,1)}, u32[]{:S(2)}, u32[]{:S(2)}) collective-permute-start(bf16[32,1536]{1,0:T(8,128)(2,1)} %get-tuple-element.145), channel_id=1, source_target_pairs={{0,48},{1,56},{2,0},{3,8},{4,16},{5,24},{6,32},{7,40},{8,49},{9,57... | collective-permute-start | bytes 294920 | tf_op jit(solution)/shard_map/ppermute | solution.py:57
  279.2 75.6 %collective-permute-start.53 = (bf16[64,1536]{1,0:T(8,128)(2,1)}, bf16[64,1536]{1,0:T(8,128)(2,1)}, u32[]{:S(2)}, u32[]{:S(2)}) collective-permute-start(bf16[64,1536]{1,0:T(8,128)(2,1)} %slice.720), channel_id=1, source_target_pairs={{0,16},{16,32},{32,48},{48,0},{1,17},{17,33},{33,49},{49,1},{2,18}... | collective-permute-start | bytes 589832 | tf_op jit(solution)/shard_map/ppermute | solution.py:74
  279.9 76.5 %collective-permute-start.54 = (bf16[64,1536]{1,0:T(8,128)(2,1)}, bf16[64,1536]{1,0:T(8,128)(2,1)}, u32[]{:S(2)}, u32[]{:S(2)}) collective-permute-start(bf16[64,1536]{1,0:T(8,128)(2,1)} %slice.721), channel_id=1, source_target_pairs={{0,48},{16,0},{32,16},{48,32},{1,49},{17,1},{33,17},{49,33},{2,50}... | collective-permute-start | bytes 589832 | tf_op jit(solution)/shard_map/ppermute | solution.py:75
  599.6 156.0 %reduce-scatter.23.cloned.1.call-start = ((), (), s32[]{:S(2)}) async-start(), calls=%async_computation.24 | async-start | bytes 3342336 | tf_op jit(solution)/shard_map/reduce_scatter | solution.py:214
  647.7 175.9 %reduce-scatter.9.cloned.1.call-start = ((), (), s32[]{:S(2)}) async-start(), calls=%async_computation.16 | async-start | bytes 2506752 | tf_op jit(solution)/shard_map/reduce_scatter | solution.py:214
  718.1 185.1 %reduce-scatter.15.cloned.1.call-start = ((), (), s32[]{:S(2)}) async-start(), calls=%async_computation.19 | async-start | bytes 3342336 | tf_op jit(solution)/shard_map/reduce_scatter | solution.py:214
  724.3 271.8 %reduce-scatter.21.cloned.1.call-start = ((), (), s32[]{:S(2)}) async-start(), calls=%async_computation.23 | async-start | bytes 6684672 | tf_op jit(solution)/shard_map/reduce_scatter | solution.py:214
  733.3 333.2 %reduce-scatter.19.cloned.1.call-start = ((), (), s32[]{:S(2)}) async-start(), calls=%async_computation.22 | async-start | bytes 1253376 | tf_op jit(solution)/shard_map/reduce_scatter | solution.py:214
  736.7 424.0 %reduce-scatter.13.cloned.1.call-start = ((), (), s32[]{:S(2)}) async-start(), calls=%async_computation.18 | async-start | bytes 6684672 | tf_op jit(solution)/shard_map/reduce_scatter | solution.py:214
  744.8 528.2 %reduce-scatter.11.cloned.1.call-start = ((), (), s32[]{:S(2)}) async-start(), calls=%async_computation.17 | async-start | bytes 1253376 | tf_op jit(solution)/shard_map/reduce_scatter | solution.py:214
  748.2 555.3 %all-gather.45.cloned.1.call-start = ((), (), s32[]{:S(2)}) async-start(), calls=%async_computation.28 | async-start | bytes 1327104 | tf_op jit(solution)/shard_map/all_gather | solution.py:222
  755.6 554.0 %all-gather.39.cloned.1.call-start = ((), (), s32[]{:S(2)}) async-start(), calls=%async_computation.25 | async-start | bytes 1769472 | tf_op jit(solution)/shard_map/all_gather | solution.py:236
  763.9 554.1 %all-gather.41.cloned.1.call-start = ((), (), s32[]{:S(2)}) async-start(), calls=%async_computation.26 | async-start | bytes 1327104 | tf_op jit(solution)/shard_map/all_gather | solution.py:222
  829.5 515.3 %all-gather.37.cloned.1.call-start = ((), (), s32[]{:S(2)}) async-start(), calls=%async_computation.20 | async-start | bytes 1769472 | tf_op jit(solution)/shard_map/all_gather | solution.py:236
  910.5 464.5 %all-gather.47.cloned.1.call-start = ((), (), s32[]{:S(2)}) async-start(), calls=%async_computation.29 | async-start | bytes 3538944 | tf_op jit(solution)/shard_map/all_gather | solution.py:222
  1007.0 398.1 %all-gather.43.cloned.1.call-start = ((), (), s32[]{:S(2)}) async-start(), calls=%async_computation.27 | async-start | bytes 3538944 | tf_op jit(solution)/shard_map/all_gather | solution.py:222
  1021.0 46.0 %collective-permute-start.46 = (bf16[32,1536]{1,0:T(8,128)(2,1)S(1)}, bf16[32,1536]{1,0:T(8,128)(2,1)S(1)}, u32[]{:S(2)}, u32[]{:S(2)}) collective-permute-start(bf16[32,1536]{1,0:T(8,128)(2,1)S(1)} %get-tuple-element.149), channel_id=1, source_target_pairs={{48,0},{56,1},{0,2},{8,3},{16,4},{24,5},{32,6},{40,7},{49,8},{57,9... | collective-permute-start | bytes 294920 | tf_op jit(solution)/shard_map/ppermute | solution.py:65
  (192 other events, 3269.6 us)
Sparse Core Ops, SparseCore 0:
  11.2 59.6 all-gather.20
  73.9 50.1 all-gather.22
  127.2 64.5 all-gather.24
  194.7 50.8 all-gather.26
  248.5 47.1 all-gather.28
  298.0 44.0 all-gather.30
  344.6 49.5 all-gather.34
  397.2 62.9 all-gather.32
  599.7 67.9 reduce-scatter.16
  672.7 75.1 reduce-scatter.22
  753.1 70.5 reduce-scatter.8
  828.1 75.0 reduce-scatter.14
  907.4 88.6 reduce-scatter.20
  1000.9 65.6 reduce-scatter.18
  1071.2 89.4 reduce-scatter.12
  1165.0 65.7 reduce-scatter.10
  1232.9 31.8 all-gather.44
  1266.9 25.5 all-gather.38
  1294.8 23.1 all-gather.40
  1320.2 24.5 all-gather.36
  1347.0 27.9 all-gather.46
  1377.3 27.7 all-gather.42

commit v2 on v1

--- a/solution.py
+++ b/solution.py
@@ -18,6 +18,9 @@
 REP = ("ylo", "x", "core")
 SHARD = ("z", "yhi")
 SPREAD = ("z", "yhi", "core")
+
+ATTN_UNIT, ATTN_SPLIT = 256, 288
+FEED_UNIT, FEED_SPLIT = 512, 384
 
 RIGHT = [(i, (i + 1) % 4) for i in range(4)]
 LEFT = [(i, (i - 1) % 4) for i in range(4)]
@@ -210,30 +213,120 @@
     return grad + grad_state, grad_gain, grad_pair.astype(BF16), grad_down.astype(BF16)
 
 
-def spread_sum(parts):
-    sums = lax.psum_scatter(parts, SPREAD, scatter_dimension=0, tiled=True)
-    return tuple(
-        (item.astype(F32) + lax.ppermute(item, "ylo", SWAP).astype(F32)).astype(BF16)
-        for item in sums
-    )
-
-
-def home_columns(pieces, widths):
-    every = lax.all_gather(pieces, ("x", "core"), axis=0, tiled=False)
+def fold(block, unit):
+    rows, columns = block.shape
+    return block.reshape(rows, columns // unit, unit).transpose(1, 0, 2).reshape(-1, unit)
+
+
+def unfold(block, rows):
+    lead, (height, unit) = block.shape[:-2], block.shape[-2:]
+    order = tuple(range(len(lead))) + tuple(len(lead) + i for i in (1, 0, 2))
+    block = block.reshape(lead + (height // rows, rows, unit)).transpose(order)
+    return block.reshape(lead + (rows, height // rows * unit))
+
+
+def pack(columns, rows, unit):
+    def each(block):
+        return fold_pieces(block.reshape((16, -1) + block.shape[1:]), unit)
+
+    return jnp.concatenate([each(columns), each(rows)], axis=1)
+
+
+def fold_pieces(block, unit):
+    pieces, rows, columns = block.shape
+    block = block.reshape(pieces, rows, columns // unit, unit).transpose(0, 2, 1, 3)
+    return block.reshape(pieces, -1, unit)
+
+
+def either(index, first, second):
+    return jnp.where(index == 0, first, second)
+
+
+def roll_home(relative, index):
+    twice = jnp.concatenate([relative, relative], axis=0)
+    return lax.dynamic_slice_in_dim(twice, (4 - index) % 4, 4, axis=0)
+
+
+def ring_stack(block, axis):
+    half = block.shape[0] // 2
+    before = lax.ppermute(block, axis, RIGHT)
+    after = lax.ppermute(block, axis, LEFT)
+    first = lax.ppermute(before[:half], axis, RIGHT)
+    second = lax.ppermute(after[half:], axis, LEFT)
+    far = jnp.concatenate([first, second], axis=0)
+    return jnp.stack([block, after, far, before])
+
+
+def spread_gather(piece, where):
+    other = lax.ppermute(piece, "yhi", SWAP)
+    pair = either(where["yhi"], jnp.stack([piece, other]), jnp.stack([other, piece]))
+    line = ring_stack(pair, "z")
+    other = lax.ppermute(line, "core", SWAP)
+    line = either(
+        where["core"], jnp.stack([line, other], axis=2), jnp.stack([other, line], axis=2)
+    )
+    return roll_home(line, where["z"]).reshape((16,) + piece.shape)
+
+
+def spread_scatter(pieces, where):
+    tall = pieces.reshape((4, 2, 2) + pieces.shape[1:])
+    mine = lax.dynamic_index_in_dim(tall, where["core"], axis=2, keepdims=False)
+    theirs = lax.dynamic_index_in_dim(tall, 1 - where["core"], axis=2, keepdims=False)
+    line = (mine.astype(F32) + lax.ppermute(theirs, "core", SWAP).astype(F32)).astype(BF16)
+
+    def step(r):
+        return lax.dynamic_index_in_dim(line, (where["z"] + r) % 4, axis=0, keepdims=False)
+
+    own, after, far, before = step(0), step(1), step(2), step(3)
+    first = lax.ppermute(far[:1], "z", RIGHT).astype(F32)
+    second = lax.ppermute(far[1:], "z", LEFT).astype(F32)
+    after = jnp.concatenate([(after[:1].astype(F32) + first).astype(BF16), after[1:]])
+    before = jnp.concatenate([before[:1], (before[1:].astype(F32) + second).astype(BF16)])
+    from_before = lax.ppermute(after, "z", RIGHT).astype(F32)
+    from_after = lax.ppermute(before, "z", LEFT).astype(F32)
+    pair = (own.astype(F32) + from_before + from_after).astype(BF16)
+    mine = lax.dynamic_index_in_dim(pair, where["yhi"], axis=0, keepdims=False)
+    theirs = lax.dynamic_index_in_dim(pair, 1 - where["yhi"], axis=0, keepdims=False)
+    return (mine.astype(F32) + lax.ppermute(theirs, "yhi", SWAP).astype(F32)).astype(BF16)
+
+
+def go_home(piece, split, where, offload):
+    piece = (piece.astype(F32) + lax.ppermute(piece, "ylo", SWAP).astype(F32)).astype(BF16)
+    moved = lax.ppermute(piece[split:], AXES, inverse(ROWS))
+    piece = jnp.concatenate([piece[:split], moved], axis=0)
+    if offload:
+        return lax.all_gather(piece, ("x", "core"), axis=0, tiled=False).reshape(
+            (4, 2) + piece.shape
+        )
+    line = ring_stack(piece, "x")
+    other = lax.ppermute(line, "core", SWAP)
+    line = either(
+        where["core"], jnp.stack([line, other], axis=1), jnp.stack([other, line], axis=1)
+    )
+    return roll_home(line, where["x"])
+
+
+def home_weights(every, split, part, widths):
+    columns = unfold(every[:, :, :split], 96)
     out = []
     start = 0
     for width in widths:
-        part = every[:, :, start : start + width]
-        rows = part.shape[1]
-        part = part.reshape(4, 2, rows, width).transpose(1, 2, 0, 3)
-        out.append(part.reshape(2 * rows, 4 * width).astype(F32))
+        block = columns[..., start : start + width].transpose(1, 2, 0, 3)
+        out.append(block.reshape(192, 4 * width).astype(F32))
         start += width
+    rows = unfold(every[:, :, split:], part)
+    out.append(rows.reshape(8 * part, -1).astype(F32))
     return out
 
 
-def home_rows(piece):
-    piece = lax.ppermute(piece, AXES, inverse(ROWS))
-    return lax.all_gather(piece, ("x", "core"), axis=0, tiled=True).astype(F32)
+def butterfly(values):
+    for axis, size in (("core", 2), ("x", 4), ("z", 4), ("yhi", 2), ("ylo", 2)):
+        step = 1
+        while step < size:
+            pairs = [(i, i ^ step) for i in range(size)]
+            values = values + lax.ppermute(values, axis, pairs)
+            step *= 2
+    return values
 
 
 def body(tokens, lengths, grad_output, *weights):
@@ -257,23 +350,31 @@
             weight, (core * (rows // 2), x * (columns // 4)), (rows // 2, columns // 4)
         )
 
+    where = {"x": x, "core": core, "z": z, "yhi": yhi}
     layers = []
-    gains = jnp.stack([weights[0], weights[5], weights[9], weights[14]])
-    gains = lax.dynamic_slice_in_dim(gains, core * 96, 96, axis=1)[None]
-    gathered_gains = None
-    for index, base in enumerate((0, 9)):
+    for base in (0, 9):
         w_q, w_k, w_v, w_out = weights[base + 1 : base + 5]
         w_gate, w_up, w_down = weights[base + 6 : base + 9]
-        w_qkv = jnp.concatenate([columns_piece(w) for w in (w_q, w_k, w_v)], axis=1)
-        pair = jnp.concatenate([columns_piece(w_gate), columns_piece(w_up)], axis=1)
+        gains = jnp.stack([weights[base], weights[base + 5]])
+        gains = lax.dynamic_slice_in_dim(gains, core * 96, 96, axis=1)
+        gains = jnp.pad(gains, ((0, 14), (0, ATTN_UNIT - 96)))
         out_piece = lax.ppermute(rows_piece(w_out), AXES, ROWS)
         down_piece = lax.ppermute(rows_piece(w_down), AXES, ROWS)
-        attn = (w_qkv, out_piece) + ((gains,) if index == 0 else ())
-        attn = lax.all_gather(attn, SPREAD, axis=0, tiled=True)
-        feed = lax.all_gather((pair, down_piece), SPREAD, axis=0, tiled=True)
-        if index == 0:
-            gathered_gains = attn[2].transpose(1, 0, 2).reshape(4, width).astype(F32)
-        layers.append((attn[0], attn[1], feed[0], feed[1]))
+        w_qkv = jnp.concatenate([columns_piece(w) for w in (w_q, w_k, w_v)], axis=1)
+        attn = [fold(w_qkv, ATTN_UNIT), fold(out_piece, ATTN_UNIT), gains]
+        attn = spread_gather(jnp.concatenate(attn, axis=0), where)
+        pair = jnp.concatenate([columns_piece(w_gate), columns_piece(w_up)], axis=1)
+        feed = jnp.concatenate([fold(pair, FEED_UNIT), fold(down_piece, FEED_UNIT)], axis=0)
+        feed = lax.all_gather(feed, SPREAD, axis=0, tiled=False)
+        layers.append(
+            (
+                unfold(attn[:, :ATTN_SPLIT], 96).reshape(width, -1),
+                unfold(attn[:, ATTN_SPLIT:-16], 24).reshape(-1, width),
+                attn[:, -16:-14, :96].transpose(1, 0, 2).reshape(2, width).astype(F32),
+                unfold(feed[:, :FEED_SPLIT], 96).reshape(width, -1),
+                unfold(feed[:, FEED_SPLIT:], 64).reshape(-1, width),
+            )
+        )
 
     state = to_lines(tokens[0], z).astype(F32)
     length = lax.ppermute(lengths, AXES, LINES_LENGTH)[0]
@@ -304,9 +405,9 @@
 
     records = []
     for index, window in enumerate((WINDOW, span)):
-        w_qkv, w_out, pair, down = layers[index]
-        attn = (gathered_gains[2 * index], w_qkv, w_out)
-        feed = (gathered_gains[2 * index + 1], pair, down)
+        w_qkv, w_out, gains, pair, down = layers[index]
+        attn = (gains[0], w_qkv, w_out)
+        feed = (gains[1], pair, down)
         state, attn_saved = attention_forward(state, attn, context, window)
         state, feed_saved = feed_forward(state, feed)
         records.append((attn, feed, attn_saved, feed_saved, window))
@@ -318,23 +419,23 @@
         attn, feed, attn_saved, feed_saved, window = records[index]
         base = 9 * index
         grad, gain_grads[2 * index + 1], g_pair, g_down = feed_backward(grad, feed_saved, feed)
-        g_pair, g_down = spread_sum((g_pair, g_down))
-        results[base + 6], results[base + 7] = home_columns(g_pair, (1024, 1024))
-        results[base + 8] = home_rows(g_down)
+        packed = pack(g_pair, g_down, FEED_UNIT)
+        if index:
+            piece = lax.psum_scatter(packed, SPREAD, scatter_dimension=0, tiled=True)[0]
+        else:
+            piece = spread_scatter(packed, where)
+        every = go_home(piece, FEED_SPLIT, where, index)
+        results[base + 6 : base + 9] = home_weights(every, FEED_SPLIT, 64, (1024, 1024))
         grad, gain_grads[2 * index], g_qkv, g_out = attention_backward(
             grad, attn_saved, attn, context, window
         )
-        if index:
-            g_qkv, g_out = spread_sum((g_qkv, g_out))
-        else:
-            g_gain = jnp.stack(gain_grads).astype(BF16).reshape(4, 16, 96).transpose(1, 0, 2)
-            g_qkv, g_out, g_gain = spread_sum((g_qkv, g_out, g_gain))
-            g_gain = lax.all_gather(g_gain[0], ("x", "core"), axis=0, tiled=False).astype(F32)
-            g_gain = g_gain.reshape(4, 2, 4, 96).sum(axis=0).transpose(1, 0, 2).reshape(4, 192)
-        results[base + 1 : base + 4] = home_columns(g_qkv, (384, 192, 192))
-        results[base + 4] = home_rows(g_out)
+        piece = spread_scatter(pack(g_qkv, g_out, ATTN_UNIT), where)
+        every = go_home(piece, ATTN_SPLIT, where, 0)
+        results[base + 1 : base + 5] = home_weights(every, ATTN_SPLIT, 24, (384, 192, 192))
+    gain_sums = butterfly(jnp.stack(gain_grads))
+    gain_sums = lax.dynamic_slice_in_dim(gain_sums, (2 * z + yhi) * 192, 192, axis=1)
     for index, slot in enumerate((0, 5, 9, 14)):
-        results[slot] = g_gain[index]
+        results[slot] = gain_sums[index]
     input_grad = from_lines(grad.astype(BF16), z).astype(F32)[None]
     return (output, input_grad, *results)
 

time: 1430 us -> 1180 us (0.83)
  waiting for transfers between devices: 683 us -> 177 us
  local copies, waits for them, and re-layouts: 114 us -> 344 us
  blocking collectives: 150 us -> 0 us
  starting transfers between devices: 207 us -> 317 us
  other arithmetic: 65.8 us -> 146 us
  matrix products: 187 us -> 162 us
    reduce_scatter x8 -> x1, waiting for transfers between devices: 317 us -> 0.01 us  [body(): piece = lax.psum_scatter(packed, SPREAD, scatter_dimension=0, tiled=True)[0]]
    all_gather x14 -> x3, waiting for transfers between devices: 197 us -> 0.01 us  [the longest x2 0.01 us: body(): feed = lax.all_gather(feed, SPREAD, axis=0, tiled=False)]
    ppermute x13 -> x60, starting transfers between devices: 7.63 us -> 123 us  [the longest x5 30.9 us: ring_stack(): after = lax.ppermute(block, axis, LEFT)]
    all_gather x4 -> x0, blocking collectives: 88 us -> none  [the longest x2 40.2 us: home_rows(): return lax.all_gather(piece, ('x', 'core'), axis=0, tiled=True).astype(F32)]
    another operation x8 -> x16, local copies, waits for them, and re-layouts: 0.36 us -> 67.3 us  [the longest x10 56.5 us: fold_pieces(): block.reshape(pieces, rows, columns // unit, unit).transpose(0, 2, 1, 3)]
    unnamed x1 -> x0, blocking collectives: 62.5 us -> none
    transpose x1 -> x23, local copies, waits for them, and re-layouts: 0.01 us -> 53.3 us  [the longest x9 32.8 us: unfold(): block = block.reshape(lead + (height // rows, rows, unit)).transpose(order)]
    ppermute x13 -> x60, waiting for transfers between devices: 39.4 us -> 87 us  [the longest x5 14.6 us: ring_stack(): before = lax.ppermute(block, axis, RIGHT)]
  transfers between devices with their start and end apart: 124 -> 153, of which waited for: 58 -> 47; matrix products, arithmetic and copies ran while one was open for 20% -> 50% of each run, Pallas kernels for 0% -> 0%
where the time goes in v2:
time: 1180 us; the launch traced here: 1170 us
  local copies, waits for them, and re-layouts  344 us (29%)
  starting transfers between devices  317 us (27%)
  waiting for transfers between devices  177 us (15%)
  matrix products  162 us (14%)
  other arithmetic  146 us (12%)
  between operations  19.1 us (2%)
    unnamed x442, local copies, waits for them, and re-layouts  90.6 us
    another operation x10, local copies, waits for them, and re-layouts, fold_pieces(): block.reshape(pieces, rows, columns // unit, unit).transpose(0, 2, 1, 3)  56.5 us
    ppermute x8, starting transfers between devices, to_lines(): out.append(lax.ppermute(piece, AXES, LINES[k]))  55 us
    transpose x9, local copies, waits for them, and re-layouts, unfold(): block = block.reshape(lead + (height // rows, rows, unit)).transpose(order)  32.8 us
    ppermute x5, starting transfers between devices, ring_stack(): after = lax.ppermute(block, axis, LEFT)  30.9 us
    ppermute x8, waiting for transfers between devices, ring_gather(): far_first = lax.ppermute(from_left[:half], 'x', RIGHT)  30.4 us
    dot_general x2, matrix products, attention_backward(): jnp.einsum('kgqp,pkd->qkgd', grad_raw, keys, preferred_element_type=F32)  29.8 us
    dot_general x2, matrix products, attention_backward(): jnp.einsum('kgqp,qkgd->pkd', grad_raw, queries, preferred_element_type=F32)  29.7 us
  transfers between devices with their start and end apart: 153, of which 47 were waited for; matrix products, arithmetic and copies ran while one was open for 50% of the time, Pallas kernels for 0%

profile of v2, /device:TPU:1, one launch (start us, length us, event | category | flops | bytes accessed | tf_op | source)
XLA Modules:
  0.0 1165.4 jit_solution(3929251346370068729)
XLA Ops:
  16.8 26.4 %collective-permute-start = (bf16[32,1536]{1,0:T(8,128)(2,1)}, bf16[32,1536]{1,0:T(8,128)(2,1)S(1)}, u32[]{:S(2)}, u32[]{:S(2)}) collective-permute-start(bf16[32,1536]{1,0:T(8,128)(2,1)} %get-tuple-element.179), channel_id=1, source_target_pairs={{0,0},{1,8},{2,16},{3,24},{4,32},{5,40},{6,48},{7,56},{8,1},{9,9},... | collective-permute-start | bytes 294920 | tf_op jit(solution)/shard_map/ppermute | solution.py:60
  50.4 8.6 collective-permute-done.31
  66.0 6.8 collective-permute-done.33
  93.8 7.8 collective-permute-done.7
  111.9 11.7 %collective-permute-start.3 = (bf16[32,1536]{1,0:T(8,128)(2,1)}, bf16[32,1536]{1,0:T(8,128)(2,1)S(1)}, u32[]{:S(2)}, u32[]{:S(2)}) collective-permute-start(bf16[32,1536]{1,0:T(8,128)(2,1)} %get-tuple-element.181), channel_id=1, source_target_pairs={{0,48},{1,56},{2,0},{3,8},{4,16},{5,24},{6,32},{7,40},{8,49},{9,57... | collective-permute-start | bytes 294920 | tf_op jit(solution)/shard_map/ppermute | solution.py:60
  225.7 6.1 collective-permute-done.20
  239.4 7.1 collective-permute-start.59
  276.0 7.8 copy.202
  343.4 6.4 reshape_reshape.56
  368.1 7.0 collective-permute-start.41
  424.5 7.8 copy.217
  484.8 11.2 reshape_reshape.66
  524.9 7.3 collective-permute-start.55
  552.1 10.4 collective-permute-start.74
  563.1 6.2 collective-permute-done.73
  578.9 14.7 %fusion.31 = f32[2,96,1024,1]{2,1,3,0:T(8,128)S(1)} fusion(f32[2,1024,512,2]{2,1,3,0:T(8,128)} %fusion.254, bf16[512,2,2,48]{0,3,2,1:T(8,128)(2,1)} %bitcast.786, bf16[512,2,2,48]{0,3,2,1:T(8,128)(2,1)S(1)} %bitcast.784, f32[2,1024,512,2]{2,1,3,0:T(8,128)} %copy-done.28, f32[2,2,512]{2,1,0:T(2,128)} %log_add_fusion.1, pred[512,1024]{0,1:T(8,128)(4,1)} %get-tuple-element.201), kind=kOutput, calls=%fused_computation.72 | convolution fusion | flops 430705664 | bytes 18489344 | tf_op jit(solution)/shard_map/kgqp,qkgd->pkd/dot_general | solution.py:163
  596.6 15.0 %fusion.32 = f32[2,96,2,512]{3,1,2,0:T(8,128)} fusion(bf16[1024,2,96,1]{0,2,3,1:T(8,128)(2,1)} %bitcast.774, f32[2,1024,512,2]{2,1,3,0:T(8,128)} %fusion.254, f32[2,1024,512,2]{2,1,3,0:T(8,128)} %copy-done.28, f32[2,2,512]{2,1,0:T(2,128)} %log_add_fusion.1, pred[512,1024]{0,1:T(8,128)(4,1)} %get-tuple-element.201), kind=kOutput, calls=%fused_computation.73 | convolution fusion | flops 429919232 | bytes 18489344 | tf_op jit(solution)/shard_map/kgqp,pkd->qkgd/dot_general | solution.py:171
  687.2 6.9 convolution_convert_fusion.1
  707.1 11.1 reshape_reshape.62
  752.2 6.0 collective-permute-done.90
  764.2 15.0 %fusion.34 = f32[2,96,1024,1]{2,1,3,0:T(8,128)} fusion(f32[2,1024,512,2]{2,1,3,0:T(8,128)} %fusion.255, bf16[512,2,2,48]{0,3,2,1:T(8,128)(2,1)} %bitcast.781, bf16[512,2,2,48]{0,3,2,1:T(8,128)(2,1)} %bitcast.779, f32[2,1024,512,2]{2,1,3,0:T(8,128)} %copy-done.27, f32[2,2,512]{2,1,0:T(2,128)S(1)} %copy-done.156, pred[512,1024]{0,1:T(8,128)(4,1)} %copy-done.73), kind=kOutput, calls=%fused_computation.75 | convolution fusion | flops 430705664 | bytes 18489344 | tf_op jit(solution)/shard_map/kgqp,qkgd->pkd/dot_general | solution.py:163
  779.2 6.2 fusion.24
  789.2 14.8 %fusion.35 = f32[2,96,2,512]{3,1,2,0:T(8,128)} fusion(bf16[1024,2,96,1]{0,2,3,1:T(8,128)(2,1)} %bitcast.768, f32[2,1024,512,2]{2,1,3,0:T(8,128)} %fusion.255, f32[2,1024,512,2]{2,1,3,0:T(8,128)} %copy-done.27, f32[2,2,512]{2,1,0:T(2,128)S(1)} %copy-done.156, pred[512,1024]{0,1:T(8,128)(4,1)} %copy-done.73), kind=kOutput, calls=%fused_computation.76 | convolution fusion | flops 429919232 | bytes 18489344 | tf_op jit(solution)/shard_map/kgqp,pkd->qkgd/dot_general | solution.py:171
  847.6 6.1 reshape_reshape.60
  923.3 8.4 collective-permute-done.147
  941.9 6.7 collective-permute-start.111
  949.5 15.6 %collective-permute-start.126 = (bf16[576,512]{1,0:T(8,128)(2,1)}, bf16[576,512]{1,0:T(8,128)(2,1)S(1)}, u32[]{:S(2)}, u32[]{:S(2)}) collective-permute-start(bf16[576,512]{1,0:T(8,128)(2,1)} %dynamic-slice_bitcast_fusion.6), channel_id=1, source_target_pairs={{0,1},{1,0},{2,3},{3,2},{4,5},{5,4},{6,7},{7,6},{8,9},{9,8},{10,11... | collective-permute-start | bytes 1769480 | tf_op jit(solution)/shard_map/ppermute | solution.py:290
  973.7 7.9 collective-permute-done.126
  984.8 8.1 collective-permute-done.110
  1006.9 6.5 collective-permute-start.129
  1017.6 11.5 collective-permute-start.116
  1029.1 9.3 collective-permute-start.117
  (1159 shorter events, 838.0 us)
Async XLA Ops:
  7.2 261.4 %all-gather.7.cloned.1.call-start = ((), (), s32[]{:S(2)}) async-start(), calls=%async_computation.2 | async-start | bytes 10027008 | tf_op jit(solution)/shard_map/all_gather | solution.py:368
  12.8 393.4 %all-gather.9.cloned.1.call-start = ((), (), s32[]{:S(2)}) async-start(), calls=%async_computation.3 | async-start | bytes 10027008 | tf_op jit(solution)/shard_map/all_gather | solution.py:368
  13.7 36.3 %collective-permute-start.30 = (bf16[24,1536]{1,0:T(8,128)(2,1)S(1)}, bf16[24,1536]{1,0:T(8,128)(2,1)S(1)}, u32[]{:S(2)}, u32[]{:S(2)}) collective-permute-start(bf16[24,1536]{1,0:T(8,128)(2,1)S(1)} %constant_dynamic-slice_fusion.10), channel_id=1, source_target_pairs={{0,0},{1,4},{2,16},{3,20},{4,32},{5,36},{6,48},{7,52},{8,8},{9,12}... | collective-permute-start | bytes 221192 | tf_op jit(solution)/shard_map/ppermute | solution.py:361
  15.3 49.4 %collective-permute-start.4 = (bf16[24,1536]{1,0:T(8,128)(2,1)S(1)}, bf16[24,1536]{1,0:T(8,128)(2,1)S(1)}, u32[]{:S(2)}, u32[]{:S(2)}) collective-permute-start(bf16[24,1536]{1,0:T(8,128)(2,1)S(1)} %constant_dynamic-slice_fusion.13), channel_id=1, source_target_pairs={{0,0},{1,4},{2,16},{3,20},{4,32},{5,36},{6,48},{7,52},{8,8},{9,12}... | collective-permute-start | bytes 221192 | tf_op jit(solution)/shard_map/ppermute | solution.py:361
  16.8 114.0 %collective-permute-start = (bf16[32,1536]{1,0:T(8,128)(2,1)}, bf16[32,1536]{1,0:T(8,128)(2,1)S(1)}, u32[]{:S(2)}, u32[]{:S(2)}) collective-permute-start(bf16[32,1536]{1,0:T(8,128)(2,1)} %get-tuple-element.179), channel_id=1, source_target_pairs={{0,0},{1,8},{2,16},{3,24},{4,32},{5,40},{6,48},{7,56},{8,1},{9,9},... | collective-permute-start | bytes 294920 | tf_op jit(solution)/shard_map/ppermute | solution.py:60
  82.0 52.0 %collective-permute-start.1 = (bf16[32,1536]{1,0:T(8,128)(2,1)}, bf16[32,1536]{1,0:T(8,128)(2,1)S(1)}, u32[]{:S(2)}, u32[]{:S(2)}) collective-permute-start(bf16[32,1536]{1,0:T(8,128)(2,1)} %get-tuple-element.180), channel_id=1, source_target_pairs={{0,16},{1,24},{2,32},{3,40},{4,48},{5,56},{6,0},{7,8},{8,17},{9,25... | collective-permute-start | bytes 294920 | tf_op jit(solution)/shard_map/ppermute | solution.py:60
  88.8 50.6 %collective-permute-start.36 = (bf16[4,2,448,256]{3,2,1,0:T(8,128)(2,1)}, bf16[4,2,448,256]{3,2,1,0:T(8,128)(2,1)}, u32[]{:S(2)}, u32[]{:S(2)}) collective-permute-start(bf16[4,2,448,256]{3,2,1,0:T(8,128)(2,1)} %get-tuple-element.89), channel_id=1, source_target_pairs={{0,8},{8,0},{1,9},{9,1},{2,10},{10,2},{3,11},{11,3},{4,12},{12,4},... | collective-permute-start | bytes 5505032 | tf_op jit(solution)/shard_map/ppermute | solution.py:264
  136.0 55.8 %collective-permute-start.50 = (bf16[64,1536]{1,0:T(8,128)(2,1)}, bf16[64,1536]{1,0:T(8,128)(2,1)}, u32[]{:S(2)}, u32[]{:S(2)}) collective-permute-start(bf16[64,1536]{1,0:T(8,128)(2,1)} %constant_dynamic-slice_fusion.8), channel_id=1, source_target_pairs={{0,0},{1,4},{2,16},{3,20},{4,32},{5,36},{6,48},{7,52},{8,8},{9,12}... | collective-permute-start | bytes 589832 | tf_op jit(solution)/shard_map/ppermute | solution.py:362
  194.0 719.3 %reduce-scatter.2.cloned.1.call-start = ((), (), s32[]{:S(2)}) async-start(), calls=%async_computation.1 | async-start | bytes 10027008 | tf_op jit(solution)/shard_map/reduce_scatter | solution.py:424
  246.5 70.1 %collective-permute-start.62 = (bf16[32,1536]{1,0:T(8,128)(2,1)S(1)}, bf16[32,1536]{1,0:T(8,128)(2,1)}, u32[]{:S(2)}, u32[]{:S(2)}) collective-permute-start(bf16[32,1536]{1,0:T(8,128)(2,1)S(1)} %get-tuple-element.171), channel_id=1, source_target_pairs={{0,48},{1,56},{2,0},{3,8},{4,16},{5,24},{6,32},{7,40},{8,49},{9,57... | collective-permute-start | bytes 294920 | tf_op jit(solution)/shard_map/ppermute | solution.py:60
  249.4 65.7 %collective-permute-start.61 = (bf16[32,1536]{1,0:T(8,128)(2,1)S(1)}, bf16[32,1536]{1,0:T(8,128)(2,1)}, u32[]{:S(2)}, u32[]{:S(2)}) collective-permute-start(bf16[32,1536]{1,0:T(8,128)(2,1)S(1)} %get-tuple-element.172), channel_id=1, source_target_pairs={{0,32},{1,40},{2,48},{3,56},{4,0},{5,8},{6,16},{7,24},{8,33},{9,41... | collective-permute-start | bytes 294920 | tf_op jit(solution)/shard_map/ppermute | solution.py:60
  252.7 55.4 %collective-permute-start.60 = (bf16[32,1536]{1,0:T(8,128)(2,1)S(1)}, bf16[32,1536]{1,0:T(8,128)(2,1)}, u32[]{:S(2)}, u32[]{:S(2)}) collective-permute-start(bf16[32,1536]{1,0:T(8,128)(2,1)S(1)} %get-tuple-element.173), channel_id=1, source_target_pairs={{0,16},{1,24},{2,32},{3,40},{4,48},{5,56},{6,0},{7,8},{8,17},{9,25... | collective-permute-start | bytes 294920 | tf_op jit(solution)/shard_map/ppermute | solution.py:60
  330.6 74.2 %collective-permute-start.66 = (bf16[64,1536]{1,0:T(8,128)(2,1)}, bf16[64,1536]{1,0:T(8,128)(2,1)S(1)}, u32[]{:S(2)}, u32[]{:S(2)}) collective-permute-start(bf16[64,1536]{1,0:T(8,128)(2,1)} %slice.1001), channel_id=1, source_target_pairs={{0,48},{16,0},{32,16},{48,32},{1,49},{17,1},{33,17},{49,33},{2,50}... | collective-permute-start | bytes 589832 | tf_op jit(solution)/shard_map/ppermute | solution.py:78
  334.7 62.4 %collective-permute-start.65 = (bf16[64,1536]{1,0:T(8,128)(2,1)}, bf16[64,1536]{1,0:T(8,128)(2,1)}, u32[]{:S(2)}, u32[]{:S(2)}) collective-permute-start(bf16[64,1536]{1,0:T(8,128)(2,1)} %slice.1000), channel_id=1, source_target_pairs={{0,16},{16,32},{32,48},{48,0},{1,17},{17,33},{33,49},{49,1},{2,18}... | collective-permute-start | bytes 589832 | tf_op jit(solution)/shard_map/ppermute | solution.py:77
  465.3 35.4 %collective-permute-start.67 = (bf16[64,1536]{1,0:T(8,128)(2,1)}, bf16[64,1536]{1,0:T(8,128)(2,1)}, u32[]{:S(2)}, u32[]{:S(2)}) collective-permute-start(bf16[64,1536]{1,0:T(8,128)(2,1)} %get-tuple-element.116), channel_id=1, source_target_pairs={{0,16},{16,32},{32,48},{48,0},{1,17},{17,33},{33,49},{49,1},{2,18}... | collective-permute-start | bytes 589832 | tf_op jit(solution)/shard_map/ppermute | solution.py:89
  465.3 35.4 %collective-permute-start.69 = (bf16[64,1536]{1,0:T(8,128)(2,1)}, bf16[64,1536]{1,0:T(8,128)(2,1)}, u32[]{:S(2)}, u32[]{:S(2)}) collective-permute-start(bf16[64,1536]{1,0:T(8,128)(2,1)} %get-tuple-element.117), channel_id=1, source_target_pairs={{0,48},{16,0},{32,16},{48,32},{1,49},{17,1},{33,17},{49,33},{2,50}... | collective-permute-start | bytes 589832 | tf_op jit(solution)/shard_map/ppermute | solution.py:90
  513.5 621.5 %all-gather.11.cloned.1.call-start = ((), (), s32[]{:S(2)}) async-start(), calls=%async_computation.4 | async-start | bytes 5308416 | tf_op jit(solution)/shard_map/all_gather | solution.py:298
  539.5 89.0 %collective-permute-start.58 = (bf16[32,1536]{1,0:T(8,128)(2,1)S(1)}, bf16[32,1536]{1,0:T(8,128)(2,1)}, u32[]{:S(2)}, u32[]{:S(2)}) collective-permute-start(bf16[32,1536]{1,0:T(8,128)(2,1)S(1)} %get-tuple-element.175), channel_id=1, source_target_pairs={{48,0},{56,1},{0,2},{8,3},{16,4},{24,5},{32,6},{40,7},{49,8},{57,9... | collective-permute-start | bytes 294920 | tf_op jit(solution)/shard_map/ppermute | solution.py:68
  539.5 79.7 %collective-permute-start.57 = (bf16[32,1536]{1,0:T(8,128)(2,1)}, bf16[32,1536]{1,0:T(8,128)(2,1)}, u32[]{:S(2)}, u32[]{:S(2)}) collective-permute-start(bf16[32,1536]{1,0:T(8,128)(2,1)} %get-tuple-element.176), channel_id=1, source_target_pairs={{32,0},{40,1},{48,2},{56,3},{0,4},{8,5},{16,6},{24,7},{33,8},{41,9... | collective-permute-start | bytes 294920 | tf_op jit(solution)/shard_map/ppermute | solution.py:68
  662.0 70.7 %collective-permute-start.134 = (bf16[4,2,432,256]{3,2,1,0:T(8,128)(2,1)}, bf16[4,2,432,256]{3,2,1,0:T(8,128)(2,1)}, u32[]{:S(2)}, u32[]{:S(2)}) collective-permute-start(bf16[4,2,432,256]{3,2,1,0:T(8,128)(2,1)} %fusion.58), channel_id=1, source_target_pairs={{0,8},{8,0},{1,9},{9,1},{2,10},{10,2},{3,11},{11,3},{4,12},{12,4},... | collective-permute-start | bytes 5308424 | tf_op jit(solution)/shard_map/ppermute | solution.py:275
  695.0 36.4 %collective-permute-start.87 = (bf16[128,1536]{1,0:T(8,128)(2,1)}, bf16[128,1536]{1,0:T(8,128)(2,1)S(1)}, u32[]{:S(2)}, u32[]{:S(2)}) collective-permute-start(bf16[128,1536]{1,0:T(8,128)(2,1)} %pad_maximum_fusion.49), channel_id=1, source_target_pairs={{0,48},{16,0},{32,16},{48,32},{1,49},{17,1},{33,17},{49,33},{2,50}... | collective-permute-start | bytes 1179656 | tf_op jit(solution)/shard_map/ppermute | solution.py:94
  696.1 35.2 %collective-permute-start.85 = (bf16[128,1536]{1,0:T(8,128)(2,1)}, bf16[128,1536]{1,0:T(8,128)(2,1)}, u32[]{:S(2)}, u32[]{:S(2)}) collective-permute-start(bf16[128,1536]{1,0:T(8,128)(2,1)} %pad_maximum_fusion.48), channel_id=1, source_target_pairs={{0,16},{16,32},{32,48},{48,0},{1,17},{17,33},{33,49},{49,1},{2,18}... | collective-permute-start | bytes 1179656 | tf_op jit(solution)/shard_map/ppermute | solution.py:93
  728.3 147.5 %collective-permute-start.121 = (bf16[4,2,576,512]{3,2,1,0:T(8,128)(2,1)}, bf16[4,2,576,512]{3,2,1,0:T(8,128)(2,1)}, u32[]{:S(2)}, u32[]{:S(2)}) collective-permute-start(bf16[4,2,576,512]{3,2,1,0:T(8,128)(2,1)} %fusion.21), channel_id=1, source_target_pairs={{0,8},{8,0},{1,9},{9,1},{2,10},{10,2},{3,11},{11,3},{4,12},{12,4},... | collective-permute-start | bytes 14155784 | tf_op jit(solution)/shard_map/ppermute | solution.py:275
  744.3 63.2 %collective-permute-start.138 = (bf16[2,432,256]{2,1,0:T(8,128)(2,1)}, bf16[2,432,256]{2,1,0:T(8,128)(2,1)}, u32[]{:S(2)}, u32[]{:S(2)}) collective-permute-start(bf16[2,432,256]{2,1,0:T(8,128)(2,1)} %pad_maximum_fusion.27), channel_id=1, source_target_pairs={{0,6},{2,0},{4,2},{6,4},{1,7},{3,1},{5,3},{7,5},{8,14},{10,8},{12,... | collective-permute-start | bytes 1327112 | tf_op jit(solution)/shard_map/ppermute | solution.py:286
  747.0 60.5 %collective-permute-start.136 = (bf16[2,432,256]{2,1,0:T(8,128)(2,1)}, bf16[2,432,256]{2,1,0:T(8,128)(2,1)}, u32[]{:S(2)}, u32[]{:S(2)}) collective-permute-start(bf16[2,432,256]{2,1,0:T(8,128)(2,1)} %pad_maximum_fusion.26), channel_id=1, source_target_pairs={{0,2},{2,4},{4,6},{6,0},{1,3},{3,5},{5,7},{7,1},{8,10},{10,12},{12... | collective-permute-start | bytes 1327112 | tf_op jit(solution)/shard_map/ppermute | solution.py:285
  786.4 34.2 %collective-permute-start.92 = (bf16[512,384]{0,1:T(8,128)(2,1)}, bf16[512,384]{0,1:T(8,128)(2,1)}, u32[]{:S(2)}, u32[]{:S(2)}) collective-permute-start(bf16[512,384]{0,1:T(8,128)(2,1)} %fusion.92), channel_id=1, source_target_pairs={{0,8},{8,0},{1,9},{9,1},{2,10},{10,2},{3,11},{11,3},{4,12},{12,4},... | collective-permute-start | bytes 1179656 | tf_op jit(solution)/shard_map/ppermute | solution.py:170
  831.5 37.1 %collective-permute-start.96 = (bf16[128,1536]{1,0:T(8,128)(2,1)}, bf16[128,1536]{1,0:T(8,128)(2,1)}, u32[]{:S(2)}, u32[]{:S(2)}) collective-permute-start(bf16[128,1536]{1,0:T(8,128)(2,1)} %pad_maximum_fusion.52), channel_id=1, source_target_pairs={{0,48},{16,0},{32,16},{48,32},{1,49},{17,1},{33,17},{49,33},{2,50}... | collective-permute-start | bytes 1179656 | tf_op jit(solution)/shard_map/ppermute | solution.py:94
  866.2 48.8 %collective-permute-start.108 = (bf16[4,2,432,256]{3,2,1,0:T(8,128)(2,1)}, bf16[4,2,432,256]{3,2,1,0:T(8,128)(2,1)}, u32[]{:S(2)}, u32[]{:S(2)}) collective-permute-start(bf16[4,2,432,256]{3,2,1,0:T(8,128)(2,1)} %fusion.62), channel_id=1, source_target_pairs={{0,8},{8,0},{1,9},{9,1},{2,10},{10,2},{3,11},{11,3},{4,12},{12,4},... | collective-permute-start | bytes 5308424 | tf_op jit(solution)/shard_map/ppermute | solution.py:275
  911.5 129.2 %collective-permute-start.146 = (bf16[4,432,256]{2,1,0:T(8,128)(2,1)}, bf16[4,432,256]{2,1,0:T(8,128)(2,1)}, u32[]{:S(2)}, u32[]{:S(2)}) collective-permute-start(bf16[4,432,256]{2,1,0:T(8,128)(2,1)} %get-tuple-element.149), channel_id=1, source_target_pairs={{0,8},{8,0},{1,9},{9,1},{2,10},{10,2},{3,11},{11,3},{4,12},{12,4},... | collective-permute-start | bytes 2654216 | tf_op jit(solution)/shard_map/ppermute | solution.py:302
  931.7 34.4 %collective-permute-start.104 = (f32[4,1536]{1,0:T(4,128)}, f32[4,1536]{1,0:T(4,128)S(1)}, u32[]{:S(2)}, u32[]{:S(2)}) collective-permute-start(f32[4,1536]{1,0:T(4,128)} %add.1126), channel_id=1, source_target_pairs={{0,2},{2,0},{4,6},{6,4},{1,3},{3,1},{5,7},{7,5},{8,10},{10,8},{12,... | collective-permute-start | bytes 73736 | tf_op jit(solution)/shard_map/ppermute | solution.py:327
  932.5 34.5 %collective-permute-start.109 = (bf16[1,432,256]{2,1,0:T(8,128)(2,1)}, bf16[1,432,256]{2,1,0:T(8,128)(2,1)}, u32[]{:S(2)}, u32[]{:S(2)}) collective-permute-start(bf16[1,432,256]{2,1,0:T(8,128)(2,1)} %get-tuple-element.100), channel_id=1, source_target_pairs={{0,2},{2,4},{4,6},{6,0},{1,3},{3,5},{5,7},{7,1},{8,10},{10,12},{12... | collective-permute-start | bytes 663560 | tf_op jit(solution)/shard_map/ppermute | solution.py:281
  1050.0 50.2 %collective-permute-start.133 = (bf16[4,576,512]{2,1,0:T(8,128)(2,1)}, bf16[4,576,512]{2,1,0:T(8,128)(2,1)}, u32[]{:S(2)}, u32[]{:S(2)}) collective-permute-start(bf16[4,576,512]{2,1,0:T(8,128)(2,1)} %get-tuple-element.87), channel_id=1, source_target_pairs={{0,8},{8,0},{1,9},{9,1},{2,10},{10,2},{3,11},{11,3},{4,12},{12,4},... | collective-permute-start | bytes 7077896 | tf_op jit(solution)/shard_map/ppermute | solution.py:302
  (320 other events, 4381.6 us)
Sparse Core Ops, SparseCore 0:
  12.9 109.5 all-gather.6
  194.1 78.4 all-gather.8
  513.6 112.0 reduce-scatter.1
  949.6 50.2 all-gather.10

commit v3 on v1

v3 whole, which is shorter than its diff:
```python
import functools
import jax
import jax.numpy as jnp
from jax import lax
from jax.experimental import pallas as pl
from jax.experimental.pallas import tpu as pltpu
from jax.sharding import Mesh
from jax.sharding import PartitionSpec as P

F32 = jnp.float32
BF16 = jnp.bfloat16
HEAD_DIM = 96
NEGATIVE = -1e30
MIB = 1 << 20

OFFSETS = (0, 128, 256, 384, 448)
SIZES_OF = (128, 128, 128, 64, 64)


def params(mib, semantics=None):
    return pltpu.CompilerParams(vmem_limit_bytes=mib * MIB, dimension_semantics=semantics)


def cost(flops, nbytes, transcendentals=0):
    return pl.CostEstimate(
        flops=int(flops), bytes_accessed=int(nbytes), transcendentals=int(transcendentals)
    )


def fill(target, refs):
    start = 0
    for ref in refs:
        rows = ref.shape[0]
        target[start : start + rows, :] = ref[...]
        start += rows


def nn(a, b):
    return lax.dot_general(a, b, (((1,), (0,)), ((), ())), preferred_element_type=F32)


def nt(a, b):
    return lax.dot_general(a, b, (((1,), (1,)), ((), ())), preferred_element_type=F32)


def tn(a, b):
    return lax.dot_general(a, b, (((0,), (0,)), ((), ())), preferred_element_type=F32)


def whole(shape):
    return pl.BlockSpec(shape, lambda *_: (0,) * len(shape))


PIECES = [whole((rows, 1536)) for rows in SIZES_OF]
PARTIAL_SHAPES = [
    jax.ShapeDtypeStruct((128, 1536), F32),
    jax.ShapeDtypeStruct((128, 1536), F32),
    jax.ShapeDtypeStruct((128, 1536), F32),
    jax.ShapeDtypeStruct((128, 1536), BF16),
]
PARTIALS = [whole((128, 1536))] * 4


def emit(total, outs):
    for place, out in enumerate(outs):
        out[...] = total[128 * place : 128 * (place + 1), :].astype(out.dtype)


def down_parts(block):
    left = block[:, 0:64, :].reshape(256, 1024)
    right = jnp.concatenate([block[:, 64:96, 0:512], block[:, 64:96, 512:1024]], axis=1)
    return left, right.reshape(256, 512)


def feed_forward_kernel(*refs):
    pieces, (wg, wu, wd), outs = refs[:5], refs[5:8], refs[8:12]
    gate, up, hidden, flat, total = refs[12:]
    step = pl.program_id(0)

    @pl.when(step == 0)
    def _():
        fill(flat, pieces)

    rows = flat[...]
    g = nn(rows, wg[...])
    u = nn(rows, wu[...])
    gate[...] = g
    up[...] = u
    h = (g * jax.nn.sigmoid(g) * u).astype(BF16)
    hidden[...] = h
    left, right = down_parts(wd[...])
    left, right = nn(h, left), nn(h, right)

    @pl.when(step == 0)
    def _():
        total[:, :1024] = left
        total[:, 1024:] = right

    @pl.when(step > 0)
    def _():
        total[:, :1024] += left
        total[:, 1024:] += right

    @pl.when(step == 3)
    def _():
        emit(total, outs)


def feed_specs():
    return [
        pl.BlockSpec((1536, 256), lambda b: (0, b)),
        pl.BlockSpec((1536, 256), lambda b: (0, 4 + b)),
        pl.BlockSpec((4, 96, 1024), lambda b: (b, 0, 2)),
    ]


def column_block(rows):
    return pl.BlockSpec((rows, 256), lambda b: (0, b))


def feed_forward_call(pieces, packed):
    flat_packed = packed.reshape(1536, 3072)
    return pl.pallas_call(
        feed_forward_kernel,
        grid=(4,),
        in_specs=PIECES + feed_specs(),
        out_specs=PARTIALS + [column_block(512)] * 3,
        out_shape=PARTIAL_SHAPES
        + [
            jax.ShapeDtypeStruct((512, 1024), F32),
            jax.ShapeDtypeStruct((512, 1024), F32),
            jax.ShapeDtypeStruct((512, 1024), BF16),
        ],
        scratch_shapes=[pltpu.VMEM((512, 1536), BF16), pltpu.VMEM((512, 1536), F32)],
        compiler_params=params(40),
        cost_estimate=cost(4.9e9, 18e6),
        name="feed_forward",
    )(*pieces, flat_packed, flat_packed, packed)


def feed_backward_kernel(*refs):
    pieces, (wg, wu, wd, gate, up), outs = refs[:5], refs[5:10], refs[10:14]
    low_gate, low_up, flat, total = refs[14:]
    step = pl.program_id(0)

    @pl.when(step == 0)
    def _():
        fill(flat, pieces)

    rows = flat[...]
    left, right = down_parts(wd[...])
    grad = nt(rows[:, :1024], left) + nt(rows[:, 1024:], right)
    g = gate[...]
    s = jax.nn.sigmoid(g)
    a = (grad * up[...] * s * (1.0 + g * (1.0 - s))).astype(BF16)
    b = (grad * (g * s)).astype(BF16)
    low_gate[...] = a
    low_up[...] = b
    part = nt(a, wg[...]) + nt(b, wu[...])

    @pl.when(step == 0)
    def _():
        total[...] = part

    @pl.when(step > 0)
    def _():
        total[...] += part

    @pl.when(step == 3)
    def _():
        emit(total, outs)


def feed_backward_call(pieces, packed, gate, up):
    flat_packed = packed.reshape(1536, 3072)
    return pl.pallas_call(
        feed_backward_kernel,
        grid=(4,),
        in_specs=PIECES + feed_specs() + [column_block(512)] * 2,
        out_specs=PARTIALS + [column_block(512)] * 2,
        out_shape=PARTIAL_SHAPES + [jax.ShapeDtypeStruct((512, 1024), BF16)] * 2,
        scratch_shapes=[pltpu.VMEM((512, 1536), BF16), pltpu.VMEM((512, 1536), F32)],
        compiler_params=params(40),
        cost_estimate=cost(4.9e9, 20e6),
        name="feed_backward",
    )(*pieces, flat_packed, flat_packed, packed, gate, up)


def store_halves(side, mine, theirs, even, odd, rows, columns):
    @pl.when(side == 0)
    def _():
        mine[:, rows, columns] = even
        theirs[:, rows, columns] = odd

    @pl.when(side != 0)
    def _():
        mine[:, rows, columns] = odd
        theirs[:, rows, columns] = even


def feed_weights_kernel(side_ref, *refs):
    flats, grads = refs[:5], refs[5:10]
    low_gate, low_up, hidden, mine, theirs, flat_t, hidden_t, grad = refs[10:]
    step = pl.program_id(0)
    side = side_ref[0]

    @pl.when(step == 0)
    def _():
        start = 0
        for ref in flats:
            n = ref.shape[0]
            flat_t[:, start : start + n] = ref[...].T
            start += n

    @pl.when(step == 4)
    def _():
        hidden_t[...] = hidden[...].T
        fill(grad, grads)

    def columns(block):
        out = nn(flat_t[...], block).astype(BF16).reshape(8, 192, 256)
        store_halves(
            side, mine, theirs, out[:, :96], out[:, 96:], slice(0, 96), slice(0, 256)
        )

    @pl.when(step < 4)
    def _():
        columns(low_gate[...])

    @pl.when((step >= 4) & (step < 8))
    def _():
        columns(low_up[...])

    for q in range(4):

        @pl.when(step == 8 + q)
        def _():
            top = nn(hidden_t[...], grad[:, 256 * q : 256 * (q + 1)]).astype(BF16)
            top = top.reshape(8, 128, 256)
            store_halves(
                side, mine, theirs, top[:, :64], top[:, 64:], slice(0, 64), slice(0, 256)
            )
            half = 32 * (q // 2)
            some = hidden_t[...].reshape(16, 64, 512)[:, half : half + 32].reshape(512, 512)
            start = 1024 + 256 * (q % 2)
            low = nn(some, grad[:, start : start + 256]).astype(BF16).reshape(8, 64, 256)
            store_halves(
                side, mine, theirs, low[:, :32], low[:, 32:], slice(64, 96), slice(0, 256)
            )


def feed_weights_call(side, flats, grads, low_gate, low_up, hidden):
    block = pl.BlockSpec((8, 96, 256), lambda b, s: (0, 0, b))
    shape = jax.ShapeDtypeStruct((8, 96, 3072), BF16)
    spec = pltpu.PrefetchScalarGridSpec(
        num_scalar_prefetch=1,
        grid=(12,),
        in_specs=PIECES
        + PIECES
        + [
            pl.BlockSpec((512, 256), lambda b, s: (0, jnp.minimum(b, 3))),
            pl.BlockSpec((512, 256), lambda b, s: (0, jnp.clip(b - 4, 0, 3))),
            whole((512, 1024)),
        ],
        out_specs=[block, block],
        scratch_shapes=[
            pltpu.VMEM((1536, 512), BF16),
            pltpu.VMEM((1024, 512), BF16),
            pltpu.VMEM((512, 1536), BF16),
        ],
    )
    return pl.pallas_call(
        feed_weights_kernel,
        grid_spec=spec,
        out_shape=[shape, shape],
        compiler_params=params(40),
        cost_estimate=cost(4.9e9, 18e6),
        name="feed_weights",
    )(side, *flats, *grads, low_gate, low_up, hidden)


def piece_specs(pieces):
    return [whole(item.shape) for item in pieces]


def turn_columns(block, cosine, sine):
    out = []
    for start in range(0, block.shape[1], HEAD_DIM):
        a = block[:, start : start + 48]
        b = block[:, start + 48 : start + HEAD_DIM]
        out.append(a * cosine - b * sine)
        out.append(b * cosine + a * sine)
    return jnp.concatenate(out, axis=1)


def project_kernel(raw, count, *refs):
    pieces, (gain, weight, cosine, sine, queries, pair) = refs[:count], refs[count : count + 6]
    if raw:
        flat = refs[-1]
        start = 0
        for ref in pieces:
            n = ref.shape[0]
            rows = ref[...].astype(F32)
            scale = lax.rsqrt(jnp.mean(rows * rows, axis=-1, keepdims=True) + 1e-05)
            flat[start : start + n, :] = (rows * scale * gain[...]).astype(BF16)
            start += n
    else:
        flat = refs[-1]
        fill(flat, pieces)
    both = nn(flat[...], weight[...])
    cos, sin = cosine[...], sine[...]
    queries[...] = turn_columns(both[:, :384], cos, sin).astype(BF16)
    keys = turn_columns(both[:, 384:576], cos, sin)
    pair[...] = jnp.concatenate([keys, both[:, 576:768]], axis=1).astype(BF16)


def project_call(raw, pieces, gain, packed, cosine, sine):
    wide = packed.shape[-1]
    shape = jax.ShapeDtypeStruct((512, 384), BF16)
    flat_shape = jax.ShapeDtypeStruct((512, 1536), BF16)
    return pl.pallas_call(
        functools.partial(project_kernel, raw, len(pieces)),
        grid=(1,),
        in_specs=piece_specs(pieces)
        + [whole((1, 1536)), whole((1536, 768)), whole((512, 48)), whole((512, 48))],
        out_specs=[whole((512, 384))] * 2 + ([whole((512, 1536))] if raw else []),
        out_shape=[shape, shape] + ([flat_shape] if raw else []),
        scratch_shapes=[] if raw else [pltpu.VMEM((512, 1536), BF16)],
        compiler_params=params(40),
        cost_estimate=cost(1.3e9, 6e6),
        name="project",
    )(*pieces, gain.reshape(1, 1536), packed.reshape(1536, wide), cosine, sine)


def fill_bias(bias, length, places, key_places, window):
    gap = places[...] - key_places[...]
    inside = (key_places[...] < length) & (gap >= 0) & (gap < window)
    bias[...] = jnp.where(inside | (gap == 0), 0.0, NEGATIVE)


def both_rows(own, other, start):
    return jnp.concatenate(
        [own[:, start : start + HEAD_DIM], other[:, start : start + HEAD_DIM]], axis=0
    )


def attend_kernel(window, length, queries, own, other, places, key_places, w_out, *refs):
    outs, (mixed, log_total, total, bias) = refs[:4], refs[4:]
    fill_bias(bias, length[0], places, key_places, window)
    sums = []
    stats = []
    for head in range(4):
        if head % 2 == 0:
            keys = both_rows(own[...], other[...], HEAD_DIM * (head // 2))
            values = both_rows(own[...], other[...], 192 + HEAD_DIM * (head // 2)).T
        query = queries[:, HEAD_DIM * head : HEAD_DIM * (head + 1)]
        scores = nt(keys, query) * HEAD_DIM ** (-0.5) + bias[...]
        peak = jnp.max(scores, axis=0, keepdims=True)
        probs = jnp.exp(scores - peak)
        totals = jnp.sum(probs, axis=0, keepdims=True)
        part = nn(values, probs.astype(BF16)) / totals
        sums.append(part.astype(BF16).astype(F32).T.astype(BF16))
        stats.append(peak + jnp.log(totals))
        for block in range(4):
            cols = slice(384 * block, 384 * (block + 1))
            value = nn(sums[-1], w_out[4 * head + block])
            if head == 0:
                total[:, cols] = value
            else:
                total[:, cols] += value
    mixed[...] = jnp.concatenate(sums, axis=1)
    log_total[...] = jnp.concatenate(stats + stats, axis=0)
    emit(total, outs)


def line_specs():
    return [whole((512, 384))] * 3 + [whole((1, 512)), whole((1024, 1))]


def out_spec():
    return pl.BlockSpec((16, 96, 384), lambda *_: (0, 0, 2))


def attend_call(window, length, queries, own, other, places, key_places, packed):
    return pl.pallas_call(
        functools.partial(attend_kernel, window),
        grid=(1,),
        in_specs=[pl.BlockSpec(memory_space=pltpu.SMEM)] + line_specs() + [out_spec()],
        out_specs=PARTIALS + [whole((512, 384)), whole((8, 512))],
        out_shape=PARTIAL_SHAPES
        + [jax.ShapeDtypeStruct((512, 384), BF16), jax.ShapeDtypeStruct((8, 512), F32)],
        scratch_shapes=[pltpu.VMEM((512, 1536), F32), pltpu.VMEM((1024, 512), F32)],
        compiler_params=params(48),
        cost_estimate=cost(3e9, 6e6, 2e6),
        name="attend",
    )(length, queries, own, other, places, key_places, packed)


def attend_backward_kernel(window, length, *refs):
    pieces, refs = refs[:5], refs[5:]
    queries, own, other, places, key_places, w_out, log_total, cosine, sine = refs[:9]
    low_queries, pair_own, pair_other, grad, bias = refs[9:]
    fill(grad, pieces)
    fill_bias(bias, length[0], places, key_places, window)
    cos, sin = cosine[...], sine[...]
    lows = []
    key_sums = []
    value_sums = []
    for head in range(4):
        if head % 2 == 0:
            keys = both_rows(own[...], other[...], HEAD_DIM * (head // 2))
            values = both_rows(own[...], other[...], 192 + HEAD_DIM * (head // 2))
            keys_t = keys.T
        query = queries[:, HEAD_DIM * head : HEAD_DIM * (head + 1)]
        mixed = nt(grad[:, :384], w_out[4 * head])
        for block in range(1, 4):
            mixed += nt(grad[:, 384 * block : 384 * (block + 1)], w_out[4 * head + block])
        mixed = mixed.astype(BF16)
        scores = nt(keys, query) * HEAD_DIM ** (-0.5) + bias[...]
        probs = jnp.exp(scores - log_total[head : head + 1, :])
        slopes = nt(values, mixed)
        inner = jnp.sum(probs * slopes, axis=0, keepdims=True)
        raw = (probs * (slopes - inner) * HEAD_DIM ** (-0.5)).astype(BF16)
        key_part = nn(raw, query)
        value_part = nn(probs.astype(BF16), mixed)
        if head % 2 == 0:
            key_sums.append(key_part)
            value_sums.append(value_part)
        else:
            key_sums[-1] += key_part
            value_sums[-1] += value_part
        turned = nn(keys_t, raw)
        a, b = turned[:48], turned[48:]
        turned = jnp.concatenate([a * cos + b * sin, b * cos - a * sin], axis=0)
        lows.append(turned.T.astype(BF16))
    low_queries[...] = jnp.concatenate(lows, axis=1)
    both = jnp.concatenate(key_sums + value_sums, axis=1)
    pair_own[...] = both[:512]
    pair_other[...] = both[512:].astype(BF16)


def attend_backward_call(
    window, length, pieces, queries, own, other, places, key_places, packed, log_total, cosine, sine
):
    return pl.pallas_call(
        functools.partial(attend_backward_kernel, window),
        grid=(1,),
        in_specs=[pl.BlockSpec(memory_space=pltpu.SMEM)]
        + PIECES
        + line_specs()
        + [out_spec(), whole((8, 512)), whole((48, 512)), whole((48, 512))],
        out_specs=[whole((512, 384))] * 3,
        out_shape=[
            jax.ShapeDtypeStruct((512, 384), BF16),
            jax.ShapeDtypeStruct((512, 384), F32),
            jax.ShapeDtypeStruct((512, 384), BF16),
        ],
        scratch_shapes=[pltpu.VMEM((512, 1536), BF16), pltpu.VMEM((1024, 512), F32)],
        compiler_params=params(52),
        cost_estimate=cost(6e9, 6e6, 2e6),
        name="attend_backward",
    )(
        length,
        *pieces,
        queries,
        own,
        other,
        places,
        key_places,
        packed,
        log_total,
        cosine,
        sine,
    )


def unproject_kernel(low_queries, pair_own, pair_came, cosine, sine, weight, *refs):
    outs, low = refs[:4], refs[4]
    both = pair_own[...] + pair_came[...].astype(F32)
    keys = turn_columns(both[:, :192], cosine[...], -sine[...])
    rows = jnp.concatenate(
        [low_queries[...], keys.astype(BF16), both[:, 192:].astype(BF16)], axis=1
    )
    low[...] = rows
    emit(nt(rows, weight[...]), outs)


def unproject_call(low_queries, pair_own, pair_came, cosine, sine, packed):
    wide = packed.shape[-1]
    return pl.pallas_call(
        unproject_kernel,
        grid=(1,),
        in_specs=[whole((512, 384))] * 3 + [whole((512, 48))] * 2 + [whole((1536, 768))],
        out_specs=PARTIALS + [whole((512, 768))],
        out_shape=PARTIAL_SHAPES + [jax.ShapeDtypeStruct((512, 768), BF16)],
        compiler_params=params(40),
        cost_estimate=cost(1.3e9, 7e6),
        name="unproject",
    )(low_queries, pair_own, pair_came, cosine, sine, packed.reshape(1536, wide))


def attend_weights_kernel(count, side_ref, *refs):
    flats, grads, (low, mixed) = refs[:count], refs[count : count + 5], refs[count + 5 : count + 7]
    mine, theirs, flat_t, grad = refs[count + 7 :]
    side = side_ref[0]
    start = 0
    for ref in flats:
        n = ref.shape[0]
        flat_t[:, start : start + n] = ref[...].T
        start += n
    fill(grad, grads)
    for block in range(3):
        cols = slice(256 * block, 256 * (block + 1))
        out = nn(flat_t[...], low[:, cols]).astype(BF16).reshape(8, 192, 256)
        store_halves(side, mine, theirs, out[:, :96], out[:, 96:], slice(0, 96), cols)
    mixed_t = mixed[...].T
    for half in range(2):
        out = [
            nn(mixed_t, grad[:, 384 * q : 384 * (q + 1)]).astype(BF16).reshape(4, 96, 384)
            for q in (2 * half, 2 * half + 1)
        ]
        for head in range(4):
            place = slice(2 * head + half, 2 * head + half + 1)
            store_at(side, mine, theirs, out[0][head : head + 1], out[1][head : head + 1], place)


def store_at(side, mine, theirs, even, odd, place):
    cols = slice(768, 1152)

    @pl.when(side == 0)
    def _():
        mine[place, :, cols] = even
        theirs[place, :, cols] = odd

    @pl.when(side != 0)
    def _():
        mine[place, :, cols] = odd
        theirs[place, :, cols] = even


def attend_weights_call(side, flats, grads, low, mixed):
    shape = jax.ShapeDtypeStruct((8, 96, 1152), BF16)
    return pl.pallas_call(
        functools.partial(attend_weights_kernel, len(flats)),
        grid=(1,),
        in_specs=[pl.BlockSpec(memory_space=pltpu.SMEM)]
        + piece_specs(flats)
        + PIECES
        + [whole((512, 768)), whole((512, 384))],
        out_specs=[whole((8, 96, 1152))] * 2,
        out_shape=[shape, shape],
        scratch_shapes=[pltpu.VMEM((1536, 512), BF16), pltpu.VMEM((512, 1536), BF16)],
        compiler_params=params(40),
        cost_estimate=cost(1.9e9, 10e6),
        name="attend_weights",
    )(side, *flats, *grads, low, mixed)


def unpack_attention(side, blocks, refs):
    wq, wk, wv, wo = refs
    for x, block in enumerate(blocks):
        wq[:, 384 * x : 384 * (x + 1)] = block[:, :384].astype(F32)
    wk[...] = jnp.concatenate([block[:, 384:576].astype(F32) for block in blocks], axis=1)
    wv[...] = jnp.concatenate([block[:, 576:768].astype(F32) for block in blocks], axis=1)
    for x, block in enumerate(blocks):
        rows = slice(96 * (x // 2), 96 * (x // 2) + 96)
        for core in range(2):
            start = 384 * (2 * (x % 2) + core)

            @pl.when(side == core)
            def _(rows=rows, start=start, block=block):
                wo[rows, start : start + 384] = block[:, 768:1152].astype(F32)


def unpack_feed(blocks, refs):
    gate, up, down = refs
    for x, block in enumerate(blocks):
        for s in range(8):
            cols = slice(512 * s + 128 * x, 512 * s + 128 * (x + 1))
            gate[:, cols] = block[:, 128 * s : 128 * (s + 1)].astype(F32)
            up[:, cols] = block[:, 1024 + 128 * s : 1024 + 128 * (s + 1)].astype(F32)
        down[x, 0, :, :1024] = block[0:64, 2048:3072].astype(F32)
        down[x, 0, 0:32, 1024:] = block[64:96, 2048:2560].astype(F32)
        down[x, 0, 32:64, 1024:] = block[64:96, 2560:3072].astype(F32)


ATTENTION_SPECS = [
    pl.BlockSpec((96, 1536), lambda b, s: (b, 0)),
    pl.BlockSpec((96, 768), lambda b, s: (b, 0)),
    pl.BlockSpec((96, 768), lambda b, s: (b, 0)),
    pl.BlockSpec((192, 1536), lambda b, s: (0, 0)),
]
ATTENTION_SHAPES = [
    jax.ShapeDtypeStruct((192, 1536), F32),
    jax.ShapeDtypeStruct((192, 768), F32),
    jax.ShapeDtypeStruct((192, 768), F32),
    jax.ShapeDtypeStruct((192, 1536), F32),
]
FEED_OUT_SPECS = [
    pl.BlockSpec((96, 4096), lambda b, s: (b, 0)),
    pl.BlockSpec((96, 4096), lambda b, s: (b, 0)),
    pl.BlockSpec((4, 1, 64, 1536), lambda b, s: (0, b, 0, 0)),
]
FEED_SHAPES = [
    jax.ShapeDtypeStruct((192, 4096), F32),
    jax.ShapeDtypeStruct((192, 4096), F32),
    jax.ShapeDtypeStruct((4, 2, 64, 1536), F32),
]


def unpack_kernel(attention, feed, me, *refs):
    side = pl.program_id(0)
    blocks = [ref[0, 0] for ref in refs[:4]]
    refs = refs[4:]
    if attention:
        unpack_attention(side, [block[:, :1152] for block in blocks], refs[:4])
        refs = refs[4:]
    if feed:
        start = 1152 if attention else 0
        unpack_feed([block[:, start : start + 3072] for block in blocks], refs)


def unpack_call(attention, feed, me, every):
    wide = every.shape[-1]
    specs = [
        pl.BlockSpec((1, 1, 96, wide), lambda b, s, x=x: (lax.rem(x - s[0] + 4, 4), b, 0, 0))
        for x in range(4)
    ]
    out_specs = (ATTENTION_SPECS if attention else []) + (FEED_OUT_SPECS if feed else [])
    shapes = (ATTENTION_SHAPES if attention else []) + (FEED_SHAPES if feed else [])
    out = pl.pallas_call(
        functools.partial(unpack_kernel, attention, feed),
        grid_spec=pltpu.PrefetchScalarGridSpec(
            num_scalar_prefetch=1, grid=(2,), in_specs=specs, out_specs=out_specs
        ),
        out_shape=shapes,
        compiler_params=params(48),
        cost_estimate=cost(1e6, 30e6),
        name="unpack",
    )(me, every, every, every, every)
    if feed:
        out = list(out[:-1]) + [out[-1].reshape(512, 1536)]
    return out


def pack_feed_kernel(where, w_gate, w_up, w_down, out):
    x = where[0]
    for s in range(8):
        cols = pl.ds(pl.multiple_of(512 * s + 128 * x, 128), 128)
        out[:, 128 * s : 128 * (s + 1)] = w_gate[:, cols]
        out[:, 1024 + 128 * s : 1024 + 128 * (s + 1)] = w_up[:, cols]
    out[0:64, 2048:3072] = w_down[:, 0:1024]
    out[64:96, 2048:2560] = w_down[0:32, 1024:1536]
    out[64:96, 2560:3072] = w_down[32:64, 1024:1536]


def pack_feed_call(where, w_gate, w_up, w_down):
    return pl.pallas_call(
        pack_feed_kernel,
        grid_spec=pltpu.PrefetchScalarGridSpec(
            num_scalar_prefetch=1,
            grid=(1,),
            in_specs=[
                pl.BlockSpec((96, 4096), lambda b, w: (w[1], 0)),
                pl.BlockSpec((96, 4096), lambda b, w: (w[1], 0)),
                pl.BlockSpec((64, 1536), lambda b, w: (2 * w[0] + w[1], 0)),
            ],
            out_specs=pl.BlockSpec((96, 3072), lambda b, w: (0, 0)),
        ),
        out_shape=jax.ShapeDtypeStruct((96, 3072), BF16),
        compiler_params=params(24),
        cost_estimate=cost(1e3, 24e5),
        name="pack_feed",
    )(where, w_gate, w_up, w_down)


WINDOW = 512
EPSILON = 1e-05
ROPE_BASE = 100000.0

AXES = ("ylo", "x", "core", "z", "yhi")
SIZES = (2, 4, 2, 4, 2)
REP = ("ylo", "x", "core")
SHARD = ("z", "yhi")
SPREAD = ("z", "yhi", "core")

RIGHT = [(i, (i + 1) % 4) for i in range(4)]
LEFT = [(i, (i - 1) % 4) for i in range(4)]
SWAP = [(0, 1), (1, 0)]


def number(ylo, x, core, z, yhi):
    return (((ylo * 4 + x) * 2 + core) * 4 + z) * 2 + yhi


def permutation(place):
    pairs = []
    for ylo in range(2):
        for x in range(4):
            for core in range(2):
                for z in range(4):
                    for yhi in range(2):
                        pairs.append(
                            (number(ylo, x, core, z, yhi), number(ylo, *place(x, core, z, yhi)))
                        )
    return pairs


def inverse(pairs):
    return [(there, here) for here, there in pairs]


LINES = [permutation(lambda x, c, z, h, k=k: ((z + k) % 4, h, x, c)) for k in range(4)]
LINES_LENGTH = permutation(lambda x, c, z, h: (z, h, x, c))
ROWS = permutation(lambda x, c, z, h: (z, c, 2 * h + x // 2, x % 2))


def to_lines(block, z):
    part = block.shape[0] // 4
    out = []
    for k in range(4):
        piece = lax.dynamic_slice_in_dim(block, ((z + k) % 4) * part, part, axis=0)
        out.append(lax.ppermute(piece, AXES, LINES[k]))
    return jnp.concatenate(out, axis=0)


def from_lines(block, z):
    part = block.shape[0] // 4
    out = jnp.zeros_like(block)
    for k in range(4):
        piece = lax.ppermute(block[part * k : part * (k + 1)], AXES, inverse(LINES[k]))
        out = lax.dynamic_update_slice_in_dim(out, piece, ((z + k) % 4) * part, axis=0)
    return out


def ring_gather(block):
    half = block.shape[0] // 2
    from_left = lax.ppermute(block, "x", RIGHT)
    from_right = lax.ppermute(block, "x", LEFT)
    far_first = lax.ppermute(from_left[:half], "x", RIGHT)
    far_second = lax.ppermute(from_right[half:], "x", LEFT)
    return block, from_left, from_right, far_first, far_second


def ring_scatter(own, left, right, far):
    half = far.shape[0] // 2
    first = lax.ppermute(far[:half], "x", RIGHT).astype(F32)
    second = lax.ppermute(far[half:], "x", LEFT).astype(F32)
    right = jnp.concatenate([right[:half] + first, right[half:]], axis=0).astype(BF16)
    left = jnp.concatenate([left[:half], left[half:] + second], axis=0).astype(BF16)
    from_left = lax.ppermute(right, "x", RIGHT).astype(F32)
    from_right = lax.ppermute(left, "x", LEFT).astype(F32)
    return own + from_left + from_right


def rms_norm(values, gain):
    return values * lax.rsqrt(jnp.mean(values * values, axis=-1, keepdims=True) + EPSILON) * gain


def either(index, first, second):
    return jnp.where(index == 0, first, second)


def add_low(mine, came):
    return (mine.astype(F32) + came.astype(F32)).astype(BF16)


def ring_stack(block, axis):
    half = block.shape[0] // 2
    before = lax.ppermute(block, axis, RIGHT)
    after = lax.ppermute(block, axis, LEFT)
    first = lax.ppermute(before[:half], axis, RIGHT)
    second = lax.ppermute(after[half:], axis, LEFT)
    far = jnp.concatenate([first, second], axis=0)
    return jnp.stack([block, after, far, before])


def core_sum(mine, theirs):
    return add_low(mine, lax.ppermute(theirs, "core", SWAP))


def z_sum(line, where, offload):
    if offload:
        return lax.psum_scatter(line, "z", scatter_dimension=0, tiled=True)
    tall = line.reshape((4, 2) + line.shape[1:])

    def step(r):
        return lax.dynamic_index_in_dim(tall, (where["z"] + r) % 4, axis=0, keepdims=False)

    own, after, far, before = step(0), step(1), step(2), step(3)
    first = lax.ppermute(far[:1], "z", RIGHT)
    second = lax.ppermute(far[1:], "z", LEFT)
    after = jnp.concatenate([add_low(after[:1], first), after[1:]])
    before = jnp.concatenate([before[:1], add_low(before[1:], second)])
    from_before = lax.ppermute(after, "z", RIGHT).astype(F32)
    from_after = lax.ppermute(before, "z", LEFT).astype(F32)
    return (own.astype(F32) + from_before + from_after).astype(BF16)


def y_sum(pair, where):
    mine = lax.dynamic_index_in_dim(pair, where["yhi"], axis=0, keepdims=False)
    theirs = lax.dynamic_index_in_dim(pair, 1 - where["yhi"], axis=0, keepdims=False)
    piece = add_low(mine, lax.ppermute(theirs, "yhi", SWAP))
    return add_low(piece, lax.ppermute(piece, "ylo", SWAP))


def out_home(piece):
    moved = lax.ppermute(piece[:, 768:1152], AXES, inverse(ROWS))
    return jnp.concatenate([piece[:, :768], moved, piece[:, 1152:]], axis=1)


def butterfly(values):
    for axis, size in (("core", 2), ("x", 4), ("z", 4), ("yhi", 2), ("ylo", 2)):
        step = 1
        while step < size:
            pairs = [(i, i ^ step) for i in range(size)]
            values = values + lax.ppermute(values, axis, pairs)
            step *= 2
    return values


def norm_back(grad, own_normed, state, gain):
    grad_state, grad_gain = jax.vjp(rms_norm, state, gain)[1](own_normed)
    return grad + grad_state, grad_gain


def body(tokens, lengths, grad_output, *weights):
    stretch, width = tokens.shape[1:]
    x = lax.axis_index("x")
    core = lax.axis_index("core")
    z = lax.axis_index("z")
    yhi = lax.axis_index("yhi")
    where = {"x": x, "core": core, "z": z, "yhi": yhi}
    pair_index = jnp.stack([x, core]).astype(jnp.int32)
    side = core.astype(jnp.int32).reshape(1)

    gains = jnp.stack([weights[0], weights[5], weights[9], weights[14]])
    gains = lax.dynamic_slice_in_dim(gains, core * 96, 96, axis=1).T
    gains = jnp.pad(gains, ((0, 0), (0, 124)))
    packed = []
    for index, base in enumerate((0, 9)):
        w_q, w_k, w_v, w_out = weights[base + 1 : base + 5]
        out_block = lax.dynamic_slice(
            w_out, (96 * (x // 2), 384 * (2 * (x % 2) + core)), (96, 384)
        )
        out_block = lax.ppermute(out_block, AXES, ROWS)
        parts = [
            lax.dynamic_slice(w, (core * 96, x * (w.shape[1] // 4)), (96, w.shape[1] // 4))
            for w in (w_q, w_k, w_v)
        ]
        parts += [out_block] + ([] if index else [gains])
        attn = lax.all_gather(jnp.concatenate(parts, axis=1), SPREAD, axis=0, tiled=False)
        feed = pack_feed_call(pair_index, *weights[base + 6 : base + 9])
        feed = lax.all_gather(feed, SPREAD, axis=0, tiled=False)
        packed.append((attn, feed))
    gains = packed[0][0][:, :, 1152:1156].transpose(2, 0, 1).reshape(4, width).astype(F32)

    here = (2 * z + yhi) * stretch + jnp.arange(stretch, dtype=jnp.int32)
    valid = (here < lengths[0])[:, None]
    length = lax.ppermute(lengths, AXES, LINES_LENGTH)
    rows = to_lines(tokens[0], z)
    pieces = ring_gather(rows)
    state = rows.astype(F32)
    grad_rows = to_lines(jnp.where(valid, grad_output[0], 0).astype(BF16), z)
    grad_pieces = ring_gather(grad_rows)
    grad = grad_rows.astype(F32)

    part = stretch // 4

    def member_places(member, side_index):
        block = jnp.arange(4, dtype=jnp.int32)
        inner = jnp.arange(part, dtype=jnp.int32)
        home = (member - block + 4) % 4
        return (
            home[:, None] * (2 * stretch) + side_index * stretch + member * part + inner[None, :]
        ).reshape(-1)

    def line_places(side_index):
        return jnp.concatenate([member_places((x + step) % 4, side_index) for step in (0, 3, 1, 2)])

    places = line_places(core)
    key_places = jnp.concatenate([places, line_places(1 - core)]).reshape(1024, 1)
    half = HEAD_DIM // 2
    freq = ROPE_BASE ** (-jnp.arange(half, dtype=F32) * (2.0 / HEAD_DIM))
    angle = places.astype(F32)[:, None] * freq[None, :]
    cosine, sine = jnp.cos(angle), jnp.sin(angle)
    cosine_t, sine_t = cosine.T, sine.T
    places = places.reshape(1, 512)

    records = []
    for index, window in enumerate((WINDOW, 8 * stretch)):
        attn, feed = packed[index]
        gain_attn, gain_feed = gains[2 * index], gains[2 * index + 1]
        if index == 0:
            queries, own, flat = project_call(True, pieces, gain_attn, attn, cosine, sine)
            flats = (flat,)
        else:
            flats = ring_gather(rms_norm(state, gain_attn).astype(BF16))
            queries, own = project_call(False, flats, gain_attn, attn, cosine, sine)
        other = lax.ppermute(own, "core", SWAP)
        line = (queries, own, other, places, key_places)
        *partial, mixed, log_total = attend_call(window, length, *line, attn)
        saved_attn = (state, flats, line, mixed, log_total)
        state = state + ring_scatter(*partial)
        flats = ring_gather(rms_norm(state, gain_feed).astype(BF16))
        *partial, gate, up, hidden = feed_forward_call(flats, feed)
        saved_feed = (state, flats, gate, up, hidden)
        state = state + ring_scatter(*partial)
        records.append((saved_attn, saved_feed, window))
    output = from_lines(state.astype(BF16), z)[None]

    results = [None] * 18
    gain_grads = [None] * 4
    zero = jnp.zeros((1,), jnp.int32)
    for index in (1, 0):
        attn, feed = packed[index]
        gain_attn, gain_feed = gains[2 * index], gains[2 * index + 1]
        saved_attn, saved_feed, window = records[index]
        base = 9 * index

        state, flats, gate, up, hidden = saved_feed
        if index == 0:
            grad_pieces = ring_gather(grad.astype(BF16))
        *partial, low_gate, low_up = feed_backward_call(grad_pieces, feed, gate, up)
        grad, gain_grads[2 * index + 1] = norm_back(grad, ring_scatter(*partial), state, gain_feed)
        halves = feed_weights_call(side, flats, grad_pieces, low_gate, low_up, hidden)
        feed_pair = z_sum(core_sum(*halves), where, True)

        state, flats, line, mixed, log_total = saved_attn
        grad_pieces = ring_gather(grad.astype(BF16))
        low_queries, pair_own, pair_other = attend_backward_call(
            window, length, grad_pieces, *line, attn, log_total, cosine_t, sine_t
        )
        came = lax.ppermute(pair_other, "core", SWAP)
        *partial, low = unproject_call(low_queries, pair_own, came, cosine, sine, attn)
        grad, gain_grads[2 * index] = norm_back(grad, ring_scatter(*partial), state, gain_attn)
        halves = attend_weights_call(side, flats, grad_pieces, low, mixed)
        line_sum = core_sum(*halves)
        if index:
            attn_pair = z_sum(line_sum, where, True)
            piece = y_sum(jnp.concatenate([attn_pair, feed_pair], axis=2), where)
            every = lax.all_gather(out_home(piece), ("x", "core"), axis=0, tiled=False)
            out = unpack_call(True, True, zero, every.reshape(4, 2, 96, -1))
            results[base + 1 : base + 5] = out[:4]
            results[base + 6 : base + 9] = out[4:]
        else:
            every = lax.all_gather(y_sum(feed_pair, where), ("x", "core"), axis=0, tiled=False)
            results[base + 6 : base + 9] = unpack_call(
                False, True, zero, every.reshape(4, 2, 96, -1)
            )
            piece = out_home(y_sum(z_sum(line_sum, where, False), where))
            ring = ring_stack(piece, "x")
            came = lax.ppermute(ring, "core", SWAP)
            every = either(core, jnp.stack([ring, came], axis=1), jnp.stack([came, ring], axis=1))
            results[base + 1 : base + 5] = unpack_call(
                True, False, x.astype(jnp.int32).reshape(1), every
            )
    gain_sums = butterfly(jnp.stack(gain_grads))
    gain_sums = lax.dynamic_slice_in_dim(gain_sums, (2 * z + yhi) * 192, 192, axis=1)
    for index, slot in enumerate((0, 5, 9, 14)):
        results[slot] = gain_sums[index]
    input_grad = from_lines(grad.astype(BF16), z).astype(F32)[None]
    return (output, input_grad, *results)


def solution(mesh):
    fine = Mesh(mesh.devices.reshape(SIZES), AXES)
    token = P(REP, SHARD, None)
    vector = P(SHARD)
    matrix = P(SHARD, None)
    layer = (vector, matrix, matrix, matrix, matrix, vector, matrix, matrix, matrix)
    return jax.shard_map(
        body,
        mesh=fine,
        in_specs=(token, P(REP), token) + layer + layer,
        out_specs=(token, token) + layer + layer,
        check_vma=False,
    )
```

time: 1430 us -> 843 us (0.59)
  waiting for transfers between devices: 683 us -> 316 us
  matrix products: 187 us -> 0 us
  Pallas kernels: 0 us -> 152 us
  blocking collectives: 150 us -> 0 us
  local copies, waits for them, and re-layouts: 114 us -> 78.1 us
  other arithmetic: 65.8 us -> 39.1 us
  starting transfers between devices: 207 us -> 230 us
    reduce_scatter x8 -> x3, waiting for transfers between devices: 317 us -> 29 us  [z_sum(): return lax.psum_scatter(line, 'z', scatter_dimension=0, tiled=True)]
    dot_general x38 -> x0, matrix products: 187 us -> none  [the longest x2 29.7 us: attention_backward(): jnp.einsum('kgqp,pkd->qkgd', grad_raw, keys, preferred_element_type=F32)]
    all_gather x14 -> x6, waiting for transfers between devices: 197 us -> 36.8 us  [the longest x2 29.4 us: body(): feed = lax.all_gather(feed, SPREAD, axis=0, tiled=False)]
    pallas_call x0 -> x21, Pallas kernels: none -> 152 us  [the longest x2 27.4 us: feed_weights_call(): pl.pallas_call(feed_weights_kernel, grid_spec=spec, out_shape=[shape, sha...]
    all_gather x4 -> x0, blocking collectives: 88 us -> none  [the longest x2 40.2 us: home_rows(): return lax.all_gather(piece, ('x', 'core'), axis=0, tiled=True).astype(F32)]
    unnamed x1 -> x0, blocking collectives: 62.5 us -> none
    ppermute x8, waiting for transfers between devices: 15.2 us -> 55.3 us  [ring_scatter(): from_left = lax.ppermute(right, 'x', RIGHT).astype(F32)]
    ppermute x22 -> x35, waiting for transfers between devices: 39.5 us -> 77.3 us  [the longest x3 18.6 us: y_sum(): piece = add_low(mine, lax.ppermute(theirs, 'yhi', SWAP))]
  transfers between devices with their start and end apart: 124 -> 124, of which waited for: 58 -> 51; matrix products, arithmetic and copies ran while one was open for 20% -> 8% of each run, Pallas kernels for 0% -> 12%
where the time goes in v3:
time: 843 us; the launch traced here: 832 us
  waiting for transfers between devices  316 us (37%)
  starting transfers between devices  230 us (27%)
  Pallas kernels  152 us (18%)
  local copies, waits for them, and re-layouts  78.1 us (9%)
  other arithmetic  39.1 us (5%)
  between operations  17.7 us (2%)
    ppermute x8, waiting for transfers between devices, ring_scatter(): from_left = lax.ppermute(right, 'x', RIGHT).astype(F32)  55.3 us
    ppermute x8, waiting for transfers between devices, ring_gather(): from_left = lax.ppermute(block, 'x', RIGHT)  53 us
    ppermute x8, starting transfers between devices, to_lines(): out.append(lax.ppermute(piece, AXES, LINES[k]))  48.2 us
    unnamed x275, local copies, waits for them, and re-layouts  44.2 us
    ppermute x8, starting transfers between devices, from_lines(): lax.ppermute(block[part * k:part * (k + 1)], AXES, inverse(LINES[k]))  33.7 us
    all_gather x2, waiting for transfers between devices, body(): feed = lax.all_gather(feed, SPREAD, axis=0, tiled=False)  29.4 us
    reduce_scatter x3, waiting for transfers between devices, z_sum(): return lax.psum_scatter(line, 'z', scatter_dimension=0, tiled=True)  29 us
    pallas_call x2, Pallas kernels, feed_weights_call(): pl.pallas_call(feed_weights_kernel, grid_spec=spec, out_shape=[shape, sha...  27.4 us
  transfers between devices with their start and end apart: 124, of which 51 were waited for; matrix products, arithmetic and copies ran while one was open for 8% of the time, Pallas kernels for 12%

profile of v3, /device:TPU:1, one launch (start us, length us, event | category | flops | bytes accessed | tf_op | source)
XLA Modules:
  0.0 832.2 jit_solution(10462349898230767624)
XLA Ops:
  26.0 17.9 %collective-permute-start = (bf16[32,1536]{1,0:T(8,128)(2,1)S(1)}, bf16[32,1536]{1,0:T(8,128)(2,1)S(1)}, u32[]{:S(2)}, u32[]{:S(2)}) collective-permute-start(bf16[32,1536]{1,0:T(8,128)(2,1)S(1)} %get-tuple-element.246), channel_id=1, source_target_pairs={{0,0},{1,8},{2,16},{3,24},{4,32},{5,40},{6,48},{7,56},{8,1},{9,9},... | collective-permute-start | bytes 294920 | tf_op jit(solution)/shard_map/ppermute | solution.py:723
  91.3 9.1 %attend.2 = (f32[128,1536]{1,0:T(8,128)S(1)}, f32[128,1536]{1,0:T(8,128)S(1)}, f32[128,1536]{1,0:T(8,128)S(1)}, bf16[128,1536]{1,0:T(8,128)(2,1)S(1)}, bf16[512,...) custom-call(s32[1]{0:T(128)} %collective-permute-done.4.length, bf16[512,384]{1,0:T(8,128)(2,1)S(1)} %get-tuple-element.101.queries.refs_5_, ...), custom_call_target="tpu_custom_call" | custom-call | flops 3000000000 | bytes 6000000 | tf_op jit(solution)/shard_map/attend/pallas_call | solution.py:385
  111.2 7.9 collective-permute-done.12
  122.9 7.4 collective-permute-done.15.refs_1_
  137.1 22.7 %all-gather.15.cloned.1.call-done.refs_5_.refs_6_ = bf16[1536,3072]{1,0:T(8,128)(2,1)} async-done(((bf16[96,3072]{1,0:T(8,128)(2,1)}), bf16[1536,3072]{1,0:T(8,128)(2,1)}) %all-gather.15.cloned.1.call-update) | async-done | bytes 9437200 | tf_op jit(solution)/shard_map/all_gather | solution.py:854
  160.8 9.2 %feed_forward.2 = (f32[128,1536]{1,0:T(8,128)S(1)}, f32[128,1536]{1,0:T(8,128)S(1)}, f32[128,1536]{1,0:T(8,128)S(1)}, bf16[128,1536]{1,0:T(8,128)(2,1)S(1)}, f32...) custom-call(bf16[128,1536]{1,0:T(8,128)(2,1)S(1)} %multiply_convert_fusion.2.refs_0_, ...), custom_call_target="tpu_custom_call" | custom-call | flops 4899999744 | bytes 18000000 | tf_op jit(solution)/shard_map/feed_forward/pallas_call | solution.py:123
  182.6 7.3 collective-permute-done.20
  195.1 7.2 collective-permute-done.23.refs_1_
  205.9 7.2 all-gather.17.cloned.1.call-done.refs_6_.weight
  234.6 9.1 %attend.3 = (f32[128,1536]{1,0:T(8,128)S(1)}, f32[128,1536]{1,0:T(8,128)S(1)}, f32[128,1536]{1,0:T(8,128)S(1)}, bf16[128,1536]{1,0:T(8,128)(2,1)S(1)}, bf16[512,...) custom-call(s32[1]{0:T(128)} %collective-permute-done.4.length, bf16[512,384]{1,0:T(8,128)(2,1)S(1)} %get-tuple-element.111.queries.refs_5_, ...), custom_call_target="tpu_custom_call" | custom-call | flops 3000000000 | bytes 6000000 | tf_op jit(solution)/shard_map/attend/pallas_call | solution.py:385
  295.6 9.6 %feed_forward.3 = (f32[128,1536]{1,0:T(8,128)S(1)}, f32[128,1536]{1,0:T(8,128)S(1)}, f32[128,1536]{1,0:T(8,128)S(1)}, bf16[128,1536]{1,0:T(8,128)(2,1)S(1)}, f32...) custom-call(bf16[128,1536]{1,0:T(8,128)(2,1)S(1)} %multiply_convert_fusion.refs_0_, ...), custom_call_target="tpu_custom_call" | custom-call | flops 4899999744 | bytes 18000000 | tf_op jit(solution)/shard_map/feed_forward/pallas_call | solution.py:123
  308.2 12.8 %feed_backward.2 = (f32[128,1536]{1,0:T(8,128)S(1)}, f32[128,1536]{1,0:T(8,128)S(1)}, f32[128,1536]{1,0:T(8,128)S(1)}, bf16[128,1536]{1,0:T(8,128)(2,1)S(1)}, bf...) custom-call(bf16[128,1536]{1,0:T(8,128)(2,1)S(1)} %constant_dynamic-update-slice_fusion.6.refs_0_.refs_5_, ...), custom_call_target="tpu_custom_call" | custom-call | flops 4899999744 | bytes 20000000 | tf_op jit(solution)/shard_map/feed_backward/pallas_call | solution.py:176
  331.1 13.8 %collective-permute-done.54 = bf16[128,1536]{1,0:T(8,128)(2,1)S(1)} collective-permute-done((bf16[128,1536]{1,0:T(8,128)(2,1)S(1)}, bf16[128,1536]{1,0:T(8,128)(2,1)S(1)}, u32[]{:S(2)}, u32[]{:S(2)}) %collective-permute-start.54) | collective-permute-done | bytes 393248 | tf_op jit(solution)/shard_map/ppermute | solution.py:751
  360.9 13.3 %attend_backward.2 = (bf16[512,384]{1,0:T(8,128)(2,1)S(1)}, f32[512,384]{1,0:T(8,128)}, bf16[512,384]{1,0:T(8,128)(2,1)S(1)}) custom-call(s32[1]{0:T(128)} %collective-permute-done.4.length, bf16[128,1536]{1,0:T(8,128)(2,1)S(1)} %get-tuple-element.198.refs_0_.refs_5_, bf16[128,1536]{1,0:T(8,128)(2,1)} %copy-done.55, bf16[128,1536]{1,0:T(8,128)(2,1)} %copy-done.57, ...), custom_call_target="tpu_custom_call" | custom-call | flops 6000000000 | bytes 6000000 | tf_op jit(solution)/shard_map/attend_backward/pallas_call | solution.py:445
  396.4 8.1 collective-permute-done.63
  408.8 7.4 collective-permute-done.66.refs_1_.refs_6_
  422.0 12.8 %feed_backward.3 = (f32[128,1536]{1,0:T(8,128)S(1)}, f32[128,1536]{1,0:T(8,128)S(1)}, f32[128,1536]{1,0:T(8,128)S(1)}, bf16[128,1536]{1,0:T(8,128)(2,1)S(1)}, bf...) custom-call(bf16[128,1536]{1,0:T(8,128)(2,1)S(1)} %get-tuple-element.196.refs_0_.refs_5_, ...), custom_call_target="tpu_custom_call" | custom-call | flops 4899999744 | bytes 20000000 | tf_op jit(solution)/shard_map/feed_backward/pallas_call | solution.py:176
  435.7 13.0 %feed_weights.2 = (bf16[8,96,3072]{2,1,0:T(8,128)(2,1)S(1)}, bf16[8,96,3072]{2,1,0:T(8,128)(2,1)}) custom-call(s32[1]{0:T(128)} %bitcast.10.side_ref, bf16[128,1536]{1,0:T(8,128)(2,1)S(1)} %multiply_convert_fusion.2.refs_0_, bf16[128,1536]{1,0:T(8,128)(2,1)S(1)} %copy-done.17, bf16[128,1536]{1,0:T(8,128)(2,1)S(1)} %copy-done.19, ...), custom_call_target="tpu_custom_call" | custom-call | flops 4899999744 | bytes 18000000 | tf_op jit(solution)/shard_map/feed_weights/pallas_call | solution.py:272
  452.8 7.7 collective-permute-done.107
  481.3 14.4 %feed_weights.3 = (bf16[8,96,3072]{2,1,0:T(8,128)(2,1)S(1)}, bf16[8,96,3072]{2,1,0:T(8,128)(2,1)}) custom-call(s32[1]{0:T(128)} %bitcast.10.side_ref, bf16[128,1536]{1,0:T(8,128)(2,1)S(1)} %multiply_convert_fusion.refs_0_, bf16[128,1536]{1,0:T(8,128)(2,1)S(1)} %copy-done.21, bf16[128,1536]{1,0:T(8,128)(2,1)S(1)} %copy-done.23, ...), custom_call_target="tpu_custom_call" | custom-call | flops 4899999744 | bytes 18000000 | tf_op jit(solution)/shard_map/feed_weights/pallas_call | solution.py:272
  506.5 8.1 add_convert_fusion
  533.5 12.0 %collective-permute-done.108 = bf16[96,3072]{1,0:T(8,128)(2,1)S(1)} collective-permute-done((bf16[96,3072]{1,0:T(8,128)(2,1)S(1)}, bf16[96,3072]{1,0:T(8,128)(2,1)S(1)}, u32[]{:S(2)}, u32[]{:S(2)}) %collective-permute-start.108) | collective-permute-done | bytes 589856 | tf_op jit(solution)/shard_map/ppermute | solution.py:803
  553.5 11.7 %collective-permute-done.109 = bf16[96,3072]{1,0:T(8,128)(2,1)S(1)} collective-permute-done((bf16[96,3072]{1,0:T(8,128)(2,1)S(1)}, bf16[96,3072]{1,0:T(8,128)(2,1)S(1)}, u32[]{:S(2)}, u32[]{:S(2)}) %collective-permute-start.109) | collective-permute-done | bytes 589856 | tf_op jit(solution)/shard_map/ppermute | solution.py:804
  581.4 29.0 %reduce-scatter.8.cloned.1.call-done = bf16[2,96,3072]{2,1,0:T(8,128)(2,1)} async-done(((bf16[8,96,3072]{2,1,0:T(8,128)(2,1)}), bf16[2,96,3072]{2,1,0:T(8,128)(2,1)}) %reduce-scatter.8.cloned.1.call-update) | async-done | bytes 1179664 | tf_op jit(solution)/shard_map/reduce_scatter | solution.py:784
  623.4 10.6 %collective-permute-done.74.refs_1_.refs_2_ = bf16[128,1536]{1,0:T(8,128)(2,1)S(1)} collective-permute-done((bf16[128,1536]{1,0:T(8,128)(2,1)S(1)}, bf16[128,1536]{1,0:T(8,128)(2,1)S(1)}, u32[]{:S(2)}, u32[]{:S(2)}) %collective-permute-start.74) | collective-permute-done | bytes 393248 | tf_op jit(solution)/shard_map/ppermute | solution.py:738
  647.9 13.4 %attend_backward.3 = (bf16[512,384]{1,0:T(8,128)(2,1)S(1)}, f32[512,384]{1,0:T(8,128)}, bf16[512,384]{1,0:T(8,128)(2,1)S(1)}) custom-call(s32[1]{0:T(128)} %collective-permute-done.4.length, bf16[128,1536]{1,0:T(8,128)(2,1)S(1)} %get-tuple-element.194.refs_0_.refs_1_, bf16[128,1536]{1,0:T(8,128)(2,1)} %copy-done.59, bf16[128,1536]{1,0:T(8,128)(2,1)} %copy-done.61, ...), custom_call_target="tpu_custom_call" | custom-call | flops 6000000000 | bytes 6000000 | tf_op jit(solution)/shard_map/attend_backward/pallas_call | solution.py:445
  686.0 11.0 %collective-permute-start.81 = (bf16[64,1536]{1,0:T(8,128)(2,1)S(1)}, bf16[64,1536]{1,0:T(8,128)(2,1)S(1)}, u32[]{:S(2)}, u32[]{:S(2)}) collective-permute-start(bf16[64,1536]{1,0:T(8,128)(2,1)S(1)} %copy-done.114), channel_id=1, source_target_pairs={{0,48},{16,0},{32,16},{48,32},{1,49},{17,1},{33,17},{49,33},{2,50}... | collective-permute-start | bytes 589832 | tf_op jit(solution)/shard_map/ppermute | solution.py:748
  698.1 7.6 collective-permute-done.81
  711.0 7.8 collective-permute-done.80
  718.7 7.6 collective-permute-done.82
  740.7 9.0 %collective-permute-done.96 = bf16[2,96,1152]{2,1,0:T(8,128)(2,1)S(1)} collective-permute-done((bf16[2,96,1152]{2,1,0:T(8,128)(2,1)S(1)}, bf16[2,96,1152]{2,1,0:T(8,128)(2,1)S(1)}, u32[]{:S(2)}, u32[]{:S(2)}) %collective-permute-start.96) | collective-permute-done | bytes 442400 | tf_op jit(solution)/shard_map/ppermute | solution.py:795
  762.4 8.6 %collective-permute-start.83 = (bf16[32,1536]{1,0:T(8,128)(2,1)S(1)}, bf16[32,1536]{1,0:T(8,128)(2,1)S(1)}, u32[]{:S(2)}, u32[]{:S(2)}) collective-permute-start(bf16[32,1536]{1,0:T(8,128)(2,1)S(1)} %get-tuple-element.218), channel_id=1, source_target_pairs={{0,0},{8,1},{16,2},{24,3},{32,4},{40,5},{48,6},{56,7},{1,8},{9,9},... | collective-permute-start | bytes 294920 | tf_op jit(solution)/shard_map/ppermute | solution.py:731
  (732 shorter events, 460.4 us)
Async XLA Ops:
  7.2 73.2 %all-gather.13.cloned.1.call-start = ((), (), s32[]{:S(2)}) async-start(), calls=%async_computation.6 | async-start | bytes 4177920 | tf_op jit(solution)/shard_map/all_gather | solution.py:852
  15.4 144.4 %all-gather.15.cloned.1.call-start = ((), (), s32[]{:S(2)}) async-start(), calls=%async_computation.7 | async-start | bytes 10027008 | tf_op jit(solution)/shard_map/all_gather | solution.py:854
  21.3 191.8 %all-gather.17.cloned.1.call-start = ((), (), s32[]{:S(2)}) async-start(), calls=%async_computation.8 | async-start | bytes 3760128 | tf_op jit(solution)/shard_map/all_gather | solution.py:852
  25.8 269.8 %all-gather.19.cloned.1.call-start = ((), (), s32[]{:S(2)}) async-start(), calls=%async_computation.9 | async-start | bytes 10027008 | tf_op jit(solution)/shard_map/all_gather | solution.py:854
  26.0 42.2 %collective-permute-start = (bf16[32,1536]{1,0:T(8,128)(2,1)S(1)}, bf16[32,1536]{1,0:T(8,128)(2,1)S(1)}, u32[]{:S(2)}, u32[]{:S(2)}) collective-permute-start(bf16[32,1536]{1,0:T(8,128)(2,1)S(1)} %get-tuple-element.246), channel_id=1, source_target_pairs={{0,0},{1,8},{2,16},{3,24},{4,32},{5,40},{6,48},{7,56},{8,1},{9,9},... | collective-permute-start | bytes 294920 | tf_op jit(solution)/shard_map/ppermute | solution.py:723
  43.8 24.4 %collective-permute-start.1 = (bf16[32,1536]{1,0:T(8,128)(2,1)S(1)}, bf16[32,1536]{1,0:T(8,128)(2,1)S(1)}, u32[]{:S(2)}, u32[]{:S(2)}) collective-permute-start(bf16[32,1536]{1,0:T(8,128)(2,1)S(1)} %get-tuple-element.245), channel_id=1, source_target_pairs={{0,16},{1,24},{2,32},{3,40},{4,48},{5,56},{6,0},{7,8},{8,17},{9,25... | collective-permute-start | bytes 294920 | tf_op jit(solution)/shard_map/ppermute | solution.py:723
  58.3 31.8 %collective-permute-start.4 = (s32[1]{0:T(128)}, s32[1]{0:T(128)}, u32[]{:S(2)}, u32[]{:S(2)}) collective-permute-start(s32[1]{0:T(128)} %param.22), channel_id=1, source_target_pairs={{0,0},{1,8},{2,16},{3,24},{4,32},{5,40},{6,48},{7,56},{8,1},{9,9},... | collective-permute-start | bytes 20 | tf_op jit(solution)/shard_map/ppermute | solution.py:860
  67.0 448.3 %reduce-scatter.4.cloned.1.call-start = ((), (), s32[]{:S(2)}) async-start(), calls=%async_computation.3 | async-start | bytes 5898240 | tf_op jit(solution)/shard_map/reduce_scatter | solution.py:784
  218.7 25.1 %collective-permute-start.45 = (bf16[32,1536]{1,0:T(8,128)(2,1)S(1)}, bf16[32,1536]{1,0:T(8,128)(2,1)S(1)}, u32[]{:S(2)}, u32[]{:S(2)}) collective-permute-start(bf16[32,1536]{1,0:T(8,128)(2,1)S(1)} %get-tuple-element.231), channel_id=1, source_target_pairs={{0,0},{1,8},{2,16},{3,24},{4,32},{5,40},{6,48},{7,56},{8,1},{9,9},... | collective-permute-start | bytes 294920 | tf_op jit(solution)/shard_map/ppermute | solution.py:723
  221.0 32.9 %collective-permute-start.46 = (bf16[32,1536]{1,0:T(8,128)(2,1)S(1)}, bf16[32,1536]{1,0:T(8,128)(2,1)S(1)}, u32[]{:S(2)}, u32[]{:S(2)}) collective-permute-start(bf16[32,1536]{1,0:T(8,128)(2,1)S(1)} %get-tuple-element.230), channel_id=1, source_target_pairs={{0,16},{1,24},{2,32},{3,40},{4,48},{5,56},{6,0},{7,8},{8,17},{9,25... | collective-permute-start | bytes 294920 | tf_op jit(solution)/shard_map/ppermute | solution.py:723
  225.1 28.8 %collective-permute-start.47 = (bf16[32,1536]{1,0:T(8,128)(2,1)S(1)}, bf16[32,1536]{1,0:T(8,128)(2,1)S(1)}, u32[]{:S(2)}, u32[]{:S(2)}) collective-permute-start(bf16[32,1536]{1,0:T(8,128)(2,1)S(1)} %get-tuple-element.229), channel_id=1, source_target_pairs={{0,32},{1,40},{2,48},{3,56},{4,0},{5,8},{6,16},{7,24},{8,33},{9,41... | collective-permute-start | bytes 294920 | tf_op jit(solution)/shard_map/ppermute | solution.py:723
  229.3 36.9 %collective-permute-start.48 = (bf16[32,1536]{1,0:T(8,128)(2,1)}, bf16[32,1536]{1,0:T(8,128)(2,1)}, u32[]{:S(2)}, u32[]{:S(2)}) collective-permute-start(bf16[32,1536]{1,0:T(8,128)(2,1)} %get-tuple-element.228), channel_id=1, source_target_pairs={{0,48},{1,56},{2,0},{3,8},{4,16},{5,24},{6,32},{7,40},{8,49},{9,57... | collective-permute-start | bytes 294920 | tf_op jit(solution)/shard_map/ppermute | solution.py:723
  285.2 23.0 %collective-permute-start.51 = (bf16[64,1536]{1,0:T(8,128)(2,1)}, bf16[64,1536]{1,0:T(8,128)(2,1)}, u32[]{:S(2)}, u32[]{:S(2)}) collective-permute-start(bf16[64,1536]{1,0:T(8,128)(2,1)} %slice.449), channel_id=1, source_target_pairs={{0,16},{16,32},{32,48},{48,0},{1,17},{17,33},{33,49},{49,1},{2,18}... | collective-permute-start | bytes 589832 | tf_op jit(solution)/shard_map/ppermute | solution.py:740
  286.1 22.1 %collective-permute-start.52 = (bf16[64,1536]{1,0:T(8,128)(2,1)}, bf16[64,1536]{1,0:T(8,128)(2,1)}, u32[]{:S(2)}, u32[]{:S(2)}) collective-permute-start(bf16[64,1536]{1,0:T(8,128)(2,1)} %slice.450), channel_id=1, source_target_pairs={{0,48},{16,0},{32,16},{48,32},{1,49},{17,1},{33,17},{49,33},{2,50}... | collective-permute-start | bytes 589832 | tf_op jit(solution)/shard_map/ppermute | solution.py:741
  306.6 24.4 %collective-permute-start.39 = (bf16[64,1536]{1,0:T(8,128)(2,1)S(1)}, bf16[64,1536]{1,0:T(8,128)(2,1)S(1)}, u32[]{:S(2)}, u32[]{:S(2)}) collective-permute-start(bf16[64,1536]{1,0:T(8,128)(2,1)S(1)} %get-tuple-element.237), channel_id=1, source_target_pairs={{0,48},{16,0},{32,16},{48,32},{1,49},{17,1},{33,17},{49,33},{2,50}... | collective-permute-start | bytes 589832 | tf_op jit(solution)/shard_map/ppermute | solution.py:748
  464.7 114.9 %reduce-scatter.6.cloned.1.call-start = ((), (), s32[]{:S(2)}) async-start(), calls=%async_computation.4 | async-start | bytes 2211840 | tf_op jit(solution)/shard_map/reduce_scatter | solution.py:784
  500.0 110.3 %reduce-scatter.8.cloned.1.call-start = ((), (), s32[]{:S(2)}) async-start(), calls=%async_computation.5 | async-start | bytes 5898240 | tf_op jit(solution)/shard_map/reduce_scatter | solution.py:784
  514.7 296.9 %all-gather.21.cloned.1.call-start = ((), (), s32[]{:S(2)}) async-start(), calls=%async_computation.10 | async-start | bytes 5308416 | tf_op jit(solution)/shard_map/all_gather | solution.py:947
  516.6 29.0 %collective-permute-start.108 = (bf16[96,3072]{1,0:T(8,128)(2,1)S(1)}, bf16[96,3072]{1,0:T(8,128)(2,1)S(1)}, u32[]{:S(2)}, u32[]{:S(2)}) collective-permute-start(bf16[96,3072]{1,0:T(8,128)(2,1)S(1)} %dynamic-slice_bitcast_fusion.1), channel_id=1, source_target_pairs={{0,1},{1,0},{2,3},{3,2},{4,5},{5,4},{6,7},{7,6},{8,9},{9,8},{10,11... | collective-permute-start | bytes 1769480 | tf_op jit(solution)/shard_map/ppermute | solution.py:803
  519.8 51.3 %collective-permute-start.41 = (bf16[32,1536]{1,0:T(8,128)(2,1)}, bf16[32,1536]{1,0:T(8,128)(2,1)}, u32[]{:S(2)}, u32[]{:S(2)}) collective-permute-start(bf16[32,1536]{1,0:T(8,128)(2,1)} %get-tuple-element.235), channel_id=1, source_target_pairs={{0,0},{8,1},{16,2},{24,3},{32,4},{40,5},{48,6},{56,7},{1,8},{9,9},... | collective-permute-start | bytes 294920 | tf_op jit(solution)/shard_map/ppermute | solution.py:731
  523.6 96.7 %collective-permute-start.42 = (bf16[32,1536]{1,0:T(8,128)(2,1)}, bf16[32,1536]{1,0:T(8,128)(2,1)}, u32[]{:S(2)}, u32[]{:S(2)}) collective-permute-start(bf16[32,1536]{1,0:T(8,128)(2,1)} %get-tuple-element.234), channel_id=1, source_target_pairs={{16,0},{24,1},{32,2},{40,3},{48,4},{56,5},{0,6},{8,7},{17,8},{25,9... | collective-permute-start | bytes 294920 | tf_op jit(solution)/shard_map/ppermute | solution.py:731
  529.2 136.0 %collective-permute-start.43 = (bf16[32,1536]{1,0:T(8,128)(2,1)}, bf16[32,1536]{1,0:T(8,128)(2,1)}, u32[]{:S(2)}, u32[]{:S(2)}) collective-permute-start(bf16[32,1536]{1,0:T(8,128)(2,1)} %get-tuple-element.233), channel_id=1, source_target_pairs={{32,0},{40,1},{48,2},{56,3},{0,4},{8,5},{16,6},{24,7},{33,8},{41,9... | collective-permute-start | bytes 294920 | tf_op jit(solution)/shard_map/ppermute | solution.py:731
  532.2 177.2 %collective-permute-start.44 = (bf16[32,1536]{1,0:T(8,128)(2,1)}, bf16[32,1536]{1,0:T(8,128)(2,1)}, u32[]{:S(2)}, u32[]{:S(2)}) collective-permute-start(bf16[32,1536]{1,0:T(8,128)(2,1)} %get-tuple-element.232), channel_id=1, source_target_pairs={{48,0},{56,1},{0,2},{8,3},{16,4},{24,5},{32,6},{40,7},{49,8},{57,9... | collective-permute-start | bytes 294920 | tf_op jit(solution)/shard_map/ppermute | solution.py:731
  566.2 251.9 %all-gather.23.cloned.1.call-start = ((), (), s32[]{:S(2)}) async-start(), calls=%async_computation.11 | async-start | bytes 7299072 | tf_op jit(solution)/shard_map/all_gather | solution.py:942
  614.0 26.1 %collective-permute-start.112 = (bf16[96,4224]{1,0:T(8,128)(2,1)S(1)}, bf16[96,4224]{1,0:T(8,128)(2,1)S(1)}, u32[]{:S(2)}, u32[]{:S(2)}) collective-permute-start(bf16[96,4224]{1,0:T(8,128)(2,1)S(1)} %dynamic-slice_bitcast_fusion), channel_id=1, source_target_pairs={{0,1},{1,0},{2,3},{3,2},{4,5},{5,4},{6,7},{7,6},{8,9},{9,8},{10,11... | collective-permute-start | bytes 2433032 | tf_op jit(solution)/shard_map/ppermute | solution.py:803
  640.4 29.4 %collective-permute-start.113 = (bf16[96,4224]{1,0:T(8,128)(2,1)S(1)}, bf16[96,4224]{1,0:T(8,128)(2,1)S(1)}, u32[]{:S(2)}, u32[]{:S(2)}) collective-permute-start(bf16[96,4224]{1,0:T(8,128)(2,1)S(1)} %fusion), channel_id=1, source_target_pairs={{0,64},{64,0},{1,65},{65,1},{2,66},{66,2},{3,67},{67,3},{4,68},{68... | collective-permute-start | bytes 2433032 | tf_op jit(solution)/shard_map/ppermute | solution.py:804
  671.4 25.6 %collective-permute-start.79 = (bf16[64,1536]{1,0:T(8,128)(2,1)}, bf16[64,1536]{1,0:T(8,128)(2,1)}, u32[]{:S(2)}, u32[]{:S(2)}) collective-permute-start(bf16[64,1536]{1,0:T(8,128)(2,1)} %get-tuple-element.219), channel_id=1, source_target_pairs={{0,16},{16,32},{32,48},{48,0},{1,17},{17,33},{33,49},{49,1},{2,18}... | collective-permute-start | bytes 589832 | tf_op jit(solution)/shard_map/ppermute | solution.py:747
  685.4 43.1 %collective-permute-start.94 = (bf16[8,96,1152]{2,1,0:T(8,128)(2,1)S(1)}, bf16[8,96,1152]{2,1,0:T(8,128)(2,1)S(1)}, u32[]{:S(2)}, u32[]{:S(2)}) collective-permute-start(bf16[8,96,1152]{2,1,0:T(8,128)(2,1)S(1)} %get-tuple-element.153), channel_id=1, source_target_pairs={{0,8},{8,0},{1,9},{9,1},{2,10},{10,2},{3,11},{11,3},{4,12},{12,4},... | collective-permute-start | bytes 5308424 | tf_op jit(solution)/shard_map/ppermute | solution.py:779
  726.8 23.2 %collective-permute-start.87 = (f32[4,1536]{1,0:T(4,128)S(1)}, f32[4,1536]{1,0:T(4,128)S(1)}, u32[]{:S(2)}, u32[]{:S(2)}) collective-permute-start(f32[4,1536]{1,0:T(4,128)S(1)} %pad_maximum_fusion.21), channel_id=1, source_target_pairs={{0,8},{8,0},{1,9},{9,1},{2,10},{10,2},{3,11},{11,3},{4,12},{12,4},... | collective-permute-start | bytes 73736 | tf_op jit(solution)/shard_map/ppermute | solution.py:817
  756.9 23.4 %collective-permute-start.89 = (f32[4,1536]{1,0:T(4,128)S(1)}, f32[4,1536]{1,0:T(4,128)S(1)}, u32[]{:S(2)}, u32[]{:S(2)}) collective-permute-start(f32[4,1536]{1,0:T(4,128)S(1)} %fusion.52), channel_id=1, source_target_pairs={{0,32},{16,48},{32,0},{48,16},{1,33},{17,49},{33,1},{49,17},{2,34}... | collective-permute-start | bytes 73736 | tf_op jit(solution)/shard_map/ppermute | solution.py:817
  771.1 28.2 %collective-permute-start.84 = (bf16[32,1536]{1,0:T(8,128)(2,1)S(1)}, bf16[32,1536]{1,0:T(8,128)(2,1)S(1)}, u32[]{:S(2)}, u32[]{:S(2)}) collective-permute-start(bf16[32,1536]{1,0:T(8,128)(2,1)S(1)} %get-tuple-element.217), channel_id=1, source_target_pairs={{16,0},{24,1},{32,2},{40,3},{48,4},{56,5},{0,6},{8,7},{17,8},{25,9... | collective-permute-start | bytes 294920 | tf_op jit(solution)/shard_map/ppermute | solution.py:731
  775.2 30.6 %collective-permute-start.85 = (bf16[32,1536]{1,0:T(8,128)(2,1)S(1)}, bf16[32,1536]{1,0:T(8,128)(2,1)S(1)}, u32[]{:S(2)}, u32[]{:S(2)}) collective-permute-start(bf16[32,1536]{1,0:T(8,128)(2,1)S(1)} %get-tuple-element.216), channel_id=1, source_target_pairs={{32,0},{40,1},{48,2},{56,3},{0,4},{8,5},{16,6},{24,7},{33,8},{41,9... | collective-permute-start | bytes 294920 | tf_op jit(solution)/shard_map/ppermute | solution.py:731
  (223 other events, 2536.1 us)
Sparse Core Ops, SparseCore 0:
  15.5 64.8 all-gather.12
  83.4 76.3 all-gather.14
  162.9 50.1 all-gather.16
  216.0 79.5 all-gather.18
  464.9 49.0 reduce-scatter.3
  516.8 39.9 reduce-scatter.5
  559.3 51.0 reduce-scatter.7
  612.8 43.7 all-gather.20
  674.1 60.2 all-gather.22

commit v4 on v3

--- a/solution.py
+++ b/solution.py
@@ -45,6 +45,20 @@
 
 def tn(a, b):
     return lax.dot_general(a, b, (((0,), (0,)), ((), ())), preferred_element_type=F32)
+
+
+def later(kernel, count, lead=0):
+    if not count:
+        return kernel
+
+    def wrapped(*refs):
+        return kernel(*refs[:lead], *refs[lead + count :])
+
+    return wrapped
+
+
+def anywhere(after):
+    return [pl.BlockSpec(memory_space=pl.ANY)] * len(after)
 
 
 def whole(shape):
@@ -118,12 +132,12 @@
     return pl.BlockSpec((rows, 256), lambda b: (0, b))
 
 
-def feed_forward_call(pieces, packed):
+def feed_forward_call(pieces, packed, after=()):
     flat_packed = packed.reshape(1536, 3072)
     return pl.pallas_call(
-        feed_forward_kernel,
+        later(feed_forward_kernel, len(after)),
         grid=(4,),
-        in_specs=PIECES + feed_specs(),
+        in_specs=anywhere(after) + PIECES + feed_specs(),
         out_specs=PARTIALS + [column_block(512)] * 3,
         out_shape=PARTIAL_SHAPES
         + [
@@ -135,7 +149,7 @@
         compiler_params=params(40),
         cost_estimate=cost(4.9e9, 18e6),
         name="feed_forward",
-    )(*pieces, flat_packed, flat_packed, packed)
+    )(*after, *pieces, flat_packed, flat_packed, packed)
 
 
 def feed_backward_kernel(*refs):
@@ -171,19 +185,19 @@
         emit(total, outs)
 
 
-def feed_backward_call(pieces, packed, gate, up):
+def feed_backward_call(pieces, packed, gate, up, after=()):
     flat_packed = packed.reshape(1536, 3072)
     return pl.pallas_call(
-        feed_backward_kernel,
+        later(feed_backward_kernel, len(after)),
         grid=(4,),
-        in_specs=PIECES + feed_specs() + [column_block(512)] * 2,
+        in_specs=anywhere(after) + PIECES + feed_specs() + [column_block(512)] * 2,
         out_specs=PARTIALS + [column_block(512)] * 2,
         out_shape=PARTIAL_SHAPES + [jax.ShapeDtypeStruct((512, 1024), BF16)] * 2,
         scratch_shapes=[pltpu.VMEM((512, 1536), BF16), pltpu.VMEM((512, 1536), F32)],
         compiler_params=params(40),
         cost_estimate=cost(4.9e9, 20e6),
         name="feed_backward",
-    )(*pieces, flat_packed, flat_packed, packed, gate, up)
+    )(*after, *pieces, flat_packed, flat_packed, packed, gate, up)
 
 
 def store_halves(side, mine, theirs, even, odd, rows, columns):
@@ -314,14 +328,15 @@
     pair[...] = jnp.concatenate([keys, both[:, 576:768]], axis=1).astype(BF16)
 
 
-def project_call(raw, pieces, gain, packed, cosine, sine):
+def project_call(raw, pieces, gain, packed, cosine, sine, after=()):
     wide = packed.shape[-1]
     shape = jax.ShapeDtypeStruct((512, 384), BF16)
     flat_shape = jax.ShapeDtypeStruct((512, 1536), BF16)
     return pl.pallas_call(
-        functools.partial(project_kernel, raw, len(pieces)),
+        later(functools.partial(project_kernel, raw, len(pieces)), len(after)),
         grid=(1,),
-        in_specs=piece_specs(pieces)
+        in_specs=anywhere(after)
+        + piece_specs(pieces)
         + [whole((1, 1536)), whole((1536, 768)), whole((512, 48)), whole((512, 48))],
         out_specs=[whole((512, 384))] * 2 + ([whole((512, 1536))] if raw else []),
         out_shape=[shape, shape] + ([flat_shape] if raw else []),
@@ -329,7 +344,7 @@
         compiler_params=params(40),
         cost_estimate=cost(1.3e9, 6e6),
         name="project",
-    )(*pieces, gain.reshape(1, 1536), packed.reshape(1536, wide), cosine, sine)
+    )(*after, *pieces, gain.reshape(1, 1536), packed.reshape(1536, wide), cosine, sine)
 
 
 def fill_bias(bias, length, places, key_places, window):
@@ -381,11 +396,12 @@
     return pl.BlockSpec((16, 96, 384), lambda *_: (0, 0, 2))
 
 
-def attend_call(window, length, queries, own, other, places, key_places, packed):
+def attend_call(window, length, queries, own, other, places, key_places, packed, after=()):
     return pl.pallas_call(
-        functools.partial(attend_kernel, window),
+        later(functools.partial(attend_kernel, window), len(after)),
         grid=(1,),
-        in_specs=[pl.BlockSpec(memory_space=pltpu.SMEM)] + line_specs() + [out_spec()],
+        in_specs=anywhere(after)
+        + [pl.BlockSpec(memory_space=pltpu.SMEM)] + line_specs() + [out_spec()],
         out_specs=PARTIALS + [whole((512, 384)), whole((8, 512))],
         out_shape=PARTIAL_SHAPES
         + [jax.ShapeDtypeStruct((512, 384), BF16), jax.ShapeDtypeStruct((8, 512), F32)],
@@ -393,7 +409,7 @@
         compiler_params=params(48),
         cost_estimate=cost(3e9, 6e6, 2e6),
         name="attend",
-    )(length, queries, own, other, places, key_places, packed)
+    )(*after, length, queries, own, other, places, key_places, packed)
 
 
 def attend_backward_kernel(window, length, *refs):
@@ -440,12 +456,25 @@
 
 
 def attend_backward_call(
-    window, length, pieces, queries, own, other, places, key_places, packed, log_total, cosine, sine
+    window,
+    length,
+    pieces,
+    queries,
+    own,
+    other,
+    places,
+    key_places,
+    packed,
+    log_total,
+    cosine,
+    sine,
+    after=(),
 ):
     return pl.pallas_call(
-        functools.partial(attend_backward_kernel, window),
+        later(functools.partial(attend_backward_kernel, window), len(after)),
         grid=(1,),
-        in_specs=[pl.BlockSpec(memory_space=pltpu.SMEM)]
+        in_specs=anywhere(after)
+        + [pl.BlockSpec(memory_space=pltpu.SMEM)]
         + PIECES
         + line_specs()
         + [out_spec(), whole((8, 512)), whole((48, 512)), whole((48, 512))],
@@ -460,6 +489,7 @@
         cost_estimate=cost(6e9, 6e6, 2e6),
         name="attend_backward",
     )(
+        *after,
         length,
         *pieces,
         queries,
@@ -538,12 +568,13 @@
         theirs[place, :, cols] = even
 
 
-def attend_weights_call(side, flats, grads, low, mixed):
+def attend_weights_call(side, flats, grads, low, mixed, after=()):
     shape = jax.ShapeDtypeStruct((8, 96, 1152), BF16)
     return pl.pallas_call(
-        functools.partial(attend_weights_kernel, len(flats)),
+        later(functools.partial(attend_weights_kernel, len(flats)), len(after)),
         grid=(1,),
-        in_specs=[pl.BlockSpec(memory_space=pltpu.SMEM)]
+        in_specs=anywhere(after)
+        + [pl.BlockSpec(memory_space=pltpu.SMEM)]
         + piece_specs(flats)
         + PIECES
         + [whole((512, 768)), whole((512, 384))],
@@ -553,7 +584,7 @@
         compiler_params=params(40),
         cost_estimate=cost(1.9e9, 10e6),
         name="attend_weights",
-    )(side, *flats, *grads, low, mixed)
+    )(*after, side, *flats, *grads, low, mixed)
 
 
 def unpack_attention(side, blocks, refs):
@@ -654,13 +685,14 @@
     out[64:96, 2560:3072] = w_down[32:64, 1024:1536]
 
 
-def pack_feed_call(where, w_gate, w_up, w_down):
+def pack_feed_call(where, w_gate, w_up, w_down, after=()):
     return pl.pallas_call(
-        pack_feed_kernel,
+        later(pack_feed_kernel, len(after), 1),
         grid_spec=pltpu.PrefetchScalarGridSpec(
             num_scalar_prefetch=1,
             grid=(1,),
-            in_specs=[
+            in_specs=anywhere(after)
+            + [
                 pl.BlockSpec((96, 4096), lambda b, w: (w[1], 0)),
                 pl.BlockSpec((96, 4096), lambda b, w: (w[1], 0)),
                 pl.BlockSpec((64, 1536), lambda b, w: (2 * w[0] + w[1], 0)),
@@ -671,7 +703,42 @@
         compiler_params=params(24),
         cost_estimate=cost(1e3, 24e5),
         name="pack_feed",
-    )(where, w_gate, w_up, w_down)
+    )(where, *after, w_gate, w_up, w_down)
+
+
+def assemble_kernel(where, *refs):
+    pieces, out, sems = refs[:10], refs[10], refs[11]
+    z, yhi, core = where[0], where[1], where[2]
+    handles = []
+    for turn in range(2):
+        side = core if turn == 0 else 1 - core
+        pair, after, before, first, second = pieces[5 * turn : 5 * turn + 5]
+        for step, parts in (
+            (0, (pair.at[0], pair.at[1])),
+            (1, (after.at[0], after.at[1])),
+            (3, (before.at[0], before.at[1])),
+            (2, (first.at[0], second.at[0])),
+        ):
+            for other, part in enumerate(parts):
+                high = yhi if other == 0 else 1 - yhi
+                place = 4 * lax.rem(z + step, 4) + 2 * high + side
+                handles.append(pltpu.make_async_copy(part, out.at[place], sems.at[len(handles)]))
+    for handle in handles:
+        handle.start()
+    for handle in handles:
+        handle.wait()
+
+
+def assemble_call(where, pieces, width):
+    return pl.pallas_call(
+        assemble_kernel,
+        in_specs=[pl.BlockSpec(memory_space=pltpu.SMEM)] + anywhere(pieces),
+        out_specs=pl.BlockSpec(memory_space=pl.ANY),
+        out_shape=jax.ShapeDtypeStruct((16, 96, width), BF16),
+        scratch_shapes=[pltpu.SemaphoreType.DMA((16,))],
+        cost_estimate=cost(1e3, 2 * 16 * 96 * width * 2),
+        name="assemble",
+    )(where, *pieces)
 
 
 WINDOW = 512
@@ -775,6 +842,12 @@
     return jnp.stack([block, after, far, before])
 
 
+def line_gather(piece, core):
+    ring = ring_stack(piece, "x")
+    came = lax.ppermute(ring, "core", SWAP)
+    return either(core, jnp.stack([ring, came], axis=1), jnp.stack([came, ring], axis=1))
+
+
 def core_sum(mine, theirs):
     return add_low(mine, lax.ppermute(theirs, "core", SWAP))
 
@@ -837,8 +910,7 @@
     gains = jnp.stack([weights[0], weights[5], weights[9], weights[14]])
     gains = lax.dynamic_slice_in_dim(gains, core * 96, 96, axis=1).T
     gains = jnp.pad(gains, ((0, 0), (0, 124)))
-    packed = []
-    for index, base in enumerate((0, 9)):
+    def attention_piece(base, extra):
         w_q, w_k, w_v, w_out = weights[base + 1 : base + 5]
         out_block = lax.dynamic_slice(
             w_out, (96 * (x // 2), 384 * (2 * (x % 2) + core)), (96, 384)
@@ -848,19 +920,34 @@
             lax.dynamic_slice(w, (core * 96, x * (w.shape[1] // 4)), (96, w.shape[1] // 4))
             for w in (w_q, w_k, w_v)
         ]
-        parts += [out_block] + ([] if index else [gains])
-        attn = lax.all_gather(jnp.concatenate(parts, axis=1), SPREAD, axis=0, tiled=False)
-        feed = pack_feed_call(pair_index, *weights[base + 6 : base + 9])
-        feed = lax.all_gather(feed, SPREAD, axis=0, tiled=False)
-        packed.append((attn, feed))
-    gains = packed[0][0][:, :, 1152:1156].transpose(2, 0, 1).reshape(4, width).astype(F32)
-
-    here = (2 * z + yhi) * stretch + jnp.arange(stretch, dtype=jnp.int32)
-    valid = (here < lengths[0])[:, None]
+        return jnp.concatenate(parts + [out_block] + extra, axis=1)
+
+    attn_one = lax.all_gather(attention_piece(0, [gains]), SPREAD, axis=0, tiled=False)
+    gains = attn_one[:, :, 1152:1156].transpose(2, 0, 1).reshape(4, width).astype(F32)
+
     length = lax.ppermute(lengths, AXES, LINES_LENGTH)
     rows = to_lines(tokens[0], z)
     pieces = ring_gather(rows)
     state = rows.astype(F32)
+
+    feed_one = pack_feed_call(pair_index, *weights[6:9], after=(rows,))
+    across = lax.ppermute(feed_one, "yhi", SWAP)
+    pair = jnp.stack([feed_one, across])
+    before = lax.ppermute(pair, "z", RIGHT)
+    ahead = lax.ppermute(pair, "z", LEFT)
+    first = lax.ppermute(before[:1], "z", RIGHT)
+    second = lax.ppermute(ahead[1:], "z", LEFT)
+    feed_parts = [pair, ahead, before, first, second]
+    feed_parts += [lax.ppermute(item, "core", SWAP) for item in feed_parts]
+    feed_one = assemble_call(jnp.stack([z, yhi, core]).astype(jnp.int32), feed_parts, 3072)
+
+    attn_two = lax.all_gather(attention_piece(9, []), SPREAD, axis=0, tiled=False)
+    feed_two = pack_feed_call(pair_index, *weights[15:18], after=(rows,))
+    feed_two = lax.all_gather(feed_two, SPREAD, axis=0, tiled=False)
+    packed = ((attn_one, feed_one), (attn_two, feed_two))
+
+    here = (2 * z + yhi) * stretch + jnp.arange(stretch, dtype=jnp.int32)
+    valid = (here < lengths[0])[:, None]
     grad_rows = to_lines(jnp.where(valid, grad_output[0], 0).astype(BF16), z)
     grad_pieces = ring_gather(grad_rows)
     grad = grad_rows.astype(F32)
@@ -892,18 +979,22 @@
         attn, feed = packed[index]
         gain_attn, gain_feed = gains[2 * index], gains[2 * index + 1]
         if index == 0:
-            queries, own, flat = project_call(True, pieces, gain_attn, attn, cosine, sine)
+            queries, own, flat = project_call(
+                True, pieces, gain_attn, attn, cosine, sine, after=(across,)
+            )
             flats = (flat,)
         else:
             flats = ring_gather(rms_norm(state, gain_attn).astype(BF16))
             queries, own = project_call(False, flats, gain_attn, attn, cosine, sine)
         other = lax.ppermute(own, "core", SWAP)
         line = (queries, own, other, places, key_places)
-        *partial, mixed, log_total = attend_call(window, length, *line, attn)
+        after = grad_pieces[3:] if index else (ahead,)
+        *partial, mixed, log_total = attend_call(window, length, *line, attn, after=after)
         saved_attn = (state, flats, line, mixed, log_total)
         state = state + ring_scatter(*partial)
         flats = ring_gather(rms_norm(state, gain_feed).astype(BF16))
-        *partial, gate, up, hidden = feed_forward_call(flats, feed)
+        after = () if index else (grad_rows,)
+        *partial, gate, up, hidden = feed_forward_call(flats, feed, after=after)
         saved_feed = (state, flats, gate, up, hidden)
         state = state + ring_scatter(*partial)
         records.append((saved_attn, saved_feed, window))
@@ -921,40 +1012,46 @@
         state, flats, gate, up, hidden = saved_feed
         if index == 0:
             grad_pieces = ring_gather(grad.astype(BF16))
-        *partial, low_gate, low_up = feed_backward_call(grad_pieces, feed, gate, up)
+        after = () if index else (attn_sum,)
+        *partial, low_gate, low_up = feed_backward_call(grad_pieces, feed, gate, up, after=after)
         grad, gain_grads[2 * index + 1] = norm_back(grad, ring_scatter(*partial), state, gain_feed)
         halves = feed_weights_call(side, flats, grad_pieces, low_gate, low_up, hidden)
-        feed_pair = z_sum(core_sum(*halves), where, True)
+        feed_sum = core_sum(*halves)
 
         state, flats, line, mixed, log_total = saved_attn
         grad_pieces = ring_gather(grad.astype(BF16))
         low_queries, pair_own, pair_other = attend_backward_call(
-            window, length, grad_pieces, *line, attn, log_total, cosine_t, sine_t
+            window,
+            length,
+            grad_pieces,
+            *line,
+            attn,
+            log_total,
+            cosine_t,
+            sine_t,
+            after=(feed_sum,) if index else (feed_sum, output),
         )
         came = lax.ppermute(pair_other, "core", SWAP)
         *partial, low = unproject_call(low_queries, pair_own, came, cosine, sine, attn)
         grad, gain_grads[2 * index] = norm_back(grad, ring_scatter(*partial), state, gain_attn)
-        halves = attend_weights_call(side, flats, grad_pieces, low, mixed)
-        line_sum = core_sum(*halves)
+        after = () if index else (second_piece,)
+        halves = attend_weights_call(side, flats, grad_pieces, low, mixed, after=after)
+        attn_sum = core_sum(*halves)
+        feed_pair = z_sum(feed_sum, where, index)
+        attn_pair = z_sum(attn_sum, where, index)
         if index:
-            attn_pair = z_sum(line_sum, where, True)
             piece = y_sum(jnp.concatenate([attn_pair, feed_pair], axis=2), where)
-            every = lax.all_gather(out_home(piece), ("x", "core"), axis=0, tiled=False)
+            second_piece = out_home(piece)
+            every = lax.all_gather(second_piece, ("x", "core"), axis=0, tiled=False)
             out = unpack_call(True, True, zero, every.reshape(4, 2, 96, -1))
             results[base + 1 : base + 5] = out[:4]
             results[base + 6 : base + 9] = out[4:]
         else:
-            every = lax.all_gather(y_sum(feed_pair, where), ("x", "core"), axis=0, tiled=False)
-            results[base + 6 : base + 9] = unpack_call(
-                False, True, zero, every.reshape(4, 2, 96, -1)
-            )
-            piece = out_home(y_sum(z_sum(line_sum, where, False), where))
-            ring = ring_stack(piece, "x")
-            came = lax.ppermute(ring, "core", SWAP)
-            every = either(core, jnp.stack([ring, came], axis=1), jnp.stack([came, ring], axis=1))
-            results[base + 1 : base + 5] = unpack_call(
-                True, False, x.astype(jnp.int32).reshape(1), every
-            )
+            every = line_gather(y_sum(feed_pair, where), core)
+            place = x.astype(jnp.int32).reshape(1)
+            results[base + 6 : base + 9] = unpack_call(False, True, place, every)
+            every = line_gather(out_home(y_sum(attn_pair, where)), core)
+            results[base + 1 : base + 5] = unpack_call(True, False, place, every)
     gain_sums = butterfly(jnp.stack(gain_grads))
     gain_sums = lax.dynamic_slice_in_dim(gain_sums, (2 * z + yhi) * 192, 192, axis=1)
     for index, slot in enumerate((0, 5, 9, 14)):

time: 843 us -> 1150 us (1.36)
  Pallas kernels: 152 us -> 441 us
  waiting for transfers between devices: 316 us -> 249 us
  starting transfers between devices: 230 us -> 285 us
  other arithmetic: 39.1 us -> 55.7 us
  local copies, waits for them, and re-layouts: 78.1 us -> 91.7 us
    pallas_call x14 -> x15, Pallas kernels: 107 us -> 397 us  [the longest x1 288 us: assemble_call(): pl.pallas_call(assemble_kernel, in_specs=[pl.BlockSpec(memory_space=pltpu...]
    ppermute x3 -> x14, waiting for transfers between devices: 0.01 us -> 38.4 us  [the longest x1 20.1 us: body(): before = lax.ppermute(pair, 'z', RIGHT)]
    ppermute x3 -> x14, starting transfers between devices: 1.88 us -> 38.9 us  [the longest x5 22.7 us: body(): feed_parts += [lax.ppermute(item, 'core', SWAP) for item in feed_parts]]
    all_gather x6 -> x4, waiting for transfers between devices: 36.8 us -> 0.05 us  [the longest x1 0.02 us: body(): every = lax.all_gather(second_piece, ('x', 'core'), axis=0, tiled=False)]
    reduce_scatter x3 -> x2, waiting for transfers between devices: 29 us -> 0.02 us  [z_sum(): return lax.psum_scatter(line, 'z', scatter_dimension=0, tiled=True)]
    ppermute x8, waiting for transfers between devices: 53 us -> 32.6 us  [ring_gather(): from_left = lax.ppermute(block, 'x', RIGHT)]
    ppermute x8, waiting for transfers between devices: 55.3 us -> 37.9 us  [ring_scatter(): from_left = lax.ppermute(right, 'x', RIGHT).astype(F32)]
    ppermute x4, waiting for transfers between devices: 14.2 us -> 0.01 us  [core_sum(): return add_low(mine, lax.ppermute(theirs, 'core', SWAP))]
  transfers between devices with their start and end apart: 124 -> 140, of which waited for: 51 -> 48; matrix products, arithmetic and copies ran while one was open for 8% -> 9% of each run, Pallas kernels for 12% -> 33%
where the time goes in v4:
time: 1150 us; the launch traced here: 1140 us
  Pallas kernels  441 us (38%)
  starting transfers between devices  285 us (25%)
  waiting for transfers between devices  249 us (22%)
  local copies, waits for them, and re-layouts  91.7 us (8%)
  other arithmetic  55.7 us (5%)
  between operations  17.9 us (2%)
    pallas_call x1, Pallas kernels, assemble_call(): pl.pallas_call(assemble_kernel, in_specs=[pl.BlockSpec(memory_space=pltpu...  288 us
    unnamed x339, local copies, waits for them, and re-layouts  50.3 us
    ppermute x8, starting transfers between devices, to_lines(): out.append(lax.ppermute(piece, AXES, LINES[k]))  42.4 us
    ppermute x8, waiting for transfers between devices, ring_scatter(): from_left = lax.ppermute(right, 'x', RIGHT).astype(F32)  37.9 us
    ppermute x8, starting transfers between devices, from_lines(): lax.ppermute(block[part * k:part * (k + 1)], AXES, inverse(LINES[k]))  36 us
    ppermute x8, waiting for transfers between devices, ring_gather(): from_left = lax.ppermute(block, 'x', RIGHT)  32.6 us
    ppermute x3, waiting for transfers between devices, y_sum(): piece = add_low(mine, lax.ppermute(theirs, 'yhi', SWAP))  27.6 us
    pallas_call x2, Pallas kernels, feed_weights_call(): pl.pallas_call(feed_weights_kernel, grid_spec=spec, out_shape=[shape, sha...  27.2 us
  transfers between devices with their start and end apart: 140, of which 48 were waited for; matrix products, arithmetic and copies ran while one was open for 9% of the time, Pallas kernels for 33%

profile of v4, /device:TPU:1, one launch (start us, length us, event | category | flops | bytes accessed | tf_op | source)
XLA Modules:
  0.0 1140.3 jit_solution(2828701467191253148)
XLA Ops:
  21.0 16.9 %collective-permute-start = (bf16[32,1536]{1,0:T(8,128)(2,1)S(1)}, bf16[32,1536]{1,0:T(8,128)(2,1)S(1)}, u32[]{:S(2)}, u32[]{:S(2)}) collective-permute-start(bf16[32,1536]{1,0:T(8,128)(2,1)S(1)} %get-tuple-element.254), channel_id=1, source_target_pairs={{0,0},{1,8},{2,16},{3,24},{4,32},{5,40},{6,48},{7,56},{8,1},{9,9},... | collective-permute-start | bytes 294920 | tf_op jit(solution)/shard_map/ppermute | solution.py:790
  38.9 8.7 collective-permute-start.2
  70.9 13.0 %collective-permute-done.4.refs_0_ = bf16[96,3072]{1,0:T(8,128)(2,1)S(1)} collective-permute-done((bf16[96,3072]{1,0:T(8,128)(2,1)S(1)}, bf16[96,3072]{1,0:T(8,128)(2,1)S(1)}, u32[]{:S(2)}, u32[]{:S(2)}) %collective-permute-start.4) | collective-permute-done | bytes 589856 | tf_op jit(solution)/shard_map/ppermute | solution.py:934
  120.5 9.2 attend.2
  152.6 20.1 %collective-permute-done.25.refs_2_ = bf16[2,96,3072]{2,1,0:T(8,128)(2,1)S(1)} collective-permute-done((bf16[2,96,3072]{2,1,0:T(8,128)(2,1)}, bf16[2,96,3072]{2,1,0:T(8,128)(2,1)S(1)}, u32[]{:S(2)}, u32[]{:S(2)}) %collective-permute-start.25) | collective-permute-done | bytes 1179680 | tf_op jit(solution)/shard_map/ppermute | solution.py:936
  187.5 7.0 collective-permute-done.20
  194.6 18.6 %collective-permute-start.29 = (bf16[2,96,3072]{2,1,0:T(8,128)(2,1)S(1)}, bf16[2,96,3072]{2,1,0:T(8,128)(2,1)S(1)}, u32[]{:S(2)}, u32[]{:S(2)}) collective-permute-start(bf16[2,96,3072]{2,1,0:T(8,128)(2,1)S(1)} %collective-permute-done.5.refs_0_.refs_1_), channel_id=1, source_target_pairs={{0,8},{8,0},{1,9},{9,1},{2,10},{10,2},{3,11},{11,3},{4,12},{12,4},... | collective-permute-start | bytes 3538952 | tf_op jit(solution)/shard_map/ppermute | solution.py:941
  215.6 8.2 collective-permute-done.22.refs_3_.refs_2_
  232.7 287.9 %assemble.1.refs_8_ = bf16[16,96,3072]{2,1,0:T(8,128)(2,1)} custom-call(s32[3]{0:T(128)} %pad_add_fusion.1.where, bf16[2,96,3072]{2,1,0:T(8,128)(2,1)} %pad_maximum_fusion.1.refs_0_, bf16[2,96,3072]{2,1,0:T(8,128)(2,1)} %copy-done.7, bf16[2,96,3072]{2,1,0:T(8,128)(2,1)} %copy-done.117, bf16[1,96,3072]{2,1,0:T(8,128)(2,1)} %copy-done.128, ...), custom_call_target="tpu_custom_call" | custom-call | flops 1000 | bytes 18874368 | tf_op jit(solution)/shard_map/assemble/pallas_call | solution.py:733
  520.7 9.5 feed_forward.2
  543.0 7.0 collective-permute-done.34
  554.8 6.6 collective-permute-done.41.refs_1_
  573.9 6.7 collective-permute-start.46
  589.6 9.1 attend.3
  610.2 7.1 collective-permute-done.48
  622.3 6.7 collective-permute-done.51.refs_1_
  638.0 9.2 feed_forward.3
  647.3 12.7 %feed_backward.2 = (f32[128,1536]{1,0:T(8,128)S(1)}, f32[128,1536]{1,0:T(8,128)S(1)}, f32[128,1536]{1,0:T(8,128)S(1)}, bf16[128,1536]{1,0:T(8,128)(2,1)S(1)}, bf...) custom-call(bf16[128,1536]{1,0:T(8,128)(2,1)S(1)} %constant_dynamic-update-slice_fusion.6.refs_0_.refs_5_, ...), custom_call_target="tpu_custom_call" | custom-call | flops 4899999744 | bytes 20000000 | tf_op jit(solution)/shard_map/feed_backward/pallas_call | solution.py:190
  660.1 13.1 %feed_weights.2 = (bf16[8,96,3072]{2,1,0:T(8,128)(2,1)S(1)}, bf16[8,96,3072]{2,1,0:T(8,128)(2,1)}) custom-call(s32[1]{0:T(128)} %bitcast.5.side_ref.refs_1_, bf16[128,1536]{1,0:T(8,128)(2,1)S(1)} %multiply_convert_fusion.refs_0_, bf16[128,1536]{1,0:T(8,128)(2,1)S(1)} %copy-done.28, bf16[128,1536]{1,0:T(8,128)(2,1)S(1)} %copy-done.30, ...), custom_call_target="tpu_custom_call" | custom-call | flops 4899999744 | bytes 18000000 | tf_op jit(solution)/shard_map/feed_weights/pallas_call | solution.py:286
  693.2 12.8 %collective-permute-done.64 = bf16[128,1536]{1,0:T(8,128)(2,1)S(1)} collective-permute-done((bf16[128,1536]{1,0:T(8,128)(2,1)S(1)}, bf16[128,1536]{1,0:T(8,128)(2,1)S(1)}, u32[]{:S(2)}, u32[]{:S(2)}) %collective-permute-start.64) | collective-permute-done | bytes 393248 | tf_op jit(solution)/shard_map/ppermute | solution.py:818
  714.5 6.8 collective-permute-done.68.refs_3_.refs_6_
  728.7 13.3 %attend_backward.2 = (bf16[512,384]{1,0:T(8,128)(2,1)S(1)}, f32[512,384]{1,0:T(8,128)}, bf16[512,384]{1,0:T(8,128)(2,1)S(1)}) custom-call(bf16[8,96,3072]{2,1,0:T(8,128)(2,1)} %add_convert_fusion.1.refs_0_, s32[1]{0:T(128)} %collective-permute-done.6.refs_1_.refs_2_, bf16[128,1536]{1,0:T(8,128)(2,1)S(1)} %get-tuple-element.198.refs_2_.refs_5_, ...), custom_call_target="tpu_custom_call" | custom-call | flops 6000000000 | bytes 6000000 | tf_op jit(solution)/shard_map/attend_backward/pallas_call | solution.py:473
  784.4 7.0 collective-permute-done.78.refs_2_.refs_6_
  815.2 12.9 %feed_backward.3 = (f32[128,1536]{1,0:T(8,128)S(1)}, f32[128,1536]{1,0:T(8,128)S(1)}, f32[128,1536]{1,0:T(8,128)S(1)}, bf16[128,1536]{1,0:T(8,128)(2,1)S(1)}, bf...) custom-call(bf16[8,96,1152]{2,1,0:T(8,128)(2,1)S(1)} %copy-done.2, ...), custom_call_target="tpu_custom_call" | custom-call | flops 4899999744 | bytes 20000000 | tf_op jit(solution)/shard_map/feed_backward/pallas_call | solution.py:190
  829.9 14.1 %feed_weights.3 = (bf16[8,96,3072]{2,1,0:T(8,128)(2,1)S(1)}, bf16[8,96,3072]{2,1,0:T(8,128)(2,1)}) custom-call(s32[1]{0:T(128)} %bitcast.5.side_ref.refs_1_, bf16[128,1536]{1,0:T(8,128)(2,1)S(1)} %copy-done.21, bf16[128,1536]{1,0:T(8,128)(2,1)S(1)} %copy-done.40, bf16[128,1536]{1,0:T(8,128)(2,1)S(1)} %copy-done.43, bf16[64,1536]{1,0:T(8,128)(2,1)S(1)} %copy-done.71, ...), custom_call_target="tpu_custom_call" | custom-call | flops 4899999744 | bytes 18000000 | tf_op jit(solution)/shard_map/feed_weights/pallas_call | solution.py:286
  888.9 13.1 %attend_backward.3 = (bf16[512,384]{1,0:T(8,128)(2,1)S(1)}, f32[512,384]{1,0:T(8,128)}, bf16[512,384]{1,0:T(8,128)(2,1)S(1)}) custom-call(bf16[8,96,3072]{2,1,0:T(8,128)(2,1)} %add_convert_fusion.refs_0_, bf16[1,128,1536]{2,1,0:T(8,128)(2,1)} %bitcast_dynamic-update-slice_fusion.4.refs_1_, s32[1]{0:T(128)} %collective-permute-done.6.refs_1_.refs_2_, ...), custom_call_target="tpu_custom_call" | custom-call | flops 6000000000 | bytes 6000000 | tf_op jit(solution)/shard_map/attend_backward/pallas_call | solution.py:473
  948.3 11.6 %collective-permute-done.107 = bf16[96,4224]{1,0:T(8,128)(2,1)S(1)} collective-permute-done((bf16[96,4224]{1,0:T(8,128)(2,1)S(1)}, bf16[96,4224]{1,0:T(8,128)(2,1)S(1)}, u32[]{:S(2)}, u32[]{:S(2)}) %collective-permute-start.107) | collective-permute-done | bytes 811040 | tf_op jit(solution)/shard_map/ppermute | solution.py:876
  963.2 14.8 %collective-permute-done.108 = bf16[96,4224]{1,0:T(8,128)(2,1)S(1)} collective-permute-done((bf16[96,4224]{1,0:T(8,128)(2,1)S(1)}, bf16[96,4224]{1,0:T(8,128)(2,1)S(1)}, u32[]{:S(2)}, u32[]{:S(2)}) %collective-permute-start.108) | collective-permute-done | bytes 811040 | tf_op jit(solution)/shard_map/ppermute | solution.py:877
  1001.6 8.2 collective-permute-start.96
  1018.1 16.0 %collective-permute-done.127 = bf16[96,3072]{1,0:T(8,128)(2,1)S(1)} collective-permute-done((bf16[96,3072]{1,0:T(8,128)(2,1)S(1)}, bf16[96,3072]{1,0:T(8,128)(2,1)S(1)}, u32[]{:S(2)}, u32[]{:S(2)}) %collective-permute-start.127) | collective-permute-done | bytes 589856 | tf_op jit(solution)/shard_map/ppermute | solution.py:876
  1041.2 7.6 collective-permute-done.128
  1126.1 7.1 unpack.5
  (840 shorter events, 499.7 us)
Async XLA Ops:
  7.2 85.7 %all-gather.9.cloned.1.call-start = ((), (), s32[]{:S(2)}) async-start(), calls=%async_computation.4 | async-start | bytes 4177920 | tf_op jit(solution)/shard_map/all_gather | solution.py:925
  15.5 552.9 %all-gather.11.cloned.1.call-start = ((), (), s32[]{:S(2)}) async-start(), calls=%async_computation.5 | async-start | bytes 3760128 | tf_op jit(solution)/shard_map/all_gather | solution.py:944
  20.9 615.3 %all-gather.13.cloned.1.call-start = ((), (), s32[]{:S(2)}) async-start(), calls=%async_computation.6 | async-start | bytes 10027008 | tf_op jit(solution)/shard_map/all_gather | solution.py:946
  21.0 36.4 %collective-permute-start = (bf16[32,1536]{1,0:T(8,128)(2,1)S(1)}, bf16[32,1536]{1,0:T(8,128)(2,1)S(1)}, u32[]{:S(2)}, u32[]{:S(2)}) collective-permute-start(bf16[32,1536]{1,0:T(8,128)(2,1)S(1)} %get-tuple-element.254), channel_id=1, source_target_pairs={{0,0},{1,8},{2,16},{3,24},{4,32},{5,40},{6,48},{7,56},{8,1},{9,9},... | collective-permute-start | bytes 294920 | tf_op jit(solution)/shard_map/ppermute | solution.py:790
  50.7 60.5 %collective-permute-start.6 = (s32[1]{0:T(128)}, s32[1]{0:T(128)}, u32[]{:S(2)}, u32[]{:S(2)}) collective-permute-start(s32[1]{0:T(128)} %param.22), channel_id=1, source_target_pairs={{0,0},{1,8},{2,16},{3,24},{4,32},{5,40},{6,48},{7,56},{8,1},{9,9},... | collective-permute-start | bytes 20 | tf_op jit(solution)/shard_map/ppermute | solution.py:928
  61.8 844.1 %reduce-scatter.3.cloned.1.call-start = ((), (), s32[]{:S(2)}) async-start(), calls=%async_computation.2 | async-start | bytes 2211840 | tf_op jit(solution)/shard_map/reduce_scatter | solution.py:857
  134.1 38.5 %collective-permute-start.25 = (bf16[2,96,3072]{2,1,0:T(8,128)(2,1)}, bf16[2,96,3072]{2,1,0:T(8,128)(2,1)S(1)}, u32[]{:S(2)}, u32[]{:S(2)}) collective-permute-start(bf16[2,96,3072]{2,1,0:T(8,128)(2,1)} %pad_maximum_fusion.1.refs_0_), channel_id=1, source_target_pairs={{0,2},{2,4},{4,6},{6,0},{1,3},{3,5},{5,7},{7,1},{8,10},{10,12},{12... | collective-permute-start | bytes 3538952 | tf_op jit(solution)/shard_map/ppermute | solution.py:936
  140.6 36.8 %collective-permute-start.14 = (bf16[128,1536]{1,0:T(8,128)(2,1)}, bf16[128,1536]{1,0:T(8,128)(2,1)}, u32[]{:S(2)}, u32[]{:S(2)}) collective-permute-start(bf16[128,1536]{1,0:T(8,128)(2,1)} %pad_maximum_fusion.8), channel_id=1, source_target_pairs={{0,16},{16,32},{32,48},{48,0},{1,17},{17,33},{33,49},{49,1},{2,18}... | collective-permute-start | bytes 1179656 | tf_op jit(solution)/shard_map/ppermute | solution.py:818
  142.5 37.3 %collective-permute-start.16 = (bf16[128,1536]{1,0:T(8,128)(2,1)}, bf16[128,1536]{1,0:T(8,128)(2,1)}, u32[]{:S(2)}, u32[]{:S(2)}) collective-permute-start(bf16[128,1536]{1,0:T(8,128)(2,1)} %pad_maximum_fusion.9), channel_id=1, source_target_pairs={{0,48},{16,0},{32,16},{48,32},{1,49},{17,1},{33,17},{49,33},{2,50}... | collective-permute-start | bytes 1179656 | tf_op jit(solution)/shard_map/ppermute | solution.py:819
  145.4 38.8 %collective-permute-start.17 = (bf16[32,1536]{1,0:T(8,128)(2,1)}, bf16[32,1536]{1,0:T(8,128)(2,1)S(1)}, u32[]{:S(2)}, u32[]{:S(2)}) collective-permute-start(bf16[32,1536]{1,0:T(8,128)(2,1)} %get-tuple-element.249), channel_id=1, source_target_pairs={{0,0},{1,8},{2,16},{3,24},{4,32},{5,40},{6,48},{7,56},{8,1},{9,9},... | collective-permute-start | bytes 294920 | tf_op jit(solution)/shard_map/ppermute | solution.py:790
  150.2 34.5 %collective-permute-start.18 = (bf16[32,1536]{1,0:T(8,128)(2,1)}, bf16[32,1536]{1,0:T(8,128)(2,1)S(1)}, u32[]{:S(2)}, u32[]{:S(2)}) collective-permute-start(bf16[32,1536]{1,0:T(8,128)(2,1)} %get-tuple-element.248), channel_id=1, source_target_pairs={{0,16},{1,24},{2,32},{3,40},{4,48},{5,56},{6,0},{7,8},{8,17},{9,25... | collective-permute-start | bytes 294920 | tf_op jit(solution)/shard_map/ppermute | solution.py:790
  177.4 50.6 %collective-permute-start.28 = (bf16[2,96,3072]{2,1,0:T(8,128)(2,1)}, bf16[2,96,3072]{2,1,0:T(8,128)(2,1)S(1)}, u32[]{:S(2)}, u32[]{:S(2)}) collective-permute-start(bf16[2,96,3072]{2,1,0:T(8,128)(2,1)} %pad_maximum_fusion.1.refs_0_), channel_id=1, source_target_pairs={{0,8},{8,0},{1,9},{9,1},{2,10},{10,2},{3,11},{11,3},{4,12},{12,4},... | collective-permute-start | bytes 3538952 | tf_op jit(solution)/shard_map/ppermute | solution.py:941
  179.7 33.4 %collective-permute-start.26 = (bf16[1,96,3072]{2,1,0:T(8,128)(2,1)}, bf16[1,96,3072]{2,1,0:T(8,128)(2,1)S(1)}, u32[]{:S(2)}, u32[]{:S(2)}) collective-permute-start(bf16[1,96,3072]{2,1,0:T(8,128)(2,1)} %slice.491), channel_id=1, source_target_pairs={{0,2},{2,4},{4,6},{6,0},{1,3},{3,5},{5,7},{7,1},{8,10},{10,12},{12... | collective-permute-start | bytes 1769480 | tf_op jit(solution)/shard_map/ppermute | solution.py:938
  194.6 36.3 %collective-permute-start.29 = (bf16[2,96,3072]{2,1,0:T(8,128)(2,1)S(1)}, bf16[2,96,3072]{2,1,0:T(8,128)(2,1)S(1)}, u32[]{:S(2)}, u32[]{:S(2)}) collective-permute-start(bf16[2,96,3072]{2,1,0:T(8,128)(2,1)S(1)} %collective-permute-done.5.refs_0_.refs_1_), channel_id=1, source_target_pairs={{0,8},{8,0},{1,9},{9,1},{2,10},{10,2},{3,11},{11,3},{4,12},{12,4},... | collective-permute-start | bytes 3538952 | tf_op jit(solution)/shard_map/ppermute | solution.py:941
  228.1 292.5 %collective-permute-start.23 = (bf16[64,1536]{1,0:T(8,128)(2,1)}, bf16[64,1536]{1,0:T(8,128)(2,1)S(1)}, u32[]{:S(2)}, u32[]{:S(2)}) collective-permute-start(bf16[64,1536]{1,0:T(8,128)(2,1)} %slice.489), channel_id=1, source_target_pairs={{0,16},{16,32},{32,48},{48,0},{1,17},{17,33},{33,49},{49,1},{2,18}... | collective-permute-start | bytes 589832 | tf_op jit(solution)/shard_map/ppermute | solution.py:807
  228.1 292.5 %collective-permute-start.24 = (bf16[64,1536]{1,0:T(8,128)(2,1)}, bf16[64,1536]{1,0:T(8,128)(2,1)}, u32[]{:S(2)}, u32[]{:S(2)}) collective-permute-start(bf16[64,1536]{1,0:T(8,128)(2,1)} %slice.490), channel_id=1, source_target_pairs={{0,48},{16,0},{32,16},{48,32},{1,49},{17,1},{33,17},{49,33},{2,50}... | collective-permute-start | bytes 589832 | tf_op jit(solution)/shard_map/ppermute | solution.py:808
  673.2 51.2 %collective-permute-start.67 = (bf16[8,96,3072]{2,1,0:T(8,128)(2,1)}, bf16[8,96,3072]{2,1,0:T(8,128)(2,1)S(1)}, u32[]{:S(2)}, u32[]{:S(2)}) collective-permute-start(bf16[8,96,3072]{2,1,0:T(8,128)(2,1)} %get-tuple-element.131), channel_id=1, source_target_pairs={{0,8},{8,0},{1,9},{9,1},{2,10},{10,2},{3,11},{11,3},{4,12},{12,4},... | collective-permute-start | bytes 14155784 | tf_op jit(solution)/shard_map/ppermute | solution.py:852
  770.0 162.5 %reduce-scatter.5.cloned.1.call-start = ((), (), s32[]{:S(2)}) async-start(), calls=%async_computation.3 | async-start | bytes 5898240 | tf_op jit(solution)/shard_map/reduce_scatter | solution.py:857
  796.0 50.2 %collective-permute-start.59 = (bf16[32,1536]{1,0:T(8,128)(2,1)S(1)}, bf16[32,1536]{1,0:T(8,128)(2,1)S(1)}, u32[]{:S(2)}, u32[]{:S(2)}) collective-permute-start(bf16[32,1536]{1,0:T(8,128)(2,1)S(1)} %get-tuple-element.239), channel_id=1, source_target_pairs={{0,0},{8,1},{16,2},{24,3},{32,4},{40,5},{48,6},{56,7},{1,8},{9,9},... | collective-permute-start | bytes 294920 | tf_op jit(solution)/shard_map/ppermute | solution.py:798
  802.6 46.5 %collective-permute-start.60 = (bf16[32,1536]{1,0:T(8,128)(2,1)}, bf16[32,1536]{1,0:T(8,128)(2,1)}, u32[]{:S(2)}, u32[]{:S(2)}) collective-permute-start(bf16[32,1536]{1,0:T(8,128)(2,1)} %get-tuple-element.238), channel_id=1, source_target_pairs={{16,0},{24,1},{32,2},{40,3},{48,4},{56,5},{0,6},{8,7},{17,8},{25,9... | collective-permute-start | bytes 294920 | tf_op jit(solution)/shard_map/ppermute | solution.py:798
  805.3 55.0 %collective-permute-start.61 = (bf16[32,1536]{1,0:T(8,128)(2,1)}, bf16[32,1536]{1,0:T(8,128)(2,1)}, u32[]{:S(2)}, u32[]{:S(2)}) collective-permute-start(bf16[32,1536]{1,0:T(8,128)(2,1)} %get-tuple-element.237), channel_id=1, source_target_pairs={{32,0},{40,1},{48,2},{56,3},{0,4},{8,5},{16,6},{24,7},{33,8},{41,9... | collective-permute-start | bytes 294920 | tf_op jit(solution)/shard_map/ppermute | solution.py:798
  806.3 65.8 %collective-permute-start.62 = (bf16[32,1536]{1,0:T(8,128)(2,1)}, bf16[32,1536]{1,0:T(8,128)(2,1)}, u32[]{:S(2)}, u32[]{:S(2)}) collective-permute-start(bf16[32,1536]{1,0:T(8,128)(2,1)} %get-tuple-element.236), channel_id=1, source_target_pairs={{48,0},{56,1},{0,2},{8,3},{16,4},{24,5},{32,6},{40,7},{49,8},{57,9... | collective-permute-start | bytes 294920 | tf_op jit(solution)/shard_map/ppermute | solution.py:798
  846.2 35.9 %collective-permute-start.86 = (bf16[8,96,3072]{2,1,0:T(8,128)(2,1)}, bf16[8,96,3072]{2,1,0:T(8,128)(2,1)}, u32[]{:S(2)}, u32[]{:S(2)}) collective-permute-start(bf16[8,96,3072]{2,1,0:T(8,128)(2,1)} %get-tuple-element.154), channel_id=1, source_target_pairs={{0,8},{8,0},{1,9},{9,1},{2,10},{10,2},{3,11},{11,3},{4,12},{12,4},... | collective-permute-start | bytes 14155784 | tf_op jit(solution)/shard_map/ppermute | solution.py:852
  847.7 278.4 %all-gather.15.cloned.1.call-start = ((), (), s32[]{:S(2)}) async-start(), calls=%async_computation.7 | async-start | bytes 7299072 | tf_op jit(solution)/shard_map/all_gather | solution.py:1045
  943.7 69.3 %collective-permute-start.124 = (bf16[2,96,3072]{2,1,0:T(8,128)(2,1)}, bf16[2,96,3072]{2,1,0:T(8,128)(2,1)}, u32[]{:S(2)}, u32[]{:S(2)}) collective-permute-start(bf16[2,96,3072]{2,1,0:T(8,128)(2,1)} %pad_maximum_fusion.2), channel_id=1, source_target_pairs={{0,2},{2,4},{4,6},{6,0},{1,3},{3,5},{5,7},{7,1},{8,10},{10,12},{12... | collective-permute-start | bytes 3538952 | tf_op jit(solution)/shard_map/ppermute | solution.py:868
  945.2 68.5 %collective-permute-start.126 = (bf16[2,96,3072]{2,1,0:T(8,128)(2,1)}, bf16[2,96,3072]{2,1,0:T(8,128)(2,1)}, u32[]{:S(2)}, u32[]{:S(2)}) collective-permute-start(bf16[2,96,3072]{2,1,0:T(8,128)(2,1)} %pad_maximum_fusion.3), channel_id=1, source_target_pairs={{0,6},{2,0},{4,2},{6,4},{1,7},{3,1},{5,3},{7,5},{8,14},{10,8},{12,... | collective-permute-start | bytes 3538952 | tf_op jit(solution)/shard_map/ppermute | solution.py:869
  1001.6 59.4 %collective-permute-start.96 = (bf16[32,1536]{1,0:T(8,128)(2,1)S(1)}, bf16[32,1536]{1,0:T(8,128)(2,1)S(1)}, u32[]{:S(2)}, u32[]{:S(2)}) collective-permute-start(bf16[32,1536]{1,0:T(8,128)(2,1)S(1)} %get-tuple-element.226), channel_id=1, source_target_pairs={{0,0},{8,1},{16,2},{24,3},{32,4},{40,5},{48,6},{56,7},{1,8},{9,9},... | collective-permute-start | bytes 294920 | tf_op jit(solution)/shard_map/ppermute | solution.py:798
  1009.8 85.7 %collective-permute-start.97 = (bf16[32,1536]{1,0:T(8,128)(2,1)S(1)}, bf16[32,1536]{1,0:T(8,128)(2,1)S(1)}, u32[]{:S(2)}, u32[]{:S(2)}) collective-permute-start(bf16[32,1536]{1,0:T(8,128)(2,1)S(1)} %get-tuple-element.225), channel_id=1, source_target_pairs={{16,0},{24,1},{32,2},{40,3},{48,4},{56,5},{0,6},{8,7},{17,8},{25,9... | collective-permute-start | bytes 294920 | tf_op jit(solution)/shard_map/ppermute | solution.py:798
  1013.0 48.2 %collective-permute-start.103 = (f32[4,1536]{1,0:T(4,128)S(1)}, f32[4,1536]{1,0:T(4,128)S(1)}, u32[]{:S(2)}, u32[]{:S(2)}) collective-permute-start(f32[4,1536]{1,0:T(4,128)S(1)} %add.975), channel_id=1, source_target_pairs={{0,2},{2,0},{4,6},{6,4},{1,3},{3,1},{5,7},{7,5},{8,10},{10,8},{12,... | collective-permute-start | bytes 73736 | tf_op jit(solution)/shard_map/ppermute | solution.py:890
  1061.2 46.0 %collective-permute-start.98 = (bf16[32,1536]{1,0:T(8,128)(2,1)S(1)}, bf16[32,1536]{1,0:T(8,128)(2,1)S(1)}, u32[]{:S(2)}, u32[]{:S(2)}) collective-permute-start(bf16[32,1536]{1,0:T(8,128)(2,1)S(1)} %get-tuple-element.224), channel_id=1, source_target_pairs={{32,0},{40,1},{48,2},{56,3},{0,4},{8,5},{16,6},{24,7},{33,8},{41,9... | collective-permute-start | bytes 294920 | tf_op jit(solution)/shard_map/ppermute | solution.py:798
  1067.1 32.0 %collective-permute-start.104 = (f32[4,1536]{1,0:T(4,128)S(1)}, f32[4,1536]{1,0:T(4,128)S(1)}, u32[]{:S(2)}, u32[]{:S(2)}) collective-permute-start(f32[4,1536]{1,0:T(4,128)S(1)} %add.976), channel_id=1, source_target_pairs={{0,4},{2,6},{4,0},{6,2},{1,5},{3,7},{5,1},{7,3},{8,12},{10,14},{12... | collective-permute-start | bytes 73736 | tf_op jit(solution)/shard_map/ppermute | solution.py:890
  1086.8 32.1 %collective-permute-start.133 = (bf16[4,96,3072]{2,1,0:T(8,128)(2,1)S(1)}, bf16[4,96,3072]{2,1,0:T(8,128)(2,1)S(1)}, u32[]{:S(2)}, u32[]{:S(2)}) collective-permute-start(bf16[4,96,3072]{2,1,0:T(8,128)(2,1)S(1)} %get-tuple-element.213), channel_id=1, source_target_pairs={{0,8},{8,0},{1,9},{9,1},{2,10},{10,2},{3,11},{11,3},{4,12},{12,4},... | collective-permute-start | bytes 7077896 | tf_op jit(solution)/shard_map/ppermute | solution.py:847
  (270 other events, 4606.9 us)
Sparse Core Ops, SparseCore 0:
  15.6 66.7 all-gather.8
  84.8 53.9 all-gather.10
  141.9 84.4 all-gather.12
  770.1 25.8 reduce-scatter.2
  847.8 52.0 reduce-scatter.4
  984.9 56.2 all-gather.14

commit v5 on v4

--- a/solution.py
+++ b/solution.py
@@ -72,6 +72,7 @@
     jax.ShapeDtypeStruct((128, 1536), F32),
     jax.ShapeDtypeStruct((128, 1536), BF16),
 ]
+LOW_PARTIAL_SHAPES = PARTIAL_SHAPES[:1] + [jax.ShapeDtypeStruct((128, 1536), BF16)] * 3
 PARTIALS = [whole((128, 1536))] * 4
 
 
@@ -133,7 +134,7 @@
 
 
 def feed_forward_call(pieces, packed, after=()):
-    flat_packed = packed.reshape(1536, 3072)
+    flat_packed = packed.reshape(1536, -1)
     return pl.pallas_call(
         later(feed_forward_kernel, len(after)),
         grid=(4,),
@@ -186,13 +187,13 @@
 
 
 def feed_backward_call(pieces, packed, gate, up, after=()):
-    flat_packed = packed.reshape(1536, 3072)
+    flat_packed = packed.reshape(1536, -1)
     return pl.pallas_call(
         later(feed_backward_kernel, len(after)),
         grid=(4,),
         in_specs=anywhere(after) + PIECES + feed_specs() + [column_block(512)] * 2,
         out_specs=PARTIALS + [column_block(512)] * 2,
-        out_shape=PARTIAL_SHAPES + [jax.ShapeDtypeStruct((512, 1024), BF16)] * 2,
+        out_shape=LOW_PARTIAL_SHAPES + [jax.ShapeDtypeStruct((512, 1024), BF16)] * 2,
         scratch_shapes=[pltpu.VMEM((512, 1536), BF16), pltpu.VMEM((512, 1536), F32)],
         compiler_params=params(40),
         cost_estimate=cost(4.9e9, 20e6),
@@ -337,7 +338,7 @@
         grid=(1,),
         in_specs=anywhere(after)
         + piece_specs(pieces)
-        + [whole((1, 1536)), whole((1536, 768)), whole((512, 48)), whole((512, 48))],
+        + [whole((1, 1536)), projection_spec(), whole((512, 48)), whole((512, 48))],
         out_specs=[whole((512, 384))] * 2 + ([whole((512, 1536))] if raw else []),
         out_shape=[shape, shape] + ([flat_shape] if raw else []),
         scratch_shapes=[] if raw else [pltpu.VMEM((512, 1536), BF16)],
@@ -393,7 +394,11 @@
 
 
 def out_spec():
-    return pl.BlockSpec((16, 96, 384), lambda *_: (0, 0, 2))
+    return pl.BlockSpec((16, 96, 384), lambda *_: (0, 0, 10))
+
+
+def projection_spec():
+    return pl.BlockSpec((1536, 768), lambda *_: (0, 4))
 
 
 def attend_call(window, length, queries, own, other, places, key_places, packed, after=()):
@@ -515,18 +520,21 @@
     emit(nt(rows, weight[...]), outs)
 
 
-def unproject_call(low_queries, pair_own, pair_came, cosine, sine, packed):
+def unproject_call(low_queries, pair_own, pair_came, cosine, sine, packed, after=()):
     wide = packed.shape[-1]
     return pl.pallas_call(
-        unproject_kernel,
+        later(unproject_kernel, len(after)),
         grid=(1,),
-        in_specs=[whole((512, 384))] * 3 + [whole((512, 48))] * 2 + [whole((1536, 768))],
+        in_specs=anywhere(after)
+        + [whole((512, 384))] * 3
+        + [whole((512, 48))] * 2
+        + [projection_spec()],
         out_specs=PARTIALS + [whole((512, 768))],
-        out_shape=PARTIAL_SHAPES + [jax.ShapeDtypeStruct((512, 768), BF16)],
+        out_shape=LOW_PARTIAL_SHAPES + [jax.ShapeDtypeStruct((512, 768), BF16)],
         compiler_params=params(40),
         cost_estimate=cost(1.3e9, 7e6),
         name="unproject",
-    )(low_queries, pair_own, pair_came, cosine, sine, packed.reshape(1536, wide))
+    )(*after, low_queries, pair_own, pair_came, cosine, sine, packed.reshape(1536, wide))
 
 
 def attend_weights_kernel(count, side_ref, *refs):
@@ -644,11 +652,11 @@
     blocks = [ref[0, 0] for ref in refs[:4]]
     refs = refs[4:]
     if attention:
-        unpack_attention(side, [block[:, :1152] for block in blocks], refs[:4])
+        start = 3072 if feed else 0
+        unpack_attention(side, [block[:, start : start + 1152] for block in blocks], refs[:4])
         refs = refs[4:]
     if feed:
-        start = 1152 if attention else 0
-        unpack_feed([block[:, start : start + 3072] for block in blocks], refs)
+        unpack_feed([block[:, :3072] for block in blocks], refs)
 
 
 def unpack_call(attention, feed, me, every):
@@ -706,41 +714,6 @@
     )(where, *after, w_gate, w_up, w_down)
 
 
-def assemble_kernel(where, *refs):
-    pieces, out, sems = refs[:10], refs[10], refs[11]
-    z, yhi, core = where[0], where[1], where[2]
-    handles = []
-    for turn in range(2):
-        side = core if turn == 0 else 1 - core
-        pair, after, before, first, second = pieces[5 * turn : 5 * turn + 5]
-        for step, parts in (
-            (0, (pair.at[0], pair.at[1])),
-            (1, (after.at[0], after.at[1])),
-            (3, (before.at[0], before.at[1])),
-            (2, (first.at[0], second.at[0])),
-        ):
-            for other, part in enumerate(parts):
-                high = yhi if other == 0 else 1 - yhi
-                place = 4 * lax.rem(z + step, 4) + 2 * high + side
-                handles.append(pltpu.make_async_copy(part, out.at[place], sems.at[len(handles)]))
-    for handle in handles:
-        handle.start()
-    for handle in handles:
-        handle.wait()
-
-
-def assemble_call(where, pieces, width):
-    return pl.pallas_call(
-        assemble_kernel,
-        in_specs=[pl.BlockSpec(memory_space=pltpu.SMEM)] + anywhere(pieces),
-        out_specs=pl.BlockSpec(memory_space=pl.ANY),
-        out_shape=jax.ShapeDtypeStruct((16, 96, width), BF16),
-        scratch_shapes=[pltpu.SemaphoreType.DMA((16,))],
-        cost_estimate=cost(1e3, 2 * 16 * 96 * width * 2),
-        name="assemble",
-    )(where, *pieces)
-
-
 WINDOW = 512
 EPSILON = 1e-05
 ROPE_BASE = 100000.0
@@ -753,6 +726,7 @@
 
 RIGHT = [(i, (i + 1) % 4) for i in range(4)]
 LEFT = [(i, (i - 1) % 4) for i in range(4)]
+ACROSS = [(i, (i + 2) % 4) for i in range(4)]
 SWAP = [(0, 1), (1, 0)]
 
 
@@ -820,6 +794,17 @@
     return own + from_left + from_right
 
 
+def ring_scatter_direct(own, left, right, far):
+    from_left = lax.ppermute(right, "x", RIGHT).astype(F32)
+    from_right = lax.ppermute(left, "x", LEFT).astype(F32)
+    from_far = lax.ppermute(far, "x", ACROSS).astype(F32)
+    return own + from_left + from_right + from_far
+
+
+def tie(value, *others):
+    return lax.optimization_barrier((value, *others))[0]
+
+
 def rms_norm(values, gain):
     return values * lax.rsqrt(jnp.mean(values * values, axis=-1, keepdims=True) + EPSILON) * gain
 
@@ -877,9 +862,10 @@
     return add_low(piece, lax.ppermute(piece, "ylo", SWAP))
 
 
-def out_home(piece):
-    moved = lax.ppermute(piece[:, 768:1152], AXES, inverse(ROWS))
-    return jnp.concatenate([piece[:, :768], moved, piece[:, 1152:]], axis=1)
+def out_home(piece, start):
+    first, last = start + 768, start + 1152
+    moved = lax.ppermute(piece[:, first:last], AXES, inverse(ROWS))
+    return jnp.concatenate([piece[:, :first], moved], axis=1)
 
 
 def butterfly(values):
@@ -910,41 +896,28 @@
     gains = jnp.stack([weights[0], weights[5], weights[9], weights[14]])
     gains = lax.dynamic_slice_in_dim(gains, core * 96, 96, axis=1).T
     gains = jnp.pad(gains, ((0, 0), (0, 124)))
-    def attention_piece(base, extra):
+    def line_weights(base, extra, after):
         w_q, w_k, w_v, w_out = weights[base + 1 : base + 5]
         out_block = lax.dynamic_slice(
             w_out, (96 * (x // 2), 384 * (2 * (x % 2) + core)), (96, 384)
         )
         out_block = lax.ppermute(out_block, AXES, ROWS)
-        parts = [
+        parts = [pack_feed_call(pair_index, *weights[base + 6 : base + 9], after=after)]
+        parts += [
             lax.dynamic_slice(w, (core * 96, x * (w.shape[1] // 4)), (96, w.shape[1] // 4))
             for w in (w_q, w_k, w_v)
         ]
-        return jnp.concatenate(parts + [out_block] + extra, axis=1)
-
-    attn_one = lax.all_gather(attention_piece(0, [gains]), SPREAD, axis=0, tiled=False)
-    gains = attn_one[:, :, 1152:1156].transpose(2, 0, 1).reshape(4, width).astype(F32)
+        piece = jnp.concatenate(parts + [out_block] + extra, axis=1)
+        return lax.all_gather(piece, SPREAD, axis=0, tiled=False)
+
+    first_weights = line_weights(0, [gains], ())
+    gains = first_weights[:, :, 4224:4228].transpose(2, 0, 1).reshape(4, width).astype(F32)
 
     length = lax.ppermute(lengths, AXES, LINES_LENGTH)
     rows = to_lines(tokens[0], z)
     pieces = ring_gather(rows)
     state = rows.astype(F32)
-
-    feed_one = pack_feed_call(pair_index, *weights[6:9], after=(rows,))
-    across = lax.ppermute(feed_one, "yhi", SWAP)
-    pair = jnp.stack([feed_one, across])
-    before = lax.ppermute(pair, "z", RIGHT)
-    ahead = lax.ppermute(pair, "z", LEFT)
-    first = lax.ppermute(before[:1], "z", RIGHT)
-    second = lax.ppermute(ahead[1:], "z", LEFT)
-    feed_parts = [pair, ahead, before, first, second]
-    feed_parts += [lax.ppermute(item, "core", SWAP) for item in feed_parts]
-    feed_one = assemble_call(jnp.stack([z, yhi, core]).astype(jnp.int32), feed_parts, 3072)
-
-    attn_two = lax.all_gather(attention_piece(9, []), SPREAD, axis=0, tiled=False)
-    feed_two = pack_feed_call(pair_index, *weights[15:18], after=(rows,))
-    feed_two = lax.all_gather(feed_two, SPREAD, axis=0, tiled=False)
-    packed = ((attn_one, feed_one), (attn_two, feed_two))
+    packed = (first_weights, line_weights(9, [], (rows,)))
 
     here = (2 * z + yhi) * stretch + jnp.arange(stretch, dtype=jnp.int32)
     valid = (here < lengths[0])[:, None]
@@ -976,19 +949,17 @@
 
     records = []
     for index, window in enumerate((WINDOW, 8 * stretch)):
-        attn, feed = packed[index]
+        attn = feed = packed[index]
         gain_attn, gain_feed = gains[2 * index], gains[2 * index + 1]
         if index == 0:
-            queries, own, flat = project_call(
-                True, pieces, gain_attn, attn, cosine, sine, after=(across,)
-            )
+            queries, own, flat = project_call(True, pieces, gain_attn, attn, cosine, sine)
             flats = (flat,)
         else:
             flats = ring_gather(rms_norm(state, gain_attn).astype(BF16))
             queries, own = project_call(False, flats, gain_attn, attn, cosine, sine)
         other = lax.ppermute(own, "core", SWAP)
         line = (queries, own, other, places, key_places)
-        after = grad_pieces[3:] if index else (ahead,)
+        after = grad_pieces[3:] if index else ()
         *partial, mixed, log_total = attend_call(window, length, *line, attn, after=after)
         saved_attn = (state, flats, line, mixed, log_total)
         state = state + ring_scatter(*partial)
@@ -1004,17 +975,20 @@
     gain_grads = [None] * 4
     zero = jnp.zeros((1,), jnp.int32)
     for index in (1, 0):
-        attn, feed = packed[index]
+        line_packed = packed[index]
         gain_attn, gain_feed = gains[2 * index], gains[2 * index + 1]
         saved_attn, saved_feed, window = records[index]
         base = 9 * index
 
         state, flats, gate, up, hidden = saved_feed
         if index == 0:
-            grad_pieces = ring_gather(grad.astype(BF16))
-        after = () if index else (attn_sum,)
-        *partial, low_gate, low_up = feed_backward_call(grad_pieces, feed, gate, up, after=after)
-        grad, gain_grads[2 * index + 1] = norm_back(grad, ring_scatter(*partial), state, gain_feed)
+            grad_pieces = ring_gather(tie(grad.astype(BF16), output))
+        after = () if index else (second_feed, second_sum)
+        *partial, low_gate, low_up = feed_backward_call(
+            grad_pieces, line_packed, gate, up, after=after
+        )
+        own_normed = ring_scatter_direct(*partial)
+        grad, gain_grads[2 * index + 1] = norm_back(grad, own_normed, state, gain_feed)
         halves = feed_weights_call(side, flats, grad_pieces, low_gate, low_up, hidden)
         feed_sum = core_sum(*halves)
 
@@ -1025,32 +999,42 @@
             length,
             grad_pieces,
             *line,
-            attn,
+            line_packed,
             log_total,
             cosine_t,
             sine_t,
-            after=(feed_sum,) if index else (feed_sum, output),
+            after=(feed_sum,) if index else (feed_sum, second_attn),
         )
         came = lax.ppermute(pair_other, "core", SWAP)
-        *partial, low = unproject_call(low_queries, pair_own, came, cosine, sine, attn)
-        grad, gain_grads[2 * index] = norm_back(grad, ring_scatter(*partial), state, gain_attn)
-        after = () if index else (second_piece,)
-        halves = attend_weights_call(side, flats, grad_pieces, low, mixed, after=after)
+        *partial, low = unproject_call(
+            low_queries,
+            pair_own,
+            came,
+            cosine,
+            sine,
+            line_packed,
+            after=() if index else (second_piece,),
+        )
+        own_normed = ring_scatter_direct(*partial)
+        grad, gain_grads[2 * index] = norm_back(grad, own_normed, state, gain_attn)
+        halves = attend_weights_call(side, flats, grad_pieces, low, mixed)
         attn_sum = core_sum(*halves)
-        feed_pair = z_sum(feed_sum, where, index)
-        attn_pair = z_sum(attn_sum, where, index)
         if index:
-            piece = y_sum(jnp.concatenate([attn_pair, feed_pair], axis=2), where)
-            second_piece = out_home(piece)
+            second_sum = attn_sum
+            second_feed = z_sum(feed_sum, where, True)
+            second_attn = z_sum(attn_sum, where, True)
+            piece = y_sum(jnp.concatenate([second_feed, second_attn], axis=2), where)
+            second_piece = out_home(piece, 3072)
             every = lax.all_gather(second_piece, ("x", "core"), axis=0, tiled=False)
             out = unpack_call(True, True, zero, every.reshape(4, 2, 96, -1))
             results[base + 1 : base + 5] = out[:4]
             results[base + 6 : base + 9] = out[4:]
         else:
-            every = line_gather(y_sum(feed_pair, where), core)
             place = x.astype(jnp.int32).reshape(1)
+            every = line_gather(y_sum(z_sum(feed_sum, where, False), where), core)
             results[base + 6 : base + 9] = unpack_call(False, True, place, every)
-            every = line_gather(out_home(y_sum(attn_pair, where)), core)
+            piece = y_sum(z_sum(attn_sum, where, False), where)
+            every = line_gather(out_home(piece, 0), core)
             results[base + 1 : base + 5] = unpack_call(True, False, place, every)
     gain_sums = butterfly(jnp.stack(gain_grads))
     gain_sums = lax.dynamic_slice_in_dim(gain_sums, (2 * z + yhi) * 192, 192, axis=1)

time: 1150 us -> 828 us (0.72)
  Pallas kernels: 441 us -> 156 us
  starting transfers between devices: 285 us -> 248 us
  waiting for transfers between devices: 249 us -> 284 us
  local copies, waits for them, and re-layouts: 91.7 us -> 70 us
  other arithmetic: 55.7 us -> 42.6 us
    pallas_call x3 -> x2, Pallas kernels: 292 us -> 7.23 us  [unproject_call(): pl.pallas_call(later(unproject_kernel, len(after)), grid=(1,), in_specs=a...]
    all_gather x3 -> x2, waiting for transfers between devices: 0.03 us -> 52.4 us  [line_weights(): return lax.all_gather(piece, SPREAD, axis=0, tiled=False)]
    ppermute x8 -> x4, waiting for transfers between devices: 37.9 us -> 11.5 us  [ring_scatter(): from_left = lax.ppermute(right, 'x', RIGHT).astype(F32)]
    ppermute x3, waiting for transfers between devices: 25.2 us -> 6.49 us  [y_sum(): return add_low(piece, lax.ppermute(piece, 'ylo', SWAP))]
    ppermute x14 -> x16, waiting for transfers between devices: 38.4 us -> 56.6 us  [the longest x4 26.3 us: ring_scatter_direct(): from_far = lax.ppermute(far, 'x', ACROSS).astype(F32)]
    ppermute x2, starting transfers between devices: 0.95 us -> 15.9 us  [ring_stack(): second = lax.ppermute(after[half:], axis, LEFT)]
    ppermute x14 -> x16, starting transfers between devices: 32.1 us -> 17.5 us  [the longest x4 11.2 us: ring_scatter_direct(): from_right = lax.ppermute(left, 'x', LEFT).astype(F32)]
    ppermute x8, waiting for transfers between devices: 32.6 us -> 44.9 us  [ring_gather(): from_left = lax.ppermute(block, 'x', RIGHT)]
  transfers between devices with their start and end apart: 140 -> 125, of which waited for: 48 -> 50; matrix products, arithmetic and copies ran while one was open for 9% -> 8% of each run, Pallas kernels for 33% -> 13%
where the time goes in v5:
time: 828 us; the launch traced here: 818 us
  waiting for transfers between devices  284 us (34%)
  starting transfers between devices  248 us (30%)
  Pallas kernels  156 us (19%)
  local copies, waits for them, and re-layouts  70 us (8%)
  other arithmetic  42.6 us (5%)
  between operations  17 us (2%)
    all_gather x2, waiting for transfers between devices, line_weights(): return lax.all_gather(piece, SPREAD, axis=0, tiled=False)  52.4 us
    ppermute x8, waiting for transfers between devices, ring_gather(): from_left = lax.ppermute(block, 'x', RIGHT)  44.9 us
    ppermute x8, starting transfers between devices, to_lines(): out.append(lax.ppermute(piece, AXES, LINES[k]))  40.2 us
    unnamed x219, local copies, waits for them, and re-layouts  38.3 us
    ppermute x8, starting transfers between devices, from_lines(): lax.ppermute(block[part * k:part * (k + 1)], AXES, inverse(LINES[k]))  36 us
    ppermute x3, waiting for transfers between devices, y_sum(): piece = add_low(mine, lax.ppermute(theirs, 'yhi', SWAP))  30.7 us
    pallas_call x2, Pallas kernels, feed_weights_call(): pl.pallas_call(feed_weights_kernel, grid_spec=spec, out_shape=[shape, sha...  27.3 us
    pallas_call x2, Pallas kernels, feed_backward_call(): pl.pallas_call(later(feed_backward_kernel, len(after)), grid=(4,), in_spe...  26.4 us
  transfers between devices with their start and end apart: 125, of which 50 were waited for; matrix products, arithmetic and copies ran while one was open for 8% of the time, Pallas kernels for 13%

profile of v5, /device:TPU:1, one launch (start us, length us, event | category | flops | bytes accessed | tf_op | source)
XLA Modules:
  0.0 817.8 jit_solution(13549619703135512309)
XLA Ops:
  20.8 11.2 %collective-permute-start = (bf16[32,1536]{1,0:T(8,128)(2,1)S(1)}, bf16[32,1536]{1,0:T(8,128)(2,1)S(1)}, u32[]{:S(2)}, u32[]{:S(2)}) collective-permute-start(bf16[32,1536]{1,0:T(8,128)(2,1)S(1)} %get-tuple-element.250), channel_id=1, source_target_pairs={{0,0},{1,8},{2,16},{3,24},{4,32},{5,40},{6,48},{7,56},{8,1},{9,9},... | collective-permute-start | bytes 294920 | tf_op jit(solution)/shard_map/ppermute | solution.py:764
  33.3 7.4 collective-permute-start.2
  73.8 52.4 %all-gather.7.cloned.1.call-done.refs_6_.refs_7_.refs_8_ = bf16[1536,4352]{1,0:T(8,128)(2,1)} async-done(((bf16[96,4352]{1,0:T(8,128)(2,1)}), bf16[1536,4352]{1,0:T(8,128)(2,1)}) %all-gather.7.cloned.1.call-update) | async-done | bytes 13369360 | tf_op jit(solution)/shard_map/all_gather | solution.py:911
  139.2 9.1 %attend.2 = (f32[128,1536]{1,0:T(8,128)S(1)}, f32[128,1536]{1,0:T(8,128)S(1)}, f32[128,1536]{1,0:T(8,128)S(1)}, bf16[128,1536]{1,0:T(8,128)(2,1)S(1)}, bf16[512,...) custom-call(s32[1]{0:T(128)} %collective-permute-done.4.length.refs_2_.refs_1_, ...), custom_call_target="tpu_custom_call" | custom-call | flops 3000000000 | bytes 6000000 | tf_op jit(solution)/shard_map/attend/pallas_call | solution.py:405
  169.9 8.7 %collective-permute-start.18 = (bf16[32,1536]{1,0:T(8,128)(2,1)}, bf16[32,1536]{1,0:T(8,128)(2,1)S(1)}, u32[]{:S(2)}, u32[]{:S(2)}) collective-permute-start(bf16[32,1536]{1,0:T(8,128)(2,1)} %get-tuple-element.242), channel_id=1, source_target_pairs={{0,48},{1,56},{2,0},{3,8},{4,16},{5,24},{6,32},{7,40},{8,49},{9,57... | collective-permute-start | bytes 294920 | tf_op jit(solution)/shard_map/ppermute | solution.py:764
  183.0 7.6 collective-permute-done.19.refs_2_.refs_1_
  196.8 9.3 %feed_forward.2 = (f32[128,1536]{1,0:T(8,128)S(1)}, f32[128,1536]{1,0:T(8,128)S(1)}, f32[128,1536]{1,0:T(8,128)S(1)}, bf16[128,1536]{1,0:T(8,128)(2,1)S(1)}, f32...) custom-call(bf16[128,1536]{1,0:T(8,128)(2,1)S(1)} %constant_dynamic-update-slice_fusion.6.refs_0_.refs_5, ...), custom_call_target="tpu_custom_call" | custom-call | flops 4899999744 | bytes 18000000 | tf_op jit(solution)/shard_map/feed_forward/pallas_call | solution.py:138
  246.1 8.4 %collective-permute-start.36 = (bf16[512,384]{1,0:T(8,128)(2,1)S(1)}, bf16[512,384]{1,0:T(8,128)(2,1)S(1)}, u32[]{:S(2)}, u32[]{:S(2)}) collective-permute-start(bf16[512,384]{1,0:T(8,128)(2,1)S(1)} %get-tuple-element.113.refs_4_.refs_8_), channel_id=1, source_target_pairs={{0,8},{8,0},{1,9},{9,1},{2,10},{10,2},{3,11},{11,3},{4,12},{12,4},... | collective-permute-start | bytes 1179656 | tf_op jit(solution)/shard_map/ppermute | solution.py:960
  262.8 9.1 %attend.3 = (f32[128,1536]{1,0:T(8,128)S(1)}, f32[128,1536]{1,0:T(8,128)S(1)}, f32[128,1536]{1,0:T(8,128)S(1)}, bf16[128,1536]{1,0:T(8,128)(2,1)S(1)}, bf16[512,...) custom-call(bf16[64,1536]{1,0:T(8,128)(2,1)S(1)} %collective-permute-done.28.refs_0_.refs_3_.refs_8_, ...), custom_call_target="tpu_custom_call" | custom-call | flops 3000000000 | bytes 6000000 | tf_op jit(solution)/shard_map/attend/pallas_call | solution.py:405
  306.5 9.2 %feed_forward.3 = (f32[128,1536]{1,0:T(8,128)S(1)}, f32[128,1536]{1,0:T(8,128)S(1)}, f32[128,1536]{1,0:T(8,128)S(1)}, bf16[128,1536]{1,0:T(8,128)(2,1)S(1)}, f32...) custom-call(bf16[128,1536]{1,0:T(8,128)(2,1)S(1)} %multiply_convert_fusion.refs_0_, ...), custom_call_target="tpu_custom_call" | custom-call | flops 4899999744 | bytes 18000000 | tf_op jit(solution)/shard_map/feed_forward/pallas_call | solution.py:138
  319.1 12.6 %feed_backward.2 = (f32[128,1536]{1,0:T(8,128)S(1)}, bf16[128,1536]{1,0:T(8,128)(2,1)S(1)}, bf16[128,1536]{1,0:T(8,128)(2,1)S(1)}, bf16[128,1536]{1,0:T(8,128)(2...) custom-call(bf16[128,1536]{1,0:T(8,128)(2,1)S(1)} %constant_dynamic-update-slice_fusion.6.refs_0_.refs_5_, ...), custom_call_target="tpu_custom_call" | custom-call | flops 4899999744 | bytes 20000000 | tf_op jit(solution)/shard_map/feed_backward/pallas_call | solution.py:191
  334.9 13.1 %feed_weights.2 = (bf16[8,96,3072]{2,1,0:T(8,128)(2,1)S(1)}, bf16[8,96,3072]{2,1,0:T(8,128)(2,1)}) custom-call(s32[1]{0:T(128)} %bitcast.5.side_ref, bf16[128,1536]{1,0:T(8,128)(2,1)S(1)} %multiply_convert_fusion.refs_0_, bf16[128,1536]{1,0:T(8,128)(2,1)S(1)} %collective-permute-done.41.refs_1_, bf16[128,1536]{1,0:T(8,128)(2,1)S(1)} %collective-permute-done.42.refs_2_, ...), custom_call_target="tpu_custom_call" | custom-call | flops 4899999744 | bytes 18000000 | tf_op jit(solution)/shard_map/feed_weights/pallas_call | solution.py:287
  353.4 7.7 collective-permute-done.56
  378.6 9.3 %collective-permute-done.55 = bf16[128,1536]{1,0:T(8,128)(2,1)S(1)} collective-permute-done((bf16[128,1536]{1,0:T(8,128)(2,1)}, bf16[128,1536]{1,0:T(8,128)(2,1)S(1)}, u32[]{:S(2)}, u32[]{:S(2)}) %collective-permute-start.55) | collective-permute-done | bytes 393248 | tf_op jit(solution)/shard_map/ppermute | solution.py:800
  391.4 7.2 collective-permute-done.57.refs_3_.refs_6_
  404.8 12.9 %attend_backward.2 = (bf16[512,384]{1,0:T(8,128)(2,1)S(1)}, f32[512,384]{1,0:T(8,128)}, bf16[512,384]{1,0:T(8,128)(2,1)S(1)}) custom-call(bf16[8,96,3072]{2,1,0:T(8,128)(2,1)} %add_convert_fusion.1.refs_0_, s32[1]{0:T(128)} %collective-permute-done.4.length.refs_2_.refs_1_, bf16[128,1536]{1,0:T(8,128)(2,1)S(1)} %fusion.38.refs_2_.refs_5_, ...), custom_call_target="tpu_custom_call" | custom-call | flops 6000000000 | bytes 6000000 | tf_op jit(solution)/shard_map/attend_backward/pallas_call | solution.py:478
  441.7 7.4 collective-permute-done.64
  458.4 15.0 %collective-permute-start.49 = (bf16[32,1536]{1,0:T(8,128)(2,1)S(1)}, bf16[32,1536]{1,0:T(8,128)(2,1)}, u32[]{:S(2)}, u32[]{:S(2)}) collective-permute-start(bf16[32,1536]{1,0:T(8,128)(2,1)S(1)} %get-tuple-element.235), channel_id=1, source_target_pairs={{0,0},{8,1},{16,2},{24,3},{32,4},{40,5},{48,6},{56,7},{1,8},{9,9},... | collective-permute-start | bytes 294920 | tf_op jit(solution)/shard_map/ppermute | solution.py:772
  473.5 7.2 collective-permute-start.51
  496.6 8.4 %collective-permute-done.66.refs_3_.refs_6_ = bf16[128,1536]{1,0:T(8,128)(2,1)S(1)} collective-permute-done((bf16[128,1536]{1,0:T(8,128)(2,1)S(1)}, bf16[128,1536]{1,0:T(8,128)(2,1)S(1)}, u32[]{:S(2)}, u32[]{:S(2)}) %collective-permute-start.66) | collective-permute-done | bytes 393248 | tf_op jit(solution)/shard_map/ppermute | solution.py:779
  520.1 13.8 %feed_backward.3 = (f32[128,1536]{1,0:T(8,128)S(1)}, bf16[128,1536]{1,0:T(8,128)(2,1)}, bf16[128,1536]{1,0:T(8,128)(2,1)}, bf16[128,1536]{1,0:T(8,128)(2,1)}, bf...) custom-call(bf16[2,96,3072]{2,1,0:T(8,128)(2,1)S(1)} %copy-done.2, bf16[8,96,1152]{2,1,0:T(8,128)(2,1)S(1)} %copy-done, ...), custom_call_target="tpu_custom_call" | custom-call | flops 4899999744 | bytes 20000000 | tf_op jit(solution)/shard_map/feed_backward/pallas_call | solution.py:191
  534.9 14.2 %feed_weights.3 = (bf16[8,96,3072]{2,1,0:T(8,128)(2,1)S(1)}, bf16[8,96,3072]{2,1,0:T(8,128)(2,1)}) custom-call(s32[1]{0:T(128)} %bitcast.5.side_ref, bf16[128,1536]{1,0:T(8,128)(2,1)S(1)} %copy-done.11, bf16[128,1536]{1,0:T(8,128)(2,1)S(1)} %copy-done.19, bf16[128,1536]{1,0:T(8,128)(2,1)S(1)} %copy-done.21, bf16[64,1536]{1,0:T(8,128)(2,1)S(1)} %copy-done.54, ...), custom_call_target="tpu_custom_call" | custom-call | flops 4899999744 | bytes 18000000 | tf_op jit(solution)/shard_map/feed_weights/pallas_call | solution.py:287
  564.6 7.2 collective-permute-done.71
  575.3 7.5 collective-permute-done.73
  622.7 13.0 %attend_backward.3 = (bf16[512,384]{1,0:T(8,128)(2,1)S(1)}, f32[512,384]{1,0:T(8,128)}, bf16[512,384]{1,0:T(8,128)(2,1)S(1)}) custom-call(bf16[8,96,3072]{2,1,0:T(8,128)(2,1)} %copy-done.92, bf16[2,96,1152]{2,1,0:T(8,128)(2,1)} %reduce-scatter.5.cloned.1.call-done.refs_1_, s32[1]{0:T(128)} %collective-permute-done.4.length.refs_2_.refs_1_, ...), custom_call_target="tpu_custom_call" | custom-call | flops 6000000000 | bytes 6000000 | tf_op jit(solution)/shard_map/attend_backward/pallas_call | solution.py:478
  657.1 16.8 %collective-permute-done.82 = bf16[128,1536]{1,0:T(8,128)(2,1)S(1)} collective-permute-done((bf16[128,1536]{1,0:T(8,128)(2,1)S(1)}, bf16[128,1536]{1,0:T(8,128)(2,1)S(1)}, u32[]{:S(2)}, u32[]{:S(2)}) %collective-permute-start.82) | collective-permute-done | bytes 393248 | tf_op jit(solution)/shard_map/ppermute | solution.py:798
  678.0 7.7 collective-permute-done.84
  691.5 10.2 %collective-permute-done.112 = bf16[2,96,3072]{2,1,0:T(8,128)(2,1)S(1)} collective-permute-done((bf16[2,96,3072]{2,1,0:T(8,128)(2,1)S(1)}, bf16[2,96,3072]{2,1,0:T(8,128)(2,1)S(1)}, u32[]{:S(2)}, u32[]{:S(2)}) %collective-permute-start.112) | collective-permute-done | bytes 1179680 | tf_op jit(solution)/shard_map/ppermute | solution.py:854
  714.1 7.4 collective-permute-done.113
  723.0 15.8 %collective-permute-done.101 = bf16[96,1152]{1,0:T(8,128)(2,1)S(1)} collective-permute-done((bf16[96,1152]{1,0:T(8,128)(2,1)S(1)}, bf16[96,1152]{1,0:T(8,128)(2,1)S(1)}, u32[]{:S(2)}, u32[]{:S(2)}) %collective-permute-start.101) | collective-permute-done | bytes 221216 | tf_op jit(solution)/shard_map/ppermute | solution.py:861
  744.6 9.3 %collective-permute-start.85 = (bf16[32,1536]{1,0:T(8,128)(2,1)S(1)}, bf16[32,1536]{1,0:T(8,128)(2,1)S(1)}, u32[]{:S(2)}, u32[]{:S(2)}) collective-permute-start(bf16[32,1536]{1,0:T(8,128)(2,1)S(1)} %get-tuple-element.230), channel_id=1, source_target_pairs={{0,0},{8,1},{16,2},{24,3},{32,4},{40,5},{48,6},{56,7},{1,8},{9,9},... | collective-permute-start | bytes 294920 | tf_op jit(solution)/shard_map/ppermute | solution.py:772
  758.8 14.2 %collective-permute-start.118 = (bf16[48,3072]{1,0:T(8,128)(2,1)S(1)}, bf16[48,3072]{1,0:T(8,128)(2,1)S(1)}, u32[]{:S(2)}, u32[]{:S(2)}) collective-permute-start(bf16[48,3072]{1,0:T(8,128)(2,1)S(1)} %slice.412), channel_id=1, source_target_pairs={{0,48},{16,0},{32,16},{48,32},{1,49},{17,1},{33,17},{49,33},{2,50}... | collective-permute-start | bytes 884744 | tf_op jit(solution)/shard_map/ppermute | solution.py:825
  (656 shorter events, 430.2 us)
Async XLA Ops:
  7.2 119.0 %all-gather.7.cloned.1.call-start = ((), (), s32[]{:S(2)}) async-start(), calls=%async_computation.4 | async-start | bytes 14204928 | tf_op jit(solution)/shard_map/all_gather | solution.py:911
  20.7 218.4 %all-gather.9.cloned.1.call-start = ((), (), s32[]{:S(2)}) async-start(), calls=%async_computation.5 | async-start | bytes 13787136 | tf_op jit(solution)/shard_map/all_gather | solution.py:911
  20.8 26.2 %collective-permute-start = (bf16[32,1536]{1,0:T(8,128)(2,1)S(1)}, bf16[32,1536]{1,0:T(8,128)(2,1)S(1)}, u32[]{:S(2)}, u32[]{:S(2)}) collective-permute-start(bf16[32,1536]{1,0:T(8,128)(2,1)S(1)} %get-tuple-element.250), channel_id=1, source_target_pairs={{0,0},{1,8},{2,16},{3,24},{4,32},{5,40},{6,48},{7,56},{8,1},{9,9},... | collective-permute-start | bytes 294920 | tf_op jit(solution)/shard_map/ppermute | solution.py:764
  56.2 458.4 %reduce-scatter.3.cloned.1.call-start = ((), (), s32[]{:S(2)}) async-start(), calls=%async_computation.2 | async-start | bytes 5898240 | tf_op jit(solution)/shard_map/reduce_scatter | solution.py:842
  56.2 79.8 %collective-permute-start.4 = (s32[1]{0:T(128)}, s32[1]{0:T(128)}, u32[]{:S(2)}, u32[]{:S(2)}) collective-permute-start(s32[1]{0:T(128)} %param.22), channel_id=1, source_target_pairs={{0,0},{1,8},{2,16},{3,24},{4,32},{5,40},{6,48},{7,56},{8,1},{9,9},... | collective-permute-start | bytes 20 | tf_op jit(solution)/shard_map/ppermute | solution.py:916
  69.9 59.3 %collective-permute-start.7 = (bf16[64,1536]{1,0:T(8,128)(2,1)S(1)}, bf16[64,1536]{1,0:T(8,128)(2,1)S(1)}, u32[]{:S(2)}, u32[]{:S(2)}) collective-permute-start(bf16[64,1536]{1,0:T(8,128)(2,1)S(1)} %slice.366), channel_id=1, source_target_pairs={{0,16},{16,32},{32,48},{48,0},{1,17},{17,33},{33,49},{49,1},{2,18}... | collective-permute-start | bytes 589832 | tf_op jit(solution)/shard_map/ppermute | solution.py:781
  73.3 55.9 %collective-permute-start.8 = (bf16[64,1536]{1,0:T(8,128)(2,1)S(1)}, bf16[64,1536]{1,0:T(8,128)(2,1)S(1)}, u32[]{:S(2)}, u32[]{:S(2)}) collective-permute-start(bf16[64,1536]{1,0:T(8,128)(2,1)S(1)} %slice.367), channel_id=1, source_target_pairs={{0,48},{16,0},{32,16},{48,32},{1,49},{17,1},{33,17},{49,33},{2,50}... | collective-permute-start | bytes 589832 | tf_op jit(solution)/shard_map/ppermute | solution.py:782
  156.8 21.9 %collective-permute-start.12 = (bf16[128,1536]{1,0:T(8,128)(2,1)}, bf16[128,1536]{1,0:T(8,128)(2,1)}, u32[]{:S(2)}, u32[]{:S(2)}) collective-permute-start(bf16[128,1536]{1,0:T(8,128)(2,1)} %pad_maximum_fusion.7), channel_id=1, source_target_pairs={{0,16},{16,32},{32,48},{48,0},{1,17},{17,33},{33,49},{49,1},{2,18}... | collective-permute-start | bytes 1179656 | tf_op jit(solution)/shard_map/ppermute | solution.py:792
  157.7 21.0 %collective-permute-start.14 = (bf16[128,1536]{1,0:T(8,128)(2,1)}, bf16[128,1536]{1,0:T(8,128)(2,1)S(1)}, u32[]{:S(2)}, u32[]{:S(2)}) collective-permute-start(bf16[128,1536]{1,0:T(8,128)(2,1)} %pad_maximum_fusion.8), channel_id=1, source_target_pairs={{0,48},{16,0},{32,16},{48,32},{1,49},{17,1},{33,17},{49,33},{2,50}... | collective-permute-start | bytes 1179656 | tf_op jit(solution)/shard_map/ppermute | solution.py:793
  169.9 23.9 %collective-permute-start.18 = (bf16[32,1536]{1,0:T(8,128)(2,1)}, bf16[32,1536]{1,0:T(8,128)(2,1)S(1)}, u32[]{:S(2)}, u32[]{:S(2)}) collective-permute-start(bf16[32,1536]{1,0:T(8,128)(2,1)} %get-tuple-element.242), channel_id=1, source_target_pairs={{0,48},{1,56},{2,0},{3,8},{4,16},{5,24},{6,32},{7,40},{8,49},{9,57... | collective-permute-start | bytes 294920 | tf_op jit(solution)/shard_map/ppermute | solution.py:764
  365.4 191.7 %reduce-scatter.5.cloned.1.call-start = ((), (), s32[]{:S(2)}) async-start(), calls=%async_computation.3 | async-start | bytes 2211840 | tf_op jit(solution)/shard_map/reduce_scatter | solution.py:842
  373.4 50.0 %collective-permute-start.47 = (bf16[64,1536]{1,0:T(8,128)(2,1)S(1)}, bf16[64,1536]{1,0:T(8,128)(2,1)S(1)}, u32[]{:S(2)}, u32[]{:S(2)}) collective-permute-start(bf16[64,1536]{1,0:T(8,128)(2,1)S(1)} %get-tuple-element.237), channel_id=1, source_target_pairs={{0,48},{16,0},{32,16},{48,32},{1,49},{17,1},{33,17},{49,33},{2,50}... | collective-permute-start | bytes 589832 | tf_op jit(solution)/shard_map/ppermute | solution.py:789
  401.4 48.0 %collective-permute-start.46 = (bf16[128,1536]{1,0:T(8,128)(2,1)S(1)}, bf16[128,1536]{1,0:T(8,128)(2,1)S(1)}, u32[]{:S(2)}, u32[]{:S(2)}) collective-permute-start(bf16[128,1536]{1,0:T(8,128)(2,1)S(1)} %pad_maximum_fusion.13), channel_id=1, source_target_pairs={{0,16},{16,32},{32,48},{48,0},{1,17},{17,33},{33,49},{49,1},{2,18}... | collective-permute-start | bytes 1179656 | tf_op jit(solution)/shard_map/ppermute | solution.py:792
  437.7 42.9 %collective-permute-start.65 = (bf16[8,96,1152]{2,1,0:T(8,128)(2,1)S(1)}, bf16[8,96,1152]{2,1,0:T(8,128)(2,1)S(1)}, u32[]{:S(2)}, u32[]{:S(2)}) collective-permute-start(bf16[8,96,1152]{2,1,0:T(8,128)(2,1)S(1)} %get-tuple-element.144), channel_id=1, source_target_pairs={{0,8},{8,0},{1,9},{9,1},{2,10},{10,2},{3,11},{11,3},{4,12},{12,4},... | collective-permute-start | bytes 5308424 | tf_op jit(solution)/shard_map/ppermute | solution.py:837
  458.4 24.0 %collective-permute-start.49 = (bf16[32,1536]{1,0:T(8,128)(2,1)S(1)}, bf16[32,1536]{1,0:T(8,128)(2,1)}, u32[]{:S(2)}, u32[]{:S(2)}) collective-permute-start(bf16[32,1536]{1,0:T(8,128)(2,1)S(1)} %get-tuple-element.235), channel_id=1, source_target_pairs={{0,0},{8,1},{16,2},{24,3},{32,4},{40,5},{48,6},{56,7},{1,8},{9,9},... | collective-permute-start | bytes 294920 | tf_op jit(solution)/shard_map/ppermute | solution.py:772
  482.3 321.6 %all-gather.11.cloned.1.call-start = ((), (), s32[]{:S(2)}) async-start(), calls=%async_computation.6 | async-start | bytes 7299072 | tf_op jit(solution)/shard_map/all_gather | solution.py:1028
  551.2 54.9 %collective-permute-start.76 = (bf16[8,96,3072]{2,1,0:T(8,128)(2,1)}, bf16[8,96,3072]{2,1,0:T(8,128)(2,1)}, u32[]{:S(2)}, u32[]{:S(2)}) collective-permute-start(bf16[8,96,3072]{2,1,0:T(8,128)(2,1)} %get-tuple-element.156), channel_id=1, source_target_pairs={{0,8},{8,0},{1,9},{9,1},{2,10},{10,2},{3,11},{11,3},{4,12},{12,4},... | collective-permute-start | bytes 14155784 | tf_op jit(solution)/shard_map/ppermute | solution.py:837
  561.0 21.8 %collective-permute-start.73 = (bf16[96,4224]{1,0:T(8,128)(2,1)}, bf16[96,4224]{1,0:T(8,128)(2,1)}, u32[]{:S(2)}, u32[]{:S(2)}) collective-permute-start(bf16[96,4224]{1,0:T(8,128)(2,1)} %dynamic-slice_bitcast_fusion), channel_id=1, source_target_pairs={{0,1},{1,0},{2,3},{3,2},{4,5},{5,4},{6,7},{7,6},{8,9},{9,8},{10,11... | collective-permute-start | bytes 2433032 | tf_op jit(solution)/shard_map/ppermute | solution.py:861
  596.3 26.4 %collective-permute-start.79 = (bf16[64,1536]{1,0:T(8,128)(2,1)S(1)}, bf16[64,1536]{1,0:T(8,128)(2,1)S(1)}, u32[]{:S(2)}, u32[]{:S(2)}) collective-permute-start(bf16[64,1536]{1,0:T(8,128)(2,1)S(1)} %slice.399), channel_id=1, source_target_pairs={{0,16},{16,32},{32,48},{48,0},{1,17},{17,33},{33,49},{49,1},{2,18}... | collective-permute-start | bytes 589832 | tf_op jit(solution)/shard_map/ppermute | solution.py:781
  596.4 26.3 %collective-permute-start.80 = (bf16[64,1536]{1,0:T(8,128)(2,1)S(1)}, bf16[64,1536]{1,0:T(8,128)(2,1)S(1)}, u32[]{:S(2)}, u32[]{:S(2)}) collective-permute-start(bf16[64,1536]{1,0:T(8,128)(2,1)S(1)} %slice.400), channel_id=1, source_target_pairs={{0,48},{16,0},{32,16},{48,32},{1,49},{17,1},{33,17},{49,33},{2,50}... | collective-permute-start | bytes 589832 | tf_op jit(solution)/shard_map/ppermute | solution.py:782
  605.5 33.8 %collective-permute-start.75 = (bf16[96,384]{1,0:T(8,128)(2,1)S(1)}, bf16[96,384]{1,0:T(8,128)(2,1)S(1)}, u32[]{:S(2)}, u32[]{:S(2)}) collective-permute-start(bf16[96,384]{1,0:T(8,128)(2,1)S(1)} %slice.398), channel_id=1, source_target_pairs={{0,0},{4,1},{16,2},{20,3},{32,4},{36,5},{48,6},{52,7},{8,8},{12,9}... | collective-permute-start | bytes 221192 | tf_op jit(solution)/shard_map/ppermute | solution.py:867
  614.8 38.9 %collective-permute-start.109 = (bf16[1,96,3072]{2,1,0:T(8,128)(2,1)}, bf16[1,96,3072]{2,1,0:T(8,128)(2,1)}, u32[]{:S(2)}, u32[]{:S(2)}) collective-permute-start(bf16[1,96,3072]{2,1,0:T(8,128)(2,1)} %get-tuple-element.212), channel_id=1, source_target_pairs={{0,2},{2,4},{4,6},{6,0},{1,3},{3,5},{5,7},{7,1},{8,10},{10,12},{12... | collective-permute-start | bytes 1769480 | tf_op jit(solution)/shard_map/ppermute | solution.py:849
  619.0 34.7 %collective-permute-start.111 = (bf16[1,96,3072]{2,1,0:T(8,128)(2,1)}, bf16[1,96,3072]{2,1,0:T(8,128)(2,1)}, u32[]{:S(2)}, u32[]{:S(2)}) collective-permute-start(bf16[1,96,3072]{2,1,0:T(8,128)(2,1)} %get-tuple-element.214), channel_id=1, source_target_pairs={{0,6},{2,0},{4,2},{6,4},{1,7},{3,1},{5,3},{7,5},{8,14},{10,8},{12,... | collective-permute-start | bytes 1769480 | tf_op jit(solution)/shard_map/ppermute | solution.py:850
  650.6 53.1 %collective-permute-start.96 = (bf16[8,96,1152]{2,1,0:T(8,128)(2,1)S(1)}, bf16[8,96,1152]{2,1,0:T(8,128)(2,1)S(1)}, u32[]{:S(2)}, u32[]{:S(2)}) collective-permute-start(bf16[8,96,1152]{2,1,0:T(8,128)(2,1)S(1)} %get-tuple-element.169), channel_id=1, source_target_pairs={{0,8},{8,0},{1,9},{9,1},{2,10},{10,2},{3,11},{11,3},{4,12},{12,4},... | collective-permute-start | bytes 5308424 | tf_op jit(solution)/shard_map/ppermute | solution.py:837
  651.0 22.9 %collective-permute-start.82 = (bf16[128,1536]{1,0:T(8,128)(2,1)S(1)}, bf16[128,1536]{1,0:T(8,128)(2,1)S(1)}, u32[]{:S(2)}, u32[]{:S(2)}) collective-permute-start(bf16[128,1536]{1,0:T(8,128)(2,1)S(1)} %get-tuple-element.162), channel_id=1, source_target_pairs={{0,16},{16,32},{32,48},{48,0},{1,17},{17,33},{33,49},{49,1},{2,18}... | collective-permute-start | bytes 1179656 | tf_op jit(solution)/shard_map/ppermute | solution.py:798
  651.0 27.0 %collective-permute-start.83 = (bf16[128,1536]{1,0:T(8,128)(2,1)S(1)}, bf16[128,1536]{1,0:T(8,128)(2,1)S(1)}, u32[]{:S(2)}, u32[]{:S(2)}) collective-permute-start(bf16[128,1536]{1,0:T(8,128)(2,1)S(1)} %get-tuple-element.163), channel_id=1, source_target_pairs={{0,48},{16,0},{32,16},{48,32},{1,49},{17,1},{33,17},{49,33},{2,50}... | collective-permute-start | bytes 1179656 | tf_op jit(solution)/shard_map/ppermute | solution.py:799
  653.7 32.0 %collective-permute-start.84 = (bf16[128,1536]{1,0:T(8,128)(2,1)S(1)}, bf16[128,1536]{1,0:T(8,128)(2,1)S(1)}, u32[]{:S(2)}, u32[]{:S(2)}) collective-permute-start(bf16[128,1536]{1,0:T(8,128)(2,1)S(1)} %get-tuple-element.164), channel_id=1, source_target_pairs={{0,32},{16,48},{32,0},{48,16},{1,33},{17,49},{33,1},{49,17},{2,34}... | collective-permute-start | bytes 1179656 | tf_op jit(solution)/shard_map/ppermute | solution.py:800
  656.0 35.5 %collective-permute-start.110 = (bf16[2,96,3072]{2,1,0:T(8,128)(2,1)S(1)}, bf16[2,96,3072]{2,1,0:T(8,128)(2,1)S(1)}, u32[]{:S(2)}, u32[]{:S(2)}) collective-permute-start(bf16[2,96,3072]{2,1,0:T(8,128)(2,1)S(1)} %pad_maximum_fusion.1), channel_id=1, source_target_pairs={{0,2},{2,4},{4,6},{6,0},{1,3},{3,5},{5,7},{7,1},{8,10},{10,12},{12... | collective-permute-start | bytes 3538952 | tf_op jit(solution)/shard_map/ppermute | solution.py:853
  673.9 27.9 %collective-permute-start.112 = (bf16[2,96,3072]{2,1,0:T(8,128)(2,1)S(1)}, bf16[2,96,3072]{2,1,0:T(8,128)(2,1)S(1)}, u32[]{:S(2)}, u32[]{:S(2)}) collective-permute-start(bf16[2,96,3072]{2,1,0:T(8,128)(2,1)S(1)} %pad_maximum_fusion.2), channel_id=1, source_target_pairs={{0,6},{2,0},{4,2},{6,4},{1,7},{3,1},{5,3},{7,5},{8,14},{10,8},{12,... | collective-permute-start | bytes 3538952 | tf_op jit(solution)/shard_map/ppermute | solution.py:854
  688.2 34.7 %collective-permute-start.90 = (f32[4,1536]{1,0:T(4,128)S(1)}, f32[4,1536]{1,0:T(4,128)S(1)}, u32[]{:S(2)}, u32[]{:S(2)}) collective-permute-start(f32[4,1536]{1,0:T(4,128)S(1)} %fusion.36), channel_id=1, source_target_pairs={{0,16},{16,0},{32,48},{48,32},{1,17},{17,1},{33,49},{49,33},{2,18}... | collective-permute-start | bytes 73736 | tf_op jit(solution)/shard_map/ppermute | solution.py:876
  722.9 31.1 %collective-permute-start.91 = (f32[4,1536]{1,0:T(4,128)S(1)}, f32[4,1536]{1,0:T(4,128)S(1)}, u32[]{:S(2)}, u32[]{:S(2)}) collective-permute-start(f32[4,1536]{1,0:T(4,128)S(1)} %fusion.52), channel_id=1, source_target_pairs={{0,32},{16,48},{32,0},{48,16},{1,33},{17,49},{33,1},{49,17},{2,34}... | collective-permute-start | bytes 73736 | tf_op jit(solution)/shard_map/ppermute | solution.py:876
  754.1 21.0 %collective-permute-start.105 = (bf16[96,1152]{1,0:T(8,128)(2,1)S(1)}, bf16[96,1152]{1,0:T(8,128)(2,1)S(1)}, u32[]{:S(2)}, u32[]{:S(2)}) collective-permute-start(bf16[96,1152]{1,0:T(8,128)(2,1)S(1)} %get-tuple-element.253), channel_id=1, source_target_pairs={{0,16},{16,32},{32,48},{48,0},{1,17},{17,33},{33,49},{49,1},{2,18}... | collective-permute-start | bytes 663560 | tf_op jit(solution)/shard_map/ppermute | solution.py:822
  (197 other events, 2028.0 us)
Sparse Core Ops, SparseCore 0:
  20.8 105.3 all-gather.6
  129.2 94.5 all-gather.8
  365.5 58.9 reduce-scatter.2
  482.4 30.1 reduce-scatter.4
  640.4 53.6 all-gather.10

commit v6 on v5

--- a/solution.py
+++ b/solution.py
@@ -855,27 +855,30 @@
     return (own.astype(F32) + from_before + from_after).astype(BF16)
 
 
-def y_sum(pair, where):
+def yhi_sum(pair, where):
     mine = lax.dynamic_index_in_dim(pair, where["yhi"], axis=0, keepdims=False)
     theirs = lax.dynamic_index_in_dim(pair, 1 - where["yhi"], axis=0, keepdims=False)
-    piece = add_low(mine, lax.ppermute(theirs, "yhi", SWAP))
+    return add_low(mine, lax.ppermute(theirs, "yhi", SWAP))
+
+
+def ylo_sum(piece):
     return add_low(piece, lax.ppermute(piece, "ylo", SWAP))
+
+
+def y_sum(pair, where):
+    return ylo_sum(yhi_sum(pair, where))
 
 
 def out_home(piece, start):
     first, last = start + 768, start + 1152
     moved = lax.ppermute(piece[:, first:last], AXES, inverse(ROWS))
-    return jnp.concatenate([piece[:, :first], moved], axis=1)
-
-
-def butterfly(values):
-    for axis, size in (("core", 2), ("x", 4), ("z", 4), ("yhi", 2), ("ylo", 2)):
-        step = 1
-        while step < size:
-            pairs = [(i, i ^ step) for i in range(size)]
-            values = values + lax.ppermute(values, axis, pairs)
-            step *= 2
-    return values
+    return jnp.concatenate([piece[:, :first], moved, piece[:, last:]], axis=1)
+
+
+def gain_halves(grads, core):
+    tall = grads.astype(BF16).T.reshape(8, 2, 96, 4)
+    tall = jnp.pad(tall, ((0, 0), (0, 0), (0, 0), (0, 124)))
+    return either(core, tall[:, 0], tall[:, 1]), either(core, tall[:, 1], tall[:, 0])
 
 
 def norm_back(grad, own_normed, state, gain):
@@ -969,78 +972,73 @@
         saved_feed = (state, flats, gate, up, hidden)
         state = state + ring_scatter(*partial)
         records.append((saved_attn, saved_feed, window))
-    output = from_lines(state.astype(BF16), z)[None]
+    last_rows = state.astype(BF16)
 
     results = [None] * 18
     gain_grads = [None] * 4
     zero = jnp.zeros((1,), jnp.int32)
-    for index in (1, 0):
-        line_packed = packed[index]
-        gain_attn, gain_feed = gains[2 * index], gains[2 * index + 1]
-        saved_attn, saved_feed, window = records[index]
-        base = 9 * index
-
-        state, flats, gate, up, hidden = saved_feed
-        if index == 0:
-            grad_pieces = ring_gather(tie(grad.astype(BF16), output))
-        after = () if index else (second_feed, second_sum)
+    place = x.astype(jnp.int32).reshape(1)
+
+    def feed_back(index, grad, pieces, after):
+        state, flats, gate, up, hidden = records[index][1]
         *partial, low_gate, low_up = feed_backward_call(
-            grad_pieces, line_packed, gate, up, after=after
+            pieces, packed[index], gate, up, after=after
         )
         own_normed = ring_scatter_direct(*partial)
-        grad, gain_grads[2 * index + 1] = norm_back(grad, own_normed, state, gain_feed)
-        halves = feed_weights_call(side, flats, grad_pieces, low_gate, low_up, hidden)
-        feed_sum = core_sum(*halves)
-
-        state, flats, line, mixed, log_total = saved_attn
-        grad_pieces = ring_gather(grad.astype(BF16))
+        grad, gain_grads[2 * index + 1] = norm_back(
+            grad, own_normed, state, gains[2 * index + 1]
+        )
+        return grad, feed_weights_call(side, flats, pieces, low_gate, low_up, hidden)
+
+    def attention_back(index, grad, pieces, after):
+        state, flats, line, mixed, log_total = records[index][0]
+        window = records[index][2]
         low_queries, pair_own, pair_other = attend_backward_call(
-            window,
-            length,
-            grad_pieces,
-            *line,
-            line_packed,
-            log_total,
-            cosine_t,
-            sine_t,
-            after=(feed_sum,) if index else (feed_sum, second_attn),
+            window, length, pieces, *line, packed[index], log_total, cosine_t, sine_t, after=after
         )
         came = lax.ppermute(pair_other, "core", SWAP)
-        *partial, low = unproject_call(
-            low_queries,
-            pair_own,
-            came,
-            cosine,
-            sine,
-            line_packed,
-            after=() if index else (second_piece,),
-        )
+        *partial, low = unproject_call(low_queries, pair_own, came, cosine, sine, packed[index])
         own_normed = ring_scatter_direct(*partial)
-        grad, gain_grads[2 * index] = norm_back(grad, own_normed, state, gain_attn)
-        halves = attend_weights_call(side, flats, grad_pieces, low, mixed)
-        attn_sum = core_sum(*halves)
-        if index:
-            second_sum = attn_sum
-            second_feed = z_sum(feed_sum, where, True)
-            second_attn = z_sum(attn_sum, where, True)
-            piece = y_sum(jnp.concatenate([second_feed, second_attn], axis=2), where)
-            second_piece = out_home(piece, 3072)
-            every = lax.all_gather(second_piece, ("x", "core"), axis=0, tiled=False)
-            out = unpack_call(True, True, zero, every.reshape(4, 2, 96, -1))
-            results[base + 1 : base + 5] = out[:4]
-            results[base + 6 : base + 9] = out[4:]
-        else:
-            place = x.astype(jnp.int32).reshape(1)
-            every = line_gather(y_sum(z_sum(feed_sum, where, False), where), core)
-            results[base + 6 : base + 9] = unpack_call(False, True, place, every)
-            piece = y_sum(z_sum(attn_sum, where, False), where)
-            every = line_gather(out_home(piece, 0), core)
-            results[base + 1 : base + 5] = unpack_call(True, False, place, every)
-    gain_sums = butterfly(jnp.stack(gain_grads))
-    gain_sums = lax.dynamic_slice_in_dim(gain_sums, (2 * z + yhi) * 192, 192, axis=1)
+        grad, gain_grads[2 * index] = norm_back(grad, own_normed, state, gains[2 * index])
+        return grad, attend_weights_call(side, flats, pieces, low, mixed)
+
+    def swap_after(halves, *others):
+        return halves[0], tie(halves[1], *others)
+
+    grad, halves = feed_back(1, grad, grad_pieces, ())
+    low = grad.astype(BF16)
+    feed_sum = core_sum(*swap_after(halves, low))
+    grad, halves = attention_back(1, grad, ring_gather(low), (feed_sum, last_rows))
+    low = grad.astype(BF16)
+    attn_sum = core_sum(*swap_after(halves, low))
+    both_sum = jnp.concatenate([feed_sum, attn_sum], axis=2)
+
+    grad, halves = feed_back(0, grad, ring_gather(low), (both_sum,))
+    second_pair = z_sum(both_sum, where, True)
+    low = grad.astype(BF16)
+    feed_sum = core_sum(*swap_after(halves, low))
+    grad, halves = attention_back(0, grad, ring_gather(low), (feed_sum,))
+    attn_sum = core_sum(*halves)
+    gain_sum = core_sum(*gain_halves(jnp.stack(gain_grads), core))
+    feed_pair = z_sum(feed_sum, where, False)
+    output = from_lines(tie(last_rows, feed_pair), z)[None]
+
+    second_piece = out_home(y_sum(tie(second_pair, halves[0]), where), 3072)
+    every = lax.all_gather(second_piece, ("x", "core"), axis=0, tiled=False)
+    out = unpack_call(True, True, zero, every.reshape(4, 2, 96, -1))
+    results[10:14] = out[:4]
+    results[15:18] = out[4:]
+
+    every = line_gather(y_sum(feed_pair, where), core)
+    results[6:9] = unpack_call(False, True, place, every)
+    attn_sum = jnp.concatenate([attn_sum, gain_sum], axis=2)
+    piece = y_sum(z_sum(attn_sum, where, False), where)
+    every = line_gather(out_home(piece, 0), core)
+    results[1:5] = unpack_call(True, False, place, every)
+    gain_sums = every[..., 1152:1156].astype(F32).sum(axis=0).reshape(192, 4).T
+    input_grad = from_lines(grad.astype(BF16), z).astype(F32)[None]
     for index, slot in enumerate((0, 5, 9, 14)):
         results[slot] = gain_sums[index]
-    input_grad = from_lines(grad.astype(BF16), z).astype(F32)[None]
     return (output, input_grad, *results)
 
 

time: 828 us -> 781 us (0.943)
  starting transfers between devices: 248 us -> 215 us
  local copies, waits for them, and re-layouts: 70 us -> 42.6 us
  other arithmetic: 42.6 us -> 59.5 us
    ppermute x4, waiting for transfers between devices: 26.3 us -> 4.18 us  [ring_scatter_direct(): from_far = lax.ppermute(far, 'x', ACROSS).astype(F32)]
    unnamed x219 -> x220, local copies, waits for them, and re-layouts: 38.3 us -> 18.2 us
    ppermute x8, waiting for transfers between devices: 6.47 us -> 26.5 us  [from_lines(): lax.ppermute(block[part * k:part * (k + 1)], AXES, inverse(LINES[k]))]
    ppermute x4, waiting for transfers between devices: 23 us -> 6.92 us  [ring_scatter_direct(): from_left = lax.ppermute(right, 'x', RIGHT).astype(F32)]
    ppermute x8, starting transfers between devices: 36 us -> 21.6 us  [from_lines(): lax.ppermute(block[part * k:part * (k + 1)], AXES, inverse(LINES[k]))]
    ppermute x4, waiting for transfers between devices: 0.01 us -> 14.3 us  [ring_scatter(): second = lax.ppermute(far[half:], 'x', LEFT).astype(F32)]
    ppermute x4, waiting for transfers between devices: 11.6 us -> 0.01 us  [ring_scatter(): first = lax.ppermute(far[:half], 'x', RIGHT).astype(F32)]
    ppermute x4, waiting for transfers between devices: 6.74 us -> 17.3 us  [ring_scatter(): from_right = lax.ppermute(left, 'x', LEFT).astype(F32)]
  transfers between devices with their start and end apart: 125 -> 118, of which waited for: 50 -> 53; matrix products, arithmetic and copies ran while one was open for 8% -> 10% of each run, Pallas kernels for 13% -> 13%
where the time goes in v6:
time: 781 us; the launch traced here: 771 us
  waiting for transfers between devices  280 us (36%)
  starting transfers between devices  215 us (28%)
  Pallas kernels  157 us (20%)
  other arithmetic  59.5 us (8%)
  local copies, waits for them, and re-layouts  42.6 us (5%)
  between operations  17.1 us (2%)
    all_gather x2, waiting for transfers between devices, line_weights(): return lax.all_gather(piece, SPREAD, axis=0, tiled=False)  52.3 us
    ppermute x8, waiting for transfers between devices, ring_gather(): from_left = lax.ppermute(block, 'x', RIGHT)  51.1 us
    ppermute x8, starting transfers between devices, to_lines(): out.append(lax.ppermute(piece, AXES, LINES[k]))  41.3 us
    ppermute x8, waiting for transfers between devices, from_lines(): lax.ppermute(block[part * k:part * (k + 1)], AXES, inverse(LINES[k]))  26.5 us
    pallas_call x2, Pallas kernels, attend_backward_call(): pl.pallas_call(later(functools.partial(attend_backward_kernel, window), l...  26.5 us
    pallas_call x2, Pallas kernels, feed_weights_call(): pl.pallas_call(feed_weights_kernel, grid_spec=spec, out_shape=[shape, sha...  26.1 us
    pallas_call x2, Pallas kernels, feed_backward_call(): pl.pallas_call(later(feed_backward_kernel, len(after)), grid=(4,), in_spe...  25.4 us
    ppermute x8, starting transfers between devices, ring_gather(): far_second = lax.ppermute(from_right[half:], 'x', LEFT)  22.2 us
  transfers between devices with their start and end apart: 118, of which 53 were waited for; matrix products, arithmetic and copies ran while one was open for 10% of the time, Pallas kernels for 13%

profile of v6, /device:TPU:1, one launch (start us, length us, event | category | flops | bytes accessed | tf_op | source)
XLA Modules:
  0.0 771.3 jit_solution(17048010562955248608)
XLA Ops:
  20.9 11.2 %collective-permute-start = (bf16[32,1536]{1,0:T(8,128)(2,1)S(1)}, bf16[32,1536]{1,0:T(8,128)(2,1)S(1)}, u32[]{:S(2)}, u32[]{:S(2)}) collective-permute-start(bf16[32,1536]{1,0:T(8,128)(2,1)S(1)} %get-tuple-element.259), channel_id=1, source_target_pairs={{0,0},{1,8},{2,16},{3,24},{4,32},{5,40},{6,48},{7,56},{8,1},{9,9},... | collective-permute-start | bytes 294920 | tf_op jit(solution)/shard_map/ppermute | solution.py:764
  33.3 7.4 collective-permute-start.2
  73.8 52.3 %all-gather.7.cloned.1.call-done.refs_6_.refs_7_.weight = bf16[1536,4352]{1,0:T(8,128)(2,1)} async-done(((bf16[96,4352]{1,0:T(8,128)(2,1)}), bf16[1536,4352]{1,0:T(8,128)(2,1)}) %all-gather.7.cloned.1.call-update) | async-done | bytes 13369360 | tf_op jit(solution)/shard_map/all_gather | solution.py:914
  137.3 9.2 %attend.2 = (f32[128,1536]{1,0:T(8,128)S(1)}, f32[128,1536]{1,0:T(8,128)S(1)}, f32[128,1536]{1,0:T(8,128)S(1)}, bf16[128,1536]{1,0:T(8,128)(2,1)S(1)}, bf16[512,...) custom-call(s32[1]{0:T(128)} %collective-permute-done.4.length.refs_2_.refs_1_, ...), custom_call_target="tpu_custom_call" | custom-call | flops 3000000000 | bytes 6000000 | tf_op jit(solution)/shard_map/attend/pallas_call | solution.py:405
  168.3 9.3 %collective-permute-start.18 = (bf16[32,1536]{1,0:T(8,128)(2,1)}, bf16[32,1536]{1,0:T(8,128)(2,1)}, u32[]{:S(2)}, u32[]{:S(2)}) collective-permute-start(bf16[32,1536]{1,0:T(8,128)(2,1)} %get-tuple-element.251), channel_id=1, source_target_pairs={{0,48},{1,56},{2,0},{3,8},{4,16},{5,24},{6,32},{7,40},{8,49},{9,57... | collective-permute-start | bytes 294920 | tf_op jit(solution)/shard_map/ppermute | solution.py:764
  185.8 7.7 collective-permute-done.19.refs_2_.refs_1_
  201.5 9.3 %feed_forward.2 = (f32[128,1536]{1,0:T(8,128)S(1)}, f32[128,1536]{1,0:T(8,128)S(1)}, f32[128,1536]{1,0:T(8,128)S(1)}, bf16[128,1536]{1,0:T(8,128)(2,1)S(1)}, f32...) custom-call(bf16[128,1536]{1,0:T(8,128)(2,1)S(1)} %constant_dynamic-update-slice_fusion.6.refs_0_.refs_5, ...), custom_call_target="tpu_custom_call" | custom-call | flops 4899999744 | bytes 18000000 | tf_op jit(solution)/shard_map/feed_forward/pallas_call | solution.py:138
  256.0 7.2 collective-permute-start.36
  272.0 9.1 %attend.3 = (f32[128,1536]{1,0:T(8,128)S(1)}, f32[128,1536]{1,0:T(8,128)S(1)}, f32[128,1536]{1,0:T(8,128)S(1)}, bf16[128,1536]{1,0:T(8,128)(2,1)S(1)}, bf16[512,...) custom-call(bf16[64,1536]{1,0:T(8,128)(2,1)S(1)} %collective-permute-done.28.refs_0_.refs_3_.refs_8_, ...), custom_call_target="tpu_custom_call" | custom-call | flops 3000000000 | bytes 6000000 | tf_op jit(solution)/shard_map/attend/pallas_call | solution.py:405
  307.2 6.3 collective-permute-done.41.refs_1_
  319.4 9.2 %feed_forward.3 = (f32[128,1536]{1,0:T(8,128)S(1)}, f32[128,1536]{1,0:T(8,128)S(1)}, f32[128,1536]{1,0:T(8,128)S(1)}, bf16[128,1536]{1,0:T(8,128)(2,1)S(1)}, f32...) custom-call(bf16[128,1536]{1,0:T(8,128)(2,1)S(1)} %multiply_convert_fusion.refs_0_, ...), custom_call_target="tpu_custom_call" | custom-call | flops 4899999744 | bytes 18000000 | tf_op jit(solution)/shard_map/feed_forward/pallas_call | solution.py:138
  328.6 12.6 %feed_backward.2 = (f32[128,1536]{1,0:T(8,128)S(1)}, bf16[128,1536]{1,0:T(8,128)(2,1)S(1)}, bf16[128,1536]{1,0:T(8,128)(2,1)S(1)}, bf16[128,1536]{1,0:T(8,128)(2...) custom-call(bf16[128,1536]{1,0:T(8,128)(2,1)S(1)} %constant_dynamic-update-slice_fusion.6.refs_0_.refs_5_, ...), custom_call_target="tpu_custom_call" | custom-call | flops 4899999744 | bytes 20000000 | tf_op jit(solution)/shard_map/feed_backward/pallas_call | solution.py:191
  347.3 13.0 %feed_weights.2 = (bf16[8,96,3072]{2,1,0:T(8,128)(2,1)S(1)}, bf16[8,96,3072]{2,1,0:T(8,128)(2,1)}) custom-call(s32[1]{0:T(128)} %bitcast.5.side_ref, bf16[128,1536]{1,0:T(8,128)(2,1)S(1)} %multiply_convert_fusion.refs_0_, bf16[128,1536]{1,0:T(8,128)(2,1)S(1)} %collective-permute-done.41.refs_1_, bf16[128,1536]{1,0:T(8,128)(2,1)S(1)} %collective-permute-done.42.refs_2_, ...), custom_call_target="tpu_custom_call" | custom-call | flops 4899999744 | bytes 18000000 | tf_op jit(solution)/shard_map/feed_weights/pallas_call | solution.py:287
  384.6 8.8 %collective-permute-done.53.refs_4_.refs_6_ = bf16[128,1536]{1,0:T(8,128)(2,1)S(1)} collective-permute-done((bf16[128,1536]{1,0:T(8,128)(2,1)S(1)}, bf16[128,1536]{1,0:T(8,128)(2,1)S(1)}, u32[]{:S(2)}, u32[]{:S(2)}) %collective-permute-start.53) | collective-permute-done | bytes 393248 | tf_op jit(solution)/shard_map/ppermute | solution.py:779
  396.4 6.4 add_convert_fusion.1.refs_0_
  402.9 13.1 %attend_backward.2 = (bf16[512,384]{1,0:T(8,128)(2,1)S(1)}, f32[512,384]{1,0:T(8,128)}, bf16[512,384]{1,0:T(8,128)(2,1)S(1)}) custom-call(bf16[8,96,3072]{2,1,0:T(8,128)(2,1)} %add_convert_fusion.1.refs_0_, bf16[128,1536]{1,0:T(8,128)(2,1)S(1)} %get-tuple-element.163.refs_1_, s32[1]{0:T(128)} %collective-permute-done.4.length.refs_2_.refs_1_, ...), custom_call_target="tpu_custom_call" | custom-call | flops 6000000000 | bytes 6000000 | tf_op jit(solution)/shard_map/attend_backward/pallas_call | solution.py:478
  435.7 6.7 collective-permute-done.59
  460.1 9.0 %collective-permute-done.61.refs_2_.refs_6_ = bf16[128,1536]{1,0:T(8,128)(2,1)S(1)} collective-permute-done((bf16[128,1536]{1,0:T(8,128)(2,1)S(1)}, bf16[128,1536]{1,0:T(8,128)(2,1)S(1)}, u32[]{:S(2)}, u32[]{:S(2)}) %collective-permute-start.61) | collective-permute-done | bytes 393248 | tf_op jit(solution)/shard_map/ppermute | solution.py:779
  477.5 12.8 %feed_backward.3 = (f32[128,1536]{1,0:T(8,128)S(1)}, bf16[128,1536]{1,0:T(8,128)(2,1)S(1)}, bf16[128,1536]{1,0:T(8,128)(2,1)S(1)}, bf16[128,1536]{1,0:T(8,128)(2...) custom-call(bf16[8,96,4224]{2,1,0:T(8,128)(2,1)} %pad_maximum_fusion.refs_0_, ...), custom_call_target="tpu_custom_call" | custom-call | flops 4899999744 | bytes 20000000 | tf_op jit(solution)/shard_map/feed_backward/pallas_call | solution.py:191
  493.9 13.1 %feed_weights.3 = (bf16[8,96,3072]{2,1,0:T(8,128)(2,1)S(1)}, bf16[8,96,3072]{2,1,0:T(8,128)(2,1)}) custom-call(s32[1]{0:T(128)} %bitcast.5.side_ref, bf16[128,1536]{1,0:T(8,128)(2,1)S(1)} %copy-done.8, bf16[128,1536]{1,0:T(8,128)(2,1)S(1)} %copy-done.18, bf16[128,1536]{1,0:T(8,128)(2,1)S(1)} %copy-done.20, bf16[64,1536]{1,0:T(8,128)(2,1)S(1)} %copy-done.40, ...), custom_call_target="tpu_custom_call" | custom-call | flops 4899999744 | bytes 18000000 | tf_op jit(solution)/shard_map/feed_weights/pallas_call | solution.py:287
  516.6 9.3 %collective-permute-done.78.refs_3_.refs_2_ = bf16[128,1536]{1,0:T(8,128)(2,1)S(1)} collective-permute-done((bf16[128,1536]{1,0:T(8,128)(2,1)S(1)}, bf16[128,1536]{1,0:T(8,128)(2,1)S(1)}, u32[]{:S(2)}, u32[]{:S(2)}) %collective-permute-start.78) | collective-permute-done | bytes 393248 | tf_op jit(solution)/shard_map/ppermute | solution.py:779
  528.9 8.2 %add_convert_fusion.refs_0_ = bf16[8,96,3072]{2,1,0:T(8,128)(2,1)} fusion(bf16[8,96,3072]{2,1,0:T(8,128)(2,1)} %collective-permute-done.69, bf16[8,96,3072]{2,1,0:T(8,128)(2,1)} %copy-done), kind=kLoop, calls=%fused_computation | loop fusion | flops 9437184 | bytes 14155776 | tf_op jit(solution)/shard_map/convert_element_type | solution.py:817
  537.1 13.4 %attend_backward.3 = (bf16[512,384]{1,0:T(8,128)(2,1)S(1)}, f32[512,384]{1,0:T(8,128)}, bf16[512,384]{1,0:T(8,128)(2,1)S(1)}) custom-call(bf16[8,96,3072]{2,1,0:T(8,128)(2,1)} %add_convert_fusion.refs_0_, s32[1]{0:T(128)} %collective-permute-done.4.length.refs_2_.refs_1_, bf16[128,1536]{1,0:T(8,128)(2,1)S(1)} %get-tuple-element.205.refs_2_.refs_1_, ...), custom_call_target="tpu_custom_call" | custom-call | flops 6000000000 | bytes 6000000 | tf_op jit(solution)/shard_map/attend_backward/pallas_call | solution.py:478
  590.2 21.6 %collective-permute-done.86 = bf16[32,1536]{1,0:T(8,128)(2,1)S(1)} collective-permute-done((bf16[32,1536]{1,0:T(8,128)(2,1)}, bf16[32,1536]{1,0:T(8,128)(2,1)S(1)}, u32[]{:S(2)}, u32[]{:S(2)}) %collective-permute-start.86) | collective-permute-done | bytes 98336 | tf_op jit(solution)/shard_map/ppermute | solution.py:772
  622.7 19.4 %collective-permute-done.112 = bf16[96,4224]{1,0:T(8,128)(2,1)S(1)} collective-permute-done((bf16[96,4224]{1,0:T(8,128)(2,1)S(1)}, bf16[96,4224]{1,0:T(8,128)(2,1)S(1)}, u32[]{:S(2)}, u32[]{:S(2)}) %collective-permute-start.112) | collective-permute-done | bytes 811040 | tf_op jit(solution)/shard_map/ppermute | solution.py:865
  653.3 8.6 %collective-permute-start.104 = (bf16[96,3072]{1,0:T(8,128)(2,1)S(1)}, bf16[96,3072]{1,0:T(8,128)(2,1)S(1)}, u32[]{:S(2)}, u32[]{:S(2)}) collective-permute-start(bf16[96,3072]{1,0:T(8,128)(2,1)S(1)} %dynamic-slice_bitcast_fusion.7), channel_id=1, source_target_pairs={{0,1},{1,0},{2,3},{3,2},{4,5},{5,4},{6,7},{7,6},{8,9},{9,8},{10,11... | collective-permute-start | bytes 1769480 | tf_op jit(solution)/shard_map/ppermute | solution.py:861
  663.8 9.7 %collective-permute-done.104 = bf16[96,3072]{1,0:T(8,128)(2,1)S(1)} collective-permute-done((bf16[96,3072]{1,0:T(8,128)(2,1)S(1)}, bf16[96,3072]{1,0:T(8,128)(2,1)S(1)}, u32[]{:S(2)}, u32[]{:S(2)}) %collective-permute-start.104) | collective-permute-done | bytes 589856 | tf_op jit(solution)/shard_map/ppermute | solution.py:861
  681.4 11.0 %collective-permute-done.96 = bf16[96,1280]{1,0:T(8,128)(2,1)S(1)} collective-permute-done((bf16[96,1280]{1,0:T(8,128)(2,1)S(1)}, bf16[96,1280]{1,0:T(8,128)(2,1)S(1)}, u32[]{:S(2)}, u32[]{:S(2)}) %collective-permute-start.96) | collective-permute-done | bytes 245792 | tf_op jit(solution)/shard_map/ppermute | solution.py:861
  698.3 9.0 %collective-permute-start.74 = (bf16[32,1536]{1,0:T(8,128)(2,1)S(1)}, bf16[32,1536]{1,0:T(8,128)(2,1)S(1)}, u32[]{:S(2)}, u32[]{:S(2)}) collective-permute-start(bf16[32,1536]{1,0:T(8,128)(2,1)S(1)} %get-tuple-element.244), channel_id=1, source_target_pairs={{0,0},{8,1},{16,2},{24,3},{32,4},{40,5},{48,6},{56,7},{1,8},{9,9},... | collective-permute-start | bytes 294920 | tf_op jit(solution)/shard_map/ppermute | solution.py:772
  717.4 7.0 collective-permute-start.76
  727.4 9.2 %collective-permute-start.102 = (bf16[48,1280]{1,0:T(8,128)(2,1)S(1)}, bf16[48,1280]{1,0:T(8,128)(2,1)S(1)}, u32[]{:S(2)}, u32[]{:S(2)}) collective-permute-start(bf16[48,1280]{1,0:T(8,128)(2,1)S(1)} %slice.421), channel_id=1, source_target_pairs={{0,48},{16,0},{32,16},{48,32},{1,49},{17,1},{33,17},{49,33},{2,50}... | collective-permute-start | bytes 368648 | tf_op jit(solution)/shard_map/ppermute | solution.py:825
  757.5 7.1 unpack.5
  (643 shorter events, 387.4 us)
Async XLA Ops:
  7.2 119.0 %all-gather.7.cloned.1.call-start = ((), (), s32[]{:S(2)}) async-start(), calls=%async_computation.2 | async-start | bytes 14204928 | tf_op jit(solution)/shard_map/all_gather | solution.py:914
  20.7 230.0 %all-gather.9.cloned.1.call-start = ((), (), s32[]{:S(2)}) async-start(), calls=%async_computation.3 | async-start | bytes 13787136 | tf_op jit(solution)/shard_map/all_gather | solution.py:914
  20.9 26.2 %collective-permute-start = (bf16[32,1536]{1,0:T(8,128)(2,1)S(1)}, bf16[32,1536]{1,0:T(8,128)(2,1)S(1)}, u32[]{:S(2)}, u32[]{:S(2)}) collective-permute-start(bf16[32,1536]{1,0:T(8,128)(2,1)S(1)} %get-tuple-element.259), channel_id=1, source_target_pairs={{0,0},{1,8},{2,16},{3,24},{4,32},{5,40},{6,48},{7,56},{8,1},{9,9},... | collective-permute-start | bytes 294920 | tf_op jit(solution)/shard_map/ppermute | solution.py:764
  54.8 527.1 %reduce-scatter.2.cloned.1.call-start = ((), (), s32[]{:S(2)}) async-start(), calls=%async_computation.1 | async-start | bytes 8110080 | tf_op jit(solution)/shard_map/reduce_scatter | solution.py:842
  54.9 81.3 %collective-permute-start.4 = (s32[1]{0:T(128)}, s32[1]{0:T(128)}, u32[]{:S(2)}, u32[]{:S(2)}) collective-permute-start(s32[1]{0:T(128)} %param.22), channel_id=1, source_target_pairs={{0,0},{1,8},{2,16},{3,24},{4,32},{5,40},{6,48},{7,56},{8,1},{9,9},... | collective-permute-start | bytes 20 | tf_op jit(solution)/shard_map/ppermute | solution.py:919
  69.3 60.1 %collective-permute-start.7 = (bf16[64,1536]{1,0:T(8,128)(2,1)S(1)}, bf16[64,1536]{1,0:T(8,128)(2,1)S(1)}, u32[]{:S(2)}, u32[]{:S(2)}) collective-permute-start(bf16[64,1536]{1,0:T(8,128)(2,1)S(1)} %slice.384), channel_id=1, source_target_pairs={{0,16},{16,32},{32,48},{48,0},{1,17},{17,33},{33,49},{49,1},{2,18}... | collective-permute-start | bytes 589832 | tf_op jit(solution)/shard_map/ppermute | solution.py:781
  73.3 56.1 %collective-permute-start.8 = (bf16[64,1536]{1,0:T(8,128)(2,1)S(1)}, bf16[64,1536]{1,0:T(8,128)(2,1)S(1)}, u32[]{:S(2)}, u32[]{:S(2)}) collective-permute-start(bf16[64,1536]{1,0:T(8,128)(2,1)S(1)} %slice.385), channel_id=1, source_target_pairs={{0,48},{16,0},{32,16},{48,32},{1,49},{17,1},{33,17},{49,33},{2,50}... | collective-permute-start | bytes 589832 | tf_op jit(solution)/shard_map/ppermute | solution.py:782
  154.0 23.7 %collective-permute-start.14 = (bf16[128,1536]{1,0:T(8,128)(2,1)}, bf16[128,1536]{1,0:T(8,128)(2,1)S(1)}, u32[]{:S(2)}, u32[]{:S(2)}) collective-permute-start(bf16[128,1536]{1,0:T(8,128)(2,1)} %pad_maximum_fusion.10), channel_id=1, source_target_pairs={{0,48},{16,0},{32,16},{48,32},{1,49},{17,1},{33,17},{49,33},{2,50}... | collective-permute-start | bytes 1179656 | tf_op jit(solution)/shard_map/ppermute | solution.py:793
  158.2 19.5 %collective-permute-start.12 = (bf16[128,1536]{1,0:T(8,128)(2,1)}, bf16[128,1536]{1,0:T(8,128)(2,1)S(1)}, u32[]{:S(2)}, u32[]{:S(2)}) collective-permute-start(bf16[128,1536]{1,0:T(8,128)(2,1)} %pad_maximum_fusion.9), channel_id=1, source_target_pairs={{0,16},{16,32},{32,48},{48,0},{1,17},{17,33},{33,49},{49,1},{2,18}... | collective-permute-start | bytes 1179656 | tf_op jit(solution)/shard_map/ppermute | solution.py:792
  162.3 21.7 %collective-permute-start.16 = (bf16[32,1536]{1,0:T(8,128)(2,1)}, bf16[32,1536]{1,0:T(8,128)(2,1)}, u32[]{:S(2)}, u32[]{:S(2)}) collective-permute-start(bf16[32,1536]{1,0:T(8,128)(2,1)} %get-tuple-element.253), channel_id=1, source_target_pairs={{0,16},{1,24},{2,32},{3,40},{4,48},{5,56},{6,0},{7,8},{8,17},{9,25... | collective-permute-start | bytes 294920 | tf_op jit(solution)/shard_map/ppermute | solution.py:764
  164.6 20.4 %collective-permute-start.17 = (bf16[32,1536]{1,0:T(8,128)(2,1)}, bf16[32,1536]{1,0:T(8,128)(2,1)}, u32[]{:S(2)}, u32[]{:S(2)}) collective-permute-start(bf16[32,1536]{1,0:T(8,128)(2,1)} %get-tuple-element.252), channel_id=1, source_target_pairs={{0,32},{1,40},{2,48},{3,56},{4,0},{5,8},{6,16},{7,24},{8,33},{9,41... | collective-permute-start | bytes 294920 | tf_op jit(solution)/shard_map/ppermute | solution.py:764
  168.3 28.7 %collective-permute-start.18 = (bf16[32,1536]{1,0:T(8,128)(2,1)}, bf16[32,1536]{1,0:T(8,128)(2,1)}, u32[]{:S(2)}, u32[]{:S(2)}) collective-permute-start(bf16[32,1536]{1,0:T(8,128)(2,1)} %get-tuple-element.251), channel_id=1, source_target_pairs={{0,48},{1,56},{2,0},{3,8},{4,16},{5,24},{6,32},{7,40},{8,49},{9,57... | collective-permute-start | bytes 294920 | tf_op jit(solution)/shard_map/ppermute | solution.py:764
  341.2 27.0 %collective-permute-start.51 = (bf16[128,1536]{1,0:T(8,128)(2,1)S(1)}, bf16[128,1536]{1,0:T(8,128)(2,1)S(1)}, u32[]{:S(2)}, u32[]{:S(2)}) collective-permute-start(bf16[128,1536]{1,0:T(8,128)(2,1)S(1)} %get-tuple-element.131), channel_id=1, source_target_pairs={{0,32},{16,48},{32,0},{48,16},{1,33},{17,49},{33,1},{49,17},{2,34}... | collective-permute-start | bytes 1179656 | tf_op jit(solution)/shard_map/ppermute | solution.py:800
  343.2 25.0 %collective-permute-start.50 = (bf16[128,1536]{1,0:T(8,128)(2,1)S(1)}, bf16[128,1536]{1,0:T(8,128)(2,1)S(1)}, u32[]{:S(2)}, u32[]{:S(2)}) collective-permute-start(bf16[128,1536]{1,0:T(8,128)(2,1)S(1)} %get-tuple-element.130), channel_id=1, source_target_pairs={{0,48},{16,0},{32,16},{48,32},{1,49},{17,1},{33,17},{49,33},{2,50}... | collective-permute-start | bytes 1179656 | tf_op jit(solution)/shard_map/ppermute | solution.py:799
  344.5 23.8 %collective-permute-start.49 = (bf16[128,1536]{1,0:T(8,128)(2,1)S(1)}, bf16[128,1536]{1,0:T(8,128)(2,1)S(1)}, u32[]{:S(2)}, u32[]{:S(2)}) collective-permute-start(bf16[128,1536]{1,0:T(8,128)(2,1)S(1)} %get-tuple-element.129), channel_id=1, source_target_pairs={{0,16},{16,32},{32,48},{48,0},{1,17},{17,33},{33,49},{49,1},{2,18}... | collective-permute-start | bytes 1179656 | tf_op jit(solution)/shard_map/ppermute | solution.py:798
  345.0 19.5 %collective-permute-start.47 = (bf16[64,1536]{1,0:T(8,128)(2,1)S(1)}, bf16[64,1536]{1,0:T(8,128)(2,1)S(1)}, u32[]{:S(2)}, u32[]{:S(2)}) collective-permute-start(bf16[64,1536]{1,0:T(8,128)(2,1)S(1)} %get-tuple-element.246), channel_id=1, source_target_pairs={{0,48},{16,0},{32,16},{48,32},{1,49},{17,1},{33,17},{49,33},{2,50}... | collective-permute-start | bytes 589832 | tf_op jit(solution)/shard_map/ppermute | solution.py:789
  347.3 20.8 %collective-permute-start.45 = (bf16[64,1536]{1,0:T(8,128)(2,1)S(1)}, bf16[64,1536]{1,0:T(8,128)(2,1)S(1)}, u32[]{:S(2)}, u32[]{:S(2)}) collective-permute-start(bf16[64,1536]{1,0:T(8,128)(2,1)S(1)} %get-tuple-element.245), channel_id=1, source_target_pairs={{0,16},{16,32},{32,48},{48,0},{1,17},{17,33},{33,49},{49,1},{2,18}... | collective-permute-start | bytes 589832 | tf_op jit(solution)/shard_map/ppermute | solution.py:788
  424.7 20.0 %collective-permute-start.58 = (bf16[128,1536]{1,0:T(8,128)(2,1)S(1)}, bf16[128,1536]{1,0:T(8,128)(2,1)S(1)}, u32[]{:S(2)}, u32[]{:S(2)}) collective-permute-start(bf16[128,1536]{1,0:T(8,128)(2,1)S(1)} %get-tuple-element.143), channel_id=1, source_target_pairs={{0,16},{16,32},{32,48},{48,0},{1,17},{17,33},{33,49},{49,1},{2,18}... | collective-permute-start | bytes 1179656 | tf_op jit(solution)/shard_map/ppermute | solution.py:798
  456.5 301.0 %all-gather.11.cloned.1.call-start = ((), (), s32[]{:S(2)}) async-start(), calls=%async_computation.4 | async-start | bytes 7299072 | tf_op jit(solution)/shard_map/all_gather | solution.py:1027
  561.2 20.0 %collective-permute-start.83 = (bf16[128,1536]{1,0:T(8,128)(2,1)S(1)}, bf16[128,1536]{1,0:T(8,128)(2,1)S(1)}, u32[]{:S(2)}, u32[]{:S(2)}) collective-permute-start(bf16[128,1536]{1,0:T(8,128)(2,1)S(1)} %get-tuple-element.169), channel_id=1, source_target_pairs={{0,16},{16,32},{32,48},{48,0},{1,17},{17,33},{33,49},{49,1},{2,18}... | collective-permute-start | bytes 1179656 | tf_op jit(solution)/shard_map/ppermute | solution.py:798
  569.8 78.5 %collective-permute-start.90 = (bf16[8,96,1152]{2,1,0:T(8,128)(2,1)}, bf16[8,96,1152]{2,1,0:T(8,128)(2,1)}, u32[]{:S(2)}, u32[]{:S(2)}) collective-permute-start(bf16[8,96,1152]{2,1,0:T(8,128)(2,1)} %get-tuple-element.176), channel_id=1, source_target_pairs={{0,8},{8,0},{1,9},{9,1},{2,10},{10,2},{3,11},{11,3},{4,12},{12,4},... | collective-permute-start | bytes 5308424 | tf_op jit(solution)/shard_map/ppermute | solution.py:837
  573.8 72.0 %collective-permute-start.73 = (bf16[2,96,3072]{2,1,0:T(8,128)(2,1)}, bf16[2,96,3072]{2,1,0:T(8,128)(2,1)}, u32[]{:S(2)}, u32[]{:S(2)}) collective-permute-start(bf16[2,96,3072]{2,1,0:T(8,128)(2,1)} %pad_maximum_fusion.4), channel_id=1, source_target_pairs={{0,6},{2,0},{4,2},{6,4},{1,7},{3,1},{5,3},{7,5},{8,14},{10,8},{12,... | collective-permute-start | bytes 3538952 | tf_op jit(solution)/shard_map/ppermute | solution.py:854
  576.7 69.1 %collective-permute-start.71 = (bf16[2,96,3072]{2,1,0:T(8,128)(2,1)}, bf16[2,96,3072]{2,1,0:T(8,128)(2,1)}, u32[]{:S(2)}, u32[]{:S(2)}) collective-permute-start(bf16[2,96,3072]{2,1,0:T(8,128)(2,1)} %pad_maximum_fusion.3), channel_id=1, source_target_pairs={{0,2},{2,4},{4,6},{6,0},{1,3},{3,5},{5,7},{7,1},{8,10},{10,12},{12... | collective-permute-start | bytes 3538952 | tf_op jit(solution)/shard_map/ppermute | solution.py:853
  583.1 30.2 %collective-permute-start.111 = (bf16[96,4224]{1,0:T(8,128)(2,1)S(1)}, bf16[96,4224]{1,0:T(8,128)(2,1)}, u32[]{:S(2)}, u32[]{:S(2)}) collective-permute-start(bf16[96,4224]{1,0:T(8,128)(2,1)S(1)} %dynamic-slice_bitcast_fusion), channel_id=1, source_target_pairs={{0,1},{1,0},{2,3},{3,2},{4,5},{5,4},{6,7},{7,6},{8,9},{9,8},{10,11... | collective-permute-start | bytes 2433032 | tf_op jit(solution)/shard_map/ppermute | solution.py:861
  587.4 24.4 %collective-permute-start.86 = (bf16[32,1536]{1,0:T(8,128)(2,1)}, bf16[32,1536]{1,0:T(8,128)(2,1)S(1)}, u32[]{:S(2)}, u32[]{:S(2)}) collective-permute-start(bf16[32,1536]{1,0:T(8,128)(2,1)} %get-tuple-element.239), channel_id=1, source_target_pairs={{0,0},{8,1},{16,2},{24,3},{32,4},{40,5},{48,6},{56,7},{1,8},{9,9},... | collective-permute-start | bytes 294920 | tf_op jit(solution)/shard_map/ppermute | solution.py:772
  619.2 22.9 %collective-permute-start.112 = (bf16[96,4224]{1,0:T(8,128)(2,1)S(1)}, bf16[96,4224]{1,0:T(8,128)(2,1)S(1)}, u32[]{:S(2)}, u32[]{:S(2)}) collective-permute-start(bf16[96,4224]{1,0:T(8,128)(2,1)S(1)} %fusion.2), channel_id=1, source_target_pairs={{0,64},{64,0},{1,65},{65,1},{2,66},{66,2},{3,67},{67,3},{4,68},{68... | collective-permute-start | bytes 2433032 | tf_op jit(solution)/shard_map/ppermute | solution.py:865
  622.7 57.7 %collective-permute-start.89 = (bf16[32,1536]{1,0:T(8,128)(2,1)S(1)}, bf16[32,1536]{1,0:T(8,128)(2,1)S(1)}, u32[]{:S(2)}, u32[]{:S(2)}) collective-permute-start(bf16[32,1536]{1,0:T(8,128)(2,1)S(1)} %get-tuple-element.236), channel_id=1, source_target_pairs={{48,0},{56,1},{0,2},{8,3},{16,4},{24,5},{32,6},{40,7},{49,8},{57,9... | collective-permute-start | bytes 294920 | tf_op jit(solution)/shard_map/ppermute | solution.py:772
  653.3 20.2 %collective-permute-start.104 = (bf16[96,3072]{1,0:T(8,128)(2,1)S(1)}, bf16[96,3072]{1,0:T(8,128)(2,1)S(1)}, u32[]{:S(2)}, u32[]{:S(2)}) collective-permute-start(bf16[96,3072]{1,0:T(8,128)(2,1)S(1)} %dynamic-slice_bitcast_fusion.7), channel_id=1, source_target_pairs={{0,1},{1,0},{2,3},{3,2},{4,5},{5,4},{6,7},{7,6},{8,9},{9,8},{10,11... | collective-permute-start | bytes 1769480 | tf_op jit(solution)/shard_map/ppermute | solution.py:861
  692.7 20.8 %collective-permute-start.107 = (bf16[96,3072]{1,0:T(8,128)(2,1)S(1)}, bf16[96,3072]{1,0:T(8,128)(2,1)S(1)}, u32[]{:S(2)}, u32[]{:S(2)}) collective-permute-start(bf16[96,3072]{1,0:T(8,128)(2,1)S(1)} %add_convert_fusion.5), channel_id=1, source_target_pairs={{0,16},{16,32},{32,48},{48,0},{1,17},{17,33},{33,49},{49,1},{2,18}... | collective-permute-start | bytes 1769480 | tf_op jit(solution)/shard_map/ppermute | solution.py:822
  707.3 37.1 %collective-permute-start.75 = (bf16[32,1536]{1,0:T(8,128)(2,1)S(1)}, bf16[32,1536]{1,0:T(8,128)(2,1)S(1)}, u32[]{:S(2)}, u32[]{:S(2)}) collective-permute-start(bf16[32,1536]{1,0:T(8,128)(2,1)S(1)} %get-tuple-element.243), channel_id=1, source_target_pairs={{16,0},{24,1},{32,2},{40,3},{48,4},{56,5},{0,6},{8,7},{17,8},{25,9... | collective-permute-start | bytes 294920 | tf_op jit(solution)/shard_map/ppermute | solution.py:772
  714.8 23.7 %collective-permute-start.108 = (bf16[48,3072]{1,0:T(8,128)(2,1)S(1)}, bf16[48,3072]{1,0:T(8,128)(2,1)S(1)}, u32[]{:S(2)}, u32[]{:S(2)}) collective-permute-start(bf16[48,3072]{1,0:T(8,128)(2,1)S(1)} %slice.425), channel_id=1, source_target_pairs={{0,16},{16,32},{32,48},{48,0},{1,17},{17,33},{33,49},{49,1},{2,18}... | collective-permute-start | bytes 884744 | tf_op jit(solution)/shard_map/ppermute | solution.py:824
  717.4 27.0 %collective-permute-start.76 = (bf16[32,1536]{1,0:T(8,128)(2,1)S(1)}, bf16[32,1536]{1,0:T(8,128)(2,1)S(1)}, u32[]{:S(2)}, u32[]{:S(2)}) collective-permute-start(bf16[32,1536]{1,0:T(8,128)(2,1)S(1)} %get-tuple-element.242), channel_id=1, source_target_pairs={{32,0},{40,1},{48,2},{56,3},{0,4},{8,5},{16,6},{24,7},{33,8},{41,9... | collective-permute-start | bytes 294920 | tf_op jit(solution)/shard_map/ppermute | solution.py:772
  (190 other events, 2249.0 us)
Sparse Core Ops, SparseCore 0:
  20.8 105.2 all-gather.6
  129.2 93.2 all-gather.8
  456.6 63.8 reduce-scatter.1
  645.9 45.5 all-gather.10

commit v7 on v6

--- a/solution.py
+++ b/solution.py
@@ -82,8 +82,8 @@
 
 
 def down_parts(block):
-    left = block[:, 0:64, :].reshape(256, 1024)
-    right = jnp.concatenate([block[:, 64:96, 0:512], block[:, 64:96, 512:1024]], axis=1)
+    left = block[:, 0:128, :].reshape(256, 1024)
+    right = jnp.concatenate([block[:, 128:192, 0:512], block[:, 128:192, 512:1024]], axis=1)
     return left, right.reshape(256, 512)
 
 
@@ -125,7 +125,7 @@
     return [
         pl.BlockSpec((1536, 256), lambda b: (0, b)),
         pl.BlockSpec((1536, 256), lambda b: (0, 4 + b)),
-        pl.BlockSpec((4, 96, 1024), lambda b: (b, 0, 2)),
+        pl.BlockSpec((2, 192, 1024), lambda b: (b, 0, 2)),
     ]
 
 
@@ -201,23 +201,10 @@
     )(*after, *pieces, flat_packed, flat_packed, packed, gate, up)
 
 
-def store_halves(side, mine, theirs, even, odd, rows, columns):
-    @pl.when(side == 0)
-    def _():
-        mine[:, rows, columns] = even
-        theirs[:, rows, columns] = odd
-
-    @pl.when(side != 0)
-    def _():
-        mine[:, rows, columns] = odd
-        theirs[:, rows, columns] = even
-
-
-def feed_weights_kernel(side_ref, *refs):
+def feed_weights_kernel(*refs):
     flats, grads = refs[:5], refs[5:10]
-    low_gate, low_up, hidden, mine, theirs, flat_t, hidden_t, grad = refs[10:]
+    low_gate, low_up, hidden, out, flat_t, hidden_t, grad = refs[10:]
     step = pl.program_id(0)
-    side = side_ref[0]
 
     @pl.when(step == 0)
     def _():
@@ -232,66 +219,49 @@
         hidden_t[...] = hidden[...].T
         fill(grad, grads)
 
-    def columns(block):
-        out = nn(flat_t[...], block).astype(BF16).reshape(8, 192, 256)
-        store_halves(
-            side, mine, theirs, out[:, :96], out[:, 96:], slice(0, 96), slice(0, 256)
-        )
-
     @pl.when(step < 4)
     def _():
-        columns(low_gate[...])
+        out[...] = nn(flat_t[...], low_gate[...]).astype(BF16).reshape(8, 192, 256)
 
     @pl.when((step >= 4) & (step < 8))
     def _():
-        columns(low_up[...])
+        out[...] = nn(flat_t[...], low_up[...]).astype(BF16).reshape(8, 192, 256)
 
     for q in range(4):
 
         @pl.when(step == 8 + q)
         def _():
             top = nn(hidden_t[...], grad[:, 256 * q : 256 * (q + 1)]).astype(BF16)
-            top = top.reshape(8, 128, 256)
-            store_halves(
-                side, mine, theirs, top[:, :64], top[:, 64:], slice(0, 64), slice(0, 256)
-            )
-            half = 32 * (q // 2)
-            some = hidden_t[...].reshape(16, 64, 512)[:, half : half + 32].reshape(512, 512)
+            out[:, 0:128, :] = top.reshape(8, 128, 256)
+            half = 64 * (q // 2)
+            some = hidden_t[...].reshape(8, 128, 512)[:, half : half + 64].reshape(512, 512)
             start = 1024 + 256 * (q % 2)
-            low = nn(some, grad[:, start : start + 256]).astype(BF16).reshape(8, 64, 256)
-            store_halves(
-                side, mine, theirs, low[:, :32], low[:, 32:], slice(64, 96), slice(0, 256)
-            )
-
-
-def feed_weights_call(side, flats, grads, low_gate, low_up, hidden):
-    block = pl.BlockSpec((8, 96, 256), lambda b, s: (0, 0, b))
-    shape = jax.ShapeDtypeStruct((8, 96, 3072), BF16)
-    spec = pltpu.PrefetchScalarGridSpec(
-        num_scalar_prefetch=1,
+            low = nn(some, grad[:, start : start + 256]).astype(BF16)
+            out[:, 128:192, :] = low.reshape(8, 64, 256)
+
+
+def feed_weights_call(flats, grads, low_gate, low_up, hidden):
+    return pl.pallas_call(
+        feed_weights_kernel,
         grid=(12,),
         in_specs=PIECES
         + PIECES
         + [
-            pl.BlockSpec((512, 256), lambda b, s: (0, jnp.minimum(b, 3))),
-            pl.BlockSpec((512, 256), lambda b, s: (0, jnp.clip(b - 4, 0, 3))),
+            pl.BlockSpec((512, 256), lambda b: (0, jnp.minimum(b, 3))),
+            pl.BlockSpec((512, 256), lambda b: (0, jnp.clip(b - 4, 0, 3))),
             whole((512, 1024)),
         ],
-        out_specs=[block, block],
+        out_specs=pl.BlockSpec((8, 192, 256), lambda b: (0, 0, b)),
+        out_shape=jax.ShapeDtypeStruct((8, 192, 3072), BF16),
         scratch_shapes=[
             pltpu.VMEM((1536, 512), BF16),
             pltpu.VMEM((1024, 512), BF16),
             pltpu.VMEM((512, 1536), BF16),
         ],
-    )
-    return pl.pallas_call(
-        feed_weights_kernel,
-        grid_spec=spec,
-        out_shape=[shape, shape],
         compiler_params=params(40),
         cost_estimate=cost(4.9e9, 18e6),
         name="feed_weights",
-    )(side, *flats, *grads, low_gate, low_up, hidden)
+    )(*flats, *grads, low_gate, low_up, hidden)
 
 
 def piece_specs(pieces):
@@ -379,7 +349,7 @@
         stats.append(peak + jnp.log(totals))
         for block in range(4):
             cols = slice(384 * block, 384 * (block + 1))
-            value = nn(sums[-1], w_out[4 * head + block])
+            value = nn(sums[-1], out_block(w_out, head, block))
             if head == 0:
                 total[:, cols] = value
             else:
@@ -394,11 +364,16 @@
 
 
 def out_spec():
-    return pl.BlockSpec((16, 96, 384), lambda *_: (0, 0, 10))
+    return pl.BlockSpec((8, 192, 384), lambda *_: (0, 0, 2))
+
+
+def out_block(w_out, head, block):
+    start = 96 * (head % 2)
+    return w_out[2 * block + head // 2, start : start + 96, :]
 
 
 def projection_spec():
-    return pl.BlockSpec((1536, 768), lambda *_: (0, 4))
+    return pl.BlockSpec((1536, 768), lambda *_: (0, 0))
 
 
 def attend_call(window, length, queries, own, other, places, key_places, packed, after=()):
@@ -433,9 +408,11 @@
             values = both_rows(own[...], other[...], 192 + HEAD_DIM * (head // 2))
             keys_t = keys.T
         query = queries[:, HEAD_DIM * head : HEAD_DIM * (head + 1)]
-        mixed = nt(grad[:, :384], w_out[4 * head])
+        mixed = nt(grad[:, :384], out_block(w_out, head, 0))
         for block in range(1, 4):
-            mixed += nt(grad[:, 384 * block : 384 * (block + 1)], w_out[4 * head + block])
+            mixed += nt(
+                grad[:, 384 * block : 384 * (block + 1)], out_block(w_out, head, block)
+            )
         mixed = mixed.astype(BF16)
         scores = nt(keys, query) * HEAD_DIM ** (-0.5) + bias[...]
         probs = jnp.exp(scores - log_total[head : head + 1, :])
@@ -537,10 +514,9 @@
     )(*after, low_queries, pair_own, pair_came, cosine, sine, packed.reshape(1536, wide))
 
 
-def attend_weights_kernel(count, side_ref, *refs):
+def attend_weights_kernel(count, *refs):
     flats, grads, (low, mixed) = refs[:count], refs[count : count + 5], refs[count + 5 : count + 7]
-    mine, theirs, flat_t, grad = refs[count + 7 :]
-    side = side_ref[0]
+    out, flat_t, grad = refs[count + 7 :]
     start = 0
     for ref in flats:
         n = ref.shape[0]
@@ -549,137 +525,68 @@
     fill(grad, grads)
     for block in range(3):
         cols = slice(256 * block, 256 * (block + 1))
-        out = nn(flat_t[...], low[:, cols]).astype(BF16).reshape(8, 192, 256)
-        store_halves(side, mine, theirs, out[:, :96], out[:, 96:], slice(0, 96), cols)
+        out[:, :, cols] = nn(flat_t[...], low[:, cols]).astype(BF16).reshape(8, 192, 256)
     mixed_t = mixed[...].T
-    for half in range(2):
-        out = [
-            nn(mixed_t, grad[:, 384 * q : 384 * (q + 1)]).astype(BF16).reshape(4, 96, 384)
-            for q in (2 * half, 2 * half + 1)
-        ]
-        for head in range(4):
-            place = slice(2 * head + half, 2 * head + half + 1)
-            store_at(side, mine, theirs, out[0][head : head + 1], out[1][head : head + 1], place)
-
-
-def store_at(side, mine, theirs, even, odd, place):
-    cols = slice(768, 1152)
-
-    @pl.when(side == 0)
-    def _():
-        mine[place, :, cols] = even
-        theirs[place, :, cols] = odd
-
-    @pl.when(side != 0)
-    def _():
-        mine[place, :, cols] = odd
-        theirs[place, :, cols] = even
-
-
-def attend_weights_call(side, flats, grads, low, mixed, after=()):
-    shape = jax.ShapeDtypeStruct((8, 96, 1152), BF16)
+    for block in range(4):
+        part = nn(mixed_t, grad[:, 384 * block : 384 * (block + 1)]).astype(BF16)
+        out[2 * block : 2 * block + 2, :, 768:1152] = part.reshape(2, 192, 384)
+
+
+def attend_weights_call(flats, grads, low, mixed):
     return pl.pallas_call(
-        later(functools.partial(attend_weights_kernel, len(flats)), len(after)),
+        functools.partial(attend_weights_kernel, len(flats)),
         grid=(1,),
-        in_specs=anywhere(after)
-        + [pl.BlockSpec(memory_space=pltpu.SMEM)]
-        + piece_specs(flats)
-        + PIECES
-        + [whole((512, 768)), whole((512, 384))],
-        out_specs=[whole((8, 96, 1152))] * 2,
-        out_shape=[shape, shape],
+        in_specs=piece_specs(flats) + PIECES + [whole((512, 768)), whole((512, 384))],
+        out_specs=whole((8, 192, 1152)),
+        out_shape=jax.ShapeDtypeStruct((8, 192, 1152), BF16),
         scratch_shapes=[pltpu.VMEM((1536, 512), BF16), pltpu.VMEM((512, 1536), BF16)],
         compiler_params=params(40),
         cost_estimate=cost(1.9e9, 10e6),
         name="attend_weights",
-    )(*after, side, *flats, *grads, low, mixed)
-
-
-def unpack_attention(side, blocks, refs):
-    wq, wk, wv, wo = refs
+    )(*flats, *grads, low, mixed)
+
+
+def unpack_kernel(*refs):
+    every, wq, wk, wv, wo, gate, up, down = refs
+    side = pl.program_id(0)
+    blocks = [every[x, 0] for x in range(4)]
     for x, block in enumerate(blocks):
-        wq[:, 384 * x : 384 * (x + 1)] = block[:, :384].astype(F32)
-    wk[...] = jnp.concatenate([block[:, 384:576].astype(F32) for block in blocks], axis=1)
-    wv[...] = jnp.concatenate([block[:, 576:768].astype(F32) for block in blocks], axis=1)
-    for x, block in enumerate(blocks):
-        rows = slice(96 * (x // 2), 96 * (x // 2) + 96)
-        for core in range(2):
-            start = 384 * (2 * (x % 2) + core)
-
-            @pl.when(side == core)
-            def _(rows=rows, start=start, block=block):
-                wo[rows, start : start + 384] = block[:, 768:1152].astype(F32)
-
-
-def unpack_feed(blocks, refs):
-    gate, up, down = refs
-    for x, block in enumerate(blocks):
+        wq[:, 384 * x : 384 * (x + 1)] = block[:, 3072:3456].astype(F32)
+        wo[:, 384 * x : 384 * (x + 1)] = block[:, 3840:4224].astype(F32)
         for s in range(8):
             cols = slice(512 * s + 128 * x, 512 * s + 128 * (x + 1))
             gate[:, cols] = block[:, 128 * s : 128 * (s + 1)].astype(F32)
             up[:, cols] = block[:, 1024 + 128 * s : 1024 + 128 * (s + 1)].astype(F32)
-        down[x, 0, :, :1024] = block[0:64, 2048:3072].astype(F32)
-        down[x, 0, 0:32, 1024:] = block[64:96, 2048:2560].astype(F32)
-        down[x, 0, 32:64, 1024:] = block[64:96, 2560:3072].astype(F32)
-
-
-ATTENTION_SPECS = [
-    pl.BlockSpec((96, 1536), lambda b, s: (b, 0)),
-    pl.BlockSpec((96, 768), lambda b, s: (b, 0)),
-    pl.BlockSpec((96, 768), lambda b, s: (b, 0)),
-    pl.BlockSpec((192, 1536), lambda b, s: (0, 0)),
-]
-ATTENTION_SHAPES = [
-    jax.ShapeDtypeStruct((192, 1536), F32),
-    jax.ShapeDtypeStruct((192, 768), F32),
-    jax.ShapeDtypeStruct((192, 768), F32),
-    jax.ShapeDtypeStruct((192, 1536), F32),
-]
-FEED_OUT_SPECS = [
-    pl.BlockSpec((96, 4096), lambda b, s: (b, 0)),
-    pl.BlockSpec((96, 4096), lambda b, s: (b, 0)),
-    pl.BlockSpec((4, 1, 64, 1536), lambda b, s: (0, b, 0, 0)),
-]
-FEED_SHAPES = [
-    jax.ShapeDtypeStruct((192, 4096), F32),
-    jax.ShapeDtypeStruct((192, 4096), F32),
-    jax.ShapeDtypeStruct((4, 2, 64, 1536), F32),
-]
-
-
-def unpack_kernel(attention, feed, me, *refs):
-    side = pl.program_id(0)
-    blocks = [ref[0, 0] for ref in refs[:4]]
-    refs = refs[4:]
-    if attention:
-        start = 3072 if feed else 0
-        unpack_attention(side, [block[:, start : start + 1152] for block in blocks], refs[:4])
-        refs = refs[4:]
-    if feed:
-        unpack_feed([block[:, :3072] for block in blocks], refs)
-
-
-def unpack_call(attention, feed, me, every):
-    wide = every.shape[-1]
-    specs = [
-        pl.BlockSpec((1, 1, 96, wide), lambda b, s, x=x: (lax.rem(x - s[0] + 4, 4), b, 0, 0))
-        for x in range(4)
-    ]
-    out_specs = (ATTENTION_SPECS if attention else []) + (FEED_OUT_SPECS if feed else [])
-    shapes = (ATTENTION_SHAPES if attention else []) + (FEED_SHAPES if feed else [])
+
+        @pl.when(side == 0)
+        def _(x=x, block=block):
+            down[x, 0:96, :1024] = block[:, 2048:3072].astype(F32)
+
+        @pl.when(side == 1)
+        def _(x=x, block=block):
+            down[x, 96:128, :1024] = block[0:32, 2048:3072].astype(F32)
+            down[x, 0:64, 1024:] = block[32:96, 2048:2560].astype(F32)
+            down[x, 64:128, 1024:] = block[32:96, 2560:3072].astype(F32)
+
+    wk[...] = jnp.concatenate([block[:, 3456:3648].astype(F32) for block in blocks], axis=1)
+    wv[...] = jnp.concatenate([block[:, 3648:3840].astype(F32) for block in blocks], axis=1)
+
+
+def unpack_call(every):
+    widths = (1536, 768, 768, 1536, 4096, 4096)
     out = pl.pallas_call(
-        functools.partial(unpack_kernel, attention, feed),
-        grid_spec=pltpu.PrefetchScalarGridSpec(
-            num_scalar_prefetch=1, grid=(2,), in_specs=specs, out_specs=out_specs
-        ),
-        out_shape=shapes,
+        unpack_kernel,
+        grid=(2,),
+        in_specs=[pl.BlockSpec((4, 1, 96, 4224), lambda b: (0, b, 0, 0))],
+        out_specs=[pl.BlockSpec((96, width), lambda b: (b, 0)) for width in widths]
+        + [whole((4, 128, 1536))],
+        out_shape=[jax.ShapeDtypeStruct((192, width), F32) for width in widths]
+        + [jax.ShapeDtypeStruct((4, 128, 1536), F32)],
         compiler_params=params(48),
         cost_estimate=cost(1e6, 30e6),
         name="unpack",
-    )(me, every, every, every, every)
-    if feed:
-        out = list(out[:-1]) + [out[-1].reshape(512, 1536)]
-    return out
+    )(every)
+    return out[:4], (out[4], out[5], out[6].reshape(512, 1536))
 
 
 def pack_feed_kernel(where, w_gate, w_up, w_down, out):
@@ -688,9 +595,9 @@
         cols = pl.ds(pl.multiple_of(512 * s + 128 * x, 128), 128)
         out[:, 128 * s : 128 * (s + 1)] = w_gate[:, cols]
         out[:, 1024 + 128 * s : 1024 + 128 * (s + 1)] = w_up[:, cols]
-    out[0:64, 2048:3072] = w_down[:, 0:1024]
-    out[64:96, 2048:2560] = w_down[0:32, 1024:1536]
-    out[64:96, 2560:3072] = w_down[32:64, 1024:1536]
+    out[0:128, 2048:3072] = w_down[:, 0:1024]
+    out[128:192, 2048:2560] = w_down[0:64, 1024:1536]
+    out[128:192, 2560:3072] = w_down[64:128, 1024:1536]
 
 
 def pack_feed_call(where, w_gate, w_up, w_down, after=()):
@@ -701,15 +608,15 @@
             grid=(1,),
             in_specs=anywhere(after)
             + [
-                pl.BlockSpec((96, 4096), lambda b, w: (w[1], 0)),
-                pl.BlockSpec((96, 4096), lambda b, w: (w[1], 0)),
-                pl.BlockSpec((64, 1536), lambda b, w: (2 * w[0] + w[1], 0)),
+                pl.BlockSpec((192, 4096), lambda b, w: (0, 0)),
+                pl.BlockSpec((192, 4096), lambda b, w: (0, 0)),
+                pl.BlockSpec((128, 1536), lambda b, w: (w[0], 0)),
             ],
-            out_specs=pl.BlockSpec((96, 3072), lambda b, w: (0, 0)),
+            out_specs=pl.BlockSpec((192, 3072), lambda b, w: (0, 0)),
         ),
-        out_shape=jax.ShapeDtypeStruct((96, 3072), BF16),
+        out_shape=jax.ShapeDtypeStruct((192, 3072), BF16),
         compiler_params=params(24),
-        cost_estimate=cost(1e3, 24e5),
+        cost_estimate=cost(1e3, 5e6),
         name="pack_feed",
     )(where, *after, w_gate, w_up, w_down)
 
@@ -722,7 +629,7 @@
 SIZES = (2, 4, 2, 4, 2)
 REP = ("ylo", "x", "core")
 SHARD = ("z", "yhi")
-SPREAD = ("z", "yhi", "core")
+SPREAD = ("z", "core")
 
 RIGHT = [(i, (i + 1) % 4) for i in range(4)]
 LEFT = [(i, (i - 1) % 4) for i in range(4)]
@@ -734,16 +641,16 @@
     return (((ylo * 4 + x) * 2 + core) * 4 + z) * 2 + yhi
 
 
-def permutation(place):
+def permutation(place, taken=None):
     pairs = []
     for ylo in range(2):
         for x in range(4):
             for core in range(2):
                 for z in range(4):
                     for yhi in range(2):
-                        pairs.append(
-                            (number(ylo, x, core, z, yhi), number(ylo, *place(x, core, z, yhi)))
-                        )
+                        here = (ylo, x, core, z, yhi)
+                        if taken is None or taken(*here):
+                            pairs.append((number(*here), number(*place(*here))))
     return pairs
 
 
@@ -751,9 +658,22 @@
     return [(there, here) for here, there in pairs]
 
 
-LINES = [permutation(lambda x, c, z, h, k=k: ((z + k) % 4, h, x, c)) for k in range(4)]
-LINES_LENGTH = permutation(lambda x, c, z, h: (z, h, x, c))
-ROWS = permutation(lambda x, c, z, h: (z, c, 2 * h + x // 2, x % 2))
+def at_home(ylo, x, core, z, yhi):
+    return core == yhi
+
+
+def not_home(*place):
+    return not at_home(*place)
+
+
+LINES = [
+    permutation(lambda l, x, c, z, h, k=k: (l, (z + k) % 4, h, x, c)) for k in range(4)
+]
+TURN = permutation(lambda l, x, c, z, h: (l, z, h, x, c))
+SHARE = permutation(lambda l, x, c, z, h: (l, x, c, z, 1 - h), at_home)
+COLLECT = permutation(lambda l, x, c, z, h: (l, x, c, z, 1 - h), not_home)
+BESIDE = permutation(lambda l, x, c, z, h: (1 - l, x, c, z, h), at_home)
+CROSS = permutation(lambda l, x, c, z, h: (l, z, c, x, h), at_home)
 
 
 def to_lines(block, z):
@@ -809,76 +729,31 @@
     return values * lax.rsqrt(jnp.mean(values * values, axis=-1, keepdims=True) + EPSILON) * gain
 
 
-def either(index, first, second):
-    return jnp.where(index == 0, first, second)
-
-
 def add_low(mine, came):
     return (mine.astype(F32) + came.astype(F32)).astype(BF16)
 
 
-def ring_stack(block, axis):
-    half = block.shape[0] // 2
-    before = lax.ppermute(block, axis, RIGHT)
-    after = lax.ppermute(block, axis, LEFT)
-    first = lax.ppermute(before[:half], axis, RIGHT)
-    second = lax.ppermute(after[half:], axis, LEFT)
-    far = jnp.concatenate([first, second], axis=0)
-    return jnp.stack([block, after, far, before])
-
-
-def line_gather(piece, core):
-    ring = ring_stack(piece, "x")
-    came = lax.ppermute(ring, "core", SWAP)
-    return either(core, jnp.stack([ring, came], axis=1), jnp.stack([came, ring], axis=1))
-
-
-def core_sum(mine, theirs):
-    return add_low(mine, lax.ppermute(theirs, "core", SWAP))
-
-
-def z_sum(line, where, offload):
-    if offload:
-        return lax.psum_scatter(line, "z", scatter_dimension=0, tiled=True)
-    tall = line.reshape((4, 2) + line.shape[1:])
-
-    def step(r):
-        return lax.dynamic_index_in_dim(tall, (where["z"] + r) % 4, axis=0, keepdims=False)
-
-    own, after, far, before = step(0), step(1), step(2), step(3)
-    first = lax.ppermute(far[:1], "z", RIGHT)
-    second = lax.ppermute(far[1:], "z", LEFT)
-    after = jnp.concatenate([add_low(after[:1], first), after[1:]])
-    before = jnp.concatenate([before[:1], add_low(before[1:], second)])
-    from_before = lax.ppermute(after, "z", RIGHT).astype(F32)
-    from_after = lax.ppermute(before, "z", LEFT).astype(F32)
-    return (own.astype(F32) + from_before + from_after).astype(BF16)
-
-
-def yhi_sum(pair, where):
-    mine = lax.dynamic_index_in_dim(pair, where["yhi"], axis=0, keepdims=False)
-    theirs = lax.dynamic_index_in_dim(pair, 1 - where["yhi"], axis=0, keepdims=False)
-    return add_low(mine, lax.ppermute(theirs, "yhi", SWAP))
-
-
-def ylo_sum(piece):
-    return add_low(piece, lax.ppermute(piece, "ylo", SWAP))
-
-
-def y_sum(pair, where):
-    return ylo_sum(yhi_sum(pair, where))
-
-
-def out_home(piece, start):
-    first, last = start + 768, start + 1152
-    moved = lax.ppermute(piece[:, first:last], AXES, inverse(ROWS))
-    return jnp.concatenate([piece[:, :first], moved, piece[:, last:]], axis=1)
-
-
-def gain_halves(grads, core):
-    tall = grads.astype(BF16).T.reshape(8, 2, 96, 4)
-    tall = jnp.pad(tall, ((0, 0), (0, 0), (0, 0), (0, 124)))
-    return either(core, tall[:, 0], tall[:, 1]), either(core, tall[:, 1], tall[:, 0])
+def home_sum(rows):
+    return add_low(rows, lax.ppermute(rows, AXES, COLLECT))
+
+
+def home_piece(rows, core, yhi):
+    rows = add_low(rows, lax.ppermute(rows, AXES, BESIDE))
+    moved = lax.ppermute(rows[:, 3840:], AXES, CROSS)
+    rows = jnp.concatenate([rows[:, :3840], moved], axis=1)
+    theirs = lax.dynamic_slice_in_dim(rows, 96 * (1 - core), 96, axis=0)
+    mine = lax.dynamic_slice_in_dim(rows, 96 * core, 96, axis=0)
+    return jnp.where(core == yhi, mine, lax.ppermute(theirs, "core", SWAP))
+
+
+def butterfly(values):
+    for axis, size in (("core", 2), ("x", 4), ("z", 4), ("yhi", 2), ("ylo", 2)):
+        step = 1
+        while step < size:
+            pairs = [(i, i ^ step) for i in range(size)]
+            values = values + lax.ppermute(values, axis, pairs)
+            step *= 2
+    return values
 
 
 def norm_back(grad, own_normed, state, gain):
@@ -892,35 +767,42 @@
     core = lax.axis_index("core")
     z = lax.axis_index("z")
     yhi = lax.axis_index("yhi")
-    where = {"x": x, "core": core, "z": z, "yhi": yhi}
-    pair_index = jnp.stack([x, core]).astype(jnp.int32)
-    side = core.astype(jnp.int32).reshape(1)
-
-    gains = jnp.stack([weights[0], weights[5], weights[9], weights[14]])
-    gains = lax.dynamic_slice_in_dim(gains, core * 96, 96, axis=1).T
+    member = x.astype(jnp.int32).reshape(1)
+    home = core == yhi
+
+    gains = jnp.stack([weights[0], weights[5], weights[9], weights[14]]).T
     gains = jnp.pad(gains, ((0, 0), (0, 124)))
-    def line_weights(base, extra, after):
-        w_q, w_k, w_v, w_out = weights[base + 1 : base + 5]
-        out_block = lax.dynamic_slice(
-            w_out, (96 * (x // 2), 384 * (2 * (x % 2) + core)), (96, 384)
-        )
-        out_block = lax.ppermute(out_block, AXES, ROWS)
-        parts = [pack_feed_call(pair_index, *weights[base + 6 : base + 9], after=after)]
-        parts += [
-            lax.dynamic_slice(w, (core * 96, x * (w.shape[1] // 4)), (96, w.shape[1] // 4))
-            for w in (w_q, w_k, w_v)
+
+    def shared(block):
+        return jnp.where(home, block, lax.ppermute(block, AXES, SHARE))
+
+    def attention_weights(base, extra):
+        w_out = weights[base + 4]
+        block = lax.dynamic_slice(w_out, (0, 384 * x), (192, 384))
+        block = lax.ppermute(block, AXES, TURN)
+        parts = [
+            lax.dynamic_slice(w, (0, x * (w.shape[1] // 4)), (192, w.shape[1] // 4))
+            for w in weights[base + 1 : base + 4]
         ]
-        piece = jnp.concatenate(parts + [out_block] + extra, axis=1)
+        parts = shared(jnp.concatenate(parts + extra, axis=1))
+        piece = jnp.concatenate([parts[:, :768], block, parts[:, 768:]], axis=1)
         return lax.all_gather(piece, SPREAD, axis=0, tiled=False)
 
-    first_weights = line_weights(0, [gains], ())
-    gains = first_weights[:, :, 4224:4228].transpose(2, 0, 1).reshape(4, width).astype(F32)
-
-    length = lax.ppermute(lengths, AXES, LINES_LENGTH)
+    def feed_weights(base, after):
+        piece = shared(pack_feed_call(member, *weights[base + 6 : base + 9], after=after))
+        return lax.all_gather(piece, SPREAD, axis=0, tiled=False)
+
+    attn_one = attention_weights(0, [gains])
+    gains = attn_one[:, :, 1152:1156].transpose(2, 0, 1).reshape(4, width).astype(F32)
+
+    length = lax.ppermute(lengths, AXES, TURN)
     rows = to_lines(tokens[0], z)
     pieces = ring_gather(rows)
     state = rows.astype(F32)
-    packed = (first_weights, line_weights(9, [], (rows,)))
+    feed_one = feed_weights(0, ())
+    attn_two = attention_weights(9, [])
+    feed_two = feed_weights(9, (rows,))
+    packed = ((attn_one, feed_one), (attn_two, feed_two))
 
     here = (2 * z + yhi) * stretch + jnp.arange(stretch, dtype=jnp.int32)
     valid = (here < lengths[0])[:, None]
@@ -952,7 +834,7 @@
 
     records = []
     for index, window in enumerate((WINDOW, 8 * stretch)):
-        attn = feed = packed[index]
+        attn, feed = packed[index]
         gain_attn, gain_feed = gains[2 * index], gains[2 * index + 1]
         if index == 0:
             queries, own, flat = project_call(True, pieces, gain_attn, attn, cosine, sine)
@@ -976,67 +858,69 @@
 
     results = [None] * 18
     gain_grads = [None] * 4
-    zero = jnp.zeros((1,), jnp.int32)
-    place = x.astype(jnp.int32).reshape(1)
 
     def feed_back(index, grad, pieces, after):
         state, flats, gate, up, hidden = records[index][1]
         *partial, low_gate, low_up = feed_backward_call(
-            pieces, packed[index], gate, up, after=after
+            pieces, packed[index][1], gate, up, after=after
         )
         own_normed = ring_scatter_direct(*partial)
         grad, gain_grads[2 * index + 1] = norm_back(
             grad, own_normed, state, gains[2 * index + 1]
         )
-        return grad, feed_weights_call(side, flats, pieces, low_gate, low_up, hidden)
-
-    def attention_back(index, grad, pieces, after):
+        return grad, feed_weights_call(flats, pieces, low_gate, low_up, hidden)
+
+    def attention_back(index, grad, pieces, after, late):
         state, flats, line, mixed, log_total = records[index][0]
         window = records[index][2]
+        attn = packed[index][0]
         low_queries, pair_own, pair_other = attend_backward_call(
-            window, length, pieces, *line, packed[index], log_total, cosine_t, sine_t, after=after
+            window, length, pieces, *line, attn, log_total, cosine_t, sine_t, after=after
         )
         came = lax.ppermute(pair_other, "core", SWAP)
-        *partial, low = unproject_call(low_queries, pair_own, came, cosine, sine, packed[index])
+        *partial, low = unproject_call(
+            low_queries, pair_own, came, cosine, sine, attn, after=late
+        )
         own_normed = ring_scatter_direct(*partial)
         grad, gain_grads[2 * index] = norm_back(grad, own_normed, state, gains[2 * index])
-        return grad, attend_weights_call(side, flats, pieces, low, mixed)
-
-    def swap_after(halves, *others):
-        return halves[0], tie(halves[1], *others)
-
-    grad, halves = feed_back(1, grad, grad_pieces, ())
+        return grad, attend_weights_call(flats, pieces, low, mixed)
+
+    def scatter(block, *others):
+        return lax.psum_scatter(
+            tie(block, *others), SPREAD, scatter_dimension=0, tiled=True
+        )[0]
+
+    grad, feed_grad = feed_back(1, grad, grad_pieces, ())
     low = grad.astype(BF16)
-    feed_sum = core_sum(*swap_after(halves, low))
-    grad, halves = attention_back(1, grad, ring_gather(low), (feed_sum, last_rows))
+    second_feed = scatter(feed_grad, low)
+    grad, attn_grad = attention_back(1, grad, ring_gather(low), (feed_grad, last_rows), ())
     low = grad.astype(BF16)
-    attn_sum = core_sum(*swap_after(halves, low))
-    both_sum = jnp.concatenate([feed_sum, attn_sum], axis=2)
-
-    grad, halves = feed_back(0, grad, ring_gather(low), (both_sum,))
-    second_pair = z_sum(both_sum, where, True)
+    second_attn = scatter(attn_grad, low)
+
+    grad, feed_grad = feed_back(0, grad, ring_gather(low), (attn_grad, second_feed))
+    second = home_sum(jnp.concatenate([second_feed, second_attn], axis=1))
     low = grad.astype(BF16)
-    feed_sum = core_sum(*swap_after(halves, low))
-    grad, halves = attention_back(0, grad, ring_gather(low), (feed_sum,))
-    attn_sum = core_sum(*halves)
-    gain_sum = core_sum(*gain_halves(jnp.stack(gain_grads), core))
-    feed_pair = z_sum(feed_sum, where, False)
-    output = from_lines(tie(last_rows, feed_pair), z)[None]
-
-    second_piece = out_home(y_sum(tie(second_pair, halves[0]), where), 3072)
-    every = lax.all_gather(second_piece, ("x", "core"), axis=0, tiled=False)
-    out = unpack_call(True, True, zero, every.reshape(4, 2, 96, -1))
-    results[10:14] = out[:4]
-    results[15:18] = out[4:]
-
-    every = line_gather(y_sum(feed_pair, where), core)
-    results[6:9] = unpack_call(False, True, place, every)
-    attn_sum = jnp.concatenate([attn_sum, gain_sum], axis=2)
-    piece = y_sum(z_sum(attn_sum, where, False), where)
-    every = line_gather(out_home(piece, 0), core)
-    results[1:5] = unpack_call(True, False, place, every)
-    gain_sums = every[..., 1152:1156].astype(F32).sum(axis=0).reshape(192, 4).T
-    input_grad = from_lines(grad.astype(BF16), z).astype(F32)[None]
+    first_feed = scatter(feed_grad, low)
+    second_piece = home_piece(second, core, yhi)
+    grad, attn_grad = attention_back(
+        0, grad, ring_gather(low), (feed_grad, second), (second_piece,)
+    )
+    first_attn = scatter(attn_grad)
+    gain_sums = butterfly(jnp.stack(gain_grads))
+    gain_sums = lax.dynamic_slice_in_dim(gain_sums, (2 * z + yhi) * 192, 192, axis=1)
+
+    every = lax.all_gather(tie(second_piece, first_attn), ("x", "core"), axis=0, tiled=False)
+    results[10:14], results[15:18] = unpack_call(every.reshape(4, 2, 96, -1))
+    first = home_sum(jnp.concatenate([first_feed, first_attn], axis=1))
+    first_piece = home_piece(first, core, yhi)
+    every = lax.all_gather(first_piece, ("x", "core"), axis=0, tiled=False)
+    results[1:5], results[6:9] = unpack_call(every.reshape(4, 2, 96, -1))
+
+    both = jnp.stack([last_rows, grad.astype(BF16)]).reshape(2, 4, 32, width)
+    both = both.transpose(1, 0, 2, 3).reshape(2 * stretch, width)
+    both = from_lines(both, z).reshape(4, 2, 32, width).transpose(1, 0, 2, 3)
+    both = both.reshape(2, stretch, width)
+    output, input_grad = both[:1], both[1:].astype(F32)
     for index, slot in enumerate((0, 5, 9, 14)):
         results[slot] = gain_sums[index]
     return (output, input_grad, *results)

time: 781 us -> 972 us (1.24)
  waiting for transfers between devices: 280 us -> 451 us
  starting transfers between devices: 215 us -> 246 us
  other arithmetic: 59.5 us -> 36 us
  local copies, waits for them, and re-layouts: 42.6 us -> 61.5 us
    reduce_scatter x1 -> x4, waiting for transfers between devices: 0.02 us -> 191 us  [scatter(): lax.psum_scatter(tie(block, *others), SPREAD, scatter_dimension=0, tiled=...]
    all_gather x3 -> x6, waiting for transfers between devices: 52.3 us -> 0.03 us  [the longest x1 0.02 us: body(): every = lax.all_gather(first_piece, ('x', 'core'), axis=0, tiled=False)]
    ppermute x4, waiting for transfers between devices: 4.18 us -> 35.5 us  [ring_scatter_direct(): from_far = lax.ppermute(far, 'x', ACROSS).astype(F32)]
    ppermute x34 -> x22, waiting for transfers between devices: 61.4 us -> 85.8 us  [the longest x4 35.1 us: shared(): return jnp.where(home, block, lax.ppermute(block, AXES, SHARE))]
    ppermute x34 -> x22, starting transfers between devices: 59.8 us -> 80.3 us  [the longest x2 36.3 us: home_piece(): return jnp.where(core == yhi, mine, lax.ppermute(theirs, 'core', SWAP))]
    unnamed x220 -> x293, local copies, waits for them, and re-layouts: 18.2 us -> 38.6 us
    convert_element_type x13 -> x4, other arithmetic: 21.3 us -> 1.51 us  [add_low(): return (mine.astype(F32) + came.astype(F32)).astype(BF16)]
    ppermute x4, waiting for transfers between devices: 17.3 us -> 1.29 us  [ring_scatter(): from_right = lax.ppermute(left, 'x', LEFT).astype(F32)]
  transfers between devices with their start and end apart: 118 -> 108, of which waited for: 53 -> 59; matrix products, arithmetic and copies ran while one was open for 10% -> 5% of each run, Pallas kernels for 13% -> 11%
where the time goes in v7:
time: 972 us; the launch traced here: 961 us
  waiting for transfers between devices  451 us (46%)
  starting transfers between devices  246 us (25%)
  Pallas kernels  149 us (15%)
  local copies, waits for them, and re-layouts  61.5 us (6%)
  other arithmetic  36 us (4%)
  between operations  17.4 us (2%)
    reduce_scatter x4, waiting for transfers between devices, scatter(): lax.psum_scatter(tie(block, *others), SPREAD, scatter_dimension=0, tiled=...  191 us
    ppermute x8, starting transfers between devices, to_lines(): out.append(lax.ppermute(piece, AXES, LINES[k]))  41.4 us
    unnamed x293, local copies, waits for them, and re-layouts  38.6 us
    ppermute x8, waiting for transfers between devices, ring_gather(): from_left = lax.ppermute(block, 'x', RIGHT)  38.5 us
    ppermute x2, starting transfers between devices, home_piece(): return jnp.where(core == yhi, mine, lax.ppermute(theirs, 'core', SWAP))  36.3 us
    ppermute x4, waiting for transfers between devices, ring_scatter_direct(): from_far = lax.ppermute(far, 'x', ACROSS).astype(F32)  35.5 us
    ppermute x4, waiting for transfers between devices, shared(): return jnp.where(home, block, lax.ppermute(block, AXES, SHARE))  35.1 us
    ppermute x4, waiting for transfers between devices, from_lines(): lax.ppermute(block[part * k:part * (k + 1)], AXES, inverse(LINES[k]))  27.4 us
  transfers between devices with their start and end apart: 108, of which 59 were waited for; matrix products, arithmetic and copies ran while one was open for 5% of the time, Pallas kernels for 11%

profile of v7, /device:TPU:1, one launch (start us, length us, event | category | flops | bytes accessed | tf_op | source)
XLA Modules:
  0.0 960.7 jit_solution(14805343090331332734)
XLA Ops:
  30.7 17.2 %collective-permute-done.24 = bf16[192,3072]{1,0:T(8,128)(2,1)S(1)} collective-permute-done((bf16[192,3072]{1,0:T(8,128)(2,1)S(1)}, bf16[192,3072]{1,0:T(8,128)(2,1)S(1)}, u32[]{:S(2)}, u32[]{:S(2)}) %collective-permute-start.24) | collective-permute-done | bytes 1179680 | tf_op jit(solution)/shard_map/ppermute | solution.py:777
  53.5 7.7 collective-permute-start.38
  73.9 10.8 %collective-permute-start.2 = (bf16[32,1536]{1,0:T(8,128)(2,1)S(1)}, bf16[32,1536]{1,0:T(8,128)(2,1)S(1)}, u32[]{:S(2)}, u32[]{:S(2)}) collective-permute-start(bf16[32,1536]{1,0:T(8,128)(2,1)S(1)} %get-tuple-element.224), channel_id=1, source_target_pairs={{0,32},{1,40},{2,48},{3,56},{4,0},{5,8},{6,16},{7,24},{8,33},{9,41... | collective-permute-start | bytes 294920 | tf_op jit(solution)/shard_map/ppermute | solution.py:684
  101.4 16.7 %collective-permute-done.48 = bf16[192,3072]{1,0:T(8,128)(2,1)S(1)} collective-permute-done((bf16[192,3072]{1,0:T(8,128)(2,1)S(1)}, bf16[192,3072]{1,0:T(8,128)(2,1)S(1)}, u32[]{:S(2)}, u32[]{:S(2)}) %collective-permute-start.48) | collective-permute-done | bytes 1179680 | tf_op jit(solution)/shard_map/ppermute | solution.py:777
  148.0 9.3 attend.2
  181.5 7.3 collective-permute-start.19
  211.5 9.2 feed_forward.2
  259.8 7.6 collective-permute-start.39
  276.2 9.0 attend.3
  327.3 9.6 feed_forward.3
  340.3 12.6 %feed_backward.2 = (f32[128,1536]{1,0:T(8,128)S(1)}, bf16[128,1536]{1,0:T(8,128)(2,1)S(1)}, bf16[128,1536]{1,0:T(8,128)(2,1)S(1)}, bf16[128,1536]{1,0:T(8,128)(2...) custom-call(bf16[128,1536]{1,0:T(8,128)(2,1)S(1)} %constant_dynamic-update-slice_fusion.6.refs_0_.refs_5_, ...), custom_call_target="tpu_custom_call" | custom-call | flops 4899999744 | bytes 20000000 | tf_op jit(solution)/shard_map/feed_backward/pallas_call | solution.py:191
  368.5 8.0 collective-permute-done.50
  391.1 12.6 %feed_weights.2.refs_0_ = bf16[8,192,3072]{2,1,0:T(8,128)(2,1)} custom-call(bf16[128,1536]{1,0:T(8,128)(2,1)S(1)} %multiply_convert_fusion.refs_0_, bf16[128,1536]{1,0:T(8,128)(2,1)S(1)} %copy-done.32, bf16[128,1536]{1,0:T(8,128)(2,1)S(1)} %copy-done.35, bf16[64,1536]{1,0:T(8,128)(2,1)S(1)} %collective-permute-done.46.refs_3_, ...), custom_call_target="tpu_custom_call" | custom-call | flops 4899999744 | bytes 18000000 | tf_op jit(solution)/shard_map/feed_weights/pallas_call | solution.py:244
  405.5 13.5 %attend_backward.2 = (bf16[512,384]{1,0:T(8,128)(2,1)S(1)}, f32[512,384]{1,0:T(8,128)}, bf16[512,384]{1,0:T(8,128)(2,1)S(1)}) custom-call(bf16[8,192,3072]{2,1,0:T(8,128)(2,1)} %feed_weights.2.refs_0_, bf16[128,1536]{1,0:T(8,128)(2,1)S(1)} %get-tuple-element.207.refs_1_, s32[1]{0:T(128)} %collective-permute-done.4.length.refs_2_, ...), custom_call_target="tpu_custom_call" | custom-call | flops 6000000000 | bytes 6000000 | tf_op jit(solution)/shard_map/attend_backward/pallas_call | solution.py:455
  442.0 8.3 collective-permute-done.63
  454.5 39.2 %reduce-scatter.7.cloned.1.call-done = bf16[1,192,1152]{2,1,0:T(8,128)(2,1)} async-done(((bf16[8,192,1152]{2,1,0:T(8,128)(2,1)}), bf16[1,192,1152]{2,1,0:T(8,128)(2,1)}) %reduce-scatter.7.cloned.1.call-update) | async-done | bytes 442384 | tf_op jit(solution)/shard_map/reduce_scatter | solution.py:889
  493.7 61.1 %reduce-scatter.5.cloned.1.call-done = bf16[1,192,3072]{2,1,0:T(8,128)(2,1)} async-done(((bf16[8,192,3072]{2,1,0:T(8,128)(2,1)}), bf16[1,192,3072]{2,1,0:T(8,128)(2,1)}) %reduce-scatter.5.cloned.1.call-update) | async-done | bytes 1179664 | tf_op jit(solution)/shard_map/reduce_scatter | solution.py:889
  563.9 8.1 collective-permute-done.64.refs_3_.refs_6_
  580.2 12.8 %feed_backward.3 = (f32[128,1536]{1,0:T(8,128)S(1)}, bf16[128,1536]{1,0:T(8,128)(2,1)S(1)}, bf16[128,1536]{1,0:T(8,128)(2,1)S(1)}, bf16[128,1536]{1,0:T(8,128)(2...) custom-call(bf16[8,192,1152]{2,1,0:T(8,128)(2,1)} %attend_weights.2.refs_0_, ...), custom_call_target="tpu_custom_call" | custom-call | flops 4899999744 | bytes 20000000 | tf_op jit(solution)/shard_map/feed_backward/pallas_call | solution.py:191
  627.1 10.9 %collective-permute-start.74 = (bf16[96,4224]{1,0:T(8,128)(2,1)}, bf16[96,4224]{1,0:T(8,128)(2,1)}, u32[]{:S(2)}, u32[]{:S(2)}) collective-permute-start(bf16[96,4224]{1,0:T(8,128)(2,1)} %fusion.3), channel_id=1, source_target_pairs={{0,8},{8,0},{1,9},{9,1},{2,10},{10,2},{3,11},{11,3},{4,12},{12,4},... | collective-permute-start | bytes 2433032 | tf_op jit(solution)/shard_map/ppermute | solution.py:746
  638.1 12.0 %feed_weights.3.refs_0_ = bf16[8,192,3072]{2,1,0:T(8,128)(2,1)} custom-call(bf16[128,1536]{1,0:T(8,128)(2,1)S(1)} %copy-done.26, bf16[128,1536]{1,0:T(8,128)(2,1)S(1)} %copy-done.45, bf16[128,1536]{1,0:T(8,128)(2,1)S(1)} %copy-done.47, bf16[64,1536]{1,0:T(8,128)(2,1)S(1)} %copy-done.72, bf16[64,1536]{1,0:T(8,128)(2,1)S(1)} %copy-done.75, ...), custom_call_target="tpu_custom_call" | custom-call | flops 4899999744 | bytes 18000000 | tf_op jit(solution)/shard_map/feed_weights/pallas_call | solution.py:244
  650.2 13.3 %attend_backward.3 = (bf16[512,384]{1,0:T(8,128)(2,1)S(1)}, f32[512,384]{1,0:T(8,128)}, bf16[512,384]{1,0:T(8,128)(2,1)}) custom-call(bf16[8,192,3072]{2,1,0:T(8,128)(2,1)} %feed_weights.3.refs_0_, bf16[192,4224]{1,0:T(8,128)(2,1)} %copy-done.110, s32[1]{0:T(128)} %collective-permute-done.4.length.refs_2_, ...), custom_call_target="tpu_custom_call" | custom-call | flops 6000000000 | bytes 6000000 | tf_op jit(solution)/shard_map/attend_backward/pallas_call | solution.py:455
  681.5 29.5 %reduce-scatter.11.cloned.1.call-done = bf16[1,192,1152]{2,1,0:T(8,128)(2,1)} async-done(((bf16[8,192,1152]{2,1,0:T(8,128)(2,1)}), bf16[1,192,1152]{2,1,0:T(8,128)(2,1)}) %reduce-scatter.11.cloned.1.call-update) | async-done | bytes 442384 | tf_op jit(solution)/shard_map/reduce_scatter | solution.py:889
  711.1 61.0 %reduce-scatter.9.cloned.1.call-done = bf16[1,192,3072]{2,1,0:T(8,128)(2,1)} async-done(((bf16[8,192,3072]{2,1,0:T(8,128)(2,1)}), bf16[1,192,3072]{2,1,0:T(8,128)(2,1)}) %reduce-scatter.9.cloned.1.call-update) | async-done | bytes 1179664 | tf_op jit(solution)/shard_map/reduce_scatter | solution.py:889
  778.6 17.8 %collective-permute-done.94 = bf16[192,4224]{1,0:T(8,128)(2,1)S(1)} collective-permute-done((bf16[192,4224]{1,0:T(8,128)(2,1)S(1)}, bf16[192,4224]{1,0:T(8,128)(2,1)S(1)}, u32[]{:S(2)}, u32[]{:S(2)}) %collective-permute-start.94) | collective-permute-done | bytes 1622048 | tf_op jit(solution)/shard_map/ppermute | solution.py:737
  798.8 25.3 %collective-permute-start.97 = (bf16[96,4224]{1,0:T(8,128)(2,1)S(1)}, bf16[96,4224]{1,0:T(8,128)(2,1)S(1)}, u32[]{:S(2)}, u32[]{:S(2)}) collective-permute-start(bf16[96,4224]{1,0:T(8,128)(2,1)S(1)} %fusion), channel_id=1, source_target_pairs={{0,8},{8,0},{1,9},{9,1},{2,10},{10,2},{3,11},{11,3},{4,12},{12,4},... | collective-permute-start | bytes 2433032 | tf_op jit(solution)/shard_map/ppermute | solution.py:746
  827.2 8.9 collective-permute-start.80
  849.7 17.6 %collective-permute-done.82 = bf16[128,1536]{1,0:T(8,128)(2,1)} collective-permute-done((bf16[128,1536]{1,0:T(8,128)(2,1)S(1)}, bf16[128,1536]{1,0:T(8,128)(2,1)}, u32[]{:S(2)}, u32[]{:S(2)}) %collective-permute-start.82) | collective-permute-done | bytes 393248 | tf_op jit(solution)/shard_map/ppermute | solution.py:720
  894.5 7.7 collective-permute-start.83
  909.4 17.4 %collective-permute-done.83 = bf16[64,1536]{1,0:T(8,128)(2,1)S(1)} collective-permute-done((bf16[64,1536]{1,0:T(8,128)(2,1)S(1)}, bf16[64,1536]{1,0:T(8,128)(2,1)S(1)}, u32[]{:S(2)}, u32[]{:S(2)}) %collective-permute-start.83) | collective-permute-done | bytes 196640 | tf_op jit(solution)/shard_map/ppermute | solution.py:692
  938.7 7.4 unpack.3
  946.2 7.5 unpack.2
  (673 shorter events, 426.4 us)
Async XLA Ops:
  7.2 126.9 %all-gather.13.cloned.1.call-start = ((), (), s32[]{:S(2)}) async-start(), calls=%async_computation.8 | async-start | bytes 4423680 | tf_op jit(solution)/shard_map/all_gather | solution.py:789
  26.3 184.3 %all-gather.15.cloned.1.call-start = ((), (), s32[]{:S(2)}) async-start(), calls=%async_computation.9 | async-start | bytes 10616832 | tf_op jit(solution)/shard_map/all_gather | solution.py:793
  49.0 205.0 %all-gather.17.cloned.1.call-start = ((), (), s32[]{:S(2)}) async-start(), calls=%async_computation.10 | async-start | bytes 3981312 | tf_op jit(solution)/shard_map/all_gather | solution.py:789
  67.5 255.9 %all-gather.19.cloned.1.call-start = ((), (), s32[]{:S(2)}) async-start(), calls=%async_computation.11 | async-start | bytes 10616832 | tf_op jit(solution)/shard_map/all_gather | solution.py:793
  67.6 27.2 %collective-permute-start = (bf16[32,1536]{1,0:T(8,128)(2,1)S(1)}, bf16[32,1536]{1,0:T(8,128)(2,1)S(1)}, u32[]{:S(2)}, u32[]{:S(2)}) collective-permute-start(bf16[32,1536]{1,0:T(8,128)(2,1)S(1)} %get-tuple-element.223), channel_id=1, source_target_pairs={{0,0},{1,8},{2,16},{3,24},{4,32},{5,40},{6,48},{7,56},{8,1},{9,9},... | collective-permute-start | bytes 294920 | tf_op jit(solution)/shard_map/ppermute | solution.py:684
  73.6 21.3 %collective-permute-start.1 = (bf16[32,1536]{1,0:T(8,128)(2,1)S(1)}, bf16[32,1536]{1,0:T(8,128)(2,1)S(1)}, u32[]{:S(2)}, u32[]{:S(2)}) collective-permute-start(bf16[32,1536]{1,0:T(8,128)(2,1)S(1)} %get-tuple-element.222), channel_id=1, source_target_pairs={{0,16},{1,24},{2,32},{3,40},{4,48},{5,56},{6,0},{7,8},{8,17},{9,25... | collective-permute-start | bytes 294920 | tf_op jit(solution)/shard_map/ppermute | solution.py:684
  73.9 21.0 %collective-permute-start.2 = (bf16[32,1536]{1,0:T(8,128)(2,1)S(1)}, bf16[32,1536]{1,0:T(8,128)(2,1)S(1)}, u32[]{:S(2)}, u32[]{:S(2)}) collective-permute-start(bf16[32,1536]{1,0:T(8,128)(2,1)S(1)} %get-tuple-element.224), channel_id=1, source_target_pairs={{0,32},{1,40},{2,48},{3,56},{4,0},{5,8},{6,16},{7,24},{8,33},{9,41... | collective-permute-start | bytes 294920 | tf_op jit(solution)/shard_map/ppermute | solution.py:684
  89.7 57.0 %collective-permute-start.4 = (s32[1]{0:T(128)}, s32[1]{0:T(128)}, u32[]{:S(2)}, u32[]{:S(2)}) collective-permute-start(s32[1]{0:T(128)} %param.22), channel_id=1, source_target_pairs={{0,0},{1,8},{2,16},{3,24},{4,32},{5,40},{6,48},{7,56},{8,1},{9,9},... | collective-permute-start | bytes 20 | tf_op jit(solution)/shard_map/ppermute | solution.py:798
  119.2 374.4 %reduce-scatter.7.cloned.1.call-start = ((), (), s32[]{:S(2)}) async-start(), calls=%async_computation.5 | async-start | bytes 3981312 | tf_op jit(solution)/shard_map/reduce_scatter | solution.py:889
  165.3 23.6 %collective-permute-start.13 = (bf16[128,1536]{1,0:T(8,128)(2,1)S(1)}, bf16[128,1536]{1,0:T(8,128)(2,1)S(1)}, u32[]{:S(2)}, u32[]{:S(2)}) collective-permute-start(bf16[128,1536]{1,0:T(8,128)(2,1)S(1)} %pad_maximum_fusion.4), channel_id=1, source_target_pairs={{0,16},{16,32},{32,48},{48,0},{1,17},{17,33},{33,49},{49,1},{2,18}... | collective-permute-start | bytes 1179656 | tf_op jit(solution)/shard_map/ppermute | solution.py:712
  166.2 22.7 %collective-permute-start.15 = (bf16[128,1536]{1,0:T(8,128)(2,1)}, bf16[128,1536]{1,0:T(8,128)(2,1)S(1)}, u32[]{:S(2)}, u32[]{:S(2)}) collective-permute-start(bf16[128,1536]{1,0:T(8,128)(2,1)} %pad_maximum_fusion.5), channel_id=1, source_target_pairs={{0,48},{16,0},{32,16},{48,32},{1,49},{17,1},{33,17},{49,33},{2,50}... | collective-permute-start | bytes 1179656 | tf_op jit(solution)/shard_map/ppermute | solution.py:713
  173.0 22.1 %collective-permute-start.17 = (bf16[32,1536]{1,0:T(8,128)(2,1)S(1)}, bf16[32,1536]{1,0:T(8,128)(2,1)}, u32[]{:S(2)}, u32[]{:S(2)}) collective-permute-start(bf16[32,1536]{1,0:T(8,128)(2,1)S(1)} %get-tuple-element.217), channel_id=1, source_target_pairs={{0,16},{1,24},{2,32},{3,40},{4,48},{5,56},{6,0},{7,8},{8,17},{9,25... | collective-permute-start | bytes 294920 | tf_op jit(solution)/shard_map/ppermute | solution.py:684
  181.5 25.2 %collective-permute-start.19 = (bf16[32,1536]{1,0:T(8,128)(2,1)}, bf16[32,1536]{1,0:T(8,128)(2,1)}, u32[]{:S(2)}, u32[]{:S(2)}) collective-permute-start(bf16[32,1536]{1,0:T(8,128)(2,1)} %get-tuple-element.215), channel_id=1, source_target_pairs={{0,48},{1,56},{2,0},{3,8},{4,16},{5,24},{6,32},{7,40},{8,49},{9,57... | collective-permute-start | bytes 294920 | tf_op jit(solution)/shard_map/ppermute | solution.py:684
  356.7 21.1 %collective-permute-start.52 = (bf16[128,1536]{1,0:T(8,128)(2,1)S(1)}, bf16[128,1536]{1,0:T(8,128)(2,1)S(1)}, u32[]{:S(2)}, u32[]{:S(2)}) collective-permute-start(bf16[128,1536]{1,0:T(8,128)(2,1)S(1)} %pad_maximum_fusion.11), channel_id=1, source_target_pairs={{0,48},{16,0},{32,16},{48,32},{1,49},{17,1},{33,17},{49,33},{2,50}... | collective-permute-start | bytes 1179656 | tf_op jit(solution)/shard_map/ppermute | solution.py:713
  453.9 100.9 %reduce-scatter.5.cloned.1.call-start = ((), (), s32[]{:S(2)}) async-start(), calls=%async_computation.4 | async-start | bytes 10616832 | tf_op jit(solution)/shard_map/reduce_scatter | solution.py:889
  454.4 256.6 %reduce-scatter.11.cloned.1.call-start = ((), (), s32[]{:S(2)}) async-start(), calls=%async_computation.7 | async-start | bytes 3981312 | tf_op jit(solution)/shard_map/reduce_scatter | solution.py:889
  556.4 22.5 %collective-permute-start.71 = (bf16[192,4224]{1,0:T(8,128)(2,1)S(1)}, bf16[192,4224]{1,0:T(8,128)(2,1)S(1)}, u32[]{:S(2)}, u32[]{:S(2)}) collective-permute-start(bf16[192,4224]{1,0:T(8,128)(2,1)S(1)} %pad_maximum_fusion), channel_id=1, source_target_pairs={{1,0},{3,2},{5,4},{7,6},{8,9},{10,11},{12,13},{14,15},{17,16},{19,... | collective-permute-start | bytes 4866056 | tf_op jit(solution)/shard_map/ppermute | solution.py:737
  579.3 33.8 %collective-permute-start.72 = (bf16[192,4224]{1,0:T(8,128)(2,1)S(1)}, bf16[192,4224]{1,0:T(8,128)(2,1)S(1)}, u32[]{:S(2)}, u32[]{:S(2)}) collective-permute-start(bf16[192,4224]{1,0:T(8,128)(2,1)S(1)} %add_convert_fusion.3.refs_1_), channel_id=1, source_target_pairs={{0,64},{2,66},{4,68},{6,70},{9,73},{11,75},{13,77},{15,79},{16,80}... | collective-permute-start | bytes 4866056 | tf_op jit(solution)/shard_map/ppermute | solution.py:741
  619.6 30.5 %collective-permute-start.77 = (bf16[64,1536]{1,0:T(8,128)(2,1)}, bf16[64,1536]{1,0:T(8,128)(2,1)}, u32[]{:S(2)}, u32[]{:S(2)}) collective-permute-start(bf16[64,1536]{1,0:T(8,128)(2,1)} %slice.318), channel_id=1, source_target_pairs={{0,16},{16,32},{32,48},{48,0},{1,17},{17,33},{33,49},{49,1},{2,18}... | collective-permute-start | bytes 589832 | tf_op jit(solution)/shard_map/ppermute | solution.py:701
  620.4 29.8 %collective-permute-start.78 = (bf16[64,1536]{1,0:T(8,128)(2,1)}, bf16[64,1536]{1,0:T(8,128)(2,1)}, u32[]{:S(2)}, u32[]{:S(2)}) collective-permute-start(bf16[64,1536]{1,0:T(8,128)(2,1)} %slice.319), channel_id=1, source_target_pairs={{0,48},{16,0},{32,16},{48,32},{1,49},{17,1},{33,17},{49,33},{2,50}... | collective-permute-start | bytes 589832 | tf_op jit(solution)/shard_map/ppermute | solution.py:702
  627.1 36.6 %collective-permute-start.74 = (bf16[96,4224]{1,0:T(8,128)(2,1)}, bf16[96,4224]{1,0:T(8,128)(2,1)}, u32[]{:S(2)}, u32[]{:S(2)}) collective-permute-start(bf16[96,4224]{1,0:T(8,128)(2,1)} %fusion.3), channel_id=1, source_target_pairs={{0,8},{8,0},{1,9},{9,1},{2,10},{10,2},{3,11},{11,3},{4,12},{12,4},... | collective-permute-start | bytes 2433032 | tf_op jit(solution)/shard_map/ppermute | solution.py:746
  680.7 91.4 %reduce-scatter.9.cloned.1.call-start = ((), (), s32[]{:S(2)}) async-start(), calls=%async_computation.6 | async-start | bytes 10616832 | tf_op jit(solution)/shard_map/reduce_scatter | solution.py:889
  681.5 257.2 %all-gather.23.cloned.1.call-start = ((), (), s32[]{:S(2)}) async-start(), calls=%async_computation.13 | async-start | bytes 7299072 | tf_op jit(solution)/shard_map/all_gather | solution.py:912
  711.1 235.1 %all-gather.21.cloned.1.call-start = ((), (), s32[]{:S(2)}) async-start(), calls=%async_computation.12 | async-start | bytes 7299072 | tf_op jit(solution)/shard_map/all_gather | solution.py:916
  773.8 22.5 %collective-permute-start.94 = (bf16[192,4224]{1,0:T(8,128)(2,1)S(1)}, bf16[192,4224]{1,0:T(8,128)(2,1)S(1)}, u32[]{:S(2)}, u32[]{:S(2)}) collective-permute-start(bf16[192,4224]{1,0:T(8,128)(2,1)S(1)} %pad_maximum_fusion.1), channel_id=1, source_target_pairs={{1,0},{3,2},{5,4},{7,6},{8,9},{10,11},{12,13},{14,15},{17,16},{19,... | collective-permute-start | bytes 4866056 | tf_op jit(solution)/shard_map/ppermute | solution.py:737
  798.8 27.3 %collective-permute-start.97 = (bf16[96,4224]{1,0:T(8,128)(2,1)S(1)}, bf16[96,4224]{1,0:T(8,128)(2,1)S(1)}, u32[]{:S(2)}, u32[]{:S(2)}) collective-permute-start(bf16[96,4224]{1,0:T(8,128)(2,1)S(1)} %fusion), channel_id=1, source_target_pairs={{0,8},{8,0},{1,9},{9,1},{2,10},{10,2},{3,11},{11,3},{4,12},{12,4},... | collective-permute-start | bytes 2433032 | tf_op jit(solution)/shard_map/ppermute | solution.py:746
  827.2 21.7 %collective-permute-start.80 = (bf16[128,1536]{1,0:T(8,128)(2,1)S(1)}, bf16[128,1536]{1,0:T(8,128)(2,1)S(1)}, u32[]{:S(2)}, u32[]{:S(2)}) collective-permute-start(bf16[128,1536]{1,0:T(8,128)(2,1)S(1)} %copy-done.96), channel_id=1, source_target_pairs={{0,16},{16,32},{32,48},{48,0},{1,17},{17,33},{33,49},{49,1},{2,18}... | collective-permute-start | bytes 1179656 | tf_op jit(solution)/shard_map/ppermute | solution.py:718
  839.7 27.6 %collective-permute-start.82 = (bf16[128,1536]{1,0:T(8,128)(2,1)S(1)}, bf16[128,1536]{1,0:T(8,128)(2,1)}, u32[]{:S(2)}, u32[]{:S(2)}) collective-permute-start(bf16[128,1536]{1,0:T(8,128)(2,1)S(1)} %copy-done.92), channel_id=1, source_target_pairs={{0,32},{16,48},{32,0},{48,16},{1,33},{17,49},{33,1},{49,17},{2,34}... | collective-permute-start | bytes 1179656 | tf_op jit(solution)/shard_map/ppermute | solution.py:720
  894.5 32.3 %collective-permute-start.83 = (bf16[64,1536]{1,0:T(8,128)(2,1)S(1)}, bf16[64,1536]{1,0:T(8,128)(2,1)S(1)}, u32[]{:S(2)}, u32[]{:S(2)}) collective-permute-start(bf16[64,1536]{1,0:T(8,128)(2,1)S(1)} %bitcast.82), channel_id=1, source_target_pairs={{0,0},{8,1},{16,2},{24,3},{32,4},{40,5},{48,6},{56,7},{1,8},{9,9},... | collective-permute-start | bytes 589832 | tf_op jit(solution)/shard_map/ppermute | solution.py:692
  902.2 26.5 %collective-permute-start.84 = (bf16[64,1536]{1,0:T(8,128)(2,1)S(1)}, bf16[64,1536]{1,0:T(8,128)(2,1)S(1)}, u32[]{:S(2)}, u32[]{:S(2)}) collective-permute-start(bf16[64,1536]{1,0:T(8,128)(2,1)S(1)} %bitcast.81), channel_id=1, source_target_pairs={{16,0},{24,1},{32,2},{40,3},{48,4},{56,5},{0,6},{8,7},{17,8},{25,9... | collective-permute-start | bytes 589832 | tf_op jit(solution)/shard_map/ppermute | solution.py:692
  903.0 29.9 %collective-permute-start.85 = (bf16[64,1536]{1,0:T(8,128)(2,1)S(1)}, bf16[64,1536]{1,0:T(8,128)(2,1)S(1)}, u32[]{:S(2)}, u32[]{:S(2)}) collective-permute-start(bf16[64,1536]{1,0:T(8,128)(2,1)S(1)} %bitcast.80), channel_id=1, source_target_pairs={{32,0},{40,1},{48,2},{56,3},{0,4},{8,5},{16,6},{24,7},{33,8},{41,9... | collective-permute-start | bytes 589832 | tf_op jit(solution)/shard_map/ppermute | solution.py:692
  907.9 29.0 %collective-permute-start.86 = (bf16[64,1536]{1,0:T(8,128)(2,1)S(1)}, bf16[64,1536]{1,0:T(8,128)(2,1)S(1)}, u32[]{:S(2)}, u32[]{:S(2)}) collective-permute-start(bf16[64,1536]{1,0:T(8,128)(2,1)S(1)} %bitcast.79), channel_id=1, source_target_pairs={{48,0},{56,1},{0,2},{8,3},{16,4},{24,5},{32,6},{40,7},{49,8},{57,9... | collective-permute-start | bytes 589832 | tf_op jit(solution)/shard_map/ppermute | solution.py:692
  (216 other events, 2221.3 us)
Sparse Core Ops, SparseCore 0:
  26.4 38.7 all-gather.12
  67.5 58.3 all-gather.14
  128.1 29.4 all-gather.16
  159.8 58.2 all-gather.18
  454.0 39.6 reduce-scatter.6
  496.1 58.6 reduce-scatter.4
  680.9 30.1 reduce-scatter.10
  713.5 58.6 reduce-scatter.8
  774.4 42.2 all-gather.22
  827.3 59.3 all-gather.20

commit v8 on v7

--- a/solution.py
+++ b/solution.py
@@ -776,7 +776,7 @@
     def shared(block):
         return jnp.where(home, block, lax.ppermute(block, AXES, SHARE))
 
-    def attention_weights(base, extra):
+    def attention_weights(base, extra, after):
         w_out = weights[base + 4]
         block = lax.dynamic_slice(w_out, (0, 384 * x), (192, 384))
         block = lax.ppermute(block, AXES, TURN)
@@ -784,7 +784,7 @@
             lax.dynamic_slice(w, (0, x * (w.shape[1] // 4)), (192, w.shape[1] // 4))
             for w in weights[base + 1 : base + 4]
         ]
-        parts = shared(jnp.concatenate(parts + extra, axis=1))
+        parts = shared(tie(jnp.concatenate(parts + extra, axis=1), *after))
         piece = jnp.concatenate([parts[:, :768], block, parts[:, 768:]], axis=1)
         return lax.all_gather(piece, SPREAD, axis=0, tiled=False)
 
@@ -792,21 +792,21 @@
         piece = shared(pack_feed_call(member, *weights[base + 6 : base + 9], after=after))
         return lax.all_gather(piece, SPREAD, axis=0, tiled=False)
 
-    attn_one = attention_weights(0, [gains])
+    attn_one = attention_weights(0, [gains], ())
     gains = attn_one[:, :, 1152:1156].transpose(2, 0, 1).reshape(4, width).astype(F32)
 
     length = lax.ppermute(lengths, AXES, TURN)
     rows = to_lines(tokens[0], z)
     pieces = ring_gather(rows)
     state = rows.astype(F32)
-    feed_one = feed_weights(0, ())
-    attn_two = attention_weights(9, [])
-    feed_two = feed_weights(9, (rows,))
+    feed_one = feed_weights(0, (rows,))
+    attn_two = attention_weights(9, [], pieces[3:])
+    feed_two = feed_weights(9, pieces[3:])
     packed = ((attn_one, feed_one), (attn_two, feed_two))
 
     here = (2 * z + yhi) * stretch + jnp.arange(stretch, dtype=jnp.int32)
     valid = (here < lengths[0])[:, None]
-    grad_rows = to_lines(jnp.where(valid, grad_output[0], 0).astype(BF16), z)
+    grad_rows = to_lines(tie(jnp.where(valid, grad_output[0], 0).astype(BF16), *pieces[3:]), z)
     grad_pieces = ring_gather(grad_rows)
     grad = grad_rows.astype(F32)
 
@@ -891,30 +891,28 @@
         )[0]
 
     grad, feed_grad = feed_back(1, grad, grad_pieces, ())
-    low = grad.astype(BF16)
+    low = tie(grad.astype(BF16), feed_grad)
     second_feed = scatter(feed_grad, low)
-    grad, attn_grad = attention_back(1, grad, ring_gather(low), (feed_grad, last_rows), ())
-    low = grad.astype(BF16)
-    second_attn = scatter(attn_grad, low)
-
-    grad, feed_grad = feed_back(0, grad, ring_gather(low), (attn_grad, second_feed))
+    grad, attn_grad = attention_back(1, grad, ring_gather(low), (last_rows,), ())
+    low = tie(grad.astype(BF16), attn_grad)
+    second_attn = scatter(attn_grad, low, second_feed)
+
+    grad, feed_grad = feed_back(0, grad, ring_gather(low), (second_feed,))
+    low = tie(grad.astype(BF16), feed_grad)
+    first_feed = scatter(feed_grad, low, second_attn)
     second = home_sum(jnp.concatenate([second_feed, second_attn], axis=1))
-    low = grad.astype(BF16)
-    first_feed = scatter(feed_grad, low)
+    grad, attn_grad = attention_back(0, grad, ring_gather(low), (), (second,))
+    first_attn = scatter(attn_grad, first_feed)
     second_piece = home_piece(second, core, yhi)
-    grad, attn_grad = attention_back(
-        0, grad, ring_gather(low), (feed_grad, second), (second_piece,)
-    )
-    first_attn = scatter(attn_grad)
     gain_sums = butterfly(jnp.stack(gain_grads))
-    gain_sums = lax.dynamic_slice_in_dim(gain_sums, (2 * z + yhi) * 192, 192, axis=1)
 
     every = lax.all_gather(tie(second_piece, first_attn), ("x", "core"), axis=0, tiled=False)
     results[10:14], results[15:18] = unpack_call(every.reshape(4, 2, 96, -1))
-    first = home_sum(jnp.concatenate([first_feed, first_attn], axis=1))
-    first_piece = home_piece(first, core, yhi)
+    first = jnp.concatenate([first_feed, first_attn], axis=1)
+    first_piece = home_piece(home_sum(tie(first, gain_sums)), core, yhi)
     every = lax.all_gather(first_piece, ("x", "core"), axis=0, tiled=False)
     results[1:5], results[6:9] = unpack_call(every.reshape(4, 2, 96, -1))
+    gain_sums = lax.dynamic_slice_in_dim(gain_sums, (2 * z + yhi) * 192, 192, axis=1)
 
     both = jnp.stack([last_rows, grad.astype(BF16)]).reshape(2, 4, 32, width)
     both = both.transpose(1, 0, 2, 3).reshape(2 * stretch, width)

time: 972 us -> 859 us (0.88)
  waiting for transfers between devices: 451 us -> 300 us
  starting transfers between devices: 246 us -> 277 us
    reduce_scatter x4, waiting for transfers between devices: 191 us -> 14.7 us  [scatter(): lax.psum_scatter(tie(block, *others), SPREAD, scatter_dimension=0, tiled=...]
    ppermute x2, starting transfers between devices: 36.3 us -> 59.3 us  [home_piece(): return jnp.where(core == yhi, mine, lax.ppermute(theirs, 'core', SWAP))]
    ppermute x4, waiting for transfers between devices: 35.5 us -> 21.4 us  [ring_scatter_direct(): from_far = lax.ppermute(far, 'x', ACROSS).astype(F32)]
    ppermute x8, waiting for transfers between devices: 38.5 us -> 50.8 us  [ring_gather(): from_left = lax.ppermute(block, 'x', RIGHT)]
    ppermute x8, waiting for transfers between devices: 10.6 us -> 21.1 us  [ring_gather(): far_first = lax.ppermute(from_left[:half], 'x', RIGHT)]
    unnamed x293 -> x289, local copies, waits for them, and re-layouts: 38.6 us -> 42.9 us
  transfers between devices with their start and end apart: 108 -> 108, of which waited for: 59 -> 59; matrix products, arithmetic and copies ran while one was open for 5% -> 7% of each run, Pallas kernels for 11% -> 15%
where the time goes in v8:
time: 859 us; the launch traced here: 848 us
  waiting for transfers between devices  300 us (35%)
  starting transfers between devices  277 us (32%)
  Pallas kernels  146 us (17%)
  local copies, waits for them, and re-layouts  64.9 us (8%)
  other arithmetic  42.2 us (5%)
  between operations  17.4 us (2%)
    ppermute x2, starting transfers between devices, home_piece(): return jnp.where(core == yhi, mine, lax.ppermute(theirs, 'core', SWAP))  59.3 us
    ppermute x8, waiting for transfers between devices, ring_gather(): from_left = lax.ppermute(block, 'x', RIGHT)  50.8 us
    unnamed x289, local copies, waits for them, and re-layouts  42.9 us
    ppermute x4, waiting for transfers between devices, shared(): return jnp.where(home, block, lax.ppermute(block, AXES, SHARE))  39.9 us
    ppermute x8, starting transfers between devices, to_lines(): out.append(lax.ppermute(piece, AXES, LINES[k]))  39.8 us
    ppermute x4, waiting for transfers between devices, from_lines(): lax.ppermute(block[part * k:part * (k + 1)], AXES, inverse(LINES[k]))  36 us
    pallas_call x2, Pallas kernels, feed_backward_call(): pl.pallas_call(later(feed_backward_kernel, len(after)), grid=(4,), in_spe...  27.3 us
    pallas_call x2, Pallas kernels, attend_backward_call(): pl.pallas_call(later(functools.partial(attend_backward_kernel, window), l...  26.9 us
  transfers between devices with their start and end apart: 108, of which 59 were waited for; matrix products, arithmetic and copies ran while one was open for 7% of the time, Pallas kernels for 15%

profile of v8, /device:TPU:1, one launch (start us, length us, event | category | flops | bytes accessed | tf_op | source)
XLA Modules:
  0.0 848.3 jit_solution(3171544934883778245)
XLA Ops:
  34.4 10.0 %collective-permute-start.2 = (bf16[32,1536]{1,0:T(8,128)(2,1)S(1)}, bf16[32,1536]{1,0:T(8,128)(2,1)S(1)}, u32[]{:S(2)}, u32[]{:S(2)}) collective-permute-start(bf16[32,1536]{1,0:T(8,128)(2,1)S(1)} %get-tuple-element.238), channel_id=1, source_target_pairs={{0,32},{1,40},{2,48},{3,56},{4,0},{5,8},{6,16},{7,24},{8,33},{9,41... | collective-permute-start | bytes 294920 | tf_op jit(solution)/shard_map/ppermute | solution.py:684
  55.7 17.2 %collective-permute-done.24 = bf16[192,3072]{1,0:T(8,128)(2,1)S(1)} collective-permute-done((bf16[192,3072]{1,0:T(8,128)(2,1)S(1)}, bf16[192,3072]{1,0:T(8,128)(2,1)S(1)}, u32[]{:S(2)}, u32[]{:S(2)}) %collective-permute-start.24) | collective-permute-done | bytes 1179680 | tf_op jit(solution)/shard_map/ppermute | solution.py:777
  78.6 8.0 collective-permute-done.5.refs_1_
  118.1 16.7 %collective-permute-done.48 = bf16[192,3072]{1,0:T(8,128)(2,1)} collective-permute-done((bf16[192,3072]{1,0:T(8,128)(2,1)S(1)}, bf16[192,3072]{1,0:T(8,128)(2,1)}, u32[]{:S(2)}, u32[]{:S(2)}) %collective-permute-start.48) | collective-permute-done | bytes 1179680 | tf_op jit(solution)/shard_map/ppermute | solution.py:777
  154.0 9.0 %attend.2 = (f32[128,1536]{1,0:T(8,128)S(1)}, f32[128,1536]{1,0:T(8,128)S(1)}, f32[128,1536]{1,0:T(8,128)S(1)}, bf16[128,1536]{1,0:T(8,128)(2,1)S(1)}, bf16[512,...) custom-call(s32[1]{0:T(128)} %collective-permute-done.4.length.refs_2_.refs_1_, bf16[512,384]{1,0:T(8,128)(2,1)S(1)} %copy-done.87, ...), custom_call_target="tpu_custom_call" | custom-call | flops 3000000000 | bytes 6000000 | tf_op jit(solution)/shard_map/attend/pallas_call | solution.py:380
  193.6 9.6 %collective-permute-start.19 = (bf16[32,1536]{1,0:T(8,128)(2,1)}, bf16[32,1536]{1,0:T(8,128)(2,1)}, u32[]{:S(2)}, u32[]{:S(2)}) collective-permute-start(bf16[32,1536]{1,0:T(8,128)(2,1)} %get-tuple-element.229), channel_id=1, source_target_pairs={{0,48},{1,56},{2,0},{3,8},{4,16},{5,24},{6,32},{7,40},{8,49},{9,57... | collective-permute-start | bytes 294920 | tf_op jit(solution)/shard_map/ppermute | solution.py:684
  210.0 7.6 collective-permute-done.20.refs_2_.refs_1_
  227.2 9.3 %feed_forward.2 = (f32[128,1536]{1,0:T(8,128)S(1)}, f32[128,1536]{1,0:T(8,128)S(1)}, f32[128,1536]{1,0:T(8,128)S(1)}, bf16[128,1536]{1,0:T(8,128)(2,1)S(1)}, f32...) custom-call(bf16[128,1536]{1,0:T(8,128)(2,1)S(1)} %constant_dynamic-update-slice_fusion.6.refs_0_.refs_5, ...), custom_call_target="tpu_custom_call" | custom-call | flops 4899999744 | bytes 18000000 | tf_op jit(solution)/shard_map/feed_forward/pallas_call | solution.py:138
  296.0 9.0 %attend.3 = (f32[128,1536]{1,0:T(8,128)S(1)}, f32[128,1536]{1,0:T(8,128)S(1)}, f32[128,1536]{1,0:T(8,128)S(1)}, bf16[128,1536]{1,0:T(8,128)(2,1)S(1)}, bf16[512,...) custom-call(bf16[64,1536]{1,0:T(8,128)(2,1)S(1)} %collective-permute-done.30.refs_0_.refs_3_.refs_8_, ...), custom_call_target="tpu_custom_call" | custom-call | flops 3000000000 | bytes 6000000 | tf_op jit(solution)/shard_map/attend/pallas_call | solution.py:380
  347.3 9.6 %feed_forward.3 = (f32[128,1536]{1,0:T(8,128)S(1)}, f32[128,1536]{1,0:T(8,128)S(1)}, f32[128,1536]{1,0:T(8,128)S(1)}, bf16[128,1536]{1,0:T(8,128)(2,1)S(1)}, f32...) custom-call(bf16[128,1536]{1,0:T(8,128)(2,1)S(1)} %multiply_convert_fusion.refs_0_, ...), custom_call_target="tpu_custom_call" | custom-call | flops 4899999744 | bytes 18000000 | tf_op jit(solution)/shard_map/feed_forward/pallas_call | solution.py:138
  362.6 13.5 %feed_backward.2 = (f32[128,1536]{1,0:T(8,128)S(1)}, bf16[128,1536]{1,0:T(8,128)(2,1)}, bf16[128,1536]{1,0:T(8,128)(2,1)}, bf16[128,1536]{1,0:T(8,128)(2,1)S(1)}...) custom-call(bf16[128,1536]{1,0:T(8,128)(2,1)S(1)} %constant_dynamic-update-slice_fusion.6.refs_0_.refs_5_, ...), custom_call_target="tpu_custom_call" | custom-call | flops 4899999744 | bytes 20000000 | tf_op jit(solution)/shard_map/feed_backward/pallas_call | solution.py:191
  379.7 12.4 %feed_weights.2 = bf16[8,192,3072]{2,1,0:T(8,128)(2,1)} custom-call(bf16[128,1536]{1,0:T(8,128)(2,1)S(1)} %multiply_convert_fusion.refs_0_, bf16[128,1536]{1,0:T(8,128)(2,1)S(1)} %copy-done.34, bf16[128,1536]{1,0:T(8,128)(2,1)S(1)} %copy-done.37, bf16[64,1536]{1,0:T(8,128)(2,1)S(1)} %collective-permute-done.46.refs_3_, ...), custom_call_target="tpu_custom_call" | custom-call | flops 4899999744 | bytes 18000000 | tf_op jit(solution)/shard_map/feed_weights/pallas_call | solution.py:244
  423.2 13.8 %attend_backward.2 = (bf16[512,384]{1,0:T(8,128)(2,1)S(1)}, f32[512,384]{1,0:T(8,128)}, bf16[512,384]{1,0:T(8,128)(2,1)S(1)}) custom-call(bf16[128,1536]{1,0:T(8,128)(2,1)S(1)} %get-tuple-element.221.refs_0_, s32[1]{0:T(128)} %collective-permute-done.4.length.refs_2_.refs_1_, bf16[128,1536]{1,0:T(8,128)(2,1)} %copy-done.22, bf16[128,1536]{1,0:T(8,128)(2,1)} %copy-done.38, ...), custom_call_target="tpu_custom_call" | custom-call | flops 6000000000 | bytes 6000000 | tf_op jit(solution)/shard_map/attend_backward/pallas_call | solution.py:455
  437.0 8.8 %collective-permute-start.60 = (bf16[512,384]{1,0:T(8,128)(2,1)S(1)}, bf16[512,384]{1,0:T(8,128)(2,1)S(1)}, u32[]{:S(2)}, u32[]{:S(2)}) collective-permute-start(bf16[512,384]{1,0:T(8,128)(2,1)S(1)} %get-tuple-element.139), channel_id=1, source_target_pairs={{0,8},{8,0},{1,9},{9,1},{2,10},{10,2},{3,11},{11,3},{4,12},{12,4},... | collective-permute-start | bytes 1179656 | tf_op jit(solution)/shard_map/ppermute | solution.py:880
  464.9 7.2 collective-permute-done.62
  481.3 7.9 collective-permute-done.64.refs_2_.refs_6_
  498.7 13.8 %feed_backward.3 = (f32[128,1536]{1,0:T(8,128)S(1)}, bf16[128,1536]{1,0:T(8,128)(2,1)}, bf16[128,1536]{1,0:T(8,128)(2,1)}, bf16[128,1536]{1,0:T(8,128)(2,1)}, bf...) custom-call(bf16[192,3072]{1,0:T(8,128)(2,1)S(1)} %bitcast.53, ...), custom_call_target="tpu_custom_call" | custom-call | flops 4899999744 | bytes 20000000 | tf_op jit(solution)/shard_map/feed_backward/pallas_call | solution.py:191
  517.6 11.6 %feed_weights.3 = bf16[8,192,3072]{2,1,0:T(8,128)(2,1)} custom-call(bf16[128,1536]{1,0:T(8,128)(2,1)S(1)} %copy-done.27, bf16[128,1536]{1,0:T(8,128)(2,1)S(1)} %copy-done.47, bf16[128,1536]{1,0:T(8,128)(2,1)S(1)} %copy-done.49, bf16[64,1536]{1,0:T(8,128)(2,1)S(1)} %copy-done.80, bf16[64,1536]{1,0:T(8,128)(2,1)S(1)} %copy-done.83, ...), custom_call_target="tpu_custom_call" | custom-call | flops 4899999744 | bytes 18000000 | tf_op jit(solution)/shard_map/feed_weights/pallas_call | solution.py:244
  545.1 9.0 %collective-permute-done.72.refs_1_.refs_2_ = bf16[128,1536]{1,0:T(8,128)(2,1)S(1)} collective-permute-done((bf16[128,1536]{1,0:T(8,128)(2,1)S(1)}, bf16[128,1536]{1,0:T(8,128)(2,1)S(1)}, u32[]{:S(2)}, u32[]{:S(2)}) %collective-permute-start.72) | collective-permute-done | bytes 393248 | tf_op jit(solution)/shard_map/ppermute | solution.py:699
  560.8 13.0 %attend_backward.3 = (bf16[512,384]{1,0:T(8,128)(2,1)S(1)}, f32[512,384]{1,0:T(8,128)}, bf16[512,384]{1,0:T(8,128)(2,1)S(1)}) custom-call(s32[1]{0:T(128)} %collective-permute-done.4.length.refs_2_.refs_1_, bf16[128,1536]{1,0:T(8,128)(2,1)S(1)} %get-tuple-element.158.refs_0_.refs_1_, bf16[128,1536]{1,0:T(8,128)(2,1)} %copy-done.42, ...), custom_call_target="tpu_custom_call" | custom-call | flops 6000000000 | bytes 6000000 | tf_op jit(solution)/shard_map/attend_backward/pallas_call | solution.py:455
  585.5 11.3 %reduce-scatter.9.cloned.1.call-done = bf16[1,192,3072]{2,1,0:T(8,128)(2,1)} async-done(((bf16[8,192,3072]{2,1,0:T(8,128)(2,1)}), bf16[1,192,3072]{2,1,0:T(8,128)(2,1)}) %reduce-scatter.9.cloned.1.call-update) | async-done | bytes 1179664 | tf_op jit(solution)/shard_map/reduce_scatter | solution.py:889
  602.5 23.4 %collective-permute-start.97 = (bf16[96,4224]{1,0:T(8,128)(2,1)}, bf16[96,4224]{1,0:T(8,128)(2,1)}, u32[]{:S(2)}, u32[]{:S(2)}) collective-permute-start(bf16[96,4224]{1,0:T(8,128)(2,1)} %fusion), channel_id=1, source_target_pairs={{0,8},{8,0},{1,9},{9,1},{2,10},{10,2},{3,11},{11,3},{4,12},{12,4},... | collective-permute-start | bytes 2433032 | tf_op jit(solution)/shard_map/ppermute | solution.py:746
  643.9 7.1 collective-permute-done.77
  651.2 16.4 %collective-permute-done.79 = bf16[128,1536]{1,0:T(8,128)(2,1)} collective-permute-done((bf16[128,1536]{1,0:T(8,128)(2,1)S(1)}, bf16[128,1536]{1,0:T(8,128)(2,1)}, u32[]{:S(2)}, u32[]{:S(2)}) %collective-permute-start.79) | collective-permute-done | bytes 393248 | tf_op jit(solution)/shard_map/ppermute | solution.py:720
  697.9 18.0 %collective-permute-done.91 = bf16[192,4224]{1,0:T(8,128)(2,1)S(1)} collective-permute-done((bf16[192,4224]{1,0:T(8,128)(2,1)S(1)}, bf16[192,4224]{1,0:T(8,128)(2,1)S(1)}, u32[]{:S(2)}, u32[]{:S(2)}) %collective-permute-start.91) | collective-permute-done | bytes 1622048 | tf_op jit(solution)/shard_map/ppermute | solution.py:737
  718.4 35.9 %collective-permute-start.94 = (bf16[96,4224]{1,0:T(8,128)(2,1)S(1)}, bf16[96,4224]{1,0:T(8,128)(2,1)S(1)}, u32[]{:S(2)}, u32[]{:S(2)}) collective-permute-start(bf16[96,4224]{1,0:T(8,128)(2,1)S(1)} %fusion.3), channel_id=1, source_target_pairs={{0,8},{8,0},{1,9},{9,1},{2,10},{10,2},{3,11},{11,3},{4,12},{12,4},... | collective-permute-start | bytes 2433032 | tf_op jit(solution)/shard_map/ppermute | solution.py:746
  759.7 17.6 %collective-permute-start.81 = (bf16[64,1536]{1,0:T(8,128)(2,1)S(1)}, bf16[64,1536]{1,0:T(8,128)(2,1)S(1)}, u32[]{:S(2)}, u32[]{:S(2)}) collective-permute-start(bf16[64,1536]{1,0:T(8,128)(2,1)S(1)} %bitcast.77), channel_id=1, source_target_pairs={{16,0},{24,1},{32,2},{40,3},{48,4},{56,5},{0,6},{8,7},{17,8},{25,9... | collective-permute-start | bytes 589832 | tf_op jit(solution)/shard_map/ppermute | solution.py:692
  782.7 7.8 collective-permute-done.82
  790.5 26.2 %collective-permute-done.83 = bf16[64,1536]{1,0:T(8,128)(2,1)S(1)} collective-permute-done((bf16[64,1536]{1,0:T(8,128)(2,1)S(1)}, bf16[64,1536]{1,0:T(8,128)(2,1)S(1)}, u32[]{:S(2)}, u32[]{:S(2)}) %collective-permute-start.83) | collective-permute-done | bytes 196640 | tf_op jit(solution)/shard_map/ppermute | solution.py:692
  818.5 7.4 unpack.3
  825.9 7.8 all-gather.21.cloned.1.call-done
  833.7 7.5 unpack.2
  (669 shorter events, 427.4 us)
Async XLA Ops:
  7.2 131.6 %all-gather.13.cloned.1.call-start = ((), (), s32[]{:S(2)}) async-start(), calls=%async_computation.8 | async-start | bytes 4423680 | tf_op jit(solution)/shard_map/all_gather | solution.py:789
  26.3 200.0 %all-gather.15.cloned.1.call-start = ((), (), s32[]{:S(2)}) async-start(), calls=%async_computation.9 | async-start | bytes 10616832 | tf_op jit(solution)/shard_map/all_gather | solution.py:793
  26.5 20.2 %collective-permute-start = (bf16[32,1536]{1,0:T(8,128)(2,1)S(1)}, bf16[32,1536]{1,0:T(8,128)(2,1)S(1)}, u32[]{:S(2)}, u32[]{:S(2)}) collective-permute-start(bf16[32,1536]{1,0:T(8,128)(2,1)S(1)} %get-tuple-element.237), channel_id=1, source_target_pairs={{0,0},{1,8},{2,16},{3,24},{4,32},{5,40},{6,48},{7,56},{8,1},{9,9},... | collective-permute-start | bytes 294920 | tf_op jit(solution)/shard_map/ppermute | solution.py:684
  74.0 200.9 %all-gather.17.cloned.1.call-start = ((), (), s32[]{:S(2)}) async-start(), calls=%async_computation.10 | async-start | bytes 3981312 | tf_op jit(solution)/shard_map/all_gather | solution.py:789
  105.5 236.9 %all-gather.19.cloned.1.call-start = ((), (), s32[]{:S(2)}) async-start(), calls=%async_computation.11 | async-start | bytes 10616832 | tf_op jit(solution)/shard_map/all_gather | solution.py:793
  105.5 43.3 %collective-permute-start.4 = (s32[1]{0:T(128)}, s32[1]{0:T(128)}, u32[]{:S(2)}, u32[]{:S(2)}) collective-permute-start(s32[1]{0:T(128)} %param.22), channel_id=1, source_target_pairs={{0,0},{1,8},{2,16},{3,24},{4,32},{5,40},{6,48},{7,56},{8,1},{9,9},... | collective-permute-start | bytes 20 | tf_op jit(solution)/shard_map/ppermute | solution.py:798
  116.2 18.6 %collective-permute-start.48 = (bf16[192,3072]{1,0:T(8,128)(2,1)S(1)}, bf16[192,3072]{1,0:T(8,128)(2,1)}, u32[]{:S(2)}, u32[]{:S(2)}) collective-permute-start(bf16[192,3072]{1,0:T(8,128)(2,1)S(1)} %pack_feed.3), channel_id=1, source_target_pairs={{0,1},{2,3},{4,5},{6,7},{9,8},{11,10},{13,12},{15,14},{16,17},{18,... | collective-permute-start | bytes 3538952 | tf_op jit(solution)/shard_map/ppermute | solution.py:777
  137.2 341.3 %reduce-scatter.5.cloned.1.call-start = ((), (), s32[]{:S(2)}) async-start(), calls=%async_computation.4 | async-start | bytes 10616832 | tf_op jit(solution)/shard_map/reduce_scatter | solution.py:889
  179.4 23.8 %collective-permute-start.13 = (bf16[128,1536]{1,0:T(8,128)(2,1)}, bf16[128,1536]{1,0:T(8,128)(2,1)}, u32[]{:S(2)}, u32[]{:S(2)}) collective-permute-start(bf16[128,1536]{1,0:T(8,128)(2,1)} %pad_maximum_fusion.4), channel_id=1, source_target_pairs={{0,16},{16,32},{32,48},{48,0},{1,17},{17,33},{33,49},{49,1},{2,18}... | collective-permute-start | bytes 1179656 | tf_op jit(solution)/shard_map/ppermute | solution.py:712
  180.2 23.0 %collective-permute-start.15 = (bf16[128,1536]{1,0:T(8,128)(2,1)}, bf16[128,1536]{1,0:T(8,128)(2,1)S(1)}, u32[]{:S(2)}, u32[]{:S(2)}) collective-permute-start(bf16[128,1536]{1,0:T(8,128)(2,1)} %pad_maximum_fusion.5), channel_id=1, source_target_pairs={{0,48},{16,0},{32,16},{48,32},{1,49},{17,1},{33,17},{49,33},{2,50}... | collective-permute-start | bytes 1179656 | tf_op jit(solution)/shard_map/ppermute | solution.py:713
  190.0 19.1 %collective-permute-start.18 = (bf16[32,1536]{1,0:T(8,128)(2,1)S(1)}, bf16[32,1536]{1,0:T(8,128)(2,1)}, u32[]{:S(2)}, u32[]{:S(2)}) collective-permute-start(bf16[32,1536]{1,0:T(8,128)(2,1)S(1)} %get-tuple-element.230), channel_id=1, source_target_pairs={{0,32},{1,40},{2,48},{3,56},{4,0},{5,8},{6,16},{7,24},{8,33},{9,41... | collective-permute-start | bytes 294920 | tf_op jit(solution)/shard_map/ppermute | solution.py:684
  193.6 27.5 %collective-permute-start.19 = (bf16[32,1536]{1,0:T(8,128)(2,1)}, bf16[32,1536]{1,0:T(8,128)(2,1)}, u32[]{:S(2)}, u32[]{:S(2)}) collective-permute-start(bf16[32,1536]{1,0:T(8,128)(2,1)} %get-tuple-element.229), channel_id=1, source_target_pairs={{0,48},{1,56},{2,0},{3,8},{4,16},{5,24},{6,32},{7,40},{8,49},{9,57... | collective-permute-start | bytes 294920 | tf_op jit(solution)/shard_map/ppermute | solution.py:684
  359.5 34.8 %collective-permute-start.49 = (bf16[64,1536]{1,0:T(8,128)(2,1)}, bf16[64,1536]{1,0:T(8,128)(2,1)}, u32[]{:S(2)}, u32[]{:S(2)}) collective-permute-start(bf16[64,1536]{1,0:T(8,128)(2,1)} %get-tuple-element.223), channel_id=1, source_target_pairs={{0,16},{16,32},{32,48},{48,0},{1,17},{17,33},{33,49},{49,1},{2,18}... | collective-permute-start | bytes 589832 | tf_op jit(solution)/shard_map/ppermute | solution.py:708
  359.5 36.9 %collective-permute-start.51 = (bf16[64,1536]{1,0:T(8,128)(2,1)}, bf16[64,1536]{1,0:T(8,128)(2,1)}, u32[]{:S(2)}, u32[]{:S(2)}) collective-permute-start(bf16[64,1536]{1,0:T(8,128)(2,1)} %get-tuple-element.224), channel_id=1, source_target_pairs={{0,48},{16,0},{32,16},{48,32},{1,49},{17,1},{33,17},{49,33},{2,50}... | collective-permute-start | bytes 589832 | tf_op jit(solution)/shard_map/ppermute | solution.py:709
  377.0 22.9 %collective-permute-start.53 = (bf16[128,1536]{1,0:T(8,128)(2,1)}, bf16[128,1536]{1,0:T(8,128)(2,1)}, u32[]{:S(2)}, u32[]{:S(2)}) collective-permute-start(bf16[128,1536]{1,0:T(8,128)(2,1)} %get-tuple-element.129), channel_id=1, source_target_pairs={{0,16},{16,32},{32,48},{48,0},{1,17},{17,33},{33,49},{49,1},{2,18}... | collective-permute-start | bytes 1179656 | tf_op jit(solution)/shard_map/ppermute | solution.py:718
  377.0 22.9 %collective-permute-start.54 = (bf16[128,1536]{1,0:T(8,128)(2,1)}, bf16[128,1536]{1,0:T(8,128)(2,1)}, u32[]{:S(2)}, u32[]{:S(2)}) collective-permute-start(bf16[128,1536]{1,0:T(8,128)(2,1)} %get-tuple-element.130), channel_id=1, source_target_pairs={{0,48},{16,0},{32,16},{48,32},{1,49},{17,1},{33,17},{49,33},{2,50}... | collective-permute-start | bytes 1179656 | tf_op jit(solution)/shard_map/ppermute | solution.py:719
  379.7 20.2 %collective-permute-start.55 = (bf16[128,1536]{1,0:T(8,128)(2,1)S(1)}, bf16[128,1536]{1,0:T(8,128)(2,1)}, u32[]{:S(2)}, u32[]{:S(2)}) collective-permute-start(bf16[128,1536]{1,0:T(8,128)(2,1)S(1)} %get-tuple-element.131), channel_id=1, source_target_pairs={{0,32},{16,48},{32,0},{48,16},{1,33},{17,49},{33,1},{49,17},{2,34}... | collective-permute-start | bytes 1179656 | tf_op jit(solution)/shard_map/ppermute | solution.py:720
  405.5 130.6 %reduce-scatter.7.cloned.1.call-start = ((), (), s32[]{:S(2)}) async-start(), calls=%async_computation.5 | async-start | bytes 3981312 | tf_op jit(solution)/shard_map/reduce_scatter | solution.py:889
  452.2 19.9 %collective-permute-start.62 = (bf16[128,1536]{1,0:T(8,128)(2,1)}, bf16[128,1536]{1,0:T(8,128)(2,1)}, u32[]{:S(2)}, u32[]{:S(2)}) collective-permute-start(bf16[128,1536]{1,0:T(8,128)(2,1)} %get-tuple-element.142), channel_id=1, source_target_pairs={{0,48},{16,0},{32,16},{48,32},{1,49},{17,1},{33,17},{49,33},{2,50}... | collective-permute-start | bytes 1179656 | tf_op jit(solution)/shard_map/ppermute | solution.py:719
  455.4 18.8 %collective-permute-start.63 = (bf16[128,1536]{1,0:T(8,128)(2,1)}, bf16[128,1536]{1,0:T(8,128)(2,1)}, u32[]{:S(2)}, u32[]{:S(2)}) collective-permute-start(bf16[128,1536]{1,0:T(8,128)(2,1)} %get-tuple-element.143), channel_id=1, source_target_pairs={{0,32},{16,48},{32,0},{48,16},{1,33},{17,49},{33,1},{49,17},{2,34}... | collective-permute-start | bytes 1179656 | tf_op jit(solution)/shard_map/ppermute | solution.py:720
  478.5 118.2 %reduce-scatter.9.cloned.1.call-start = ((), (), s32[]{:S(2)}) async-start(), calls=%async_computation.6 | async-start | bytes 10616832 | tf_op jit(solution)/shard_map/reduce_scatter | solution.py:889
  536.0 98.1 %reduce-scatter.11.cloned.1.call-start = ((), (), s32[]{:S(2)}) async-start(), calls=%async_computation.7 | async-start | bytes 3981312 | tf_op jit(solution)/shard_map/reduce_scatter | solution.py:889
  537.3 38.5 %collective-permute-start.71 = (bf16[192,4224]{1,0:T(8,128)(2,1)S(1)}, bf16[192,4224]{1,0:T(8,128)(2,1)S(1)}, u32[]{:S(2)}, u32[]{:S(2)}) collective-permute-start(bf16[192,4224]{1,0:T(8,128)(2,1)S(1)} %pad_maximum_fusion), channel_id=1, source_target_pairs={{1,0},{3,2},{5,4},{7,6},{8,9},{10,11},{12,13},{14,15},{17,16},{19,... | collective-permute-start | bytes 4866056 | tf_op jit(solution)/shard_map/ppermute | solution.py:737
  596.8 221.7 %all-gather.23.cloned.1.call-start = ((), (), s32[]{:S(2)}) async-start(), calls=%async_computation.13 | async-start | bytes 7299072 | tf_op jit(solution)/shard_map/all_gather | solution.py:909
  602.5 25.7 %collective-permute-start.97 = (bf16[96,4224]{1,0:T(8,128)(2,1)}, bf16[96,4224]{1,0:T(8,128)(2,1)}, u32[]{:S(2)}, u32[]{:S(2)}) collective-permute-start(bf16[96,4224]{1,0:T(8,128)(2,1)} %fusion), channel_id=1, source_target_pairs={{0,8},{8,0},{1,9},{9,1},{2,10},{10,2},{3,11},{11,3},{4,12},{12,4},... | collective-permute-start | bytes 2433032 | tf_op jit(solution)/shard_map/ppermute | solution.py:746
  634.2 199.6 %all-gather.21.cloned.1.call-start = ((), (), s32[]{:S(2)}) async-start(), calls=%async_computation.12 | async-start | bytes 7299072 | tf_op jit(solution)/shard_map/all_gather | solution.py:913
  641.7 25.9 %collective-permute-start.79 = (bf16[128,1536]{1,0:T(8,128)(2,1)S(1)}, bf16[128,1536]{1,0:T(8,128)(2,1)}, u32[]{:S(2)}, u32[]{:S(2)}) collective-permute-start(bf16[128,1536]{1,0:T(8,128)(2,1)S(1)} %get-tuple-element.166), channel_id=1, source_target_pairs={{0,32},{16,48},{32,0},{48,16},{1,33},{17,49},{33,1},{49,17},{2,34}... | collective-permute-start | bytes 1179656 | tf_op jit(solution)/shard_map/ppermute | solution.py:720
  695.6 20.4 %collective-permute-start.91 = (bf16[192,4224]{1,0:T(8,128)(2,1)S(1)}, bf16[192,4224]{1,0:T(8,128)(2,1)S(1)}, u32[]{:S(2)}, u32[]{:S(2)}) collective-permute-start(bf16[192,4224]{1,0:T(8,128)(2,1)S(1)} %pad_maximum_fusion.1), channel_id=1, source_target_pairs={{1,0},{3,2},{5,4},{7,6},{8,9},{10,11},{12,13},{14,15},{17,16},{19,... | collective-permute-start | bytes 4866056 | tf_op jit(solution)/shard_map/ppermute | solution.py:737
  718.4 37.8 %collective-permute-start.94 = (bf16[96,4224]{1,0:T(8,128)(2,1)S(1)}, bf16[96,4224]{1,0:T(8,128)(2,1)S(1)}, u32[]{:S(2)}, u32[]{:S(2)}) collective-permute-start(bf16[96,4224]{1,0:T(8,128)(2,1)S(1)} %fusion.3), channel_id=1, source_target_pairs={{0,8},{8,0},{1,9},{9,1},{2,10},{10,2},{3,11},{11,3},{4,12},{12,4},... | collective-permute-start | bytes 2433032 | tf_op jit(solution)/shard_map/ppermute | solution.py:746
  757.8 22.8 %collective-permute-start.80 = (bf16[64,1536]{1,0:T(8,128)(2,1)S(1)}, bf16[64,1536]{1,0:T(8,128)(2,1)S(1)}, u32[]{:S(2)}, u32[]{:S(2)}) collective-permute-start(bf16[64,1536]{1,0:T(8,128)(2,1)S(1)} %bitcast.78), channel_id=1, source_target_pairs={{0,0},{8,1},{16,2},{24,3},{32,4},{40,5},{48,6},{56,7},{1,8},{9,9},... | collective-permute-start | bytes 589832 | tf_op jit(solution)/shard_map/ppermute | solution.py:692
  759.7 22.9 %collective-permute-start.81 = (bf16[64,1536]{1,0:T(8,128)(2,1)S(1)}, bf16[64,1536]{1,0:T(8,128)(2,1)S(1)}, u32[]{:S(2)}, u32[]{:S(2)}) collective-permute-start(bf16[64,1536]{1,0:T(8,128)(2,1)S(1)} %bitcast.77), channel_id=1, source_target_pairs={{16,0},{24,1},{32,2},{40,3},{48,4},{56,5},{0,6},{8,7},{17,8},{25,9... | collective-permute-start | bytes 589832 | tf_op jit(solution)/shard_map/ppermute | solution.py:692
  777.3 39.4 %collective-permute-start.83 = (bf16[64,1536]{1,0:T(8,128)(2,1)S(1)}, bf16[64,1536]{1,0:T(8,128)(2,1)S(1)}, u32[]{:S(2)}, u32[]{:S(2)}) collective-permute-start(bf16[64,1536]{1,0:T(8,128)(2,1)S(1)} %bitcast.75), channel_id=1, source_target_pairs={{48,0},{56,1},{0,2},{8,3},{16,4},{24,5},{32,6},{40,7},{49,8},{57,9... | collective-permute-start | bytes 589832 | tf_op jit(solution)/shard_map/ppermute | solution.py:692
  (214 other events, 2049.1 us)
Sparse Core Ops, SparseCore 0:
  26.4 40.6 all-gather.12
  74.2 57.1 all-gather.14
  133.6 35.3 all-gather.16
  171.1 58.2 all-gather.18
  405.6 66.1 reduce-scatter.4
  478.6 34.2 reduce-scatter.6
  536.2 60.5 reduce-scatter.8
  599.3 34.7 reduce-scatter.10
  636.4 52.8 all-gather.22
  757.4 76.2 all-gather.20

commit v9 on v8

--- a/solution.py
+++ b/solution.py
@@ -682,7 +682,7 @@
     for k in range(4):
         piece = lax.dynamic_slice_in_dim(block, ((z + k) % 4) * part, part, axis=0)
         out.append(lax.ppermute(piece, AXES, LINES[k]))
-    return jnp.concatenate(out, axis=0)
+    return out
 
 
 def from_lines(block, z):
@@ -692,6 +692,16 @@
         piece = lax.ppermute(block[part * k : part * (k + 1)], AXES, inverse(LINES[k]))
         out = lax.dynamic_update_slice_in_dim(out, piece, ((z + k) % 4) * part, axis=0)
     return out
+
+
+def interleave(first, second):
+    parts = [item[32 * k : 32 * (k + 1)] for k in range(4) for item in (first, second)]
+    return jnp.concatenate(parts, axis=0)
+
+
+def separate(block):
+    parts = [block[32 * k : 32 * (k + 1)] for k in range(8)]
+    return jnp.concatenate(parts[::2], axis=0), jnp.concatenate(parts[1::2], axis=0)
 
 
 def ring_gather(block):
@@ -773,40 +783,36 @@
     gains = jnp.stack([weights[0], weights[5], weights[9], weights[14]]).T
     gains = jnp.pad(gains, ((0, 0), (0, 124)))
 
-    def shared(block):
-        return jnp.where(home, block, lax.ppermute(block, AXES, SHARE))
-
-    def attention_weights(base, extra, after):
-        w_out = weights[base + 4]
-        block = lax.dynamic_slice(w_out, (0, 384 * x), (192, 384))
+    def weight_parts(base, extra, after, joined):
+        block = lax.dynamic_slice(tie(weights[base + 4], *after), (0, 384 * x), (192, 384))
         block = lax.ppermute(block, AXES, TURN)
         parts = [
             lax.dynamic_slice(w, (0, x * (w.shape[1] // 4)), (192, w.shape[1] // 4))
             for w in weights[base + 1 : base + 4]
         ]
-        parts = shared(tie(jnp.concatenate(parts + extra, axis=1), *after))
-        piece = jnp.concatenate([parts[:, :768], block, parts[:, 768:]], axis=1)
-        return lax.all_gather(piece, SPREAD, axis=0, tiled=False)
-
-    def feed_weights(base, after):
-        piece = shared(pack_feed_call(member, *weights[base + 6 : base + 9], after=after))
-        return lax.all_gather(piece, SPREAD, axis=0, tiled=False)
-
-    attn_one = attention_weights(0, [gains], ())
+        parts += [pack_feed_call(member, *weights[base + 6 : base + 9], after=after)]
+        parts = jnp.concatenate(parts + extra, axis=1)
+        came = tie(lax.ppermute(parts, AXES, SHARE), *joined)
+        parts = jnp.where(home, parts, came)
+        attn = jnp.concatenate([parts[:, :768], block, parts[:, 3840:]], axis=1)
+        return attn, parts[:, 768:3840]
+
+    def line_weights(piece, *after):
+        return lax.all_gather(tie(piece, *after), SPREAD, axis=0, tiled=False)
+
+    here = (2 * z + yhi) * stretch + jnp.arange(stretch, dtype=jnp.int32)
+    valid = (here < lengths[0])[:, None]
+    grad_start = jnp.where(valid, grad_output[0], 0).astype(BF16)
+    length = lax.ppermute(lengths, AXES, TURN)
+    moved = to_lines(interleave(tokens[0], grad_start), z)
+    rows, grad_rows = separate(jnp.concatenate(moved, axis=0))
+
+    attn_one, feed_one = weight_parts(0, [gains], (), moved)
+    attn_one = line_weights(attn_one)
     gains = attn_one[:, :, 1152:1156].transpose(2, 0, 1).reshape(4, width).astype(F32)
-
-    length = lax.ppermute(lengths, AXES, TURN)
-    rows = to_lines(tokens[0], z)
     pieces = ring_gather(rows)
     state = rows.astype(F32)
-    feed_one = feed_weights(0, (rows,))
-    attn_two = attention_weights(9, [], pieces[3:])
-    feed_two = feed_weights(9, pieces[3:])
-    packed = ((attn_one, feed_one), (attn_two, feed_two))
-
-    here = (2 * z + yhi) * stretch + jnp.arange(stretch, dtype=jnp.int32)
-    valid = (here < lengths[0])[:, None]
-    grad_rows = to_lines(tie(jnp.where(valid, grad_output[0], 0).astype(BF16), *pieces[3:]), z)
+    feed_one = line_weights(feed_one, *pieces[3:])
     grad_pieces = ring_gather(grad_rows)
     grad = grad_rows.astype(F32)
 
@@ -834,13 +840,17 @@
 
     records = []
     for index, window in enumerate((WINDOW, 8 * stretch)):
-        attn, feed = packed[index]
+        if index == 0:
+            attn, feed = attn_one, feed_one
+        else:
+            attn, feed = attn_two, feed_two
         gain_attn, gain_feed = gains[2 * index], gains[2 * index + 1]
         if index == 0:
             queries, own, flat = project_call(True, pieces, gain_attn, attn, cosine, sine)
             flats = (flat,)
         else:
             flats = ring_gather(rms_norm(state, gain_attn).astype(BF16))
+            feed_two = feed = line_weights(feed_two, *flats[3:])
             queries, own = project_call(False, flats, gain_attn, attn, cosine, sine)
         other = lax.ppermute(own, "core", SWAP)
         line = (queries, own, other, places, key_places)
@@ -848,13 +858,17 @@
         *partial, mixed, log_total = attend_call(window, length, *line, attn, after=after)
         saved_attn = (state, flats, line, mixed, log_total)
         state = state + ring_scatter(*partial)
+        if index == 0:
+            attn_two, feed_two = weight_parts(9, [], (mixed,), ())
         flats = ring_gather(rms_norm(state, gain_feed).astype(BF16))
-        after = () if index else (grad_rows,)
-        *partial, gate, up, hidden = feed_forward_call(flats, feed, after=after)
+        if index == 0:
+            attn_two = line_weights(attn_two, *flats[3:])
+        *partial, gate, up, hidden = feed_forward_call(flats, feed)
         saved_feed = (state, flats, gate, up, hidden)
         state = state + ring_scatter(*partial)
         records.append((saved_attn, saved_feed, window))
     last_rows = state.astype(BF16)
+    packed = ((attn_one, feed_one), (attn_two, feed_two))
 
     results = [None] * 18
     gain_grads = [None] * 4
@@ -902,23 +916,21 @@
     first_feed = scatter(feed_grad, low, second_attn)
     second = home_sum(jnp.concatenate([second_feed, second_attn], axis=1))
     grad, attn_grad = attention_back(0, grad, ring_gather(low), (), (second,))
-    first_attn = scatter(attn_grad, first_feed)
+    low = grad.astype(BF16)
+    first_attn = scatter(attn_grad, first_feed, low)
     second_piece = home_piece(second, core, yhi)
     gain_sums = butterfly(jnp.stack(gain_grads))
+    back = from_lines(interleave(last_rows, low), z)
+    output, input_grad = separate(back)
+    output, input_grad = output[None], input_grad.astype(F32)[None]
 
     every = lax.all_gather(tie(second_piece, first_attn), ("x", "core"), axis=0, tiled=False)
     results[10:14], results[15:18] = unpack_call(every.reshape(4, 2, 96, -1))
     first = jnp.concatenate([first_feed, first_attn], axis=1)
-    first_piece = home_piece(home_sum(tie(first, gain_sums)), core, yhi)
+    first_piece = home_piece(home_sum(tie(first, gain_sums, back)), core, yhi)
     every = lax.all_gather(first_piece, ("x", "core"), axis=0, tiled=False)
     results[1:5], results[6:9] = unpack_call(every.reshape(4, 2, 96, -1))
     gain_sums = lax.dynamic_slice_in_dim(gain_sums, (2 * z + yhi) * 192, 192, axis=1)
-
-    both = jnp.stack([last_rows, grad.astype(BF16)]).reshape(2, 4, 32, width)
-    both = both.transpose(1, 0, 2, 3).reshape(2 * stretch, width)
-    both = from_lines(both, z).reshape(4, 2, 32, width).transpose(1, 0, 2, 3)
-    both = both.reshape(2, stretch, width)
-    output, input_grad = both[:1], both[1:].astype(F32)
     for index, slot in enumerate((0, 5, 9, 14)):
         results[slot] = gain_sums[index]
     return (output, input_grad, *results)

time: 859 us -> 757 us (0.88)
  waiting for transfers between devices: 300 us -> 230 us
  starting transfers between devices: 277 us -> 248 us
    all_gather x1, waiting for transfers between devices: 7.8 us -> 54.6 us  [body(): every = lax.all_gather(first_piece, ('x', 'core'), axis=0, tiled=False)]
    ppermute x6 -> x4, waiting for transfers between devices: 45.4 us -> 7.23 us  [the longest x2 7.22 us: weight_parts(): came = tie(lax.ppermute(parts, AXES, SHARE), *joined)]
    ppermute x4, waiting for transfers between devices: 36 us -> 9.41 us  [from_lines(): lax.ppermute(block[part * k:part * (k + 1)], AXES, inverse(LINES[k]))]
    ppermute x8 -> x4, starting transfers between devices: 39.8 us -> 17.6 us  [to_lines(): out.append(lax.ppermute(piece, AXES, LINES[k]))]
    reduce_scatter x4, waiting for transfers between devices: 14.7 us -> 0.03 us  [scatter(): lax.psum_scatter(tie(block, *others), SPREAD, scatter_dimension=0, tiled=...]
    ppermute x4, waiting for transfers between devices: 21.4 us -> 7.01 us  [ring_scatter_direct(): from_far = lax.ppermute(far, 'x', ACROSS).astype(F32)]
    ppermute x2, starting transfers between devices: 59.3 us -> 45.3 us  [home_piece(): return jnp.where(core == yhi, mine, lax.ppermute(theirs, 'core', SWAP))]
    ppermute x7, waiting for transfers between devices: 19.2 us -> 5.96 us  [butterfly(): values = values + lax.ppermute(values, axis, pairs)]
  transfers between devices with their start and end apart: 108 -> 102, of which waited for: 59 -> 45; matrix products, arithmetic and copies ran while one was open for 7% -> 8% of each run, Pallas kernels for 15% -> 17%
where the time goes in v9:
time: 757 us; the launch traced here: 748 us
  starting transfers between devices  248 us (33%)
  waiting for transfers between devices  230 us (30%)
  Pallas kernels  144 us (19%)
  local copies, waits for them, and re-layouts  68.8 us (9%)
  other arithmetic  39.3 us (5%)
  between operations  18 us (2%)
    all_gather x1, waiting for transfers between devices, body(): every = lax.all_gather(first_piece, ('x', 'core'), axis=0, tiled=False)  54.6 us
    ppermute x2, starting transfers between devices, home_piece(): return jnp.where(core == yhi, mine, lax.ppermute(theirs, 'core', SWAP))  45.3 us
    unnamed x328, local copies, waits for them, and re-layouts  45.2 us
    ppermute x8, waiting for transfers between devices, ring_gather(): from_left = lax.ppermute(block, 'x', RIGHT)  41.8 us
    pallas_call x2, Pallas kernels, feed_backward_call(): pl.pallas_call(later(feed_backward_kernel, len(after)), grid=(4,), in_spe...  27.3 us
    pallas_call x2, Pallas kernels, attend_backward_call(): pl.pallas_call(later(functools.partial(attend_backward_kernel, window), l...  26.3 us
    ppermute x8, starting transfers between devices, ring_gather(): from_right = lax.ppermute(block, 'x', LEFT)  23.3 us
    pallas_call x2, Pallas kernels, feed_weights_call(): pl.pallas_call(feed_weights_kernel, grid=(12,), in_specs=PIECES + PIECES...  23.1 us
  transfers between devices with their start and end apart: 102, of which 45 were waited for; matrix products, arithmetic and copies ran while one was open for 8% of the time, Pallas kernels for 17%

profile of v9, /device:TPU:1, one launch (start us, length us, event | category | flops | bytes accessed | tf_op | source)
XLA Modules:
  0.0 747.8 jit_solution(14116656214522629627)
XLA Ops:
  29.8 7.4 collective-permute-start.2
  63.4 6.6 collective-permute-done.5.refs_1_
  75.9 10.4 %collective-permute-start.4 = (s32[1]{0:T(128)}, s32[1]{0:T(128)}, u32[]{:S(2)}, u32[]{:S(2)}) collective-permute-start(s32[1]{0:T(128)} %param.22), channel_id=1, source_target_pairs={{0,0},{1,8},{2,16},{3,24},{4,32},{5,40},{6,48},{7,56},{8,1},{9,9},... | collective-permute-start | bytes 20 | tf_op jit(solution)/shard_map/ppermute | solution.py:806
  88.9 6.6 all-gather.13.cloned.1.call-done.refs_6_
  106.2 9.2 %attend.2 = (f32[128,1536]{1,0:T(8,128)S(1)}, f32[128,1536]{1,0:T(8,128)S(1)}, f32[128,1536]{1,0:T(8,128)S(1)}, bf16[128,1536]{1,0:T(8,128)(2,1)S(1)}, bf16[512,...) custom-call(s32[1]{0:T(128)} %collective-permute-done.4.length.refs_2_.refs_1_, ...), custom_call_target="tpu_custom_call" | custom-call | flops 3000000000 | bytes 6000000 | tf_op jit(solution)/shard_map/attend/pallas_call | solution.py:380
  141.0 7.1 collective-permute-start.33
  151.7 7.2 collective-permute-done.32
  162.8 9.2 %feed_forward.2 = (f32[128,1536]{1,0:T(8,128)S(1)}, f32[128,1536]{1,0:T(8,128)S(1)}, f32[128,1536]{1,0:T(8,128)S(1)}, bf16[128,1536]{1,0:T(8,128)(2,1)S(1)}, f32...) custom-call(bf16[128,1536]{1,0:T(8,128)(2,1)S(1)} %multiply_convert_fusion.2.refs_0_, ...), custom_call_target="tpu_custom_call" | custom-call | flops 4899999744 | bytes 18000000 | tf_op jit(solution)/shard_map/feed_forward/pallas_call | solution.py:138
  182.8 6.8 collective-permute-done.21
  228.0 9.1 %attend.3 = (f32[128,1536]{1,0:T(8,128)S(1)}, f32[128,1536]{1,0:T(8,128)S(1)}, f32[128,1536]{1,0:T(8,128)S(1)}, bf16[128,1536]{1,0:T(8,128)(2,1)S(1)}, bf16[512,...) custom-call(bf16[64,1536]{1,0:T(8,128)(2,1)S(1)} %collective-permute-done.25.refs_0_.refs_3_.refs_8_, ...), custom_call_target="tpu_custom_call" | custom-call | flops 3000000000 | bytes 6000000 | tf_op jit(solution)/shard_map/attend/pallas_call | solution.py:380
  276.1 9.2 %feed_forward.3 = (f32[128,1536]{1,0:T(8,128)S(1)}, f32[128,1536]{1,0:T(8,128)S(1)}, f32[128,1536]{1,0:T(8,128)S(1)}, bf16[128,1536]{1,0:T(8,128)(2,1)S(1)}, f32...) custom-call(bf16[128,1536]{1,0:T(8,128)(2,1)S(1)} %multiply_convert_fusion.refs_0_, ...), custom_call_target="tpu_custom_call" | custom-call | flops 4899999744 | bytes 18000000 | tf_op jit(solution)/shard_map/feed_forward/pallas_call | solution.py:138
  290.8 13.7 %feed_backward.2 = (f32[128,1536]{1,0:T(8,128)S(1)}, bf16[128,1536]{1,0:T(8,128)(2,1)}, bf16[128,1536]{1,0:T(8,128)(2,1)}, bf16[128,1536]{1,0:T(8,128)(2,1)}, bf...) custom-call(bf16[128,1536]{1,0:T(8,128)(2,1)S(1)} %pad_maximum_fusion.9.refs_0_.refs_5_, ...), custom_call_target="tpu_custom_call" | custom-call | flops 4899999744 | bytes 20000000 | tf_op jit(solution)/shard_map/feed_backward/pallas_call | solution.py:191
  308.1 11.6 %feed_weights.2 = bf16[8,192,3072]{2,1,0:T(8,128)(2,1)} custom-call(bf16[128,1536]{1,0:T(8,128)(2,1)S(1)} %multiply_convert_fusion.refs_0_, bf16[128,1536]{1,0:T(8,128)(2,1)S(1)} %copy-done.45, bf16[128,1536]{1,0:T(8,128)(2,1)S(1)} %copy-done.48, bf16[64,1536]{1,0:T(8,128)(2,1)S(1)} %copy-done.85, bf16[64,1536]{1,0:T(8,128)(2,1)S(1)} %copy-done.88, ...), custom_call_target="tpu_custom_call" | custom-call | flops 4899999744 | bytes 18000000 | tf_op jit(solution)/shard_map/feed_weights/pallas_call | solution.py:244
  336.2 7.6 %collective-permute-done.50.refs_3_.refs_6_ = bf16[128,1536]{1,0:T(8,128)(2,1)S(1)} collective-permute-done((bf16[128,1536]{1,0:T(8,128)(2,1)S(1)}, bf16[128,1536]{1,0:T(8,128)(2,1)S(1)}, u32[]{:S(2)}, u32[]{:S(2)}) %collective-permute-start.50) | collective-permute-done | bytes 393248 | tf_op jit(solution)/shard_map/ppermute | solution.py:709
  350.9 13.3 %attend_backward.2 = (bf16[512,384]{1,0:T(8,128)(2,1)S(1)}, f32[512,384]{1,0:T(8,128)}, bf16[512,384]{1,0:T(8,128)(2,1)S(1)}) custom-call(bf16[128,1536]{1,0:T(8,128)(2,1)S(1)} %get-tuple-element.231.refs_0_, s32[1]{0:T(128)} %collective-permute-done.4.length.refs_2_.refs_1_, bf16[128,1536]{1,0:T(8,128)(2,1)} %copy-done.33, bf16[128,1536]{1,0:T(8,128)(2,1)} %copy-done.53, ...), custom_call_target="tpu_custom_call" | custom-call | flops 6000000000 | bytes 6000000 | tf_op jit(solution)/shard_map/attend_backward/pallas_call | solution.py:455
  364.2 12.1 %collective-permute-start.54 = (bf16[512,384]{1,0:T(8,128)(2,1)S(1)}, bf16[512,384]{1,0:T(8,128)(2,1)S(1)}, u32[]{:S(2)}, u32[]{:S(2)}) collective-permute-start(bf16[512,384]{1,0:T(8,128)(2,1)S(1)} %get-tuple-element.146), channel_id=1, source_target_pairs={{0,8},{8,0},{1,9},{9,1},{2,10},{10,2},{3,11},{11,3},{4,12},{12,4},... | collective-permute-start | bytes 1179656 | tf_op jit(solution)/shard_map/ppermute | solution.py:894
  394.4 7.2 collective-permute-done.56
  410.5 7.9 %collective-permute-done.58.refs_2_.refs_6_ = bf16[128,1536]{1,0:T(8,128)(2,1)S(1)} collective-permute-done((bf16[128,1536]{1,0:T(8,128)(2,1)S(1)}, bf16[128,1536]{1,0:T(8,128)(2,1)S(1)}, u32[]{:S(2)}, u32[]{:S(2)}) %collective-permute-start.58) | collective-permute-done | bytes 393248 | tf_op jit(solution)/shard_map/ppermute | solution.py:709
  428.0 13.6 %feed_backward.3 = (f32[128,1536]{1,0:T(8,128)S(1)}, bf16[128,1536]{1,0:T(8,128)(2,1)}, bf16[128,1536]{1,0:T(8,128)(2,1)}, bf16[128,1536]{1,0:T(8,128)(2,1)S(1)}...) custom-call(bf16[192,3072]{1,0:T(8,128)(2,1)S(1)} %bitcast.49, ...), custom_call_target="tpu_custom_call" | custom-call | flops 4899999744 | bytes 20000000 | tf_op jit(solution)/shard_map/feed_backward/pallas_call | solution.py:191
  445.7 11.5 %feed_weights.3 = bf16[8,192,3072]{2,1,0:T(8,128)(2,1)} custom-call(bf16[128,1536]{1,0:T(8,128)(2,1)S(1)} %copy-done.20, bf16[128,1536]{1,0:T(8,128)(2,1)S(1)} %copy-done.38, bf16[128,1536]{1,0:T(8,128)(2,1)S(1)} %copy-done.40, bf16[64,1536]{1,0:T(8,128)(2,1)S(1)} %collective-permute-done.18.refs_3_, bf16[64,1536]{1,0:T(8,128)(2,1)S(1)} %copy-done.78, ...), custom_call_target="tpu_custom_call" | custom-call | flops 4899999744 | bytes 18000000 | tf_op jit(solution)/shard_map/feed_weights/pallas_call | solution.py:244
  464.7 7.6 %collective-permute-start.65 = (bf16[192,4224]{1,0:T(8,128)(2,1)S(1)}, bf16[192,4224]{1,0:T(8,128)(2,1)S(1)}, u32[]{:S(2)}, u32[]{:S(2)}) collective-permute-start(bf16[192,4224]{1,0:T(8,128)(2,1)S(1)} %pad_maximum_fusion), channel_id=1, source_target_pairs={{1,0},{3,2},{5,4},{7,6},{8,9},{10,11},{12,13},{14,15},{17,16},{19,... | collective-permute-start | bytes 4866056 | tf_op jit(solution)/shard_map/ppermute | solution.py:747
  475.1 7.9 %collective-permute-done.66.refs_1_.refs_2_ = bf16[128,1536]{1,0:T(8,128)(2,1)S(1)} collective-permute-done((bf16[128,1536]{1,0:T(8,128)(2,1)S(1)}, bf16[128,1536]{1,0:T(8,128)(2,1)S(1)}, u32[]{:S(2)}, u32[]{:S(2)}) %collective-permute-start.66) | collective-permute-done | bytes 393248 | tf_op jit(solution)/shard_map/ppermute | solution.py:709
  490.3 13.0 %attend_backward.3 = (bf16[512,384]{1,0:T(8,128)(2,1)S(1)}, f32[512,384]{1,0:T(8,128)}, bf16[512,384]{1,0:T(8,128)(2,1)S(1)}) custom-call(s32[1]{0:T(128)} %collective-permute-done.4.length.refs_2_.refs_1_, bf16[128,1536]{1,0:T(8,128)(2,1)S(1)} %get-tuple-element.165.refs_0_.refs_1_, bf16[128,1536]{1,0:T(8,128)(2,1)} %copy-done.49, ...), custom_call_target="tpu_custom_call" | custom-call | flops 6000000000 | bytes 6000000 | tf_op jit(solution)/shard_map/attend_backward/pallas_call | solution.py:455
  546.0 20.4 %collective-permute-start.91 = (bf16[96,4224]{1,0:T(8,128)(2,1)S(1)}, bf16[96,4224]{1,0:T(8,128)(2,1)S(1)}, u32[]{:S(2)}, u32[]{:S(2)}) collective-permute-start(bf16[96,4224]{1,0:T(8,128)(2,1)S(1)} %fusion), channel_id=1, source_target_pairs={{0,8},{8,0},{1,9},{9,1},{2,10},{10,2},{3,11},{11,3},{4,12},{12,4},... | collective-permute-start | bytes 2433032 | tf_op jit(solution)/shard_map/ppermute | solution.py:756
  566.6 7.1 collective-permute-start.80
  587.4 8.8 %collective-permute-start.74 = (bf16[64,1536]{1,0:T(8,128)(2,1)S(1)}, bf16[64,1536]{1,0:T(8,128)(2,1)S(1)}, u32[]{:S(2)}, u32[]{:S(2)}) collective-permute-start(bf16[64,1536]{1,0:T(8,128)(2,1)S(1)} %pad_maximum_fusion.14), channel_id=1, source_target_pairs={{0,0},{8,1},{16,2},{24,3},{32,4},{40,5},{48,6},{56,7},{1,8},{9,9},... | collective-permute-start | bytes 589832 | tf_op jit(solution)/shard_map/ppermute | solution.py:692
  604.1 9.4 %collective-permute-done.75 = bf16[64,1536]{1,0:T(8,128)(2,1)S(1)} collective-permute-done((bf16[64,1536]{1,0:T(8,128)(2,1)S(1)}, bf16[64,1536]{1,0:T(8,128)(2,1)S(1)}, u32[]{:S(2)}, u32[]{:S(2)}) %collective-permute-start.75) | collective-permute-done | bytes 196640 | tf_op jit(solution)/shard_map/ppermute | solution.py:692
  616.1 22.0 %collective-permute-done.85 = bf16[192,4224]{1,0:T(8,128)(2,1)S(1)} collective-permute-done((bf16[192,4224]{1,0:T(8,128)(2,1)S(1)}, bf16[192,4224]{1,0:T(8,128)(2,1)S(1)}, u32[]{:S(2)}, u32[]{:S(2)}) %collective-permute-start.85) | collective-permute-done | bytes 1622048 | tf_op jit(solution)/shard_map/ppermute | solution.py:747
  640.6 24.9 %collective-permute-start.88 = (bf16[96,4224]{1,0:T(8,128)(2,1)S(1)}, bf16[96,4224]{1,0:T(8,128)(2,1)S(1)}, u32[]{:S(2)}, u32[]{:S(2)}) collective-permute-start(bf16[96,4224]{1,0:T(8,128)(2,1)S(1)} %fusion.3), channel_id=1, source_target_pairs={{0,8},{8,0},{1,9},{9,1},{2,10},{10,2},{3,11},{11,3},{4,12},{12,4},... | collective-permute-start | bytes 2433032 | tf_op jit(solution)/shard_map/ppermute | solution.py:756
  671.0 7.4 unpack.3
  678.4 54.6 %all-gather.21.cloned.1.call-done = bf16[768,4224]{1,0:T(8,128)(2,1)} async-done(((bf16[96,4224]{1,0:T(8,128)(2,1)}), bf16[768,4224]{1,0:T(8,128)(2,1)}) %all-gather.21.cloned.1.call-update) | async-done | bytes 6488080 | tf_op jit(solution)/shard_map/all_gather | solution.py:931
  733.0 7.5 unpack.2
  (707 shorter events, 351.7 us)
Async XLA Ops:
  7.2 88.3 %all-gather.13.cloned.1.call-start = ((), (), s32[]{:S(2)}) async-start(), calls=%async_computation.8 | async-start | bytes 4423680 | tf_op jit(solution)/shard_map/all_gather | solution.py:801
  16.2 34.7 %collective-permute-start.9 = (bf16[192,3968]{1,0:T(8,128)(2,1)S(1)}, bf16[192,3968]{1,0:T(8,128)(2,1)}, u32[]{:S(2)}, u32[]{:S(2)}) collective-permute-start(bf16[192,3968]{1,0:T(8,128)(2,1)S(1)} %concatenate.112), channel_id=1, source_target_pairs={{0,1},{2,3},{4,5},{6,7},{9,8},{11,10},{13,12},{15,14},{16,17},{18,... | collective-permute-start | bytes 4571144 | tf_op jit(solution)/shard_map/ppermute | solution.py:795
  27.7 18.9 %collective-permute-start.1 = (bf16[64,1536]{1,0:T(8,128)(2,1)S(1)}, bf16[64,1536]{1,0:T(8,128)(2,1)S(1)}, u32[]{:S(2)}, u32[]{:S(2)}) collective-permute-start(bf16[64,1536]{1,0:T(8,128)(2,1)S(1)} %get-tuple-element.235), channel_id=1, source_target_pairs={{0,16},{1,24},{2,32},{3,40},{4,48},{5,56},{6,0},{7,8},{8,17},{9,25... | collective-permute-start | bytes 589832 | tf_op jit(solution)/shard_map/ppermute | solution.py:684
  29.8 20.8 %collective-permute-start.2 = (bf16[64,1536]{1,0:T(8,128)(2,1)S(1)}, bf16[64,1536]{1,0:T(8,128)(2,1)S(1)}, u32[]{:S(2)}, u32[]{:S(2)}) collective-permute-start(bf16[64,1536]{1,0:T(8,128)(2,1)S(1)} %get-tuple-element.234), channel_id=1, source_target_pairs={{0,32},{1,40},{2,48},{3,56},{4,0},{5,8},{6,16},{7,24},{8,33},{9,41... | collective-permute-start | bytes 589832 | tf_op jit(solution)/shard_map/ppermute | solution.py:684
  54.4 108.3 %all-gather.15.cloned.1.call-start = ((), (), s32[]{:S(2)}) async-start(), calls=%async_computation.9 | async-start | bytes 10616832 | tf_op jit(solution)/shard_map/all_gather | solution.py:801
  75.9 134.9 %all-gather.17.cloned.1.call-start = ((), (), s32[]{:S(2)}) async-start(), calls=%async_computation.10 | async-start | bytes 3981312 | tf_op jit(solution)/shard_map/all_gather | solution.py:801
  75.9 29.1 %collective-permute-start.4 = (s32[1]{0:T(128)}, s32[1]{0:T(128)}, u32[]{:S(2)}, u32[]{:S(2)}) collective-permute-start(s32[1]{0:T(128)} %param.22), channel_id=1, source_target_pairs={{0,0},{1,8},{2,16},{3,24},{4,32},{5,40},{6,48},{7,56},{8,1},{9,9},... | collective-permute-start | bytes 20 | tf_op jit(solution)/shard_map/ppermute | solution.py:806
  131.6 27.3 %collective-permute-start.32 = (bf16[192,3840]{1,0:T(8,128)(2,1)}, bf16[192,3840]{1,0:T(8,128)(2,1)}, u32[]{:S(2)}, u32[]{:S(2)}) collective-permute-start(bf16[192,3840]{1,0:T(8,128)(2,1)} %concatenate.121), channel_id=1, source_target_pairs={{0,1},{2,3},{4,5},{6,7},{9,8},{11,10},{13,12},{15,14},{16,17},{18,... | collective-permute-start | bytes 4423688 | tf_op jit(solution)/shard_map/ppermute | solution.py:795
  141.0 20.6 %collective-permute-start.33 = (bf16[192,384]{1,0:T(8,128)(2,1)S(1)}, bf16[192,384]{1,0:T(8,128)(2,1)S(1)}, u32[]{:S(2)}, u32[]{:S(2)}) collective-permute-start(bf16[192,384]{1,0:T(8,128)(2,1)S(1)} %constant_dynamic-slice_fusion.1), channel_id=1, source_target_pairs={{0,0},{1,8},{2,16},{3,24},{4,32},{5,40},{6,48},{7,56},{8,1},{9,9},... | collective-permute-start | bytes 442376 | tf_op jit(solution)/shard_map/ppermute | solution.py:788
  162.4 109.8 %all-gather.19.cloned.1.call-start = ((), (), s32[]{:S(2)}) async-start(), calls=%async_computation.11 | async-start | bytes 10616832 | tf_op jit(solution)/shard_map/all_gather | solution.py:801
  207.6 200.1 %reduce-scatter.5.cloned.1.call-start = ((), (), s32[]{:S(2)}) async-start(), calls=%async_computation.4 | async-start | bytes 10616832 | tf_op jit(solution)/shard_map/reduce_scatter | solution.py:903
  287.9 33.9 %collective-permute-start.43 = (bf16[64,1536]{1,0:T(8,128)(2,1)}, bf16[64,1536]{1,0:T(8,128)(2,1)}, u32[]{:S(2)}, u32[]{:S(2)}) collective-permute-start(bf16[64,1536]{1,0:T(8,128)(2,1)} %get-tuple-element.244), channel_id=1, source_target_pairs={{0,16},{16,32},{32,48},{48,0},{1,17},{17,33},{33,49},{49,1},{2,18}... | collective-permute-start | bytes 589832 | tf_op jit(solution)/shard_map/ppermute | solution.py:718
  288.4 35.6 %collective-permute-start.45 = (bf16[64,1536]{1,0:T(8,128)(2,1)}, bf16[64,1536]{1,0:T(8,128)(2,1)}, u32[]{:S(2)}, u32[]{:S(2)}) collective-permute-start(bf16[64,1536]{1,0:T(8,128)(2,1)} %get-tuple-element.245), channel_id=1, source_target_pairs={{0,48},{16,0},{32,16},{48,32},{1,49},{17,1},{33,17},{49,33},{2,50}... | collective-permute-start | bytes 589832 | tf_op jit(solution)/shard_map/ppermute | solution.py:719
  305.4 21.8 %collective-permute-start.47 = (bf16[128,1536]{1,0:T(8,128)(2,1)}, bf16[128,1536]{1,0:T(8,128)(2,1)}, u32[]{:S(2)}, u32[]{:S(2)}) collective-permute-start(bf16[128,1536]{1,0:T(8,128)(2,1)} %get-tuple-element.136), channel_id=1, source_target_pairs={{0,16},{16,32},{32,48},{48,0},{1,17},{17,33},{33,49},{49,1},{2,18}... | collective-permute-start | bytes 1179656 | tf_op jit(solution)/shard_map/ppermute | solution.py:728
  305.4 21.8 %collective-permute-start.48 = (bf16[128,1536]{1,0:T(8,128)(2,1)}, bf16[128,1536]{1,0:T(8,128)(2,1)}, u32[]{:S(2)}, u32[]{:S(2)}) collective-permute-start(bf16[128,1536]{1,0:T(8,128)(2,1)} %get-tuple-element.137), channel_id=1, source_target_pairs={{0,48},{16,0},{32,16},{48,32},{1,49},{17,1},{33,17},{49,33},{2,50}... | collective-permute-start | bytes 1179656 | tf_op jit(solution)/shard_map/ppermute | solution.py:729
  308.0 19.1 %collective-permute-start.49 = (bf16[128,1536]{1,0:T(8,128)(2,1)}, bf16[128,1536]{1,0:T(8,128)(2,1)}, u32[]{:S(2)}, u32[]{:S(2)}) collective-permute-start(bf16[128,1536]{1,0:T(8,128)(2,1)} %get-tuple-element.138), channel_id=1, source_target_pairs={{0,32},{16,48},{32,0},{48,16},{1,33},{17,49},{33,1},{49,17},{2,34}... | collective-permute-start | bytes 1179656 | tf_op jit(solution)/shard_map/ppermute | solution.py:730
  332.8 130.7 %reduce-scatter.7.cloned.1.call-start = ((), (), s32[]{:S(2)}) async-start(), calls=%async_computation.5 | async-start | bytes 3981312 | tf_op jit(solution)/shard_map/reduce_scatter | solution.py:903
  381.6 20.1 %collective-permute-start.56 = (bf16[128,1536]{1,0:T(8,128)(2,1)}, bf16[128,1536]{1,0:T(8,128)(2,1)}, u32[]{:S(2)}, u32[]{:S(2)}) collective-permute-start(bf16[128,1536]{1,0:T(8,128)(2,1)} %get-tuple-element.149), channel_id=1, source_target_pairs={{0,48},{16,0},{32,16},{48,32},{1,49},{17,1},{33,17},{49,33},{2,50}... | collective-permute-start | bytes 1179656 | tf_op jit(solution)/shard_map/ppermute | solution.py:729
  384.9 18.8 %collective-permute-start.57 = (bf16[128,1536]{1,0:T(8,128)(2,1)S(1)}, bf16[128,1536]{1,0:T(8,128)(2,1)}, u32[]{:S(2)}, u32[]{:S(2)}) collective-permute-start(bf16[128,1536]{1,0:T(8,128)(2,1)S(1)} %get-tuple-element.150), channel_id=1, source_target_pairs={{0,32},{16,48},{32,0},{48,16},{1,33},{17,49},{33,1},{49,17},{2,34}... | collective-permute-start | bytes 1179656 | tf_op jit(solution)/shard_map/ppermute | solution.py:730
  407.7 128.6 %reduce-scatter.9.cloned.1.call-start = ((), (), s32[]{:S(2)}) async-start(), calls=%async_computation.6 | async-start | bytes 10616832 | tf_op jit(solution)/shard_map/reduce_scatter | solution.py:903
  463.5 111.2 %reduce-scatter.11.cloned.1.call-start = ((), (), s32[]{:S(2)}) async-start(), calls=%async_computation.7 | async-start | bytes 3981312 | tf_op jit(solution)/shard_map/reduce_scatter | solution.py:903
  464.7 38.6 %collective-permute-start.65 = (bf16[192,4224]{1,0:T(8,128)(2,1)S(1)}, bf16[192,4224]{1,0:T(8,128)(2,1)S(1)}, u32[]{:S(2)}, u32[]{:S(2)}) collective-permute-start(bf16[192,4224]{1,0:T(8,128)(2,1)S(1)} %pad_maximum_fusion), channel_id=1, source_target_pairs={{1,0},{3,2},{5,4},{7,6},{8,9},{10,11},{12,13},{14,15},{17,16},{19,... | collective-permute-start | bytes 4866056 | tf_op jit(solution)/shard_map/ppermute | solution.py:747
  511.3 21.0 %collective-permute-start.72 = (bf16[128,1536]{1,0:T(8,128)(2,1)}, bf16[128,1536]{1,0:T(8,128)(2,1)}, u32[]{:S(2)}, u32[]{:S(2)}) collective-permute-start(bf16[128,1536]{1,0:T(8,128)(2,1)} %get-tuple-element.172), channel_id=1, source_target_pairs={{0,48},{16,0},{32,16},{48,32},{1,49},{17,1},{33,17},{49,33},{2,50}... | collective-permute-start | bytes 1179656 | tf_op jit(solution)/shard_map/ppermute | solution.py:729
  514.7 19.5 %collective-permute-start.73 = (bf16[128,1536]{1,0:T(8,128)(2,1)}, bf16[128,1536]{1,0:T(8,128)(2,1)}, u32[]{:S(2)}, u32[]{:S(2)}) collective-permute-start(bf16[128,1536]{1,0:T(8,128)(2,1)} %get-tuple-element.173), channel_id=1, source_target_pairs={{0,32},{16,48},{32,0},{48,16},{1,33},{17,49},{33,1},{49,17},{2,34}... | collective-permute-start | bytes 1179656 | tf_op jit(solution)/shard_map/ppermute | solution.py:730
  536.4 134.6 %all-gather.23.cloned.1.call-start = ((), (), s32[]{:S(2)}) async-start(), calls=%async_computation.13 | async-start | bytes 7299072 | tf_op jit(solution)/shard_map/all_gather | solution.py:927
  544.9 21.6 %collective-permute-start.79 = (f32[4,1536]{1,0:T(4,128)S(1)}, f32[4,1536]{1,0:T(4,128)S(1)}, u32[]{:S(2)}, u32[]{:S(2)}) collective-permute-start(f32[4,1536]{1,0:T(4,128)S(1)} %fusion.27), channel_id=1, source_target_pairs={{0,16},{16,0},{32,48},{48,32},{1,17},{17,1},{33,49},{49,33},{2,18}... | collective-permute-start | bytes 73736 | tf_op jit(solution)/shard_map/ppermute | solution.py:764
  546.0 27.6 %collective-permute-start.91 = (bf16[96,4224]{1,0:T(8,128)(2,1)S(1)}, bf16[96,4224]{1,0:T(8,128)(2,1)S(1)}, u32[]{:S(2)}, u32[]{:S(2)}) collective-permute-start(bf16[96,4224]{1,0:T(8,128)(2,1)S(1)} %fusion), channel_id=1, source_target_pairs={{0,8},{8,0},{1,9},{9,1},{2,10},{10,2},{3,11},{11,3},{4,12},{12,4},... | collective-permute-start | bytes 2433032 | tf_op jit(solution)/shard_map/ppermute | solution.py:756
  574.8 158.2 %all-gather.21.cloned.1.call-start = ((), (), s32[]{:S(2)}) async-start(), calls=%async_computation.12 | async-start | bytes 7299072 | tf_op jit(solution)/shard_map/all_gather | solution.py:931
  575.7 37.9 %collective-permute-start.77 = (bf16[64,1536]{1,0:T(8,128)(2,1)S(1)}, bf16[64,1536]{1,0:T(8,128)(2,1)S(1)}, u32[]{:S(2)}, u32[]{:S(2)}) collective-permute-start(bf16[64,1536]{1,0:T(8,128)(2,1)S(1)} %pad_maximum_fusion.17), channel_id=1, source_target_pairs={{48,0},{56,1},{0,2},{8,3},{16,4},{24,5},{32,6},{40,7},{49,8},{57,9... | collective-permute-start | bytes 589832 | tf_op jit(solution)/shard_map/ppermute | solution.py:692
  583.9 29.7 %collective-permute-start.76 = (bf16[64,1536]{1,0:T(8,128)(2,1)S(1)}, bf16[64,1536]{1,0:T(8,128)(2,1)S(1)}, u32[]{:S(2)}, u32[]{:S(2)}) collective-permute-start(bf16[64,1536]{1,0:T(8,128)(2,1)S(1)} %pad_maximum_fusion.16), channel_id=1, source_target_pairs={{32,0},{40,1},{48,2},{56,3},{0,4},{8,5},{16,6},{24,7},{33,8},{41,9... | collective-permute-start | bytes 589832 | tf_op jit(solution)/shard_map/ppermute | solution.py:692
  613.8 24.4 %collective-permute-start.85 = (bf16[192,4224]{1,0:T(8,128)(2,1)S(1)}, bf16[192,4224]{1,0:T(8,128)(2,1)S(1)}, u32[]{:S(2)}, u32[]{:S(2)}) collective-permute-start(bf16[192,4224]{1,0:T(8,128)(2,1)S(1)} %pad_maximum_fusion.1), channel_id=1, source_target_pairs={{1,0},{3,2},{5,4},{7,6},{8,9},{10,11},{12,13},{14,15},{17,16},{19,... | collective-permute-start | bytes 4866056 | tf_op jit(solution)/shard_map/ppermute | solution.py:747
  640.6 26.8 %collective-permute-start.88 = (bf16[96,4224]{1,0:T(8,128)(2,1)S(1)}, bf16[96,4224]{1,0:T(8,128)(2,1)S(1)}, u32[]{:S(2)}, u32[]{:S(2)}) collective-permute-start(bf16[96,4224]{1,0:T(8,128)(2,1)S(1)} %fusion.3), channel_id=1, source_target_pairs={{0,8},{8,0},{1,9},{9,1},{2,10},{10,2},{3,11},{11,3},{4,12},{12,4},... | collective-permute-start | bytes 2433032 | tf_op jit(solution)/shard_map/ppermute | solution.py:756
  (227 other events, 2560.4 us)
Sparse Core Ops, SparseCore 0:
  54.6 40.8 all-gather.12
  97.7 54.1 all-gather.14
  162.6 30.2 all-gather.16
  207.7 62.8 all-gather.18
  332.9 72.6 reduce-scatter.4
  407.9 35.9 reduce-scatter.6
  463.6 62.0 reduce-scatter.8
  536.6 35.6 reduce-scatter.10
  574.9 69.0 all-gather.22
  668.7 64.3 all-gather.20

commit v10 on v9

--- a/solution.py
+++ b/solution.py
@@ -577,7 +577,7 @@
     out = pl.pallas_call(
         unpack_kernel,
         grid=(2,),
-        in_specs=[pl.BlockSpec((4, 1, 96, 4224), lambda b: (0, b, 0, 0))],
+        in_specs=[pl.BlockSpec((4, 1, 96, every.shape[-1]), lambda b: (0, b, 0, 0))],
         out_specs=[pl.BlockSpec((96, width), lambda b: (b, 0)) for width in widths]
         + [whole((4, 128, 1536))],
         out_shape=[jax.ShapeDtypeStruct((192, width), F32) for width in widths]
@@ -662,18 +662,12 @@
     return core == yhi
 
 
-def not_home(*place):
-    return not at_home(*place)
-
-
 LINES = [
     permutation(lambda l, x, c, z, h, k=k: (l, (z + k) % 4, h, x, c)) for k in range(4)
 ]
 TURN = permutation(lambda l, x, c, z, h: (l, z, h, x, c))
 SHARE = permutation(lambda l, x, c, z, h: (l, x, c, z, 1 - h), at_home)
-COLLECT = permutation(lambda l, x, c, z, h: (l, x, c, z, 1 - h), not_home)
-BESIDE = permutation(lambda l, x, c, z, h: (1 - l, x, c, z, h), at_home)
-CROSS = permutation(lambda l, x, c, z, h: (l, z, c, x, h), at_home)
+CROSS = permutation(lambda l, x, c, z, h: (l, z, c, x, h))
 
 
 def to_lines(block, z):
@@ -743,27 +737,29 @@
     return (mine.astype(F32) + came.astype(F32)).astype(BF16)
 
 
-def home_sum(rows):
-    return add_low(rows, lax.ppermute(rows, AXES, COLLECT))
-
-
-def home_piece(rows, core, yhi):
-    rows = add_low(rows, lax.ppermute(rows, AXES, BESIDE))
-    moved = lax.ppermute(rows[:, 3840:], AXES, CROSS)
-    rows = jnp.concatenate([rows[:, :3840], moved], axis=1)
+def yhi_sum(rows, core, yhi):
+    mine = lax.dynamic_slice_in_dim(rows, 96 * core, 96, axis=0)
     theirs = lax.dynamic_slice_in_dim(rows, 96 * (1 - core), 96, axis=0)
-    mine = lax.dynamic_slice_in_dim(rows, 96 * core, 96, axis=0)
-    return jnp.where(core == yhi, mine, lax.ppermute(theirs, "core", SWAP))
-
-
-def butterfly(values):
-    for axis, size in (("core", 2), ("x", 4), ("z", 4), ("yhi", 2), ("ylo", 2)):
-        step = 1
-        while step < size:
-            pairs = [(i, i ^ step) for i in range(size)]
-            values = values + lax.ppermute(values, axis, pairs)
-            step *= 2
-    return values
+    came = lax.ppermute(theirs, "core", SWAP)
+    home = core == yhi
+    kept = jnp.where(home, mine, came)
+    away = jnp.where(home, came, mine)
+    return add_low(kept, lax.ppermute(away, "yhi", SWAP))
+
+
+def ylo_sum(piece):
+    return add_low(piece, lax.ppermute(piece, "ylo", SWAP))
+
+
+def cross(piece, start):
+    first, last = start + 768, start + 1152
+    moved = lax.ppermute(piece[:, first:last], AXES, CROSS)
+    return jnp.concatenate([piece[:, :first], moved, piece[:, last:]], axis=1)
+
+
+def gain_rows(grads):
+    tall = grads.astype(BF16).T.reshape(8, 192, 4)
+    return jnp.pad(tall, ((0, 0), (0, 0), (0, 124)))
 
 
 def norm_back(grad, own_normed, state, gain):
@@ -783,19 +779,22 @@
     gains = jnp.stack([weights[0], weights[5], weights[9], weights[14]]).T
     gains = jnp.pad(gains, ((0, 0), (0, 124)))
 
-    def weight_parts(base, extra, after, joined):
+    def shared(block, *joined):
+        return jnp.where(home, block, tie(lax.ppermute(block, AXES, SHARE), *joined))
+
+    def attention_part(base, extra, after):
         block = lax.dynamic_slice(tie(weights[base + 4], *after), (0, 384 * x), (192, 384))
         block = lax.ppermute(block, AXES, TURN)
         parts = [
             lax.dynamic_slice(w, (0, x * (w.shape[1] // 4)), (192, w.shape[1] // 4))
             for w in weights[base + 1 : base + 4]
         ]
-        parts += [pack_feed_call(member, *weights[base + 6 : base + 9], after=after)]
-        parts = jnp.concatenate(parts + extra, axis=1)
-        came = tie(lax.ppermute(parts, AXES, SHARE), *joined)
-        parts = jnp.where(home, parts, came)
-        attn = jnp.concatenate([parts[:, :768], block, parts[:, 3840:]], axis=1)
-        return attn, parts[:, 768:3840]
+        parts = shared(jnp.concatenate(parts + extra, axis=1))
+        return jnp.concatenate([parts[:, :768], block, parts[:, 768:]], axis=1)
+
+    def feed_part(base, after, joined):
+        part = pack_feed_call(member, *weights[base + 6 : base + 9], after=after)
+        return shared(part, *joined)
 
     def line_weights(piece, *after):
         return lax.all_gather(tie(piece, *after), SPREAD, axis=0, tiled=False)
@@ -807,8 +806,8 @@
     moved = to_lines(interleave(tokens[0], grad_start), z)
     rows, grad_rows = separate(jnp.concatenate(moved, axis=0))
 
-    attn_one, feed_one = weight_parts(0, [gains], (), moved)
-    attn_one = line_weights(attn_one)
+    attn_one = line_weights(attention_part(0, [gains], ()))
+    feed_one = feed_part(0, (), moved)
     gains = attn_one[:, :, 1152:1156].transpose(2, 0, 1).reshape(4, width).astype(F32)
     pieces = ring_gather(rows)
     state = rows.astype(F32)
@@ -859,7 +858,8 @@
         saved_attn = (state, flats, line, mixed, log_total)
         state = state + ring_scatter(*partial)
         if index == 0:
-            attn_two, feed_two = weight_parts(9, [], (mixed,), ())
+            attn_two = attention_part(9, [], (mixed,))
+            feed_two = feed_part(9, (mixed,), ())
         flats = ring_gather(rms_norm(state, gain_feed).astype(BF16))
         if index == 0:
             attn_two = line_weights(attn_two, *flats[3:])
@@ -914,23 +914,25 @@
     grad, feed_grad = feed_back(0, grad, ring_gather(low), (second_feed,))
     low = tie(grad.astype(BF16), feed_grad)
     first_feed = scatter(feed_grad, low, second_attn)
-    second = home_sum(jnp.concatenate([second_feed, second_attn], axis=1))
+    second = yhi_sum(jnp.concatenate([second_feed, second_attn], axis=1), core, yhi)
     grad, attn_grad = attention_back(0, grad, ring_gather(low), (), (second,))
     low = grad.astype(BF16)
+    attn_grad = jnp.concatenate([attn_grad, gain_rows(jnp.stack(gain_grads))], axis=2)
     first_attn = scatter(attn_grad, first_feed, low)
-    second_piece = home_piece(second, core, yhi)
-    gain_sums = butterfly(jnp.stack(gain_grads))
+    second_piece = cross(ylo_sum(second), 3072)
+    feed_piece = ylo_sum(yhi_sum(first_feed, core, yhi))
     back = from_lines(interleave(last_rows, low), z)
     output, input_grad = separate(back)
     output, input_grad = output[None], input_grad.astype(F32)[None]
 
     every = lax.all_gather(tie(second_piece, first_attn), ("x", "core"), axis=0, tiled=False)
     results[10:14], results[15:18] = unpack_call(every.reshape(4, 2, 96, -1))
-    first = jnp.concatenate([first_feed, first_attn], axis=1)
-    first_piece = home_piece(home_sum(tie(first, gain_sums, back)), core, yhi)
+    attn_piece = ylo_sum(yhi_sum(tie(first_attn, feed_piece), core, yhi))
+    first_piece = jnp.concatenate([feed_piece, cross(attn_piece, 0)], axis=1)
     every = lax.all_gather(first_piece, ("x", "core"), axis=0, tiled=False)
-    results[1:5], results[6:9] = unpack_call(every.reshape(4, 2, 96, -1))
-    gain_sums = lax.dynamic_slice_in_dim(gain_sums, (2 * z + yhi) * 192, 192, axis=1)
+    every = every.reshape(4, 2, 96, -1)
+    results[1:5], results[6:9] = unpack_call(every)
+    gain_sums = every[..., 4224:4228].astype(F32).sum(axis=0).reshape(192, 4).T
     for index, slot in enumerate((0, 5, 9, 14)):
         results[slot] = gain_sums[index]
     return (output, input_grad, *results)

time: 757 us -> 801 us (1.058)
  waiting for transfers between devices: 230 us -> 321 us
  starting transfers between devices: 248 us -> 194 us
    reduce_scatter x4, waiting for transfers between devices: 0.03 us -> 80.5 us  [scatter(): lax.psum_scatter(tie(block, *others), SPREAD, scatter_dimension=0, tiled=...]
    ppermute x19 -> x17, starting transfers between devices: 92 us -> 36.2 us  [the longest x2 12.8 us: attention_part(): block = lax.ppermute(block, AXES, TURN)]
    ppermute x19 -> x17, waiting for transfers between devices: 37.2 us -> 71.2 us  [the longest x3 35 us: ylo_sum(): return add_low(piece, lax.ppermute(piece, 'ylo', SWAP))]
    all_gather x1, waiting for transfers between devices: 54.6 us -> 21.1 us  [body(): every = lax.all_gather(first_piece, ('x', 'core'), axis=0, tiled=False)]
    ppermute x4, waiting for transfers between devices: 9.41 us -> 20.9 us  [from_lines(): lax.ppermute(block[part * k:part * (k + 1)], AXES, inverse(LINES[k]))]
    ppermute x8, waiting for transfers between devices: 16.6 us -> 27.5 us  [ring_gather(): far_first = lax.ppermute(from_left[:half], 'x', RIGHT)]
    ppermute x1, starting transfers between devices: 10.4 us -> 1.92 us  [body(): length = lax.ppermute(lengths, AXES, TURN)]
    unnamed x328 -> x322, local copies, waits for them, and re-layouts: 45.2 us -> 48.8 us
  transfers between devices with their start and end apart: 102 -> 100, of which waited for: 45 -> 49; matrix products, arithmetic and copies ran while one was open for 8% -> 6% of each run, Pallas kernels for 17% -> 16%
where the time goes in v10:
time: 801 us; the launch traced here: 791 us
  waiting for transfers between devices  321 us (40%)
  starting transfers between devices  194 us (24%)
  Pallas kernels  145 us (18%)
  local copies, waits for them, and re-layouts  70.6 us (9%)
  other arithmetic  42.6 us (5%)
  between operations  17.6 us (2%)
    reduce_scatter x4, waiting for transfers between devices, scatter(): lax.psum_scatter(tie(block, *others), SPREAD, scatter_dimension=0, tiled=...  80.5 us
    unnamed x322, local copies, waits for them, and re-layouts  48.8 us
    ppermute x8, waiting for transfers between devices, ring_gather(): from_left = lax.ppermute(block, 'x', RIGHT)  37.6 us
    ppermute x3, waiting for transfers between devices, ylo_sum(): return add_low(piece, lax.ppermute(piece, 'ylo', SWAP))  35 us
    ppermute x8, waiting for transfers between devices, ring_gather(): far_first = lax.ppermute(from_left[:half], 'x', RIGHT)  27.5 us
    pallas_call x2, Pallas kernels, feed_backward_call(): pl.pallas_call(later(feed_backward_kernel, len(after)), grid=(4,), in_spe...  27.2 us
    pallas_call x2, Pallas kernels, attend_backward_call(): pl.pallas_call(later(functools.partial(attend_backward_kernel, window), l...  26.3 us
    ppermute x8, starting transfers between devices, ring_gather(): far_second = lax.ppermute(from_right[half:], 'x', LEFT)  25.6 us
  transfers between devices with their start and end apart: 100, of which 49 were waited for; matrix products, arithmetic and copies ran while one was open for 6% of the time, Pallas kernels for 16%

profile of v10, /device:TPU:1, one launch (start us, length us, event | category | flops | bytes accessed | tf_op | source)
XLA Modules:
  0.0 790.9 jit_solution(5744843616033226185)
XLA Ops:
  34.7 10.0 %collective-permute-start.2 = (bf16[64,1536]{1,0:T(8,128)(2,1)S(1)}, bf16[64,1536]{1,0:T(8,128)(2,1)S(1)}, u32[]{:S(2)}, u32[]{:S(2)}) collective-permute-start(bf16[64,1536]{1,0:T(8,128)(2,1)S(1)} %get-tuple-element.234), channel_id=1, source_target_pairs={{0,32},{1,40},{2,48},{3,56},{4,0},{5,8},{6,16},{7,24},{8,33},{9,41... | collective-permute-start | bytes 589832 | tf_op jit(solution)/shard_map/ppermute | solution.py:678
  63.9 8.2 %collective-permute-done.5.refs_1_ = bf16[128,1536]{1,0:T(8,128)(2,1)S(1)} collective-permute-done((bf16[128,1536]{1,0:T(8,128)(2,1)S(1)}, bf16[128,1536]{1,0:T(8,128)(2,1)S(1)}, u32[]{:S(2)}, u32[]{:S(2)}) %collective-permute-start.5) | collective-permute-done | bytes 393248 | tf_op jit(solution)/shard_map/ppermute | solution.py:703
  99.3 9.2 %attend.2 = (f32[128,1536]{1,0:T(8,128)S(1)}, f32[128,1536]{1,0:T(8,128)S(1)}, f32[128,1536]{1,0:T(8,128)S(1)}, bf16[128,1536]{1,0:T(8,128)(2,1)S(1)}, bf16[512,...) custom-call(s32[1]{0:T(128)} %collective-permute-done.4.length.refs_2_.refs_1_, ...), custom_call_target="tpu_custom_call" | custom-call | flops 3000000000 | bytes 6000000 | tf_op jit(solution)/shard_map/attend/pallas_call | solution.py:380
  134.9 6.6 collective-permute-start.34
  150.3 6.9 collective-permute-done.18.refs_3_
  158.9 9.2 %feed_forward.2 = (f32[128,1536]{1,0:T(8,128)S(1)}, f32[128,1536]{1,0:T(8,128)S(1)}, f32[128,1536]{1,0:T(8,128)S(1)}, bf16[128,1536]{1,0:T(8,128)(2,1)S(1)}, f32...) custom-call(bf16[128,1536]{1,0:T(8,128)(2,1)S(1)} %multiply_convert_fusion.2.refs_0_, ...), custom_call_target="tpu_custom_call" | custom-call | flops 4899999744 | bytes 18000000 | tf_op jit(solution)/shard_map/feed_forward/pallas_call | solution.py:138
  195.6 9.7 %collective-permute-done.44 = bf16[192,3072]{1,0:T(8,128)(2,1)S(1)} collective-permute-done((bf16[192,3072]{1,0:T(8,128)(2,1)S(1)}, bf16[192,3072]{1,0:T(8,128)(2,1)S(1)}, u32[]{:S(2)}, u32[]{:S(2)}) %collective-permute-start.44) | collective-permute-done | bytes 1179680 | tf_op jit(solution)/shard_map/ppermute | solution.py:783
  230.3 9.1 %attend.3 = (f32[128,1536]{1,0:T(8,128)S(1)}, f32[128,1536]{1,0:T(8,128)S(1)}, f32[128,1536]{1,0:T(8,128)S(1)}, bf16[128,1536]{1,0:T(8,128)(2,1)S(1)}, bf16[512,...) custom-call(bf16[64,1536]{1,0:T(8,128)(2,1)S(1)} %collective-permute-done.26.refs_0_.refs_3_.refs_8_, ...), custom_call_target="tpu_custom_call" | custom-call | flops 3000000000 | bytes 6000000 | tf_op jit(solution)/shard_map/attend/pallas_call | solution.py:380
  278.6 9.3 %feed_forward.3 = (f32[128,1536]{1,0:T(8,128)S(1)}, f32[128,1536]{1,0:T(8,128)S(1)}, f32[128,1536]{1,0:T(8,128)S(1)}, bf16[128,1536]{1,0:T(8,128)(2,1)S(1)}, f32...) custom-call(bf16[128,1536]{1,0:T(8,128)(2,1)S(1)} %multiply_convert_fusion.refs_0_, ...), custom_call_target="tpu_custom_call" | custom-call | flops 4899999744 | bytes 18000000 | tf_op jit(solution)/shard_map/feed_forward/pallas_call | solution.py:138
  293.5 13.6 %feed_backward.2 = (f32[128,1536]{1,0:T(8,128)S(1)}, bf16[128,1536]{1,0:T(8,128)(2,1)}, bf16[128,1536]{1,0:T(8,128)(2,1)}, bf16[128,1536]{1,0:T(8,128)(2,1)S(1)}...) custom-call(bf16[128,1536]{1,0:T(8,128)(2,1)S(1)} %pad_maximum_fusion.9.refs_0_.refs_5_, ...), custom_call_target="tpu_custom_call" | custom-call | flops 4899999744 | bytes 20000000 | tf_op jit(solution)/shard_map/feed_backward/pallas_call | solution.py:191
  311.1 11.6 %feed_weights.2 = bf16[8,192,3072]{2,1,0:T(8,128)(2,1)} custom-call(bf16[128,1536]{1,0:T(8,128)(2,1)S(1)} %multiply_convert_fusion.refs_0_, bf16[128,1536]{1,0:T(8,128)(2,1)S(1)} %copy-done.41, bf16[128,1536]{1,0:T(8,128)(2,1)S(1)} %copy-done.44, bf16[64,1536]{1,0:T(8,128)(2,1)S(1)} %collective-permute-done.42.refs_3_, bf16[64,1536]{1,0:T(8,128)(2,1)S(1)} %copy-done.94, ...), custom_call_target="tpu_custom_call" | custom-call | flops 4899999744 | bytes 18000000 | tf_op jit(solution)/shard_map/feed_weights/pallas_call | solution.py:244
  339.1 8.3 %collective-permute-done.52.refs_3_.refs_6_ = bf16[128,1536]{1,0:T(8,128)(2,1)S(1)} collective-permute-done((bf16[128,1536]{1,0:T(8,128)(2,1)S(1)}, bf16[128,1536]{1,0:T(8,128)(2,1)S(1)}, u32[]{:S(2)}, u32[]{:S(2)}) %collective-permute-start.52) | collective-permute-done | bytes 393248 | tf_op jit(solution)/shard_map/ppermute | solution.py:703
  353.8 13.4 %attend_backward.2 = (bf16[512,384]{1,0:T(8,128)(2,1)S(1)}, f32[512,384]{1,0:T(8,128)}, bf16[512,384]{1,0:T(8,128)(2,1)S(1)}) custom-call(bf16[128,1536]{1,0:T(8,128)(2,1)S(1)} %get-tuple-element.231.refs_0_, s32[1]{0:T(128)} %collective-permute-done.4.length.refs_2_.refs_1_, bf16[128,1536]{1,0:T(8,128)(2,1)} %copy-done.27, bf16[128,1536]{1,0:T(8,128)(2,1)} %copy-done.53, ...), custom_call_target="tpu_custom_call" | custom-call | flops 6000000000 | bytes 6000000 | tf_op jit(solution)/shard_map/attend_backward/pallas_call | solution.py:455
  367.2 12.5 %collective-permute-start.56 = (bf16[512,384]{1,0:T(8,128)(2,1)S(1)}, bf16[512,384]{1,0:T(8,128)(2,1)S(1)}, u32[]{:S(2)}, u32[]{:S(2)}) collective-permute-start(bf16[512,384]{1,0:T(8,128)(2,1)S(1)} %get-tuple-element.146), channel_id=1, source_target_pairs={{0,8},{8,0},{1,9},{9,1},{2,10},{10,2},{3,11},{11,3},{4,12},{12,4},... | collective-permute-start | bytes 1179656 | tf_op jit(solution)/shard_map/ppermute | solution.py:894
  397.7 7.2 collective-permute-done.58
  413.6 7.9 %collective-permute-done.60.refs_2_.refs_6_ = bf16[128,1536]{1,0:T(8,128)(2,1)S(1)} collective-permute-done((bf16[128,1536]{1,0:T(8,128)(2,1)S(1)}, bf16[128,1536]{1,0:T(8,128)(2,1)S(1)}, u32[]{:S(2)}, u32[]{:S(2)}) %collective-permute-start.60) | collective-permute-done | bytes 393248 | tf_op jit(solution)/shard_map/ppermute | solution.py:703
  433.9 13.7 %feed_backward.3 = (f32[128,1536]{1,0:T(8,128)S(1)}, bf16[128,1536]{1,0:T(8,128)(2,1)}, bf16[128,1536]{1,0:T(8,128)(2,1)}, bf16[128,1536]{1,0:T(8,128)(2,1)S(1)}...) custom-call(bf16[192,3072]{1,0:T(8,128)(2,1)S(1)} %bitcast.55, ...), custom_call_target="tpu_custom_call" | custom-call | flops 4899999744 | bytes 20000000 | tf_op jit(solution)/shard_map/feed_backward/pallas_call | solution.py:191
  453.2 12.6 %feed_weights.3 = bf16[8,192,3072]{2,1,0:T(8,128)(2,1)} custom-call(bf16[128,1536]{1,0:T(8,128)(2,1)S(1)} %copy-done.14, bf16[128,1536]{1,0:T(8,128)(2,1)S(1)} %copy-done.32, bf16[128,1536]{1,0:T(8,128)(2,1)S(1)} %copy-done.34, bf16[64,1536]{1,0:T(8,128)(2,1)S(1)} %copy-done.84, bf16[64,1536]{1,0:T(8,128)(2,1)S(1)} %copy-done.87, ...), custom_call_target="tpu_custom_call" | custom-call | flops 4899999744 | bytes 18000000 | tf_op jit(solution)/shard_map/feed_weights/pallas_call | solution.py:244
  476.8 7.6 collective-permute-done.69.refs_1_.refs_2_
  490.6 12.9 %attend_backward.3 = (bf16[512,384]{1,0:T(8,128)(2,1)S(1)}, f32[512,384]{1,0:T(8,128)}, bf16[512,384]{1,0:T(8,128)(2,1)S(1)}) custom-call(s32[1]{0:T(128)} %collective-permute-done.4.length.refs_2_.refs_1_, bf16[128,1536]{1,0:T(8,128)(2,1)S(1)} %get-tuple-element.165.refs_0_.refs_1_, bf16[128,1536]{1,0:T(8,128)(2,1)} %copy-done.49, ...), custom_call_target="tpu_custom_call" | custom-call | flops 6000000000 | bytes 6000000 | tf_op jit(solution)/shard_map/attend_backward/pallas_call | solution.py:455
  525.7 7.2 collective-permute-done.75
  542.1 17.6 %collective-permute-done.88 = bf16[96,4224]{1,0:T(8,128)(2,1)S(1)} collective-permute-done((bf16[96,4224]{1,0:T(8,128)(2,1)S(1)}, bf16[96,4224]{1,0:T(8,128)(2,1)S(1)}, u32[]{:S(2)}, u32[]{:S(2)}) %collective-permute-start.88) | collective-permute-done | bytes 811040 | tf_op jit(solution)/shard_map/ppermute | solution.py:751
  561.6 18.7 %reduce-scatter.11.cloned.1.call-done = bf16[1,192,1280]{2,1,0:T(8,128)(2,1)} async-done(((bf16[8,192,1280]{2,1,0:T(8,128)(2,1)}), bf16[1,192,1280]{2,1,0:T(8,128)(2,1)}) %reduce-scatter.11.cloned.1.call-update) | async-done | bytes 491536 | tf_op jit(solution)/shard_map/reduce_scatter | solution.py:903
  580.4 61.8 %reduce-scatter.9.cloned.1.call-done = bf16[1,192,3072]{2,1,0:T(8,128)(2,1)} async-done(((bf16[8,192,3072]{2,1,0:T(8,128)(2,1)}), bf16[1,192,3072]{2,1,0:T(8,128)(2,1)}) %reduce-scatter.9.cloned.1.call-update) | async-done | bytes 1179664 | tf_op jit(solution)/shard_map/reduce_scatter | solution.py:903
  650.5 13.3 %collective-permute-done.82 = bf16[96,3072]{1,0:T(8,128)(2,1)S(1)} collective-permute-done((bf16[96,3072]{1,0:T(8,128)(2,1)S(1)}, bf16[96,3072]{1,0:T(8,128)(2,1)S(1)}, u32[]{:S(2)}, u32[]{:S(2)}) %collective-permute-start.82) | collective-permute-done | bytes 589856 | tf_op jit(solution)/shard_map/ppermute | solution.py:747
  665.4 12.4 %collective-permute-done.83 = bf16[96,3072]{1,0:T(8,128)(2,1)S(1)} collective-permute-done((bf16[96,3072]{1,0:T(8,128)(2,1)S(1)}, bf16[96,3072]{1,0:T(8,128)(2,1)S(1)}, u32[]{:S(2)}, u32[]{:S(2)}) %collective-permute-start.83) | collective-permute-done | bytes 589856 | tf_op jit(solution)/shard_map/ppermute | solution.py:751
  698.6 11.8 %collective-permute-start.80 = (bf16[64,1536]{1,0:T(8,128)(2,1)S(1)}, bf16[64,1536]{1,0:T(8,128)(2,1)S(1)}, u32[]{:S(2)}, u32[]{:S(2)}) collective-permute-start(bf16[64,1536]{1,0:T(8,128)(2,1)S(1)} %pad_maximum_fusion.18), channel_id=1, source_target_pairs={{48,0},{56,1},{0,2},{8,3},{16,4},{24,5},{32,6},{40,7},{49,8},{57,9... | collective-permute-start | bytes 589832 | tf_op jit(solution)/shard_map/ppermute | solution.py:686
  723.2 8.8 %collective-permute-done.77 = bf16[64,1536]{1,0:T(8,128)(2,1)S(1)} collective-permute-done((bf16[64,1536]{1,0:T(8,128)(2,1)S(1)}, bf16[64,1536]{1,0:T(8,128)(2,1)S(1)}, u32[]{:S(2)}, u32[]{:S(2)}) %collective-permute-start.77) | collective-permute-done | bytes 196640 | tf_op jit(solution)/shard_map/ppermute | solution.py:686
  732.1 12.0 %collective-permute-done.78 = bf16[64,1536]{1,0:T(8,128)(2,1)S(1)} collective-permute-done((bf16[64,1536]{1,0:T(8,128)(2,1)S(1)}, bf16[64,1536]{1,0:T(8,128)(2,1)S(1)}, u32[]{:S(2)}, u32[]{:S(2)}) %collective-permute-start.78) | collective-permute-done | bytes 196640 | tf_op jit(solution)/shard_map/ppermute | solution.py:686
  746.0 7.4 unpack.3
  753.4 21.1 %all-gather.21.cloned.1.call-done = bf16[768,4352]{1,0:T(8,128)(2,1)} async-done(((bf16[96,4352]{1,0:T(8,128)(2,1)}), bf16[768,4352]{1,0:T(8,128)(2,1)}) %all-gather.21.cloned.1.call-update) | async-done | bytes 6684688 | tf_op jit(solution)/shard_map/all_gather | solution.py:932
  774.5 7.5 unpack.2
  (697 shorter events, 374.3 us)
Async XLA Ops:
  7.2 77.6 %all-gather.13.cloned.1.call-start = ((), (), s32[]{:S(2)}) async-start(), calls=%async_computation.8 | async-start | bytes 4423680 | tf_op jit(solution)/shard_map/all_gather | solution.py:800
  26.3 131.2 %all-gather.15.cloned.1.call-start = ((), (), s32[]{:S(2)}) async-start(), calls=%async_computation.9 | async-start | bytes 10616832 | tf_op jit(solution)/shard_map/all_gather | solution.py:800
  26.7 24.7 %collective-permute-start = (bf16[64,1536]{1,0:T(8,128)(2,1)S(1)}, bf16[64,1536]{1,0:T(8,128)(2,1)S(1)}, u32[]{:S(2)}, u32[]{:S(2)}) collective-permute-start(bf16[64,1536]{1,0:T(8,128)(2,1)S(1)} %get-tuple-element.232), channel_id=1, source_target_pairs={{0,0},{1,8},{2,16},{3,24},{4,32},{5,40},{6,48},{7,56},{8,1},{9,9},... | collective-permute-start | bytes 589832 | tf_op jit(solution)/shard_map/ppermute | solution.py:678
  33.3 18.7 %collective-permute-start.1 = (bf16[64,1536]{1,0:T(8,128)(2,1)S(1)}, bf16[64,1536]{1,0:T(8,128)(2,1)S(1)}, u32[]{:S(2)}, u32[]{:S(2)}) collective-permute-start(bf16[64,1536]{1,0:T(8,128)(2,1)S(1)} %get-tuple-element.235), channel_id=1, source_target_pairs={{0,16},{1,24},{2,32},{3,40},{4,48},{5,56},{6,0},{7,8},{8,17},{9,25... | collective-permute-start | bytes 589832 | tf_op jit(solution)/shard_map/ppermute | solution.py:678
  34.7 24.5 %collective-permute-start.2 = (bf16[64,1536]{1,0:T(8,128)(2,1)S(1)}, bf16[64,1536]{1,0:T(8,128)(2,1)S(1)}, u32[]{:S(2)}, u32[]{:S(2)}) collective-permute-start(bf16[64,1536]{1,0:T(8,128)(2,1)S(1)} %get-tuple-element.234), channel_id=1, source_target_pairs={{0,32},{1,40},{2,48},{3,56},{4,0},{5,8},{6,16},{7,24},{8,33},{9,41... | collective-permute-start | bytes 589832 | tf_op jit(solution)/shard_map/ppermute | solution.py:678
  50.1 25.1 %collective-permute-start.20 = (bf16[192,3072]{1,0:T(8,128)(2,1)S(1)}, bf16[192,3072]{1,0:T(8,128)(2,1)S(1)}, u32[]{:S(2)}, u32[]{:S(2)}) collective-permute-start(bf16[192,3072]{1,0:T(8,128)(2,1)S(1)} %pack_feed.2), channel_id=1, source_target_pairs={{0,1},{2,3},{4,5},{6,7},{9,8},{11,10},{13,12},{15,14},{16,17},{18,... | collective-permute-start | bytes 3538952 | tf_op jit(solution)/shard_map/ppermute | solution.py:783
  80.3 136.2 %all-gather.17.cloned.1.call-start = ((), (), s32[]{:S(2)}) async-start(), calls=%async_computation.10 | async-start | bytes 3981312 | tf_op jit(solution)/shard_map/all_gather | solution.py:800
  157.3 118.4 %all-gather.19.cloned.1.call-start = ((), (), s32[]{:S(2)}) async-start(), calls=%async_computation.11 | async-start | bytes 10616832 | tf_op jit(solution)/shard_map/all_gather | solution.py:800
  186.9 18.5 %collective-permute-start.44 = (bf16[192,3072]{1,0:T(8,128)(2,1)S(1)}, bf16[192,3072]{1,0:T(8,128)(2,1)S(1)}, u32[]{:S(2)}, u32[]{:S(2)}) collective-permute-start(bf16[192,3072]{1,0:T(8,128)(2,1)S(1)} %pack_feed.3), channel_id=1, source_target_pairs={{0,1},{2,3},{4,5},{6,7},{9,8},{11,10},{13,12},{15,14},{16,17},{18,... | collective-permute-start | bytes 3538952 | tf_op jit(solution)/shard_map/ppermute | solution.py:783
  212.9 197.8 %reduce-scatter.5.cloned.1.call-start = ((), (), s32[]{:S(2)}) async-start(), calls=%async_computation.4 | async-start | bytes 10616832 | tf_op jit(solution)/shard_map/reduce_scatter | solution.py:903
  290.4 34.3 %collective-permute-start.45 = (bf16[64,1536]{1,0:T(8,128)(2,1)}, bf16[64,1536]{1,0:T(8,128)(2,1)}, u32[]{:S(2)}, u32[]{:S(2)}) collective-permute-start(bf16[64,1536]{1,0:T(8,128)(2,1)} %get-tuple-element.244), channel_id=1, source_target_pairs={{0,16},{16,32},{32,48},{48,0},{1,17},{17,33},{33,49},{49,1},{2,18}... | collective-permute-start | bytes 589832 | tf_op jit(solution)/shard_map/ppermute | solution.py:712
  291.6 35.0 %collective-permute-start.47 = (bf16[64,1536]{1,0:T(8,128)(2,1)}, bf16[64,1536]{1,0:T(8,128)(2,1)}, u32[]{:S(2)}, u32[]{:S(2)}) collective-permute-start(bf16[64,1536]{1,0:T(8,128)(2,1)} %get-tuple-element.245), channel_id=1, source_target_pairs={{0,48},{16,0},{32,16},{48,32},{1,49},{17,1},{33,17},{49,33},{2,50}... | collective-permute-start | bytes 589832 | tf_op jit(solution)/shard_map/ppermute | solution.py:713
  308.0 22.1 %collective-permute-start.49 = (bf16[128,1536]{1,0:T(8,128)(2,1)}, bf16[128,1536]{1,0:T(8,128)(2,1)}, u32[]{:S(2)}, u32[]{:S(2)}) collective-permute-start(bf16[128,1536]{1,0:T(8,128)(2,1)} %get-tuple-element.136), channel_id=1, source_target_pairs={{0,16},{16,32},{32,48},{48,0},{1,17},{17,33},{33,49},{49,1},{2,18}... | collective-permute-start | bytes 1179656 | tf_op jit(solution)/shard_map/ppermute | solution.py:722
  308.0 22.1 %collective-permute-start.50 = (bf16[128,1536]{1,0:T(8,128)(2,1)}, bf16[128,1536]{1,0:T(8,128)(2,1)}, u32[]{:S(2)}, u32[]{:S(2)}) collective-permute-start(bf16[128,1536]{1,0:T(8,128)(2,1)} %get-tuple-element.137), channel_id=1, source_target_pairs={{0,48},{16,0},{32,16},{48,32},{1,49},{17,1},{33,17},{49,33},{2,50}... | collective-permute-start | bytes 1179656 | tf_op jit(solution)/shard_map/ppermute | solution.py:723
  310.6 19.5 %collective-permute-start.51 = (bf16[128,1536]{1,0:T(8,128)(2,1)S(1)}, bf16[128,1536]{1,0:T(8,128)(2,1)}, u32[]{:S(2)}, u32[]{:S(2)}) collective-permute-start(bf16[128,1536]{1,0:T(8,128)(2,1)S(1)} %get-tuple-element.138), channel_id=1, source_target_pairs={{0,32},{16,48},{32,0},{48,16},{1,33},{17,49},{33,1},{49,17},{2,34}... | collective-permute-start | bytes 1179656 | tf_op jit(solution)/shard_map/ppermute | solution.py:724
  335.3 130.5 %reduce-scatter.7.cloned.1.call-start = ((), (), s32[]{:S(2)}) async-start(), calls=%async_computation.5 | async-start | bytes 3981312 | tf_op jit(solution)/shard_map/reduce_scatter | solution.py:903
  384.8 20.1 %collective-permute-start.58 = (bf16[128,1536]{1,0:T(8,128)(2,1)}, bf16[128,1536]{1,0:T(8,128)(2,1)}, u32[]{:S(2)}, u32[]{:S(2)}) collective-permute-start(bf16[128,1536]{1,0:T(8,128)(2,1)} %get-tuple-element.149), channel_id=1, source_target_pairs={{0,48},{16,0},{32,16},{48,32},{1,49},{17,1},{33,17},{49,33},{2,50}... | collective-permute-start | bytes 1179656 | tf_op jit(solution)/shard_map/ppermute | solution.py:723
  388.2 18.8 %collective-permute-start.59 = (bf16[128,1536]{1,0:T(8,128)(2,1)S(1)}, bf16[128,1536]{1,0:T(8,128)(2,1)}, u32[]{:S(2)}, u32[]{:S(2)}) collective-permute-start(bf16[128,1536]{1,0:T(8,128)(2,1)S(1)} %get-tuple-element.150), channel_id=1, source_target_pairs={{0,32},{16,48},{32,0},{48,16},{1,33},{17,49},{33,1},{49,17},{2,34}... | collective-permute-start | bytes 1179656 | tf_op jit(solution)/shard_map/ppermute | solution.py:724
  410.8 169.5 %reduce-scatter.11.cloned.1.call-start = ((), (), s32[]{:S(2)}) async-start(), calls=%async_computation.7 | async-start | bytes 4423680 | tf_op jit(solution)/shard_map/reduce_scatter | solution.py:903
  448.5 22.3 %collective-permute-start.64 = (bf16[128,1536]{1,0:T(8,128)(2,1)}, bf16[128,1536]{1,0:T(8,128)(2,1)}, u32[]{:S(2)}, u32[]{:S(2)}) collective-permute-start(bf16[128,1536]{1,0:T(8,128)(2,1)} %get-tuple-element.158), channel_id=1, source_target_pairs={{0,16},{16,32},{32,48},{48,0},{1,17},{17,33},{33,49},{49,1},{2,18}... | collective-permute-start | bytes 1179656 | tf_op jit(solution)/shard_map/ppermute | solution.py:722
  448.5 22.3 %collective-permute-start.65 = (bf16[128,1536]{1,0:T(8,128)(2,1)}, bf16[128,1536]{1,0:T(8,128)(2,1)}, u32[]{:S(2)}, u32[]{:S(2)}) collective-permute-start(bf16[128,1536]{1,0:T(8,128)(2,1)} %get-tuple-element.159), channel_id=1, source_target_pairs={{0,48},{16,0},{32,16},{48,32},{1,49},{17,1},{33,17},{49,33},{2,50}... | collective-permute-start | bytes 1179656 | tf_op jit(solution)/shard_map/ppermute | solution.py:723
  451.8 19.0 %collective-permute-start.66 = (bf16[128,1536]{1,0:T(8,128)(2,1)S(1)}, bf16[128,1536]{1,0:T(8,128)(2,1)}, u32[]{:S(2)}, u32[]{:S(2)}) collective-permute-start(bf16[128,1536]{1,0:T(8,128)(2,1)S(1)} %get-tuple-element.160), channel_id=1, source_target_pairs={{0,32},{16,48},{32,0},{48,16},{1,33},{17,49},{33,1},{49,17},{2,34}... | collective-permute-start | bytes 1179656 | tf_op jit(solution)/shard_map/ppermute | solution.py:724
  476.6 29.8 %collective-permute-start.68 = (bf16[96,4224]{1,0:T(8,128)(2,1)S(1)}, bf16[96,4224]{1,0:T(8,128)(2,1)S(1)}, u32[]{:S(2)}, u32[]{:S(2)}) collective-permute-start(bf16[96,4224]{1,0:T(8,128)(2,1)S(1)} %broadcast_select_fusion.2), channel_id=1, source_target_pairs={{0,1},{1,0},{2,3},{3,2},{4,5},{5,4},{6,7},{7,6},{8,9},{9,8},{10,11... | collective-permute-start | bytes 2433032 | tf_op jit(solution)/shard_map/ppermute | solution.py:747
  513.4 19.5 %collective-permute-start.75 = (bf16[128,1536]{1,0:T(8,128)(2,1)}, bf16[128,1536]{1,0:T(8,128)(2,1)}, u32[]{:S(2)}, u32[]{:S(2)}) collective-permute-start(bf16[128,1536]{1,0:T(8,128)(2,1)} %get-tuple-element.172), channel_id=1, source_target_pairs={{0,48},{16,0},{32,16},{48,32},{1,49},{17,1},{33,17},{49,33},{2,50}... | collective-permute-start | bytes 1179656 | tf_op jit(solution)/shard_map/ppermute | solution.py:723
  516.6 18.3 %collective-permute-start.76 = (bf16[128,1536]{1,0:T(8,128)(2,1)}, bf16[128,1536]{1,0:T(8,128)(2,1)}, u32[]{:S(2)}, u32[]{:S(2)}) collective-permute-start(bf16[128,1536]{1,0:T(8,128)(2,1)} %get-tuple-element.173), channel_id=1, source_target_pairs={{0,32},{16,48},{32,0},{48,16},{1,33},{17,49},{33,1},{49,17},{2,34}... | collective-permute-start | bytes 1179656 | tf_op jit(solution)/shard_map/ppermute | solution.py:724
  540.8 101.4 %reduce-scatter.9.cloned.1.call-start = ((), (), s32[]{:S(2)}) async-start(), calls=%async_computation.6 | async-start | bytes 10616832 | tf_op jit(solution)/shard_map/reduce_scatter | solution.py:903
  541.6 204.4 %all-gather.23.cloned.1.call-start = ((), (), s32[]{:S(2)}) async-start(), calls=%async_computation.13 | async-start | bytes 7299072 | tf_op jit(solution)/shard_map/all_gather | solution.py:928
  541.6 18.1 %collective-permute-start.88 = (bf16[96,4224]{1,0:T(8,128)(2,1)S(1)}, bf16[96,4224]{1,0:T(8,128)(2,1)S(1)}, u32[]{:S(2)}, u32[]{:S(2)}) collective-permute-start(bf16[96,4224]{1,0:T(8,128)(2,1)S(1)} %add_convert_fusion.1.refs_0_), channel_id=1, source_target_pairs={{0,64},{64,0},{1,65},{65,1},{2,66},{66,2},{3,67},{67,3},{4,68},{68... | collective-permute-start | bytes 2433032 | tf_op jit(solution)/shard_map/ppermute | solution.py:751
  580.3 194.2 %all-gather.21.cloned.1.call-start = ((), (), s32[]{:S(2)}) async-start(), calls=%async_computation.12 | async-start | bytes 7520256 | tf_op jit(solution)/shard_map/all_gather | solution.py:932
  698.6 45.6 %collective-permute-start.80 = (bf16[64,1536]{1,0:T(8,128)(2,1)S(1)}, bf16[64,1536]{1,0:T(8,128)(2,1)S(1)}, u32[]{:S(2)}, u32[]{:S(2)}) collective-permute-start(bf16[64,1536]{1,0:T(8,128)(2,1)S(1)} %pad_maximum_fusion.18), channel_id=1, source_target_pairs={{48,0},{56,1},{0,2},{8,3},{16,4},{24,5},{32,6},{40,7},{49,8},{57,9... | collective-permute-start | bytes 589832 | tf_op jit(solution)/shard_map/ppermute | solution.py:686
  710.4 33.7 %collective-permute-start.79 = (bf16[64,1536]{1,0:T(8,128)(2,1)S(1)}, bf16[64,1536]{1,0:T(8,128)(2,1)S(1)}, u32[]{:S(2)}, u32[]{:S(2)}) collective-permute-start(bf16[64,1536]{1,0:T(8,128)(2,1)S(1)} %pad_maximum_fusion.17), channel_id=1, source_target_pairs={{32,0},{40,1},{48,2},{56,3},{0,4},{8,5},{16,6},{24,7},{33,8},{41,9... | collective-permute-start | bytes 589832 | tf_op jit(solution)/shard_map/ppermute | solution.py:686
  719.8 24.3 %collective-permute-start.78 = (bf16[64,1536]{1,0:T(8,128)(2,1)S(1)}, bf16[64,1536]{1,0:T(8,128)(2,1)S(1)}, u32[]{:S(2)}, u32[]{:S(2)}) collective-permute-start(bf16[64,1536]{1,0:T(8,128)(2,1)S(1)} %pad_maximum_fusion.16), channel_id=1, source_target_pairs={{16,0},{24,1},{32,2},{40,3},{48,4},{56,5},{0,6},{8,7},{17,8},{25,9... | collective-permute-start | bytes 589832 | tf_op jit(solution)/shard_map/ppermute | solution.py:686
  (222 other events, 1904.5 us)
Sparse Core Ops, SparseCore 0:
  26.4 45.1 all-gather.12
  80.4 51.0 all-gather.14
  157.4 31.7 all-gather.16
  213.0 57.7 all-gather.18
  335.4 72.6 reduce-scatter.4
  410.9 37.1 reduce-scatter.6
  540.9 39.3 reduce-scatter.10
  582.8 59.2 reduce-scatter.8
  644.5 42.2 all-gather.22
  698.6 75.8 all-gather.20

commit v11 on v10

--- a/solution.py
+++ b/solution.py
@@ -751,9 +751,11 @@
     return add_low(piece, lax.ppermute(piece, "ylo", SWAP))
 
 
-def cross(piece, start):
+def cross(piece, start, *others):
     first, last = start + 768, start + 1152
     moved = lax.ppermute(piece[:, first:last], AXES, CROSS)
+    if others:
+        piece, moved = lax.optimization_barrier((piece, moved, *others))[:2]
     return jnp.concatenate([piece[:, :first], moved, piece[:, last:]], axis=1)
 
 
@@ -849,7 +851,7 @@
             flats = (flat,)
         else:
             flats = ring_gather(rms_norm(state, gain_attn).astype(BF16))
-            feed_two = feed = line_weights(feed_two, *flats[3:])
+            feed_two = feed = line_weights(feed_two, *flats[1:3])
             queries, own = project_call(False, flats, gain_attn, attn, cosine, sine)
         other = lax.ppermute(own, "core", SWAP)
         line = (queries, own, other, places, key_places)
@@ -862,7 +864,7 @@
             feed_two = feed_part(9, (mixed,), ())
         flats = ring_gather(rms_norm(state, gain_feed).astype(BF16))
         if index == 0:
-            attn_two = line_weights(attn_two, *flats[3:])
+            attn_two = line_weights(attn_two, *flats[1:3])
         *partial, gate, up, hidden = feed_forward_call(flats, feed)
         saved_feed = (state, flats, gate, up, hidden)
         state = state + ring_scatter(*partial)
@@ -899,35 +901,34 @@
         grad, gain_grads[2 * index] = norm_back(grad, own_normed, state, gains[2 * index])
         return grad, attend_weights_call(flats, pieces, low, mixed)
 
-    def scatter(block, *others):
-        return lax.psum_scatter(
-            tie(block, *others), SPREAD, scatter_dimension=0, tiled=True
-        )[0]
+    def scatter(block):
+        return lax.psum_scatter(block, SPREAD, scatter_dimension=0, tiled=True)[0]
 
     grad, feed_grad = feed_back(1, grad, grad_pieces, ())
     low = tie(grad.astype(BF16), feed_grad)
-    second_feed = scatter(feed_grad, low)
+    second_feed = scatter(tie(feed_grad, low))
     grad, attn_grad = attention_back(1, grad, ring_gather(low), (last_rows,), ())
     low = tie(grad.astype(BF16), attn_grad)
-    second_attn = scatter(attn_grad, low, second_feed)
+    second_attn = scatter(tie(attn_grad, low, second_feed))
 
     grad, feed_grad = feed_back(0, grad, ring_gather(low), (second_feed,))
     low = tie(grad.astype(BF16), feed_grad)
-    first_feed = scatter(feed_grad, low, second_attn)
+    first_feed = scatter(tie(feed_grad, low, second_attn))
     second = yhi_sum(jnp.concatenate([second_feed, second_attn], axis=1), core, yhi)
     grad, attn_grad = attention_back(0, grad, ring_gather(low), (), (second,))
     low = grad.astype(BF16)
+    attn_grad = tie(attn_grad, first_feed, low)
     attn_grad = jnp.concatenate([attn_grad, gain_rows(jnp.stack(gain_grads))], axis=2)
-    first_attn = scatter(attn_grad, first_feed, low)
-    second_piece = cross(ylo_sum(second), 3072)
+    first_attn = scatter(attn_grad)
+    second_piece = cross(ylo_sum(second), 3072, first_attn)
     feed_piece = ylo_sum(yhi_sum(first_feed, core, yhi))
     back = from_lines(interleave(last_rows, low), z)
     output, input_grad = separate(back)
     output, input_grad = output[None], input_grad.astype(F32)[None]
 
-    every = lax.all_gather(tie(second_piece, first_attn), ("x", "core"), axis=0, tiled=False)
+    every = lax.all_gather(second_piece, ("x", "core"), axis=0, tiled=False)
     results[10:14], results[15:18] = unpack_call(every.reshape(4, 2, 96, -1))
-    attn_piece = ylo_sum(yhi_sum(tie(first_attn, feed_piece), core, yhi))
+    attn_piece = ylo_sum(yhi_sum(first_attn, core, yhi))
     first_piece = jnp.concatenate([feed_piece, cross(attn_piece, 0)], axis=1)
     every = lax.all_gather(first_piece, ("x", "core"), axis=0, tiled=False)
     every = every.reshape(4, 2, 96, -1)

time: 801 us -> 780 us (0.974)
  waiting for transfers between devices: 321 us -> 311 us
    ppermute x4, starting transfers between devices: 24.5 us -> 12.6 us  [from_lines(): lax.ppermute(block[part * k:part * (k + 1)], AXES, inverse(LINES[k]))]
    unnamed x322 -> x330, local copies, waits for them, and re-layouts: 48.8 us -> 41.4 us
  transfers between devices with their start and end apart: 100 -> 100, of which waited for: 49 -> 49; matrix products, arithmetic and copies ran while one was open for 6% -> 7% of each run, Pallas kernels for 16% -> 17%
where the time goes in v11:
time: 780 us; the launch traced here: 770 us
  waiting for transfers between devices  311 us (40%)
  starting transfers between devices  189 us (24%)
  Pallas kernels  147 us (19%)
  local copies, waits for them, and re-layouts  65 us (8%)
  other arithmetic  41.3 us (5%)
  between operations  17.8 us (2%)
    reduce_scatter x4, waiting for transfers between devices, scatter(): return lax.psum_scatter(block, SPREAD, scatter_dimension=0, tiled=True)[0]  80.8 us
    ppermute x8, waiting for transfers between devices, ring_gather(): from_left = lax.ppermute(block, 'x', RIGHT)  45 us
    unnamed x330, local copies, waits for them, and re-layouts  41.4 us
    ppermute x3, waiting for transfers between devices, ylo_sum(): return add_low(piece, lax.ppermute(piece, 'ylo', SWAP))  32.6 us
    pallas_call x2, Pallas kernels, feed_backward_call(): pl.pallas_call(later(feed_backward_kernel, len(after)), grid=(4,), in_spe...  27.5 us
    pallas_call x2, Pallas kernels, attend_backward_call(): pl.pallas_call(later(functools.partial(attend_backward_kernel, window), l...  26.2 us
    ppermute x4, waiting for transfers between devices, from_lines(): lax.ppermute(block[part * k:part * (k + 1)], AXES, inverse(LINES[k]))  25.9 us
    pallas_call x2, Pallas kernels, feed_weights_call(): pl.pallas_call(feed_weights_kernel, grid=(12,), in_specs=PIECES + PIECES...  24.1 us
  transfers between devices with their start and end apart: 100, of which 49 were waited for; matrix products, arithmetic and copies ran while one was open for 7% of the time, Pallas kernels for 17%

profile of v11, /device:TPU:1, one launch (start us, length us, event | category | flops | bytes accessed | tf_op | source)
XLA Modules:
  0.0 770.2 jit_solution(123474056351692539)
XLA Ops:
  26.7 6.6 collective-permute-start
  34.7 10.0 %collective-permute-start.2 = (bf16[64,1536]{1,0:T(8,128)(2,1)S(1)}, bf16[64,1536]{1,0:T(8,128)(2,1)S(1)}, u32[]{:S(2)}, u32[]{:S(2)}) collective-permute-start(bf16[64,1536]{1,0:T(8,128)(2,1)S(1)} %get-tuple-element.234), channel_id=1, source_target_pairs={{0,32},{1,40},{2,48},{3,56},{4,0},{5,8},{6,16},{7,24},{8,33},{9,41... | collective-permute-start | bytes 589832 | tf_op jit(solution)/shard_map/ppermute | solution.py:678
  63.9 8.2 %collective-permute-done.5.refs_1_ = bf16[128,1536]{1,0:T(8,128)(2,1)S(1)} collective-permute-done((bf16[128,1536]{1,0:T(8,128)(2,1)S(1)}, bf16[128,1536]{1,0:T(8,128)(2,1)S(1)}, u32[]{:S(2)}, u32[]{:S(2)}) %collective-permute-start.5) | collective-permute-done | bytes 393248 | tf_op jit(solution)/shard_map/ppermute | solution.py:703
  101.2 9.0 %attend.2 = (f32[128,1536]{1,0:T(8,128)S(1)}, f32[128,1536]{1,0:T(8,128)S(1)}, f32[128,1536]{1,0:T(8,128)S(1)}, bf16[128,1536]{1,0:T(8,128)(2,1)S(1)}, bf16[512,...) custom-call(s32[1]{0:T(128)} %collective-permute-done.4.length.refs_2_.refs_1_, bf16[512,384]{1,0:T(8,128)(2,1)S(1)} %copy-done.103, ...), custom_call_target="tpu_custom_call" | custom-call | flops 3000000000 | bytes 6000000 | tf_op jit(solution)/shard_map/attend/pallas_call | solution.py:380
  123.1 7.2 collective-permute-start.34
  140.1 11.1 %collective-permute-done.16.refs_1_ = bf16[128,1536]{1,0:T(8,128)(2,1)S(1)} collective-permute-done((bf16[128,1536]{1,0:T(8,128)(2,1)S(1)}, bf16[128,1536]{1,0:T(8,128)(2,1)S(1)}, u32[]{:S(2)}, u32[]{:S(2)}) %collective-permute-start.16) | collective-permute-done | bytes 393248 | tf_op jit(solution)/shard_map/ppermute | solution.py:703
  158.0 9.3 %feed_forward.2 = (f32[128,1536]{1,0:T(8,128)S(1)}, f32[128,1536]{1,0:T(8,128)S(1)}, f32[128,1536]{1,0:T(8,128)S(1)}, bf16[128,1536]{1,0:T(8,128)(2,1)S(1)}, f32...) custom-call(bf16[128,1536]{1,0:T(8,128)(2,1)S(1)} %multiply_convert_fusion.2.refs_0_, ...), custom_call_target="tpu_custom_call" | custom-call | flops 4899999744 | bytes 18000000 | tf_op jit(solution)/shard_map/feed_forward/pallas_call | solution.py:138
  181.0 7.5 collective-permute-done.44
  211.6 7.6 collective-permute-start.35
  227.2 9.0 %attend.3 = (f32[128,1536]{1,0:T(8,128)S(1)}, f32[128,1536]{1,0:T(8,128)S(1)}, f32[128,1536]{1,0:T(8,128)S(1)}, bf16[128,1536]{1,0:T(8,128)(2,1)S(1)}, bf16[512,...) custom-call(bf16[64,1536]{1,0:T(8,128)(2,1)S(1)} %collective-permute-done.26.refs_0_.refs_3_.refs_8_, ...), custom_call_target="tpu_custom_call" | custom-call | flops 3000000000 | bytes 6000000 | tf_op jit(solution)/shard_map/attend/pallas_call | solution.py:380
  248.5 6.9 collective-permute-done.37
  261.0 6.9 collective-permute-done.40.refs_1_
  277.9 9.2 %feed_forward.3 = (f32[128,1536]{1,0:T(8,128)S(1)}, f32[128,1536]{1,0:T(8,128)S(1)}, f32[128,1536]{1,0:T(8,128)S(1)}, bf16[128,1536]{1,0:T(8,128)(2,1)S(1)}, f32...) custom-call(bf16[128,1536]{1,0:T(8,128)(2,1)S(1)} %multiply_convert_fusion.refs_0_, ...), custom_call_target="tpu_custom_call" | custom-call | flops 4899999744 | bytes 18000000 | tf_op jit(solution)/shard_map/feed_forward/pallas_call | solution.py:138
  292.1 13.7 %feed_backward.2 = (f32[128,1536]{1,0:T(8,128)S(1)}, bf16[128,1536]{1,0:T(8,128)(2,1)}, bf16[128,1536]{1,0:T(8,128)(2,1)}, bf16[128,1536]{1,0:T(8,128)(2,1)}, bf...) custom-call(bf16[128,1536]{1,0:T(8,128)(2,1)S(1)} %pad_maximum_fusion.9.refs_0_.refs_5_, ...), custom_call_target="tpu_custom_call" | custom-call | flops 4899999744 | bytes 20000000 | tf_op jit(solution)/shard_map/feed_backward/pallas_call | solution.py:191
  309.4 11.5 %feed_weights.2 = bf16[8,192,3072]{2,1,0:T(8,128)(2,1)} custom-call(bf16[128,1536]{1,0:T(8,128)(2,1)S(1)} %multiply_convert_fusion.refs_0_, bf16[128,1536]{1,0:T(8,128)(2,1)S(1)} %copy-done.41, bf16[128,1536]{1,0:T(8,128)(2,1)S(1)} %copy-done.44, bf16[64,1536]{1,0:T(8,128)(2,1)S(1)} %collective-permute-done.42.refs_3_, bf16[64,1536]{1,0:T(8,128)(2,1)S(1)} %copy-done.91, ...), custom_call_target="tpu_custom_call" | custom-call | flops 4899999744 | bytes 18000000 | tf_op jit(solution)/shard_map/feed_weights/pallas_call | solution.py:244
  351.5 13.3 %attend_backward.2 = (bf16[512,384]{1,0:T(8,128)(2,1)S(1)}, f32[512,384]{1,0:T(8,128)}, bf16[512,384]{1,0:T(8,128)(2,1)S(1)}) custom-call(bf16[128,1536]{1,0:T(8,128)(2,1)S(1)} %get-tuple-element.231.refs_0_, s32[1]{0:T(128)} %collective-permute-done.4.length.refs_2_.refs_1_, bf16[128,1536]{1,0:T(8,128)(2,1)} %copy-done.29, bf16[128,1536]{1,0:T(8,128)(2,1)} %copy-done.53, ...), custom_call_target="tpu_custom_call" | custom-call | flops 6000000000 | bytes 6000000 | tf_op jit(solution)/shard_map/attend_backward/pallas_call | solution.py:455
  364.8 9.6 %collective-permute-start.56 = (bf16[512,384]{1,0:T(8,128)(2,1)S(1)}, bf16[512,384]{1,0:T(8,128)(2,1)S(1)}, u32[]{:S(2)}, u32[]{:S(2)}) collective-permute-start(bf16[512,384]{1,0:T(8,128)(2,1)S(1)} %get-tuple-element.146), channel_id=1, source_target_pairs={{0,8},{8,0},{1,9},{9,1},{2,10},{10,2},{3,11},{11,3},{4,12},{12,4},... | collective-permute-start | bytes 1179656 | tf_op jit(solution)/shard_map/ppermute | solution.py:896
  392.5 7.2 collective-permute-done.58
  410.4 7.7 %collective-permute-done.60.refs_2_.refs_6_ = bf16[128,1536]{1,0:T(8,128)(2,1)S(1)} collective-permute-done((bf16[128,1536]{1,0:T(8,128)(2,1)S(1)}, bf16[128,1536]{1,0:T(8,128)(2,1)S(1)}, u32[]{:S(2)}, u32[]{:S(2)}) %collective-permute-start.60) | collective-permute-done | bytes 393248 | tf_op jit(solution)/shard_map/ppermute | solution.py:703
  430.5 13.8 %feed_backward.3 = (f32[128,1536]{1,0:T(8,128)S(1)}, bf16[128,1536]{1,0:T(8,128)(2,1)}, bf16[128,1536]{1,0:T(8,128)(2,1)}, bf16[128,1536]{1,0:T(8,128)(2,1)}, bf...) custom-call(bf16[192,3072]{1,0:T(8,128)(2,1)S(1)} %bitcast.61, ...), custom_call_target="tpu_custom_call" | custom-call | flops 4899999744 | bytes 20000000 | tf_op jit(solution)/shard_map/feed_backward/pallas_call | solution.py:191
  450.0 12.6 %feed_weights.3 = bf16[8,192,3072]{2,1,0:T(8,128)(2,1)} custom-call(bf16[128,1536]{1,0:T(8,128)(2,1)S(1)} %copy-done.16, bf16[128,1536]{1,0:T(8,128)(2,1)S(1)} %copy-done.34, bf16[128,1536]{1,0:T(8,128)(2,1)S(1)} %copy-done.36, bf16[64,1536]{1,0:T(8,128)(2,1)S(1)} %copy-done.82, bf16[64,1536]{1,0:T(8,128)(2,1)S(1)} %copy-done.84, ...), custom_call_target="tpu_custom_call" | custom-call | flops 4899999744 | bytes 18000000 | tf_op jit(solution)/shard_map/feed_weights/pallas_call | solution.py:244
  487.9 12.9 %attend_backward.3 = (bf16[512,384]{1,0:T(8,128)(2,1)S(1)}, f32[512,384]{1,0:T(8,128)}, bf16[512,384]{1,0:T(8,128)(2,1)S(1)}) custom-call(s32[1]{0:T(128)} %collective-permute-done.4.length.refs_2_.refs_1_, bf16[128,1536]{1,0:T(8,128)(2,1)S(1)} %get-tuple-element.165.refs_0_.refs_1_, bf16[128,1536]{1,0:T(8,128)(2,1)} %copy-done.49, ...), custom_call_target="tpu_custom_call" | custom-call | flops 6000000000 | bytes 6000000 | tf_op jit(solution)/shard_map/attend_backward/pallas_call | solution.py:455
  522.8 7.3 collective-permute-done.75
  540.0 16.9 %collective-permute-done.88 = bf16[96,4224]{1,0:T(8,128)(2,1)S(1)} collective-permute-done((bf16[96,4224]{1,0:T(8,128)(2,1)S(1)}, bf16[96,4224]{1,0:T(8,128)(2,1)S(1)}, u32[]{:S(2)}, u32[]{:S(2)}) %collective-permute-start.88) | collective-permute-done | bytes 811040 | tf_op jit(solution)/shard_map/ppermute | solution.py:751
  558.9 21.6 %reduce-scatter.11.cloned.1.call-done = bf16[1,192,1280]{2,1,0:T(8,128)(2,1)} async-done(((bf16[8,192,1280]{2,1,0:T(8,128)(2,1)}), bf16[1,192,1280]{2,1,0:T(8,128)(2,1)}) %reduce-scatter.11.cloned.1.call-update) | async-done | bytes 491536 | tf_op jit(solution)/shard_map/reduce_scatter | solution.py:905
  584.6 57.0 %reduce-scatter.9.cloned.1.call-done = bf16[1,192,3072]{2,1,0:T(8,128)(2,1)} async-done(((bf16[8,192,3072]{2,1,0:T(8,128)(2,1)}), bf16[1,192,3072]{2,1,0:T(8,128)(2,1)}) %reduce-scatter.9.cloned.1.call-update) | async-done | bytes 1179664 | tf_op jit(solution)/shard_map/reduce_scatter | solution.py:905
  654.8 11.2 %collective-permute-done.82 = bf16[96,3072]{1,0:T(8,128)(2,1)S(1)} collective-permute-done((bf16[96,3072]{1,0:T(8,128)(2,1)S(1)}, bf16[96,3072]{1,0:T(8,128)(2,1)S(1)}, u32[]{:S(2)}, u32[]{:S(2)}) %collective-permute-start.82) | collective-permute-done | bytes 589856 | tf_op jit(solution)/shard_map/ppermute | solution.py:747
  672.3 11.9 %collective-permute-done.83 = bf16[96,3072]{1,0:T(8,128)(2,1)S(1)} collective-permute-done((bf16[96,3072]{1,0:T(8,128)(2,1)S(1)}, bf16[96,3072]{1,0:T(8,128)(2,1)S(1)}, u32[]{:S(2)}, u32[]{:S(2)}) %collective-permute-start.83) | collective-permute-done | bytes 589856 | tf_op jit(solution)/shard_map/ppermute | solution.py:751
  698.1 21.6 %collective-permute-done.77 = bf16[64,1536]{1,0:T(8,128)(2,1)S(1)} collective-permute-done((bf16[64,1536]{1,0:T(8,128)(2,1)S(1)}, bf16[64,1536]{1,0:T(8,128)(2,1)S(1)}, u32[]{:S(2)}, u32[]{:S(2)}) %collective-permute-start.77) | collective-permute-done | bytes 196640 | tf_op jit(solution)/shard_map/ppermute | solution.py:686
  726.0 7.4 unpack.3
  733.4 20.4 %all-gather.21.cloned.1.call-done = bf16[768,4352]{1,0:T(8,128)(2,1)} async-done(((bf16[96,4352]{1,0:T(8,128)(2,1)}), bf16[768,4352]{1,0:T(8,128)(2,1)}) %all-gather.21.cloned.1.call-update) | async-done | bytes 6684688 | tf_op jit(solution)/shard_map/all_gather | solution.py:933
  753.8 7.5 unpack.2
  (705 shorter events, 358.4 us)
Async XLA Ops:
  7.2 77.4 %all-gather.13.cloned.1.call-start = ((), (), s32[]{:S(2)}) async-start(), calls=%async_computation.8 | async-start | bytes 4423680 | tf_op jit(solution)/shard_map/all_gather | solution.py:802
  26.3 131.6 %all-gather.15.cloned.1.call-start = ((), (), s32[]{:S(2)}) async-start(), calls=%async_computation.9 | async-start | bytes 10616832 | tf_op jit(solution)/shard_map/all_gather | solution.py:802
  26.7 24.7 %collective-permute-start = (bf16[64,1536]{1,0:T(8,128)(2,1)S(1)}, bf16[64,1536]{1,0:T(8,128)(2,1)S(1)}, u32[]{:S(2)}, u32[]{:S(2)}) collective-permute-start(bf16[64,1536]{1,0:T(8,128)(2,1)S(1)} %get-tuple-element.232), channel_id=1, source_target_pairs={{0,0},{1,8},{2,16},{3,24},{4,32},{5,40},{6,48},{7,56},{8,1},{9,9},... | collective-permute-start | bytes 589832 | tf_op jit(solution)/shard_map/ppermute | solution.py:678
  33.3 18.7 %collective-permute-start.1 = (bf16[64,1536]{1,0:T(8,128)(2,1)S(1)}, bf16[64,1536]{1,0:T(8,128)(2,1)S(1)}, u32[]{:S(2)}, u32[]{:S(2)}) collective-permute-start(bf16[64,1536]{1,0:T(8,128)(2,1)S(1)} %get-tuple-element.235), channel_id=1, source_target_pairs={{0,16},{1,24},{2,32},{3,40},{4,48},{5,56},{6,0},{7,8},{8,17},{9,25... | collective-permute-start | bytes 589832 | tf_op jit(solution)/shard_map/ppermute | solution.py:678
  34.7 24.5 %collective-permute-start.2 = (bf16[64,1536]{1,0:T(8,128)(2,1)S(1)}, bf16[64,1536]{1,0:T(8,128)(2,1)S(1)}, u32[]{:S(2)}, u32[]{:S(2)}) collective-permute-start(bf16[64,1536]{1,0:T(8,128)(2,1)S(1)} %get-tuple-element.234), channel_id=1, source_target_pairs={{0,32},{1,40},{2,48},{3,56},{4,0},{5,8},{6,16},{7,24},{8,33},{9,41... | collective-permute-start | bytes 589832 | tf_op jit(solution)/shard_map/ppermute | solution.py:678
  50.1 25.1 %collective-permute-start.20 = (bf16[192,3072]{1,0:T(8,128)(2,1)S(1)}, bf16[192,3072]{1,0:T(8,128)(2,1)S(1)}, u32[]{:S(2)}, u32[]{:S(2)}) collective-permute-start(bf16[192,3072]{1,0:T(8,128)(2,1)S(1)} %pack_feed.2), channel_id=1, source_target_pairs={{0,1},{2,3},{4,5},{6,7},{9,8},{11,10},{13,12},{15,14},{16,17},{18,... | collective-permute-start | bytes 3538952 | tf_op jit(solution)/shard_map/ppermute | solution.py:785
  80.3 125.5 %all-gather.17.cloned.1.call-start = ((), (), s32[]{:S(2)}) async-start(), calls=%async_computation.10 | async-start | bytes 3981312 | tf_op jit(solution)/shard_map/all_gather | solution.py:802
  151.2 123.8 %all-gather.19.cloned.1.call-start = ((), (), s32[]{:S(2)}) async-start(), calls=%async_computation.11 | async-start | bytes 10616832 | tf_op jit(solution)/shard_map/all_gather | solution.py:802
  198.8 208.8 %reduce-scatter.5.cloned.1.call-start = ((), (), s32[]{:S(2)}) async-start(), calls=%async_computation.4 | async-start | bytes 10616832 | tf_op jit(solution)/shard_map/reduce_scatter | solution.py:905
  288.9 34.1 %collective-permute-start.45 = (bf16[64,1536]{1,0:T(8,128)(2,1)}, bf16[64,1536]{1,0:T(8,128)(2,1)}, u32[]{:S(2)}, u32[]{:S(2)}) collective-permute-start(bf16[64,1536]{1,0:T(8,128)(2,1)} %get-tuple-element.244), channel_id=1, source_target_pairs={{0,16},{16,32},{32,48},{48,0},{1,17},{17,33},{33,49},{49,1},{2,18}... | collective-permute-start | bytes 589832 | tf_op jit(solution)/shard_map/ppermute | solution.py:712
  289.0 36.2 %collective-permute-start.47 = (bf16[64,1536]{1,0:T(8,128)(2,1)}, bf16[64,1536]{1,0:T(8,128)(2,1)}, u32[]{:S(2)}, u32[]{:S(2)}) collective-permute-start(bf16[64,1536]{1,0:T(8,128)(2,1)} %get-tuple-element.245), channel_id=1, source_target_pairs={{0,48},{16,0},{32,16},{48,32},{1,49},{17,1},{33,17},{49,33},{2,50}... | collective-permute-start | bytes 589832 | tf_op jit(solution)/shard_map/ppermute | solution.py:713
  306.7 21.7 %collective-permute-start.49 = (bf16[128,1536]{1,0:T(8,128)(2,1)}, bf16[128,1536]{1,0:T(8,128)(2,1)}, u32[]{:S(2)}, u32[]{:S(2)}) collective-permute-start(bf16[128,1536]{1,0:T(8,128)(2,1)} %get-tuple-element.136), channel_id=1, source_target_pairs={{0,16},{16,32},{32,48},{48,0},{1,17},{17,33},{33,49},{49,1},{2,18}... | collective-permute-start | bytes 1179656 | tf_op jit(solution)/shard_map/ppermute | solution.py:722
  306.7 21.7 %collective-permute-start.50 = (bf16[128,1536]{1,0:T(8,128)(2,1)}, bf16[128,1536]{1,0:T(8,128)(2,1)}, u32[]{:S(2)}, u32[]{:S(2)}) collective-permute-start(bf16[128,1536]{1,0:T(8,128)(2,1)} %get-tuple-element.137), channel_id=1, source_target_pairs={{0,48},{16,0},{32,16},{48,32},{1,49},{17,1},{33,17},{49,33},{2,50}... | collective-permute-start | bytes 1179656 | tf_op jit(solution)/shard_map/ppermute | solution.py:723
  309.3 19.0 %collective-permute-start.51 = (bf16[128,1536]{1,0:T(8,128)(2,1)}, bf16[128,1536]{1,0:T(8,128)(2,1)}, u32[]{:S(2)}, u32[]{:S(2)}) collective-permute-start(bf16[128,1536]{1,0:T(8,128)(2,1)} %get-tuple-element.138), channel_id=1, source_target_pairs={{0,32},{16,48},{32,0},{48,16},{1,33},{17,49},{33,1},{49,17},{2,34}... | collective-permute-start | bytes 1179656 | tf_op jit(solution)/shard_map/ppermute | solution.py:724
  334.0 128.5 %reduce-scatter.7.cloned.1.call-start = ((), (), s32[]{:S(2)}) async-start(), calls=%async_computation.5 | async-start | bytes 3981312 | tf_op jit(solution)/shard_map/reduce_scatter | solution.py:905
  380.4 19.3 %collective-permute-start.58 = (bf16[128,1536]{1,0:T(8,128)(2,1)}, bf16[128,1536]{1,0:T(8,128)(2,1)}, u32[]{:S(2)}, u32[]{:S(2)}) collective-permute-start(bf16[128,1536]{1,0:T(8,128)(2,1)} %get-tuple-element.149), channel_id=1, source_target_pairs={{0,48},{16,0},{32,16},{48,32},{1,49},{17,1},{33,17},{49,33},{2,50}... | collective-permute-start | bytes 1179656 | tf_op jit(solution)/shard_map/ppermute | solution.py:723
  383.0 18.8 %collective-permute-start.59 = (bf16[128,1536]{1,0:T(8,128)(2,1)}, bf16[128,1536]{1,0:T(8,128)(2,1)}, u32[]{:S(2)}, u32[]{:S(2)}) collective-permute-start(bf16[128,1536]{1,0:T(8,128)(2,1)} %get-tuple-element.150), channel_id=1, source_target_pairs={{0,32},{16,48},{32,0},{48,16},{1,33},{17,49},{33,1},{49,17},{2,34}... | collective-permute-start | bytes 1179656 | tf_op jit(solution)/shard_map/ppermute | solution.py:724
  407.6 172.9 %reduce-scatter.11.cloned.1.call-start = ((), (), s32[]{:S(2)}) async-start(), calls=%async_computation.7 | async-start | bytes 4423680 | tf_op jit(solution)/shard_map/reduce_scatter | solution.py:905
  445.1 22.6 %collective-permute-start.64 = (bf16[128,1536]{1,0:T(8,128)(2,1)}, bf16[128,1536]{1,0:T(8,128)(2,1)}, u32[]{:S(2)}, u32[]{:S(2)}) collective-permute-start(bf16[128,1536]{1,0:T(8,128)(2,1)} %get-tuple-element.158), channel_id=1, source_target_pairs={{0,16},{16,32},{32,48},{48,0},{1,17},{17,33},{33,49},{49,1},{2,18}... | collective-permute-start | bytes 1179656 | tf_op jit(solution)/shard_map/ppermute | solution.py:722
  445.8 22.0 %collective-permute-start.65 = (bf16[128,1536]{1,0:T(8,128)(2,1)}, bf16[128,1536]{1,0:T(8,128)(2,1)}, u32[]{:S(2)}, u32[]{:S(2)}) collective-permute-start(bf16[128,1536]{1,0:T(8,128)(2,1)} %get-tuple-element.159), channel_id=1, source_target_pairs={{0,48},{16,0},{32,16},{48,32},{1,49},{17,1},{33,17},{49,33},{2,50}... | collective-permute-start | bytes 1179656 | tf_op jit(solution)/shard_map/ppermute | solution.py:723
  448.6 19.2 %collective-permute-start.66 = (bf16[128,1536]{1,0:T(8,128)(2,1)}, bf16[128,1536]{1,0:T(8,128)(2,1)}, u32[]{:S(2)}, u32[]{:S(2)}) collective-permute-start(bf16[128,1536]{1,0:T(8,128)(2,1)} %get-tuple-element.160), channel_id=1, source_target_pairs={{0,32},{16,48},{32,0},{48,16},{1,33},{17,49},{33,1},{49,17},{2,34}... | collective-permute-start | bytes 1179656 | tf_op jit(solution)/shard_map/ppermute | solution.py:724
  473.6 29.8 %collective-permute-start.68 = (bf16[96,4224]{1,0:T(8,128)(2,1)S(1)}, bf16[96,4224]{1,0:T(8,128)(2,1)S(1)}, u32[]{:S(2)}, u32[]{:S(2)}) collective-permute-start(bf16[96,4224]{1,0:T(8,128)(2,1)S(1)} %broadcast_select_fusion.2), channel_id=1, source_target_pairs={{0,1},{1,0},{2,3},{3,2},{4,5},{5,4},{6,7},{7,6},{8,9},{9,8},{10,11... | collective-permute-start | bytes 2433032 | tf_op jit(solution)/shard_map/ppermute | solution.py:747
  510.5 19.7 %collective-permute-start.75 = (bf16[128,1536]{1,0:T(8,128)(2,1)}, bf16[128,1536]{1,0:T(8,128)(2,1)}, u32[]{:S(2)}, u32[]{:S(2)}) collective-permute-start(bf16[128,1536]{1,0:T(8,128)(2,1)} %get-tuple-element.172), channel_id=1, source_target_pairs={{0,48},{16,0},{32,16},{48,32},{1,49},{17,1},{33,17},{49,33},{2,50}... | collective-permute-start | bytes 1179656 | tf_op jit(solution)/shard_map/ppermute | solution.py:723
  537.9 103.6 %reduce-scatter.9.cloned.1.call-start = ((), (), s32[]{:S(2)}) async-start(), calls=%async_computation.6 | async-start | bytes 10616832 | tf_op jit(solution)/shard_map/reduce_scatter | solution.py:905
  538.7 187.3 %all-gather.23.cloned.1.call-start = ((), (), s32[]{:S(2)}) async-start(), calls=%async_computation.13 | async-start | bytes 7299072 | tf_op jit(solution)/shard_map/all_gather | solution.py:929
  558.9 195.0 %all-gather.21.cloned.1.call-start = ((), (), s32[]{:S(2)}) async-start(), calls=%async_computation.12 | async-start | bytes 7520256 | tf_op jit(solution)/shard_map/all_gather | solution.py:933
  581.5 62.7 %collective-permute-start.84 = (bf16[96,1280]{1,0:T(8,128)(2,1)S(1)}, bf16[96,1280]{1,0:T(8,128)(2,1)S(1)}, u32[]{:S(2)}, u32[]{:S(2)}) collective-permute-start(bf16[96,1280]{1,0:T(8,128)(2,1)S(1)} %dynamic-slice_bitcast_fusion.1), channel_id=1, source_target_pairs={{0,8},{8,0},{1,9},{9,1},{2,10},{10,2},{3,11},{11,3},{4,12},{12,4},... | collective-permute-start | bytes 737288 | tf_op jit(solution)/shard_map/ppermute | solution.py:743
  647.3 18.8 %collective-permute-start.82 = (bf16[96,3072]{1,0:T(8,128)(2,1)S(1)}, bf16[96,3072]{1,0:T(8,128)(2,1)S(1)}, u32[]{:S(2)}, u32[]{:S(2)}) collective-permute-start(bf16[96,3072]{1,0:T(8,128)(2,1)S(1)} %bitcast_select_fusion), channel_id=1, source_target_pairs={{0,1},{1,0},{2,3},{3,2},{4,5},{5,4},{6,7},{7,6},{8,9},{9,8},{10,11... | collective-permute-start | bytes 1769480 | tf_op jit(solution)/shard_map/ppermute | solution.py:747
  685.5 38.7 %collective-permute-start.80 = (bf16[64,1536]{1,0:T(8,128)(2,1)S(1)}, bf16[64,1536]{1,0:T(8,128)(2,1)S(1)}, u32[]{:S(2)}, u32[]{:S(2)}) collective-permute-start(bf16[64,1536]{1,0:T(8,128)(2,1)S(1)} %pad_maximum_fusion.18), channel_id=1, source_target_pairs={{48,0},{56,1},{0,2},{8,3},{16,4},{24,5},{32,6},{40,7},{49,8},{57,9... | collective-permute-start | bytes 589832 | tf_op jit(solution)/shard_map/ppermute | solution.py:686
  687.2 36.9 %collective-permute-start.79 = (bf16[64,1536]{1,0:T(8,128)(2,1)S(1)}, bf16[64,1536]{1,0:T(8,128)(2,1)S(1)}, u32[]{:S(2)}, u32[]{:S(2)}) collective-permute-start(bf16[64,1536]{1,0:T(8,128)(2,1)S(1)} %pad_maximum_fusion.17), channel_id=1, source_target_pairs={{32,0},{40,1},{48,2},{56,3},{0,4},{8,5},{16,6},{24,7},{33,8},{41,9... | collective-permute-start | bytes 589832 | tf_op jit(solution)/shard_map/ppermute | solution.py:686
  691.6 28.1 %collective-permute-start.77 = (bf16[64,1536]{1,0:T(8,128)(2,1)S(1)}, bf16[64,1536]{1,0:T(8,128)(2,1)S(1)}, u32[]{:S(2)}, u32[]{:S(2)}) collective-permute-start(bf16[64,1536]{1,0:T(8,128)(2,1)S(1)} %pad_maximum_fusion.15), channel_id=1, source_target_pairs={{0,0},{8,1},{16,2},{24,3},{32,4},{40,5},{48,6},{56,7},{1,8},{9,9},... | collective-permute-start | bytes 589832 | tf_op jit(solution)/shard_map/ppermute | solution.py:686
  696.4 27.7 %collective-permute-start.78 = (bf16[64,1536]{1,0:T(8,128)(2,1)S(1)}, bf16[64,1536]{1,0:T(8,128)(2,1)S(1)}, u32[]{:S(2)}, u32[]{:S(2)}) collective-permute-start(bf16[64,1536]{1,0:T(8,128)(2,1)S(1)} %pad_maximum_fusion.16), channel_id=1, source_target_pairs={{16,0},{24,1},{32,2},{40,3},{48,4},{56,5},{0,6},{8,7},{17,8},{25,9... | collective-permute-start | bytes 589832 | tf_op jit(solution)/shard_map/ppermute | solution.py:686
  (226 other events, 2062.0 us)
Sparse Core Ops, SparseCore 0:
  26.4 45.1 all-gather.12
  80.4 51.0 all-gather.14
  151.3 33.0 all-gather.16
  198.9 66.0 all-gather.18
  334.1 73.3 reduce-scatter.4
  409.9 37.6 reduce-scatter.6
  538.1 42.4 reduce-scatter.10
  583.1 58.4 reduce-scatter.8
  644.0 45.4 all-gather.22
  691.6 62.1 all-gather.20

commit v12 on v11

--- a/solution.py
+++ b/solution.py
@@ -902,7 +902,7 @@
         return grad, attend_weights_call(flats, pieces, low, mixed)
 
     def scatter(block):
-        return lax.psum_scatter(block, SPREAD, scatter_dimension=0, tiled=True)[0]
+        return lax.psum_scatter(block, SPREAD, scatter_dimension=0, tiled=True)
 
     grad, feed_grad = feed_back(1, grad, grad_pieces, ())
     low = tie(grad.astype(BF16), feed_grad)
@@ -914,21 +914,21 @@
     grad, feed_grad = feed_back(0, grad, ring_gather(low), (second_feed,))
     low = tie(grad.astype(BF16), feed_grad)
     first_feed = scatter(tie(feed_grad, low, second_attn))
-    second = yhi_sum(jnp.concatenate([second_feed, second_attn], axis=1), core, yhi)
+    second = yhi_sum(jnp.concatenate([second_feed, second_attn], axis=2)[0], core, yhi)
     grad, attn_grad = attention_back(0, grad, ring_gather(low), (), (second,))
     low = grad.astype(BF16)
     attn_grad = tie(attn_grad, first_feed, low)
     attn_grad = jnp.concatenate([attn_grad, gain_rows(jnp.stack(gain_grads))], axis=2)
     first_attn = scatter(attn_grad)
     second_piece = cross(ylo_sum(second), 3072, first_attn)
-    feed_piece = ylo_sum(yhi_sum(first_feed, core, yhi))
+    feed_piece = ylo_sum(yhi_sum(first_feed[0], core, yhi))
     back = from_lines(interleave(last_rows, low), z)
     output, input_grad = separate(back)
     output, input_grad = output[None], input_grad.astype(F32)[None]
 
     every = lax.all_gather(second_piece, ("x", "core"), axis=0, tiled=False)
     results[10:14], results[15:18] = unpack_call(every.reshape(4, 2, 96, -1))
-    attn_piece = ylo_sum(yhi_sum(first_attn, core, yhi))
+    attn_piece = ylo_sum(yhi_sum(tie(first_attn, feed_piece)[0], core, yhi))
     first_piece = jnp.concatenate([feed_piece, cross(attn_piece, 0)], axis=1)
     every = lax.all_gather(first_piece, ("x", "core"), axis=0, tiled=False)
     every = every.reshape(4, 2, 96, -1)

time: 780 us -> 738 us (0.946)
  waiting for transfers between devices: 311 us -> 257 us
  starting transfers between devices: 189 us -> 201 us
    reduce_scatter x4, waiting for transfers between devices: 80.8 us -> 24.4 us  [scatter(): return lax.psum_scatter(block, SPREAD, scatter_dimension=0, tiled=True)]
    ppermute x4, starting transfers between devices: 12.6 us -> 24.4 us  [from_lines(): lax.ppermute(block[part * k:part * (k + 1)], AXES, inverse(LINES[k]))]
    ppermute x4, waiting for transfers between devices: 25.9 us -> 17.5 us  [from_lines(): lax.ppermute(block[part * k:part * (k + 1)], AXES, inverse(LINES[k]))]
    unnamed x330 -> x325, local copies, waits for them, and re-layouts: 41.4 us -> 40.4 us
  transfers between devices with their start and end apart: 100 -> 100, of which waited for: 49 -> 47; matrix products, arithmetic and copies ran while one was open for 7% -> 7% of each run, Pallas kernels for 17% -> 18%
where the time goes in v12:
time: 738 us; the launch traced here: 729 us
  waiting for transfers between devices  257 us (35%)
  starting transfers between devices  201 us (27%)
  Pallas kernels  147 us (20%)
  local copies, waits for them, and re-layouts  61.4 us (8%)
  other arithmetic  43.9 us (6%)
  between operations  18 us (2%)
    ppermute x8, waiting for transfers between devices, ring_gather(): from_left = lax.ppermute(block, 'x', RIGHT)  43.8 us
    unnamed x325, local copies, waits for them, and re-layouts  40.4 us
    ppermute x3, waiting for transfers between devices, ylo_sum(): return add_low(piece, lax.ppermute(piece, 'ylo', SWAP))  34.6 us
    pallas_call x2, Pallas kernels, feed_backward_call(): pl.pallas_call(later(feed_backward_kernel, len(after)), grid=(4,), in_spe...  27.4 us
    pallas_call x2, Pallas kernels, attend_backward_call(): pl.pallas_call(later(functools.partial(attend_backward_kernel, window), l...  27.1 us
    reduce_scatter x4, waiting for transfers between devices, scatter(): return lax.psum_scatter(block, SPREAD, scatter_dimension=0, tiled=True)  24.4 us
    ppermute x4, starting transfers between devices, from_lines(): lax.ppermute(block[part * k:part * (k + 1)], AXES, inverse(LINES[k]))  24.4 us
    ppermute x8, waiting for transfers between devices, ring_gather(): far_first = lax.ppermute(from_left[:half], 'x', RIGHT)  24.4 us
  transfers between devices with their start and end apart: 100, of which 47 were waited for; matrix products, arithmetic and copies ran while one was open for 7% of the time, Pallas kernels for 18%

profile of v12, /device:TPU:1, one launch (start us, length us, event | category | flops | bytes accessed | tf_op | source)
XLA Modules:
  0.0 728.6 jit_solution(8411499922830124090)
XLA Ops:
  26.7 6.6 collective-permute-start
  34.7 10.0 %collective-permute-start.2 = (bf16[64,1536]{1,0:T(8,128)(2,1)S(1)}, bf16[64,1536]{1,0:T(8,128)(2,1)S(1)}, u32[]{:S(2)}, u32[]{:S(2)}) collective-permute-start(bf16[64,1536]{1,0:T(8,128)(2,1)S(1)} %get-tuple-element.236), channel_id=1, source_target_pairs={{0,32},{1,40},{2,48},{3,56},{4,0},{5,8},{6,16},{7,24},{8,33},{9,41... | collective-permute-start | bytes 589832 | tf_op jit(solution)/shard_map/ppermute | solution.py:678
  63.9 8.2 %collective-permute-done.5.refs_1_ = bf16[128,1536]{1,0:T(8,128)(2,1)S(1)} collective-permute-done((bf16[128,1536]{1,0:T(8,128)(2,1)S(1)}, bf16[128,1536]{1,0:T(8,128)(2,1)S(1)}, u32[]{:S(2)}, u32[]{:S(2)}) %collective-permute-start.5) | collective-permute-done | bytes 393248 | tf_op jit(solution)/shard_map/ppermute | solution.py:703
  99.5 9.1 %attend.2 = (f32[128,1536]{1,0:T(8,128)S(1)}, f32[128,1536]{1,0:T(8,128)S(1)}, f32[128,1536]{1,0:T(8,128)S(1)}, bf16[128,1536]{1,0:T(8,128)(2,1)S(1)}, bf16[512,...) custom-call(s32[1]{0:T(128)} %collective-permute-done.4.length.refs_2_.refs_1_, ...), custom_call_target="tpu_custom_call" | custom-call | flops 3000000000 | bytes 6000000 | tf_op jit(solution)/shard_map/attend/pallas_call | solution.py:380
  121.5 6.9 collective-permute-start.34
  138.3 11.2 %collective-permute-done.16.refs_1_ = bf16[128,1536]{1,0:T(8,128)(2,1)S(1)} collective-permute-done((bf16[128,1536]{1,0:T(8,128)(2,1)S(1)}, bf16[128,1536]{1,0:T(8,128)(2,1)S(1)}, u32[]{:S(2)}, u32[]{:S(2)}) %collective-permute-start.16) | collective-permute-done | bytes 393248 | tf_op jit(solution)/shard_map/ppermute | solution.py:703
  156.3 9.3 %feed_forward.2 = (f32[128,1536]{1,0:T(8,128)S(1)}, f32[128,1536]{1,0:T(8,128)S(1)}, f32[128,1536]{1,0:T(8,128)S(1)}, bf16[128,1536]{1,0:T(8,128)(2,1)S(1)}, f32...) custom-call(bf16[128,1536]{1,0:T(8,128)(2,1)S(1)} %multiply_convert_fusion.2.refs_0_, ...), custom_call_target="tpu_custom_call" | custom-call | flops 4899999744 | bytes 18000000 | tf_op jit(solution)/shard_map/feed_forward/pallas_call | solution.py:138
  179.3 7.5 %collective-permute-done.44 = bf16[192,3072]{1,0:T(8,128)(2,1)} collective-permute-done((bf16[192,3072]{1,0:T(8,128)(2,1)S(1)}, bf16[192,3072]{1,0:T(8,128)(2,1)}, u32[]{:S(2)}, u32[]{:S(2)}) %collective-permute-start.44) | collective-permute-done | bytes 1179680 | tf_op jit(solution)/shard_map/ppermute | solution.py:785
  209.9 7.6 %collective-permute-start.35 = (bf16[512,384]{1,0:T(8,128)(2,1)S(1)}, bf16[512,384]{1,0:T(8,128)(2,1)S(1)}, u32[]{:S(2)}, u32[]{:S(2)}) collective-permute-start(bf16[512,384]{1,0:T(8,128)(2,1)S(1)} %get-tuple-element.124.refs_4_.refs_8_), channel_id=1, source_target_pairs={{0,8},{8,0},{1,9},{9,1},{2,10},{10,2},{3,11},{11,3},{4,12},{12,4},... | collective-permute-start | bytes 1179656 | tf_op jit(solution)/shard_map/ppermute | solution.py:856
  225.6 9.1 %attend.3 = (f32[128,1536]{1,0:T(8,128)S(1)}, f32[128,1536]{1,0:T(8,128)S(1)}, f32[128,1536]{1,0:T(8,128)S(1)}, bf16[128,1536]{1,0:T(8,128)(2,1)S(1)}, bf16[512,...) custom-call(bf16[64,1536]{1,0:T(8,128)(2,1)S(1)} %collective-permute-done.26.refs_0_.refs_3_.refs_8_, ...), custom_call_target="tpu_custom_call" | custom-call | flops 3000000000 | bytes 6000000 | tf_op jit(solution)/shard_map/attend/pallas_call | solution.py:380
  246.0 6.9 collective-permute-done.37
  258.4 6.8 collective-permute-done.40.refs_1_
  275.2 9.2 %feed_forward.3 = (f32[128,1536]{1,0:T(8,128)S(1)}, f32[128,1536]{1,0:T(8,128)S(1)}, f32[128,1536]{1,0:T(8,128)S(1)}, bf16[128,1536]{1,0:T(8,128)(2,1)S(1)}, f32...) custom-call(bf16[128,1536]{1,0:T(8,128)(2,1)S(1)} %multiply_convert_fusion.refs_0_, ...), custom_call_target="tpu_custom_call" | custom-call | flops 4899999744 | bytes 18000000 | tf_op jit(solution)/shard_map/feed_forward/pallas_call | solution.py:138
  290.2 13.6 %feed_backward.2 = (f32[128,1536]{1,0:T(8,128)S(1)}, bf16[128,1536]{1,0:T(8,128)(2,1)}, bf16[128,1536]{1,0:T(8,128)(2,1)}, bf16[128,1536]{1,0:T(8,128)(2,1)}, bf...) custom-call(bf16[128,1536]{1,0:T(8,128)(2,1)S(1)} %pad_maximum_fusion.9.refs_0_.refs_5_, ...), custom_call_target="tpu_custom_call" | custom-call | flops 4899999744 | bytes 20000000 | tf_op jit(solution)/shard_map/feed_backward/pallas_call | solution.py:191
  307.4 11.5 %feed_weights.2 = bf16[8,192,3072]{2,1,0:T(8,128)(2,1)} custom-call(bf16[128,1536]{1,0:T(8,128)(2,1)S(1)} %multiply_convert_fusion.refs_0_, bf16[128,1536]{1,0:T(8,128)(2,1)S(1)} %copy-done.41, bf16[128,1536]{1,0:T(8,128)(2,1)S(1)} %copy-done.44, bf16[64,1536]{1,0:T(8,128)(2,1)S(1)} %collective-permute-done.42.refs_3_, bf16[64,1536]{1,0:T(8,128)(2,1)S(1)} %copy-done.86, ...), custom_call_target="tpu_custom_call" | custom-call | flops 4899999744 | bytes 18000000 | tf_op jit(solution)/shard_map/feed_weights/pallas_call | solution.py:244
  349.6 13.4 %attend_backward.2 = (bf16[512,384]{1,0:T(8,128)(2,1)S(1)}, f32[512,384]{1,0:T(8,128)}, bf16[512,384]{1,0:T(8,128)(2,1)S(1)}) custom-call(bf16[128,1536]{1,0:T(8,128)(2,1)S(1)} %get-tuple-element.233.refs_0_, s32[1]{0:T(128)} %collective-permute-done.4.length.refs_2_.refs_1_, bf16[128,1536]{1,0:T(8,128)(2,1)} %copy-done.29, bf16[128,1536]{1,0:T(8,128)(2,1)} %copy-done.49, ...), custom_call_target="tpu_custom_call" | custom-call | flops 6000000000 | bytes 6000000 | tf_op jit(solution)/shard_map/attend_backward/pallas_call | solution.py:455
  363.0 9.7 %collective-permute-start.56 = (bf16[512,384]{1,0:T(8,128)(2,1)S(1)}, bf16[512,384]{1,0:T(8,128)(2,1)S(1)}, u32[]{:S(2)}, u32[]{:S(2)}) collective-permute-start(bf16[512,384]{1,0:T(8,128)(2,1)S(1)} %get-tuple-element.147), channel_id=1, source_target_pairs={{0,8},{8,0},{1,9},{9,1},{2,10},{10,2},{3,11},{11,3},{4,12},{12,4},... | collective-permute-start | bytes 1179656 | tf_op jit(solution)/shard_map/ppermute | solution.py:896
  390.8 7.2 collective-permute-done.58
  408.4 7.8 %collective-permute-done.60.refs_2_.refs_6_ = bf16[128,1536]{1,0:T(8,128)(2,1)S(1)} collective-permute-done((bf16[128,1536]{1,0:T(8,128)(2,1)S(1)}, bf16[128,1536]{1,0:T(8,128)(2,1)S(1)}, u32[]{:S(2)}, u32[]{:S(2)}) %collective-permute-start.60) | collective-permute-done | bytes 393248 | tf_op jit(solution)/shard_map/ppermute | solution.py:703
  425.2 13.8 %feed_backward.3 = (f32[128,1536]{1,0:T(8,128)S(1)}, bf16[128,1536]{1,0:T(8,128)(2,1)}, bf16[128,1536]{1,0:T(8,128)(2,1)}, bf16[128,1536]{1,0:T(8,128)(2,1)}, bf...) custom-call(bf16[1,192,3072]{2,1,0:T(8,128)(2,1)S(1)} %copy-done.8, ...), custom_call_target="tpu_custom_call" | custom-call | flops 4899999744 | bytes 20000000 | tf_op jit(solution)/shard_map/feed_backward/pallas_call | solution.py:191
  444.0 11.7 %feed_weights.3 = bf16[8,192,3072]{2,1,0:T(8,128)(2,1)} custom-call(bf16[128,1536]{1,0:T(8,128)(2,1)S(1)} %copy-done.16, bf16[128,1536]{1,0:T(8,128)(2,1)S(1)} %copy-done.34, bf16[128,1536]{1,0:T(8,128)(2,1)S(1)} %copy-done.36, bf16[64,1536]{1,0:T(8,128)(2,1)S(1)} %copy-done.77, bf16[64,1536]{1,0:T(8,128)(2,1)S(1)} %copy-done.79, ...), custom_call_target="tpu_custom_call" | custom-call | flops 4899999744 | bytes 18000000 | tf_op jit(solution)/shard_map/feed_weights/pallas_call | solution.py:244
  488.4 13.7 %attend_backward.3 = (bf16[512,384]{1,0:T(8,128)(2,1)S(1)}, f32[512,384]{1,0:T(8,128)}, bf16[512,384]{1,0:T(8,128)(2,1)S(1)}) custom-call(s32[1]{0:T(128)} %collective-permute-done.4.length.refs_2_.refs_1_, bf16[128,1536]{1,0:T(8,128)(2,1)S(1)} %get-tuple-element.166.refs_0_.refs_1_, bf16[128,1536]{1,0:T(8,128)(2,1)} %copy-done.45, ...), custom_call_target="tpu_custom_call" | custom-call | flops 6000000000 | bytes 6000000 | tf_op jit(solution)/shard_map/attend_backward/pallas_call | solution.py:455
  523.0 6.7 collective-permute-done.75
  539.8 17.4 %collective-permute-done.88 = bf16[96,4224]{1,0:T(8,128)(2,1)S(1)} collective-permute-done((bf16[96,4224]{1,0:T(8,128)(2,1)S(1)}, bf16[96,4224]{1,0:T(8,128)(2,1)S(1)}, u32[]{:S(2)}, u32[]{:S(2)}) %collective-permute-start.88) | collective-permute-done | bytes 811040 | tf_op jit(solution)/shard_map/ppermute | solution.py:751
  558.2 22.5 %reduce-scatter.11.cloned.1.call-done = bf16[1,192,1280]{2,1,0:T(8,128)(2,1)} async-done(((bf16[8,192,1280]{2,1,0:T(8,128)(2,1)}), bf16[1,192,1280]{2,1,0:T(8,128)(2,1)}) %reduce-scatter.11.cloned.1.call-update) | async-done | bytes 491536 | tf_op jit(solution)/shard_map/reduce_scatter | solution.py:905
  588.5 14.0 %collective-permute-done.82 = bf16[96,3072]{1,0:T(8,128)(2,1)S(1)} collective-permute-done((bf16[96,3072]{1,0:T(8,128)(2,1)S(1)}, bf16[96,3072]{1,0:T(8,128)(2,1)S(1)}, u32[]{:S(2)}, u32[]{:S(2)}) %collective-permute-start.82) | collective-permute-done | bytes 589856 | tf_op jit(solution)/shard_map/ppermute | solution.py:747
  604.3 12.4 %collective-permute-done.83 = bf16[96,3072]{1,0:T(8,128)(2,1)S(1)} collective-permute-done((bf16[96,3072]{1,0:T(8,128)(2,1)S(1)}, bf16[96,3072]{1,0:T(8,128)(2,1)S(1)}, u32[]{:S(2)}, u32[]{:S(2)}) %collective-permute-start.83) | collective-permute-done | bytes 589856 | tf_op jit(solution)/shard_map/ppermute | solution.py:751
  637.3 10.5 %collective-permute-start.80 = (bf16[64,1536]{1,0:T(8,128)(2,1)S(1)}, bf16[64,1536]{1,0:T(8,128)(2,1)S(1)}, u32[]{:S(2)}, u32[]{:S(2)}) collective-permute-start(bf16[64,1536]{1,0:T(8,128)(2,1)S(1)} %pad_maximum_fusion.18), channel_id=1, source_target_pairs={{48,0},{56,1},{0,2},{8,3},{16,4},{24,5},{32,6},{40,7},{49,8},{57,9... | collective-permute-start | bytes 589832 | tf_op jit(solution)/shard_map/ppermute | solution.py:686
  661.8 11.4 %collective-permute-done.77 = bf16[64,1536]{1,0:T(8,128)(2,1)S(1)} collective-permute-done((bf16[64,1536]{1,0:T(8,128)(2,1)S(1)}, bf16[64,1536]{1,0:T(8,128)(2,1)S(1)}, u32[]{:S(2)}, u32[]{:S(2)}) %collective-permute-start.77) | collective-permute-done | bytes 196640 | tf_op jit(solution)/shard_map/ppermute | solution.py:686
  681.3 7.4 %unpack.3 = (f32[192,1536]{1,0:T(8,128)}, f32[192,768]{1,0:T(8,128)}, f32[192,768]{1,0:T(8,128)}, f32[192,1536]{1,0:T(8,128)}, f32[192,4096]{1,0:T(8,128)}, /*in...) custom-call(bf16[4,2,96,4224]{3,2,1,0:T(8,128)(2,1)} %bitcast.81), custom_call_target="tpu_custom_call" | custom-call | flops 1000000 | bytes 30000000 | tf_op jit(solution)/shard_map/unpack/pallas_call | solution.py:577
  688.7 23.5 %all-gather.21.cloned.1.call-done = bf16[768,4352]{1,0:T(8,128)(2,1)} async-done(((bf16[96,4352]{1,0:T(8,128)(2,1)}), bf16[768,4352]{1,0:T(8,128)(2,1)}) %all-gather.21.cloned.1.call-update) | async-done | bytes 6684688 | tf_op jit(solution)/shard_map/all_gather | solution.py:933
  712.2 7.5 %unpack.2 = (f32[192,1536]{1,0:T(8,128)}, f32[192,768]{1,0:T(8,128)}, f32[192,768]{1,0:T(8,128)}, f32[192,1536]{1,0:T(8,128)}, f32[192,4096]{1,0:T(8,128)}, /*in...) custom-call(bf16[4,2,96,4352]{3,2,1,0:T(8,128)(2,1)} %bitcast.79), custom_call_target="tpu_custom_call" | custom-call | flops 1000000 | bytes 30000000 | tf_op jit(solution)/shard_map/unpack/pallas_call | solution.py:577
  (701 shorter events, 366.3 us)
Async XLA Ops:
  7.2 77.5 %all-gather.13.cloned.1.call-start = ((), (), s32[]{:S(2)}) async-start(), calls=%async_computation.8 | async-start | bytes 4423680 | tf_op jit(solution)/shard_map/all_gather | solution.py:802
  26.3 129.9 %all-gather.15.cloned.1.call-start = ((), (), s32[]{:S(2)}) async-start(), calls=%async_computation.9 | async-start | bytes 10616832 | tf_op jit(solution)/shard_map/all_gather | solution.py:802
  26.7 24.7 %collective-permute-start = (bf16[64,1536]{1,0:T(8,128)(2,1)S(1)}, bf16[64,1536]{1,0:T(8,128)(2,1)S(1)}, u32[]{:S(2)}, u32[]{:S(2)}) collective-permute-start(bf16[64,1536]{1,0:T(8,128)(2,1)S(1)} %get-tuple-element.234), channel_id=1, source_target_pairs={{0,0},{1,8},{2,16},{3,24},{4,32},{5,40},{6,48},{7,56},{8,1},{9,9},... | collective-permute-start | bytes 589832 | tf_op jit(solution)/shard_map/ppermute | solution.py:678
  33.3 18.7 %collective-permute-start.1 = (bf16[64,1536]{1,0:T(8,128)(2,1)S(1)}, bf16[64,1536]{1,0:T(8,128)(2,1)S(1)}, u32[]{:S(2)}, u32[]{:S(2)}) collective-permute-start(bf16[64,1536]{1,0:T(8,128)(2,1)S(1)} %get-tuple-element.237), channel_id=1, source_target_pairs={{0,16},{1,24},{2,32},{3,40},{4,48},{5,56},{6,0},{7,8},{8,17},{9,25... | collective-permute-start | bytes 589832 | tf_op jit(solution)/shard_map/ppermute | solution.py:678
  34.7 24.5 %collective-permute-start.2 = (bf16[64,1536]{1,0:T(8,128)(2,1)S(1)}, bf16[64,1536]{1,0:T(8,128)(2,1)S(1)}, u32[]{:S(2)}, u32[]{:S(2)}) collective-permute-start(bf16[64,1536]{1,0:T(8,128)(2,1)S(1)} %get-tuple-element.236), channel_id=1, source_target_pairs={{0,32},{1,40},{2,48},{3,56},{4,0},{5,8},{6,16},{7,24},{8,33},{9,41... | collective-permute-start | bytes 589832 | tf_op jit(solution)/shard_map/ppermute | solution.py:678
  50.1 25.1 %collective-permute-start.20 = (bf16[192,3072]{1,0:T(8,128)(2,1)S(1)}, bf16[192,3072]{1,0:T(8,128)(2,1)S(1)}, u32[]{:S(2)}, u32[]{:S(2)}) collective-permute-start(bf16[192,3072]{1,0:T(8,128)(2,1)S(1)} %pack_feed.2), channel_id=1, source_target_pairs={{0,1},{2,3},{4,5},{6,7},{9,8},{11,10},{13,12},{15,14},{16,17},{18,... | collective-permute-start | bytes 3538952 | tf_op jit(solution)/shard_map/ppermute | solution.py:785
  80.3 123.8 %all-gather.17.cloned.1.call-start = ((), (), s32[]{:S(2)}) async-start(), calls=%async_computation.10 | async-start | bytes 3981312 | tf_op jit(solution)/shard_map/all_gather | solution.py:802
  130.7 18.7 %collective-permute-start.16 = (bf16[128,1536]{1,0:T(8,128)(2,1)S(1)}, bf16[128,1536]{1,0:T(8,128)(2,1)S(1)}, u32[]{:S(2)}, u32[]{:S(2)}) collective-permute-start(bf16[128,1536]{1,0:T(8,128)(2,1)S(1)} %multiply_convert_fusion.2.refs_0_), channel_id=1, source_target_pairs={{0,16},{16,32},{32,48},{48,0},{1,17},{17,33},{33,49},{49,1},{2,18}... | collective-permute-start | bytes 1179656 | tf_op jit(solution)/shard_map/ppermute | solution.py:703
  130.7 18.7 %collective-permute-start.17 = (bf16[128,1536]{1,0:T(8,128)(2,1)S(1)}, bf16[128,1536]{1,0:T(8,128)(2,1)S(1)}, u32[]{:S(2)}, u32[]{:S(2)}) collective-permute-start(bf16[128,1536]{1,0:T(8,128)(2,1)S(1)} %multiply_convert_fusion.2.refs_0_), channel_id=1, source_target_pairs={{0,48},{16,0},{32,16},{48,32},{1,49},{17,1},{33,17},{49,33},{2,50}... | collective-permute-start | bytes 1179656 | tf_op jit(solution)/shard_map/ppermute | solution.py:704
  149.5 122.7 %all-gather.19.cloned.1.call-start = ((), (), s32[]{:S(2)}) async-start(), calls=%async_computation.11 | async-start | bytes 10616832 | tf_op jit(solution)/shard_map/all_gather | solution.py:802
  168.3 18.5 %collective-permute-start.44 = (bf16[192,3072]{1,0:T(8,128)(2,1)S(1)}, bf16[192,3072]{1,0:T(8,128)(2,1)}, u32[]{:S(2)}, u32[]{:S(2)}) collective-permute-start(bf16[192,3072]{1,0:T(8,128)(2,1)S(1)} %pack_feed.3), channel_id=1, source_target_pairs={{0,1},{2,3},{4,5},{6,7},{9,8},{11,10},{13,12},{15,14},{16,17},{18,... | collective-permute-start | bytes 3538952 | tf_op jit(solution)/shard_map/ppermute | solution.py:785
  197.1 208.4 %reduce-scatter.5.cloned.1.call-start = ((), (), s32[]{:S(2)}) async-start(), calls=%async_computation.4 | async-start | bytes 10616832 | tf_op jit(solution)/shard_map/reduce_scatter | solution.py:905
  287.0 34.1 %collective-permute-start.45 = (bf16[64,1536]{1,0:T(8,128)(2,1)}, bf16[64,1536]{1,0:T(8,128)(2,1)}, u32[]{:S(2)}, u32[]{:S(2)}) collective-permute-start(bf16[64,1536]{1,0:T(8,128)(2,1)} %get-tuple-element.246), channel_id=1, source_target_pairs={{0,16},{16,32},{32,48},{48,0},{1,17},{17,33},{33,49},{49,1},{2,18}... | collective-permute-start | bytes 589832 | tf_op jit(solution)/shard_map/ppermute | solution.py:712
  287.1 36.1 %collective-permute-start.47 = (bf16[64,1536]{1,0:T(8,128)(2,1)}, bf16[64,1536]{1,0:T(8,128)(2,1)}, u32[]{:S(2)}, u32[]{:S(2)}) collective-permute-start(bf16[64,1536]{1,0:T(8,128)(2,1)} %get-tuple-element.247), channel_id=1, source_target_pairs={{0,48},{16,0},{32,16},{48,32},{1,49},{17,1},{33,17},{49,33},{2,50}... | collective-permute-start | bytes 589832 | tf_op jit(solution)/shard_map/ppermute | solution.py:713
  304.7 21.7 %collective-permute-start.49 = (bf16[128,1536]{1,0:T(8,128)(2,1)}, bf16[128,1536]{1,0:T(8,128)(2,1)}, u32[]{:S(2)}, u32[]{:S(2)}) collective-permute-start(bf16[128,1536]{1,0:T(8,128)(2,1)} %get-tuple-element.137), channel_id=1, source_target_pairs={{0,16},{16,32},{32,48},{48,0},{1,17},{17,33},{33,49},{49,1},{2,18}... | collective-permute-start | bytes 1179656 | tf_op jit(solution)/shard_map/ppermute | solution.py:722
  304.7 21.7 %collective-permute-start.50 = (bf16[128,1536]{1,0:T(8,128)(2,1)}, bf16[128,1536]{1,0:T(8,128)(2,1)}, u32[]{:S(2)}, u32[]{:S(2)}) collective-permute-start(bf16[128,1536]{1,0:T(8,128)(2,1)} %get-tuple-element.138), channel_id=1, source_target_pairs={{0,48},{16,0},{32,16},{48,32},{1,49},{17,1},{33,17},{49,33},{2,50}... | collective-permute-start | bytes 1179656 | tf_op jit(solution)/shard_map/ppermute | solution.py:723
  307.4 19.0 %collective-permute-start.51 = (bf16[128,1536]{1,0:T(8,128)(2,1)}, bf16[128,1536]{1,0:T(8,128)(2,1)}, u32[]{:S(2)}, u32[]{:S(2)}) collective-permute-start(bf16[128,1536]{1,0:T(8,128)(2,1)} %get-tuple-element.139), channel_id=1, source_target_pairs={{0,32},{16,48},{32,0},{48,16},{1,33},{17,49},{33,1},{49,17},{2,34}... | collective-permute-start | bytes 1179656 | tf_op jit(solution)/shard_map/ppermute | solution.py:724
  332.0 129.0 %reduce-scatter.7.cloned.1.call-start = ((), (), s32[]{:S(2)}) async-start(), calls=%async_computation.5 | async-start | bytes 3981312 | tf_op jit(solution)/shard_map/reduce_scatter | solution.py:905
  378.5 19.6 %collective-permute-start.58 = (bf16[128,1536]{1,0:T(8,128)(2,1)}, bf16[128,1536]{1,0:T(8,128)(2,1)}, u32[]{:S(2)}, u32[]{:S(2)}) collective-permute-start(bf16[128,1536]{1,0:T(8,128)(2,1)} %get-tuple-element.150), channel_id=1, source_target_pairs={{0,48},{16,0},{32,16},{48,32},{1,49},{17,1},{33,17},{49,33},{2,50}... | collective-permute-start | bytes 1179656 | tf_op jit(solution)/shard_map/ppermute | solution.py:723
  381.3 18.8 %collective-permute-start.59 = (bf16[128,1536]{1,0:T(8,128)(2,1)S(1)}, bf16[128,1536]{1,0:T(8,128)(2,1)}, u32[]{:S(2)}, u32[]{:S(2)}) collective-permute-start(bf16[128,1536]{1,0:T(8,128)(2,1)S(1)} %get-tuple-element.151), channel_id=1, source_target_pairs={{0,32},{16,48},{32,0},{48,16},{1,33},{17,49},{33,1},{49,17},{2,34}... | collective-permute-start | bytes 1179656 | tf_op jit(solution)/shard_map/ppermute | solution.py:724
  405.6 129.3 %reduce-scatter.9.cloned.1.call-start = ((), (), s32[]{:S(2)}) async-start(), calls=%async_computation.6 | async-start | bytes 10616832 | tf_op jit(solution)/shard_map/reduce_scatter | solution.py:905
  461.0 119.7 %reduce-scatter.11.cloned.1.call-start = ((), (), s32[]{:S(2)}) async-start(), calls=%async_computation.7 | async-start | bytes 4423680 | tf_op jit(solution)/shard_map/reduce_scatter | solution.py:905
  473.4 30.5 %collective-permute-start.68 = (bf16[96,4224]{1,0:T(8,128)(2,1)S(1)}, bf16[96,4224]{1,0:T(8,128)(2,1)S(1)}, u32[]{:S(2)}, u32[]{:S(2)}) collective-permute-start(bf16[96,4224]{1,0:T(8,128)(2,1)S(1)} %bitcast_select_fusion), channel_id=1, source_target_pairs={{0,1},{1,0},{2,3},{3,2},{4,5},{5,4},{6,7},{7,6},{8,9},{9,8},{10,11... | collective-permute-start | bytes 2433032 | tf_op jit(solution)/shard_map/ppermute | solution.py:747
  509.9 19.8 %collective-permute-start.75 = (bf16[128,1536]{1,0:T(8,128)(2,1)}, bf16[128,1536]{1,0:T(8,128)(2,1)}, u32[]{:S(2)}, u32[]{:S(2)}) collective-permute-start(bf16[128,1536]{1,0:T(8,128)(2,1)} %get-tuple-element.173), channel_id=1, source_target_pairs={{0,48},{16,0},{32,16},{48,32},{1,49},{17,1},{33,17},{49,33},{2,50}... | collective-permute-start | bytes 1179656 | tf_op jit(solution)/shard_map/ppermute | solution.py:723
  512.9 18.9 %collective-permute-start.76 = (bf16[128,1536]{1,0:T(8,128)(2,1)}, bf16[128,1536]{1,0:T(8,128)(2,1)}, u32[]{:S(2)}, u32[]{:S(2)}) collective-permute-start(bf16[128,1536]{1,0:T(8,128)(2,1)} %get-tuple-element.174), channel_id=1, source_target_pairs={{0,32},{16,48},{32,0},{48,16},{1,33},{17,49},{33,1},{49,17},{2,34}... | collective-permute-start | bytes 1179656 | tf_op jit(solution)/shard_map/ppermute | solution.py:724
  538.4 142.8 %all-gather.23.cloned.1.call-start = ((), (), s32[]{:S(2)}) async-start(), calls=%async_computation.13 | async-start | bytes 7299072 | tf_op jit(solution)/shard_map/all_gather | solution.py:929
  538.5 18.7 %collective-permute-start.88 = (bf16[96,4224]{1,0:T(8,128)(2,1)S(1)}, bf16[96,4224]{1,0:T(8,128)(2,1)S(1)}, u32[]{:S(2)}, u32[]{:S(2)}) collective-permute-start(bf16[96,4224]{1,0:T(8,128)(2,1)S(1)} %add_convert_fusion.1.refs_0_), channel_id=1, source_target_pairs={{0,64},{64,0},{1,65},{65,1},{2,66},{66,2},{3,67},{67,3},{4,68},{68... | collective-permute-start | bytes 2433032 | tf_op jit(solution)/shard_map/ppermute | solution.py:751
  581.8 130.4 %all-gather.21.cloned.1.call-start = ((), (), s32[]{:S(2)}) async-start(), calls=%async_computation.12 | async-start | bytes 7520256 | tf_op jit(solution)/shard_map/all_gather | solution.py:933
  637.3 42.1 %collective-permute-start.80 = (bf16[64,1536]{1,0:T(8,128)(2,1)S(1)}, bf16[64,1536]{1,0:T(8,128)(2,1)S(1)}, u32[]{:S(2)}, u32[]{:S(2)}) collective-permute-start(bf16[64,1536]{1,0:T(8,128)(2,1)S(1)} %pad_maximum_fusion.18), channel_id=1, source_target_pairs={{48,0},{56,1},{0,2},{8,3},{16,4},{24,5},{32,6},{40,7},{49,8},{57,9... | collective-permute-start | bytes 589832 | tf_op jit(solution)/shard_map/ppermute | solution.py:686
  647.9 31.5 %collective-permute-start.79 = (bf16[64,1536]{1,0:T(8,128)(2,1)S(1)}, bf16[64,1536]{1,0:T(8,128)(2,1)S(1)}, u32[]{:S(2)}, u32[]{:S(2)}) collective-permute-start(bf16[64,1536]{1,0:T(8,128)(2,1)S(1)} %pad_maximum_fusion.17), channel_id=1, source_target_pairs={{32,0},{40,1},{48,2},{56,3},{0,4},{8,5},{16,6},{24,7},{33,8},{41,9... | collective-permute-start | bytes 589832 | tf_op jit(solution)/shard_map/ppermute | solution.py:686
  651.1 22.1 %collective-permute-start.77 = (bf16[64,1536]{1,0:T(8,128)(2,1)S(1)}, bf16[64,1536]{1,0:T(8,128)(2,1)S(1)}, u32[]{:S(2)}, u32[]{:S(2)}) collective-permute-start(bf16[64,1536]{1,0:T(8,128)(2,1)S(1)} %pad_maximum_fusion.15), channel_id=1, source_target_pairs={{0,0},{8,1},{16,2},{24,3},{32,4},{40,5},{48,6},{56,7},{1,8},{9,9},... | collective-permute-start | bytes 589832 | tf_op jit(solution)/shard_map/ppermute | solution.py:686
  656.0 23.4 %collective-permute-start.78 = (bf16[64,1536]{1,0:T(8,128)(2,1)S(1)}, bf16[64,1536]{1,0:T(8,128)(2,1)S(1)}, u32[]{:S(2)}, u32[]{:S(2)}) collective-permute-start(bf16[64,1536]{1,0:T(8,128)(2,1)S(1)} %pad_maximum_fusion.16), channel_id=1, source_target_pairs={{16,0},{24,1},{32,2},{40,3},{48,4},{56,5},{0,6},{8,7},{17,8},{25,9... | collective-permute-start | bytes 589832 | tf_op jit(solution)/shard_map/ppermute | solution.py:686
  (223 other events, 2026.2 us)
Sparse Core Ops, SparseCore 0:
  26.4 45.1 all-gather.12
  80.5 51.0 all-gather.14
  149.6 33.0 all-gather.16
  197.2 66.1 all-gather.18
  332.1 73.3 reduce-scatter.4
  407.9 37.6 reduce-scatter.6
  461.2 66.7 reduce-scatter.8
  538.6 42.1 reduce-scatter.10
  583.1 43.5 all-gather.22
  637.3 74.8 all-gather.20

commit v13 on v12

--- a/solution.py
+++ b/solution.py
@@ -87,9 +87,10 @@
     return left, right.reshape(256, 512)
 
 
-def feed_forward_kernel(*refs):
-    pieces, (wg, wu, wd), outs = refs[:5], refs[5:8], refs[8:12]
-    gate, up, hidden, flat, total = refs[12:]
+def feed_forward_kernel(count, parts, *refs):
+    pieces, (wg, wu, wd) = refs[:count], refs[count : count + 3]
+    outs = refs[count + 3 : count + 3 + parts]
+    gate, up, hidden, flat, total = refs[count + 3 + parts :]
     step = pl.program_id(0)
 
     @pl.when(step == 0)
@@ -133,29 +134,37 @@
     return pl.BlockSpec((rows, 256), lambda b: (0, b))
 
 
-def feed_forward_call(pieces, packed, after=()):
+def chunk_shapes(pieces, own):
+    rows = sum(item.shape[0] for item in pieces)
+    kind = F32 if own else BF16
+    return rows, [jax.ShapeDtypeStruct((128, 1536), kind)] * (rows // 128)
+
+
+def feed_forward_call(pieces, packed, own):
     flat_packed = packed.reshape(1536, -1)
+    rows, partials = chunk_shapes(pieces, own)
     return pl.pallas_call(
-        later(feed_forward_kernel, len(after)),
+        functools.partial(feed_forward_kernel, len(pieces), len(partials)),
         grid=(4,),
-        in_specs=anywhere(after) + PIECES + feed_specs(),
-        out_specs=PARTIALS + [column_block(512)] * 3,
-        out_shape=PARTIAL_SHAPES
+        in_specs=piece_specs(pieces) + feed_specs(),
+        out_specs=PARTIALS[: len(partials)] + [column_block(rows)] * 3,
+        out_shape=partials
         + [
-            jax.ShapeDtypeStruct((512, 1024), F32),
-            jax.ShapeDtypeStruct((512, 1024), F32),
-            jax.ShapeDtypeStruct((512, 1024), BF16),
+            jax.ShapeDtypeStruct((rows, 1024), F32),
+            jax.ShapeDtypeStruct((rows, 1024), F32),
+            jax.ShapeDtypeStruct((rows, 1024), BF16),
         ],
-        scratch_shapes=[pltpu.VMEM((512, 1536), BF16), pltpu.VMEM((512, 1536), F32)],
+        scratch_shapes=[pltpu.VMEM((rows, 1536), BF16), pltpu.VMEM((rows, 1536), F32)],
         compiler_params=params(40),
-        cost_estimate=cost(4.9e9, 18e6),
+        cost_estimate=cost(9.6e6 * rows, 10e6 + 12e3 * rows),
         name="feed_forward",
-    )(*after, *pieces, flat_packed, flat_packed, packed)
-
-
-def feed_backward_kernel(*refs):
-    pieces, (wg, wu, wd, gate, up), outs = refs[:5], refs[5:10], refs[10:14]
-    low_gate, low_up, flat, total = refs[14:]
+    )(*pieces, flat_packed, flat_packed, packed)
+
+
+def feed_backward_kernel(count, parts, *refs):
+    pieces, (wg, wu, wd, gate, up) = refs[:count], refs[count : count + 5]
+    outs = refs[count + 5 : count + 5 + parts]
+    low_gate, low_up, flat, total = refs[count + 5 + parts :]
     step = pl.program_id(0)
 
     @pl.when(step == 0)
@@ -186,24 +195,33 @@
         emit(total, outs)
 
 
-def feed_backward_call(pieces, packed, gate, up, after=()):
+def feed_backward_call(pieces, packed, gate, up, own, after=()):
     flat_packed = packed.reshape(1536, -1)
+    rows, partials = chunk_shapes(pieces, own)
     return pl.pallas_call(
-        later(feed_backward_kernel, len(after)),
+        later(functools.partial(feed_backward_kernel, len(pieces), len(partials)), len(after)),
         grid=(4,),
-        in_specs=anywhere(after) + PIECES + feed_specs() + [column_block(512)] * 2,
-        out_specs=PARTIALS + [column_block(512)] * 2,
-        out_shape=LOW_PARTIAL_SHAPES + [jax.ShapeDtypeStruct((512, 1024), BF16)] * 2,
-        scratch_shapes=[pltpu.VMEM((512, 1536), BF16), pltpu.VMEM((512, 1536), F32)],
+        in_specs=anywhere(after) + piece_specs(pieces) + feed_specs() + [column_block(rows)] * 2,
+        out_specs=PARTIALS[: len(partials)] + [column_block(rows)] * 2,
+        out_shape=partials + [jax.ShapeDtypeStruct((rows, 1024), BF16)] * 2,
+        scratch_shapes=[pltpu.VMEM((rows, 1536), BF16), pltpu.VMEM((rows, 1536), F32)],
         compiler_params=params(40),
-        cost_estimate=cost(4.9e9, 20e6),
+        cost_estimate=cost(9.6e6 * rows, 10e6 + 16e3 * rows),
         name="feed_backward",
     )(*after, *pieces, flat_packed, flat_packed, packed, gate, up)
 
 
+CHUNKS = (128, 256, 128)
+
+
+def chunked(pieces):
+    return pieces[:1], pieces[1:3], pieces[3:]
+
+
 def feed_weights_kernel(*refs):
     flats, grads = refs[:5], refs[5:10]
-    low_gate, low_up, hidden, out, flat_t, hidden_t, grad = refs[10:]
+    low_gate, low_up, hidden = refs[10:13], refs[13:16], refs[16:19]
+    out, flat_t, hidden_t, grad = refs[19:]
     step = pl.program_id(0)
 
     @pl.when(step == 0)
@@ -216,16 +234,24 @@
 
     @pl.when(step == 4)
     def _():
-        hidden_t[...] = hidden[...].T
+        start = 0
+        for ref in hidden:
+            n = ref.shape[0]
+            hidden_t[:, start : start + n] = ref[...].T
+            start += n
         fill(grad, grads)
 
+    def columns(blocks):
+        block = jnp.concatenate([ref[...] for ref in blocks], axis=0)
+        out[...] = nn(flat_t[...], block).astype(BF16).reshape(8, 192, 256)
+
     @pl.when(step < 4)
     def _():
-        out[...] = nn(flat_t[...], low_gate[...]).astype(BF16).reshape(8, 192, 256)
+        columns(low_gate)
 
     @pl.when((step >= 4) & (step < 8))
     def _():
-        out[...] = nn(flat_t[...], low_up[...]).astype(BF16).reshape(8, 192, 256)
+        columns(low_up)
 
     for q in range(4):
 
@@ -246,11 +272,9 @@
         grid=(12,),
         in_specs=PIECES
         + PIECES
-        + [
-            pl.BlockSpec((512, 256), lambda b: (0, jnp.minimum(b, 3))),
-            pl.BlockSpec((512, 256), lambda b: (0, jnp.clip(b - 4, 0, 3))),
-            whole((512, 1024)),
-        ],
+        + [pl.BlockSpec((n, 256), lambda b: (0, jnp.minimum(b, 3))) for n in CHUNKS]
+        + [pl.BlockSpec((n, 256), lambda b: (0, jnp.clip(b - 4, 0, 3))) for n in CHUNKS]
+        + [whole((n, 1024)) for n in CHUNKS],
         out_specs=pl.BlockSpec((8, 192, 256), lambda b: (0, 0, b)),
         out_shape=jax.ShapeDtypeStruct((8, 192, 3072), BF16),
         scratch_shapes=[
@@ -261,7 +285,7 @@
         compiler_params=params(40),
         cost_estimate=cost(4.9e9, 18e6),
         name="feed_weights",
-    )(*flats, *grads, low_gate, low_up, hidden)
+    )(*flats, *grads, *low_gate, *low_up, *hidden)
 
 
 def piece_specs(pieces):
@@ -865,9 +889,14 @@
         flats = ring_gather(rms_norm(state, gain_feed).astype(BF16))
         if index == 0:
             attn_two = line_weights(attn_two, *flats[1:3])
-        *partial, gate, up, hidden = feed_forward_call(flats, feed)
-        saved_feed = (state, flats, gate, up, hidden)
-        state = state + ring_scatter(*partial)
+        partial = []
+        saved = []
+        for number_of, chunk in enumerate(chunked(flats)):
+            *sums, gate, up, hidden = feed_forward_call(chunk, feed, number_of == 0)
+            partial += sums
+            saved.append((gate, up, hidden))
+        saved_feed = (state, flats, saved)
+        state = state + ring_scatter_direct(*partial)
         records.append((saved_attn, saved_feed, window))
     last_rows = state.astype(BF16)
     packed = ((attn_one, feed_one), (attn_two, feed_two))
@@ -876,15 +905,25 @@
     gain_grads = [None] * 4
 
     def feed_back(index, grad, pieces, after):
-        state, flats, gate, up, hidden = records[index][1]
-        *partial, low_gate, low_up = feed_backward_call(
-            pieces, packed[index][1], gate, up, after=after
-        )
+        state, flats, saved = records[index][1]
+        partial = []
+        lows = []
+        for number_of, chunk in enumerate(chunked(pieces)):
+            gate, up, _ = saved[number_of]
+            last = number_of == 2
+            *sums, low_gate, low_up = feed_backward_call(
+                chunk, packed[index][1], gate, up, number_of == 0, after=after if last else ()
+            )
+            partial += sums
+            lows.append((low_gate, low_up))
         own_normed = ring_scatter_direct(*partial)
         grad, gain_grads[2 * index + 1] = norm_back(
             grad, own_normed, state, gains[2 * index + 1]
         )
-        return grad, feed_weights_call(flats, pieces, low_gate, low_up, hidden)
+        low_gates, low_ups = zip(*lows)
+        return grad, feed_weights_call(
+            flats, pieces, low_gates, low_ups, [item[2] for item in saved]
+        )
 
     def attention_back(index, grad, pieces, after, late):
         state, flats, line, mixed, log_total = records[index][0]
@@ -920,8 +959,8 @@
     attn_grad = tie(attn_grad, first_feed, low)
     attn_grad = jnp.concatenate([attn_grad, gain_rows(jnp.stack(gain_grads))], axis=2)
     first_attn = scatter(attn_grad)
-    second_piece = cross(ylo_sum(second), 3072, first_attn)
     feed_piece = ylo_sum(yhi_sum(first_feed[0], core, yhi))
+    second_piece = cross(ylo_sum(second), 3072, first_attn, feed_piece)
     back = from_lines(interleave(last_rows, low), z)
     output, input_grad = separate(back)
     output, input_grad = output[None], input_grad.astype(F32)[None]

time: 738 us -> 750 us (1.016)
  Pallas kernels: 147 us -> 176 us
  starting transfers between devices: 201 us -> 183 us
  local copies, waits for them, and re-layouts: 61.4 us -> 75.5 us
  waiting for transfers between devices: 257 us -> 243 us
    pallas_call x4 -> x12, Pallas kernels: 46 us -> 73.8 us  [the longest x6 44.8 us: feed_backward_call(): pl.pallas_call(later(functools.partial(feed_backward_kernel, len(pieces),...]
    reduce_scatter x4, waiting for transfers between devices: 24.4 us -> 4.57 us  [scatter(): return lax.psum_scatter(block, SPREAD, scatter_dimension=0, tiled=True)]
    all_gather x1, waiting for transfers between devices: 23.5 us -> 41.8 us  [body(): every = lax.all_gather(first_piece, ('x', 'core'), axis=0, tiled=False)]
    unnamed x325 -> x343, local copies, waits for them, and re-layouts: 40.4 us -> 56 us
    ppermute x4 -> x6, waiting for transfers between devices: 6.05 us -> 17.3 us  [ring_scatter_direct(): from_far = lax.ppermute(far, 'x', ACROSS).astype(F32)]
    ppermute x8, waiting for transfers between devices: 24.4 us -> 13.8 us  [ring_gather(): far_first = lax.ppermute(from_left[:half], 'x', RIGHT)]
    all_gather x1, waiting for transfers between devices: 0.01 us -> 9.59 us  [body(): every = lax.all_gather(second_piece, ('x', 'core'), axis=0, tiled=False)]
    ppermute x4 -> x6, starting transfers between devices: 10.9 us -> 15.6 us  [ring_scatter_direct(): from_right = lax.ppermute(left, 'x', LEFT).astype(F32)]
  transfers between devices with their start and end apart: 100 -> 98, of which waited for: 47 -> 40; matrix products, arithmetic and copies ran while one was open for 7% -> 7% of each run, Pallas kernels for 18% -> 23%
where the time goes in v13:
time: 750 us; the launch traced here: 740 us
  waiting for transfers between devices  243 us (32%)
  starting transfers between devices  183 us (24%)
  Pallas kernels  176 us (23%)
  local copies, waits for them, and re-layouts  75.5 us (10%)
  other arithmetic  44.9 us (6%)
  between operations  18 us (2%)
    unnamed x343, local copies, waits for them, and re-layouts  56 us
    pallas_call x6, Pallas kernels, feed_backward_call(): pl.pallas_call(later(functools.partial(feed_backward_kernel, len(pieces),...  44.8 us
    all_gather x1, waiting for transfers between devices, body(): every = lax.all_gather(first_piece, ('x', 'core'), axis=0, tiled=False)  41.8 us
    ppermute x8, waiting for transfers between devices, ring_gather(): from_left = lax.ppermute(block, 'x', RIGHT)  37.2 us
    ppermute x3, waiting for transfers between devices, ylo_sum(): return add_low(piece, lax.ppermute(piece, 'ylo', SWAP))  32.8 us
    pallas_call x6, Pallas kernels, feed_forward_call(): pl.pallas_call(functools.partial(feed_forward_kernel, len(pieces), len(pa...  29 us
    pallas_call x2, Pallas kernels, attend_backward_call(): pl.pallas_call(later(functools.partial(attend_backward_kernel, window), l...  27.2 us
    pallas_call x2, Pallas kernels, feed_weights_call(): pl.pallas_call(feed_weights_kernel, grid=(12,), in_specs=PIECES + PIECES...  25.2 us
  transfers between devices with their start and end apart: 98, of which 40 were waited for; matrix products, arithmetic and copies ran while one was open for 7% of the time, Pallas kernels for 23%

profile of v13, /device:TPU:1, one launch (start us, length us, event | category | flops | bytes accessed | tf_op | source)
XLA Modules:
  0.0 740.2 jit_solution(5275472182884149902)
XLA Ops:
  26.7 6.6 collective-permute-start
  34.7 10.0 %collective-permute-start.2 = (bf16[64,1536]{1,0:T(8,128)(2,1)S(1)}, bf16[64,1536]{1,0:T(8,128)(2,1)S(1)}, u32[]{:S(2)}, u32[]{:S(2)}) collective-permute-start(bf16[64,1536]{1,0:T(8,128)(2,1)S(1)} %get-tuple-element.276), channel_id=1, source_target_pairs={{0,32},{1,40},{2,48},{3,56},{4,0},{5,8},{6,16},{7,24},{8,33},{9,41... | collective-permute-start | bytes 589832 | tf_op jit(solution)/shard_map/ppermute | solution.py:702
  63.9 8.2 %collective-permute-done.5.refs_1_ = bf16[128,1536]{1,0:T(8,128)(2,1)S(1)} collective-permute-done((bf16[128,1536]{1,0:T(8,128)(2,1)S(1)}, bf16[128,1536]{1,0:T(8,128)(2,1)S(1)}, u32[]{:S(2)}, u32[]{:S(2)}) %collective-permute-start.5) | collective-permute-done | bytes 393248 | tf_op jit(solution)/shard_map/ppermute | solution.py:727
  100.6 9.2 %attend.2 = (f32[128,1536]{1,0:T(8,128)S(1)}, f32[128,1536]{1,0:T(8,128)S(1)}, f32[128,1536]{1,0:T(8,128)S(1)}, bf16[128,1536]{1,0:T(8,128)(2,1)S(1)}, bf16[512,...) custom-call(s32[1]{0:T(128)} %collective-permute-done.4.length.refs_2_.refs_1_, bf16[512,384]{1,0:T(8,128)(2,1)S(1)} %copy-done.106, ...), custom_call_target="tpu_custom_call" | custom-call | flops 3000000000 | bytes 6000000 | tf_op jit(solution)/shard_map/attend/pallas_call | solution.py:404
  123.3 7.2 collective-permute-start.33
  140.2 11.5 %collective-permute-done.17.refs_0_.refs_1_ = bf16[128,1536]{1,0:T(8,128)(2,1)S(1)} collective-permute-done((bf16[128,1536]{1,0:T(8,128)(2,1)S(1)}, bf16[128,1536]{1,0:T(8,128)(2,1)S(1)}, u32[]{:S(2)}, u32[]{:S(2)}) %collective-permute-start.17) | collective-permute-done | bytes 393248 | tf_op jit(solution)/shard_map/ppermute | solution.py:727
  211.5 8.2 %collective-permute-start.34 = (bf16[512,384]{1,0:T(8,128)(2,1)S(1)}, bf16[512,384]{1,0:T(8,128)(2,1)S(1)}, u32[]{:S(2)}, u32[]{:S(2)}) collective-permute-start(bf16[512,384]{1,0:T(8,128)(2,1)S(1)} %get-tuple-element.144.refs_4_.refs_8_), channel_id=1, source_target_pairs={{0,8},{8,0},{1,9},{9,1},{2,10},{10,2},{3,11},{11,3},{4,12},{12,4},... | collective-permute-start | bytes 1179656 | tf_op jit(solution)/shard_map/ppermute | solution.py:880
  226.3 9.2 %attend.3 = (f32[128,1536]{1,0:T(8,128)S(1)}, f32[128,1536]{1,0:T(8,128)S(1)}, f32[128,1536]{1,0:T(8,128)S(1)}, bf16[128,1536]{1,0:T(8,128)(2,1)S(1)}, bf16[512,...) custom-call(bf16[64,1536]{1,0:T(8,128)(2,1)S(1)} %collective-permute-done.25.refs_0_.refs_8_, ...), custom_call_target="tpu_custom_call" | custom-call | flops 3000000000 | bytes 6000000 | tf_op jit(solution)/shard_map/attend/pallas_call | solution.py:404
  280.2 8.2 %feed_backward.7 = (bf16[128,1536]{1,0:T(8,128)(2,1)}, bf16[128,1536]{1,0:T(8,128)(2,1)}, bf16[256,1024]{1,0:T(8,128)(2,1)S(1)}, bf16[256,1024]{1,0:T(8,128)(2,1)S(1)}) custom-call(bf16[128,1536]{1,0:T(8,128)(2,1)S(1)} %copy-done.47, bf16[128,1536]{1,0:T(8,128)(2,1)S(1)} %copy-done.49, bf16[1536,3072]{1,0:T(8,128)(2,1)S(1)} %copy-done.2, ...), custom_call_target="tpu_custom_call" | custom-call | flops 2457600000 | bytes 14096000 | tf_op jit(solution)/shard_map/feed_backward/pallas_call | solution.py:201
  297.5 7.5 %feed_backward.8 = (bf16[128,1536]{1,0:T(8,128)(2,1)}, bf16[128,1024]{1,0:T(8,128)(2,1)S(1)}, bf16[128,1024]{1,0:T(8,128)(2,1)S(1)}) custom-call(bf16[64,1536]{1,0:T(8,128)(2,1)S(1)} %copy-done.92, bf16[64,1536]{1,0:T(8,128)(2,1)S(1)} %copy-done.94, bf16[1536,3072]{1,0:T(8,128)(2,1)S(1)} %bitcast.69, bf16[1536,3072]{1,0:T(8,128)(2,1)S(1)} %bitcast.69, ...), custom_call_target="tpu_custom_call" | custom-call | flops 1228800000 | bytes 12048000 | tf_op jit(solution)/shard_map/feed_backward/pallas_call | solution.py:201
  314.2 6.8 feed_backward.6
  321.9 12.7 %feed_weights.2 = bf16[8,192,3072]{2,1,0:T(8,128)(2,1)} custom-call(bf16[128,1536]{1,0:T(8,128)(2,1)S(1)} %copy-done.23, bf16[128,1536]{1,0:T(8,128)(2,1)S(1)} %copy-done.51, bf16[128,1536]{1,0:T(8,128)(2,1)S(1)} %copy-done.53, bf16[64,1536]{1,0:T(8,128)(2,1)} %collective-permute-done.44.refs_0_.refs_3_, ...), custom_call_target="tpu_custom_call" | custom-call | flops 4899999744 | bytes 18000000 | tf_op jit(solution)/shard_map/feed_weights/pallas_call | solution.py:270
  337.2 7.2 collective-permute-done.46
  360.7 13.4 %attend_backward.2 = (bf16[512,384]{1,0:T(8,128)(2,1)S(1)}, f32[512,384]{1,0:T(8,128)}, bf16[512,384]{1,0:T(8,128)(2,1)S(1)}) custom-call(bf16[128,1536]{1,0:T(8,128)(2,1)S(1)} %get-tuple-element.273.refs_0_, s32[1]{0:T(128)} %collective-permute-done.4.length.refs_2_.refs_1_, bf16[128,1536]{1,0:T(8,128)(2,1)} %copy-done.36, bf16[128,1536]{1,0:T(8,128)(2,1)} %copy-done.58, ...), custom_call_target="tpu_custom_call" | custom-call | flops 6000000000 | bytes 6000000 | tf_op jit(solution)/shard_map/attend_backward/pallas_call | solution.py:479
  398.3 7.4 collective-permute-done.56
  423.3 6.8 feed_backward.9
  432.9 8.1 %feed_backward.10 = (bf16[128,1536]{1,0:T(8,128)(2,1)S(1)}, bf16[128,1536]{1,0:T(8,128)(2,1)}, bf16[256,1024]{1,0:T(8,128)(2,1)S(1)}, bf16[256,1024]{1,0:T(8,128)(2,1)S(1)}) custom-call(bf16[128,1536]{1,0:T(8,128)(2,1)S(1)} %collective-permute-done.58.refs_0_.refs_6_, bf16[128,1536]{1,0:T(8,128)(2,1)S(1)} %collective-permute-done.59.refs_1_.refs_7_, ...), custom_call_target="tpu_custom_call" | custom-call | flops 2457600000 | bytes 14096000 | tf_op jit(solution)/shard_map/feed_backward/pallas_call | solution.py:201
  443.8 7.5 %feed_backward.11 = (bf16[128,1536]{1,0:T(8,128)(2,1)}, bf16[128,1024]{1,0:T(8,128)(2,1)S(1)}, bf16[128,1024]{1,0:T(8,128)(2,1)S(1)}) custom-call(bf16[1,192,3072]{2,1,0:T(8,128)(2,1)S(1)} %copy-done.15, bf16[64,1536]{1,0:T(8,128)(2,1)S(1)} %collective-permute-done.62.refs_1_.refs_8_, bf16[64,1536]{1,0:T(8,128)(2,1)S(1)} %collective-permute-done.63.refs_2_.refs_9_, ...), custom_call_target="tpu_custom_call" | custom-call | flops 1228800000 | bytes 12048000 | tf_op jit(solution)/shard_map/feed_backward/pallas_call | solution.py:201
  451.5 12.5 %feed_weights.3 = bf16[8,192,3072]{2,1,0:T(8,128)(2,1)} custom-call(bf16[128,1536]{1,0:T(8,128)(2,1)S(1)} %copy-done.21, bf16[128,1536]{1,0:T(8,128)(2,1)S(1)} %copy-done.43, bf16[128,1536]{1,0:T(8,128)(2,1)S(1)} %copy-done.45, bf16[64,1536]{1,0:T(8,128)(2,1)S(1)} %copy-done.90, bf16[64,1536]{1,0:T(8,128)(2,1)} %collective-permute-done.22.refs_1_.refs_4_, ...), custom_call_target="tpu_custom_call" | custom-call | flops 4899999744 | bytes 18000000 | tf_op jit(solution)/shard_map/feed_weights/pallas_call | solution.py:270
  492.8 13.8 %attend_backward.3 = (bf16[512,384]{1,0:T(8,128)(2,1)S(1)}, f32[512,384]{1,0:T(8,128)}, bf16[512,384]{1,0:T(8,128)(2,1)S(1)}) custom-call(s32[1]{0:T(128)} %collective-permute-done.4.length.refs_2_.refs_1_, bf16[128,1536]{1,0:T(8,128)(2,1)S(1)} %get-tuple-element.206.refs_0_.refs_1_, bf16[128,1536]{1,0:T(8,128)(2,1)} %copy-done.54, ...), custom_call_target="tpu_custom_call" | custom-call | flops 6000000000 | bytes 6000000 | tf_op jit(solution)/shard_map/attend_backward/pallas_call | solution.py:479
  528.2 7.9 %collective-permute-done.74 = bf16[128,1536]{1,0:T(8,128)(2,1)} collective-permute-done((bf16[128,1536]{1,0:T(8,128)(2,1)}, bf16[128,1536]{1,0:T(8,128)(2,1)}, u32[]{:S(2)}, u32[]{:S(2)}) %collective-permute-start.74) | collective-permute-done | bytes 393248 | tf_op jit(solution)/shard_map/ppermute | solution.py:748
  551.8 13.4 %collective-permute-done.80 = bf16[96,3072]{1,0:T(8,128)(2,1)S(1)} collective-permute-done((bf16[96,3072]{1,0:T(8,128)(2,1)S(1)}, bf16[96,3072]{1,0:T(8,128)(2,1)S(1)}, u32[]{:S(2)}, u32[]{:S(2)}) %collective-permute-start.80) | collective-permute-done | bytes 589856 | tf_op jit(solution)/shard_map/ppermute | solution.py:771
  565.5 16.0 %collective-permute-done.86 = bf16[96,4224]{1,0:T(8,128)(2,1)S(1)} collective-permute-done((bf16[96,4224]{1,0:T(8,128)(2,1)S(1)}, bf16[96,4224]{1,0:T(8,128)(2,1)S(1)}, u32[]{:S(2)}, u32[]{:S(2)}) %collective-permute-start.86) | collective-permute-done | bytes 811040 | tf_op jit(solution)/shard_map/ppermute | solution.py:775
  582.4 11.8 %collective-permute-done.81 = bf16[96,3072]{1,0:T(8,128)(2,1)S(1)} collective-permute-done((bf16[96,3072]{1,0:T(8,128)(2,1)S(1)}, bf16[96,3072]{1,0:T(8,128)(2,1)S(1)}, u32[]{:S(2)}, u32[]{:S(2)}) %collective-permute-start.81) | collective-permute-done | bytes 589856 | tf_op jit(solution)/shard_map/ppermute | solution.py:775
  598.8 7.9 %collective-permute-done.83 = bf16[96,1280]{1,0:T(8,128)(2,1)S(1)} collective-permute-done((bf16[96,1280]{1,0:T(8,128)(2,1)S(1)}, bf16[96,1280]{1,0:T(8,128)(2,1)S(1)}, u32[]{:S(2)}, u32[]{:S(2)}) %collective-permute-start.83) | collective-permute-done | bytes 245792 | tf_op jit(solution)/shard_map/ppermute | solution.py:771
  616.2 10.0 %collective-permute-start.78 = (bf16[64,1536]{1,0:T(8,128)(2,1)S(1)}, bf16[64,1536]{1,0:T(8,128)(2,1)S(1)}, u32[]{:S(2)}, u32[]{:S(2)}) collective-permute-start(bf16[64,1536]{1,0:T(8,128)(2,1)S(1)} %pad_maximum_fusion.14), channel_id=1, source_target_pairs={{48,0},{56,1},{0,2},{8,3},{16,4},{24,5},{32,6},{40,7},{49,8},{57,9... | collective-permute-start | bytes 589832 | tf_op jit(solution)/shard_map/ppermute | solution.py:710
  626.3 7.0 collective-permute-start.77
  645.3 17.6 %collective-permute-done.76 = bf16[64,1536]{1,0:T(8,128)(2,1)S(1)} collective-permute-done((bf16[64,1536]{1,0:T(8,128)(2,1)S(1)}, bf16[64,1536]{1,0:T(8,128)(2,1)S(1)}, u32[]{:S(2)}, u32[]{:S(2)}) %collective-permute-start.76) | collective-permute-done | bytes 196640 | tf_op jit(solution)/shard_map/ppermute | solution.py:710
  665.0 9.6 %all-gather.23.cloned.1.call-done = bf16[768,4224]{1,0:T(8,128)(2,1)} async-done(((bf16[96,4224]{1,0:T(8,128)(2,1)}), bf16[768,4224]{1,0:T(8,128)(2,1)}) %all-gather.23.cloned.1.call-update) | async-done | bytes 6488080 | tf_op jit(solution)/shard_map/all_gather | solution.py:968
  674.6 7.4 unpack.3
  682.0 41.8 %all-gather.21.cloned.1.call-done = bf16[768,4352]{1,0:T(8,128)(2,1)} async-done(((bf16[96,4352]{1,0:T(8,128)(2,1)}), bf16[768,4352]{1,0:T(8,128)(2,1)}) %all-gather.21.cloned.1.call-update) | async-done | bytes 6684688 | tf_op jit(solution)/shard_map/all_gather | solution.py:972
  723.8 7.5 %unpack.2 = (f32[192,1536]{1,0:T(8,128)}, f32[192,768]{1,0:T(8,128)}, f32[192,768]{1,0:T(8,128)}, f32[192,1536]{1,0:T(8,128)}, f32[192,4096]{1,0:T(8,128)}, /*in...) custom-call(bf16[4,2,96,4352]{3,2,1,0:T(8,128)(2,1)} %bitcast.89), custom_call_target="tpu_custom_call" | custom-call | flops 1000000 | bytes 30000000 | tf_op jit(solution)/shard_map/unpack/pallas_call | solution.py:601
  (710 shorter events, 382.4 us)
Async XLA Ops:
  7.2 77.5 %all-gather.13.cloned.1.call-start = ((), (), s32[]{:S(2)}) async-start(), calls=%async_computation.8 | async-start | bytes 4423680 | tf_op jit(solution)/shard_map/all_gather | solution.py:826
  26.3 135.5 %all-gather.15.cloned.1.call-start = ((), (), s32[]{:S(2)}) async-start(), calls=%async_computation.9 | async-start | bytes 10616832 | tf_op jit(solution)/shard_map/all_gather | solution.py:826
  26.7 24.7 %collective-permute-start = (bf16[64,1536]{1,0:T(8,128)(2,1)S(1)}, bf16[64,1536]{1,0:T(8,128)(2,1)S(1)}, u32[]{:S(2)}, u32[]{:S(2)}) collective-permute-start(bf16[64,1536]{1,0:T(8,128)(2,1)S(1)} %get-tuple-element.274), channel_id=1, source_target_pairs={{0,0},{1,8},{2,16},{3,24},{4,32},{5,40},{6,48},{7,56},{8,1},{9,9},... | collective-permute-start | bytes 589832 | tf_op jit(solution)/shard_map/ppermute | solution.py:702
  34.7 24.5 %collective-permute-start.2 = (bf16[64,1536]{1,0:T(8,128)(2,1)S(1)}, bf16[64,1536]{1,0:T(8,128)(2,1)S(1)}, u32[]{:S(2)}, u32[]{:S(2)}) collective-permute-start(bf16[64,1536]{1,0:T(8,128)(2,1)S(1)} %get-tuple-element.276), channel_id=1, source_target_pairs={{0,32},{1,40},{2,48},{3,56},{4,0},{5,8},{6,16},{7,24},{8,33},{9,41... | collective-permute-start | bytes 589832 | tf_op jit(solution)/shard_map/ppermute | solution.py:702
  50.1 25.1 %collective-permute-start.16 = (bf16[192,3072]{1,0:T(8,128)(2,1)S(1)}, bf16[192,3072]{1,0:T(8,128)(2,1)S(1)}, u32[]{:S(2)}, u32[]{:S(2)}) collective-permute-start(bf16[192,3072]{1,0:T(8,128)(2,1)S(1)} %pack_feed.2), channel_id=1, source_target_pairs={{0,1},{2,3},{4,5},{6,7},{9,8},{11,10},{13,12},{15,14},{16,17},{18,... | collective-permute-start | bytes 3538952 | tf_op jit(solution)/shard_map/ppermute | solution.py:809
  80.3 126.7 %all-gather.17.cloned.1.call-start = ((), (), s32[]{:S(2)}) async-start(), calls=%async_computation.10 | async-start | bytes 3981312 | tf_op jit(solution)/shard_map/all_gather | solution.py:826
  132.8 19.0 %collective-permute-start.18 = (bf16[128,1536]{1,0:T(8,128)(2,1)S(1)}, bf16[128,1536]{1,0:T(8,128)(2,1)S(1)}, u32[]{:S(2)}, u32[]{:S(2)}) collective-permute-start(bf16[128,1536]{1,0:T(8,128)(2,1)S(1)} %multiply_convert_fusion.2.refs_0_), channel_id=1, source_target_pairs={{0,48},{16,0},{32,16},{48,32},{1,49},{17,1},{33,17},{49,33},{2,50}... | collective-permute-start | bytes 1179656 | tf_op jit(solution)/shard_map/ppermute | solution.py:728
  151.8 117.7 %all-gather.19.cloned.1.call-start = ((), (), s32[]{:S(2)}) async-start(), calls=%async_computation.11 | async-start | bytes 10616832 | tf_op jit(solution)/shard_map/all_gather | solution.py:826
  157.5 22.9 %collective-permute-start.39 = (bf16[192,3072]{1,0:T(8,128)(2,1)}, bf16[192,3072]{1,0:T(8,128)(2,1)}, u32[]{:S(2)}, u32[]{:S(2)}) collective-permute-start(bf16[192,3072]{1,0:T(8,128)(2,1)} %pack_feed.3), channel_id=1, source_target_pairs={{0,1},{2,3},{4,5},{6,7},{9,8},{11,10},{13,12},{15,14},{16,17},{18,... | collective-permute-start | bytes 3538952 | tf_op jit(solution)/shard_map/ppermute | solution.py:809
  199.0 217.7 %reduce-scatter.5.cloned.1.call-start = ((), (), s32[]{:S(2)}) async-start(), calls=%async_computation.4 | async-start | bytes 10616832 | tf_op jit(solution)/shard_map/reduce_scatter | solution.py:944
  264.0 27.9 %collective-permute-start.44 = (bf16[64,1536]{1,0:T(8,128)(2,1)}, bf16[64,1536]{1,0:T(8,128)(2,1)}, u32[]{:S(2)}, u32[]{:S(2)}) collective-permute-start(bf16[64,1536]{1,0:T(8,128)(2,1)} %slice.381), channel_id=1, source_target_pairs={{0,16},{16,32},{32,48},{48,0},{1,17},{17,33},{33,49},{49,1},{2,18}... | collective-permute-start | bytes 589832 | tf_op jit(solution)/shard_map/ppermute | solution.py:729
  264.8 27.1 %collective-permute-start.45 = (bf16[64,1536]{1,0:T(8,128)(2,1)}, bf16[64,1536]{1,0:T(8,128)(2,1)}, u32[]{:S(2)}, u32[]{:S(2)}) collective-permute-start(bf16[64,1536]{1,0:T(8,128)(2,1)} %slice.382), channel_id=1, source_target_pairs={{0,48},{16,0},{32,16},{48,32},{1,49},{17,1},{33,17},{49,33},{2,50}... | collective-permute-start | bytes 589832 | tf_op jit(solution)/shard_map/ppermute | solution.py:730
  289.3 45.3 %collective-permute-start.47 = (bf16[128,1536]{1,0:T(8,128)(2,1)}, bf16[128,1536]{1,0:T(8,128)(2,1)}, u32[]{:S(2)}, u32[]{:S(2)}) collective-permute-start(bf16[128,1536]{1,0:T(8,128)(2,1)} %get-tuple-element.159), channel_id=1, source_target_pairs={{0,16},{16,32},{32,48},{48,0},{1,17},{17,33},{33,49},{49,1},{2,18}... | collective-permute-start | bytes 1179656 | tf_op jit(solution)/shard_map/ppermute | solution.py:746
  290.5 44.4 %collective-permute-start.48 = (bf16[128,1536]{1,0:T(8,128)(2,1)}, bf16[128,1536]{1,0:T(8,128)(2,1)}, u32[]{:S(2)}, u32[]{:S(2)}) collective-permute-start(bf16[128,1536]{1,0:T(8,128)(2,1)} %get-tuple-element.160), channel_id=1, source_target_pairs={{0,48},{16,0},{32,16},{48,32},{1,49},{17,1},{33,17},{49,33},{2,50}... | collective-permute-start | bytes 1179656 | tf_op jit(solution)/shard_map/ppermute | solution.py:747
  305.0 29.9 %collective-permute-start.49 = (bf16[128,1536]{1,0:T(8,128)(2,1)}, bf16[128,1536]{1,0:T(8,128)(2,1)}, u32[]{:S(2)}, u32[]{:S(2)}) collective-permute-start(bf16[128,1536]{1,0:T(8,128)(2,1)} %get-tuple-element.163), channel_id=1, source_target_pairs={{0,32},{16,48},{32,0},{48,16},{1,33},{17,49},{33,1},{49,17},{2,34}... | collective-permute-start | bytes 1179656 | tf_op jit(solution)/shard_map/ppermute | solution.py:748
  306.5 30.6 %collective-permute-start.42 = (bf16[128,1536]{1,0:T(8,128)(2,1)}, bf16[128,1536]{1,0:T(8,128)(2,1)}, u32[]{:S(2)}, u32[]{:S(2)}) collective-permute-start(bf16[128,1536]{1,0:T(8,128)(2,1)} %get-tuple-element.151), channel_id=1, source_target_pairs={{0,16},{16,32},{32,48},{48,0},{1,17},{17,33},{33,49},{49,1},{2,18}... | collective-permute-start | bytes 1179656 | tf_op jit(solution)/shard_map/ppermute | solution.py:746
  306.8 30.4 %collective-permute-start.43 = (bf16[128,1536]{1,0:T(8,128)(2,1)}, bf16[128,1536]{1,0:T(8,128)(2,1)}, u32[]{:S(2)}, u32[]{:S(2)}) collective-permute-start(bf16[128,1536]{1,0:T(8,128)(2,1)} %get-tuple-element.152), channel_id=1, source_target_pairs={{0,48},{16,0},{32,16},{48,32},{1,49},{17,1},{33,17},{49,33},{2,50}... | collective-permute-start | bytes 1179656 | tf_op jit(solution)/shard_map/ppermute | solution.py:747
  346.2 121.3 %reduce-scatter.7.cloned.1.call-start = ((), (), s32[]{:S(2)}) async-start(), calls=%async_computation.5 | async-start | bytes 3981312 | tf_op jit(solution)/shard_map/reduce_scatter | solution.py:944
  384.8 20.9 %collective-permute-start.56 = (bf16[128,1536]{1,0:T(8,128)(2,1)}, bf16[128,1536]{1,0:T(8,128)(2,1)}, u32[]{:S(2)}, u32[]{:S(2)}) collective-permute-start(bf16[128,1536]{1,0:T(8,128)(2,1)} %get-tuple-element.180), channel_id=1, source_target_pairs={{0,48},{16,0},{32,16},{48,32},{1,49},{17,1},{33,17},{49,33},{2,50}... | collective-permute-start | bytes 1179656 | tf_op jit(solution)/shard_map/ppermute | solution.py:747
  416.8 122.5 %reduce-scatter.9.cloned.1.call-start = ((), (), s32[]{:S(2)}) async-start(), calls=%async_computation.6 | async-start | bytes 10616832 | tf_op jit(solution)/shard_map/reduce_scatter | solution.py:944
  441.0 23.0 %collective-permute-start.60 = (bf16[128,1536]{1,0:T(8,128)(2,1)}, bf16[128,1536]{1,0:T(8,128)(2,1)}, u32[]{:S(2)}, u32[]{:S(2)}) collective-permute-start(bf16[128,1536]{1,0:T(8,128)(2,1)} %get-tuple-element.190), channel_id=1, source_target_pairs={{0,16},{16,32},{32,48},{48,0},{1,17},{17,33},{33,49},{49,1},{2,18}... | collective-permute-start | bytes 1179656 | tf_op jit(solution)/shard_map/ppermute | solution.py:746
  441.0 23.0 %collective-permute-start.61 = (bf16[128,1536]{1,0:T(8,128)(2,1)S(1)}, bf16[128,1536]{1,0:T(8,128)(2,1)}, u32[]{:S(2)}, u32[]{:S(2)}) collective-permute-start(bf16[128,1536]{1,0:T(8,128)(2,1)S(1)} %get-tuple-element.191), channel_id=1, source_target_pairs={{0,48},{16,0},{32,16},{48,32},{1,49},{17,1},{33,17},{49,33},{2,50}... | collective-permute-start | bytes 1179656 | tf_op jit(solution)/shard_map/ppermute | solution.py:747
  467.5 126.9 %reduce-scatter.11.cloned.1.call-start = ((), (), s32[]{:S(2)}) async-start(), calls=%async_computation.7 | async-start | bytes 4423680 | tf_op jit(solution)/shard_map/reduce_scatter | solution.py:944
  478.0 30.2 %collective-permute-start.66 = (bf16[96,4224]{1,0:T(8,128)(2,1)S(1)}, bf16[96,4224]{1,0:T(8,128)(2,1)S(1)}, u32[]{:S(2)}, u32[]{:S(2)}) collective-permute-start(bf16[96,4224]{1,0:T(8,128)(2,1)S(1)} %bitcast_select_fusion), channel_id=1, source_target_pairs={{0,1},{1,0},{2,3},{3,2},{4,5},{5,4},{6,7},{7,6},{8,9},{9,8},{10,11... | collective-permute-start | bytes 2433032 | tf_op jit(solution)/shard_map/ppermute | solution.py:771
  517.2 19.0 %collective-permute-start.74 = (bf16[128,1536]{1,0:T(8,128)(2,1)}, bf16[128,1536]{1,0:T(8,128)(2,1)}, u32[]{:S(2)}, u32[]{:S(2)}) collective-permute-start(bf16[128,1536]{1,0:T(8,128)(2,1)} %get-tuple-element.214), channel_id=1, source_target_pairs={{0,32},{16,48},{32,0},{48,16},{1,33},{17,49},{33,1},{49,17},{2,34}... | collective-permute-start | bytes 1179656 | tf_op jit(solution)/shard_map/ppermute | solution.py:748
  542.8 131.8 %all-gather.23.cloned.1.call-start = ((), (), s32[]{:S(2)}) async-start(), calls=%async_computation.13 | async-start | bytes 7299072 | tf_op jit(solution)/shard_map/all_gather | solution.py:968
  551.8 29.7 %collective-permute-start.86 = (bf16[96,4224]{1,0:T(8,128)(2,1)S(1)}, bf16[96,4224]{1,0:T(8,128)(2,1)S(1)}, u32[]{:S(2)}, u32[]{:S(2)}) collective-permute-start(bf16[96,4224]{1,0:T(8,128)(2,1)S(1)} %add_convert_fusion.1.refs_0_), channel_id=1, source_target_pairs={{0,64},{64,0},{1,65},{65,1},{2,66},{66,2},{3,67},{67,3},{4,68},{68... | collective-permute-start | bytes 2433032 | tf_op jit(solution)/shard_map/ppermute | solution.py:775
  565.4 28.7 %collective-permute-start.81 = (bf16[96,3072]{1,0:T(8,128)(2,1)S(1)}, bf16[96,3072]{1,0:T(8,128)(2,1)S(1)}, u32[]{:S(2)}, u32[]{:S(2)}) collective-permute-start(bf16[96,3072]{1,0:T(8,128)(2,1)S(1)} %add_convert_fusion.3), channel_id=1, source_target_pairs={{0,64},{64,0},{1,65},{65,1},{2,66},{66,2},{3,67},{67,3},{4,68},{68... | collective-permute-start | bytes 1769480 | tf_op jit(solution)/shard_map/ppermute | solution.py:775
  595.4 128.4 %all-gather.21.cloned.1.call-start = ((), (), s32[]{:S(2)}) async-start(), calls=%async_computation.12 | async-start | bytes 7520256 | tf_op jit(solution)/shard_map/all_gather | solution.py:972
  616.2 46.9 %collective-permute-start.78 = (bf16[64,1536]{1,0:T(8,128)(2,1)S(1)}, bf16[64,1536]{1,0:T(8,128)(2,1)S(1)}, u32[]{:S(2)}, u32[]{:S(2)}) collective-permute-start(bf16[64,1536]{1,0:T(8,128)(2,1)S(1)} %pad_maximum_fusion.14), channel_id=1, source_target_pairs={{48,0},{56,1},{0,2},{8,3},{16,4},{24,5},{32,6},{40,7},{49,8},{57,9... | collective-permute-start | bytes 589832 | tf_op jit(solution)/shard_map/ppermute | solution.py:710
  626.3 36.6 %collective-permute-start.77 = (bf16[64,1536]{1,0:T(8,128)(2,1)S(1)}, bf16[64,1536]{1,0:T(8,128)(2,1)S(1)}, u32[]{:S(2)}, u32[]{:S(2)}) collective-permute-start(bf16[64,1536]{1,0:T(8,128)(2,1)S(1)} %pad_maximum_fusion.13), channel_id=1, source_target_pairs={{32,0},{40,1},{48,2},{56,3},{0,4},{8,5},{16,6},{24,7},{33,8},{41,9... | collective-permute-start | bytes 589832 | tf_op jit(solution)/shard_map/ppermute | solution.py:710
  637.2 25.7 %collective-permute-start.76 = (bf16[64,1536]{1,0:T(8,128)(2,1)S(1)}, bf16[64,1536]{1,0:T(8,128)(2,1)S(1)}, u32[]{:S(2)}, u32[]{:S(2)}) collective-permute-start(bf16[64,1536]{1,0:T(8,128)(2,1)S(1)} %pad_maximum_fusion.12), channel_id=1, source_target_pairs={{16,0},{24,1},{32,2},{40,3},{48,4},{56,5},{0,6},{8,7},{17,8},{25,9... | collective-permute-start | bytes 589832 | tf_op jit(solution)/shard_map/ppermute | solution.py:710
  (230 other events, 2100.6 us)
Sparse Core Ops, SparseCore 0:
  26.4 45.1 all-gather.12
  80.5 51.0 all-gather.14
  151.9 32.8 all-gather.16
  199.1 70.3 all-gather.18
  346.3 70.3 reduce-scatter.4
  419.0 37.9 reduce-scatter.6
  467.6 66.8 reduce-scatter.8
  542.9 41.0 reduce-scatter.10
  595.5 79.0 all-gather.22
  676.8 46.9 all-gather.20

commit v14 on v12

--- a/solution.py
+++ b/solution.py
@@ -679,12 +679,18 @@
     return out
 
 
-def from_lines(block, z):
+def send_home(block):
     part = block.shape[0] // 4
-    out = jnp.zeros_like(block)
+    return [
+        lax.ppermute(block[part * k : part * (k + 1)], AXES, inverse(LINES[k])) for k in range(4)
+    ]
+
+
+def place_home(parts, z):
+    rows = parts[0].shape[0]
+    out = jnp.zeros((4 * rows,) + parts[0].shape[1:], parts[0].dtype)
     for k in range(4):
-        piece = lax.ppermute(block[part * k : part * (k + 1)], AXES, inverse(LINES[k]))
-        out = lax.dynamic_update_slice_in_dim(out, piece, ((z + k) % 4) * part, axis=0)
+        out = lax.dynamic_update_slice_in_dim(out, parts[k], ((z + k) % 4) * rows, axis=0)
     return out
 
 
@@ -915,25 +921,27 @@
     low = tie(grad.astype(BF16), feed_grad)
     first_feed = scatter(tie(feed_grad, low, second_attn))
     second = yhi_sum(jnp.concatenate([second_feed, second_attn], axis=2)[0], core, yhi)
-    grad, attn_grad = attention_back(0, grad, ring_gather(low), (), (second,))
+    second_piece = ylo_sum(second)
+    grad, attn_grad = attention_back(0, grad, ring_gather(low), (second,), (second_piece,))
     low = grad.astype(BF16)
     attn_grad = tie(attn_grad, first_feed, low)
     attn_grad = jnp.concatenate([attn_grad, gain_rows(jnp.stack(gain_grads))], axis=2)
     first_attn = scatter(attn_grad)
-    second_piece = cross(ylo_sum(second), 3072, first_attn)
-    feed_piece = ylo_sum(yhi_sum(first_feed[0], core, yhi))
-    back = from_lines(interleave(last_rows, low), z)
-    output, input_grad = separate(back)
-    output, input_grad = output[None], input_grad.astype(F32)[None]
-
-    every = lax.all_gather(second_piece, ("x", "core"), axis=0, tiled=False)
+    back = send_home(interleave(last_rows, low))
+    feed_piece = tie(yhi_sum(first_feed[0], core, yhi), back[0])
+    feed_piece = tie(ylo_sum(feed_piece), back[1])
+    every = cross(second_piece, 3072, first_attn, feed_piece)
+    every = lax.all_gather(every, ("x", "core"), axis=0, tiled=False)
     results[10:14], results[15:18] = unpack_call(every.reshape(4, 2, 96, -1))
-    attn_piece = ylo_sum(yhi_sum(tie(first_attn, feed_piece)[0], core, yhi))
+    attn_piece = tie(yhi_sum(tie(first_attn, feed_piece)[0], core, yhi), back[2])
+    attn_piece = tie(ylo_sum(attn_piece), back[3])
     first_piece = jnp.concatenate([feed_piece, cross(attn_piece, 0)], axis=1)
     every = lax.all_gather(first_piece, ("x", "core"), axis=0, tiled=False)
     every = every.reshape(4, 2, 96, -1)
     results[1:5], results[6:9] = unpack_call(every)
     gain_sums = every[..., 4224:4228].astype(F32).sum(axis=0).reshape(192, 4).T
+    output, input_grad = separate(place_home(back, z))
+    output, input_grad = output[None], input_grad.astype(F32)[None]
     for index, slot in enumerate((0, 5, 9, 14)):
         results[slot] = gain_sums[index]
     return (output, input_grad, *results)

time: 738 us -> 739 us (level)
  starting transfers between devices: 201 us -> 183 us
  waiting for transfers between devices: 257 us -> 273 us
    reduce_scatter x4, waiting for transfers between devices: 24.4 us -> 1.14 us  [scatter(): return lax.psum_scatter(block, SPREAD, scatter_dimension=0, tiled=True)]
    all_gather x1, waiting for transfers between devices: 0.01 us -> 19 us  [body(): every = lax.all_gather(every, ('x', 'core'), axis=0, tiled=False)]
    ppermute x3, waiting for transfers between devices: 20.6 us -> 39.4 us  [yhi_sum(): return add_low(kept, lax.ppermute(away, 'yhi', SWAP))]
    ppermute x3, waiting for transfers between devices: 34.6 us -> 18.1 us  [ylo_sum(): return add_low(piece, lax.ppermute(piece, 'ylo', SWAP))]
    ppermute x4, starting transfers between devices: 24.4 us -> 9.42 us  [send_home(): lax.ppermute(block[part * k:part * (k + 1)], AXES, inverse(LINES[k]))]
    all_gather x1, waiting for transfers between devices: 23.5 us -> 36.5 us  [body(): every = lax.all_gather(first_piece, ('x', 'core'), axis=0, tiled=False)]
    unnamed x325 -> x331, local copies, waits for them, and re-layouts: 40.4 us -> 41.6 us
  transfers between devices with their start and end apart: 100 -> 100, of which waited for: 47 -> 49; matrix products, arithmetic and copies ran while one was open for 7% -> 8% of each run, Pallas kernels for 18% -> 18%
where the time goes in v14:
time: 739 us; the launch traced here: 729 us
  waiting for transfers between devices  273 us (37%)
  starting transfers between devices  183 us (25%)
  Pallas kernels  146 us (20%)
  local copies, waits for them, and re-layouts  63.3 us (9%)
  other arithmetic  45.3 us (6%)
  between operations  18 us (2%)
    ppermute x8, waiting for transfers between devices, ring_gather(): from_left = lax.ppermute(block, 'x', RIGHT)  42.2 us
    unnamed x331, local copies, waits for them, and re-layouts  41.6 us
    ppermute x3, waiting for transfers between devices, yhi_sum(): return add_low(kept, lax.ppermute(away, 'yhi', SWAP))  39.4 us
    all_gather x1, waiting for transfers between devices, body(): every = lax.all_gather(first_piece, ('x', 'core'), axis=0, tiled=False)  36.5 us
    pallas_call x2, Pallas kernels, feed_backward_call(): pl.pallas_call(later(feed_backward_kernel, len(after)), grid=(4,), in_spe...  27.4 us
    pallas_call x2, Pallas kernels, attend_backward_call(): pl.pallas_call(later(functools.partial(attend_backward_kernel, window), l...  26.7 us
    ppermute x8, waiting for transfers between devices, ring_gather(): far_first = lax.ppermute(from_left[:half], 'x', RIGHT)  25.9 us
    pallas_call x2, Pallas kernels, feed_weights_call(): pl.pallas_call(feed_weights_kernel, grid=(12,), in_specs=PIECES + PIECES...  23.2 us
  transfers between devices with their start and end apart: 100, of which 49 were waited for; matrix products, arithmetic and copies ran while one was open for 8% of the time, Pallas kernels for 18%

profile of v14, /device:TPU:1, one launch (start us, length us, event | category | flops | bytes accessed | tf_op | source)
XLA Modules:
  0.0 728.5 jit_solution(5472930312039902936)
XLA Ops:
  26.7 6.6 collective-permute-start
  34.7 10.0 %collective-permute-start.2 = (bf16[64,1536]{1,0:T(8,128)(2,1)S(1)}, bf16[64,1536]{1,0:T(8,128)(2,1)S(1)}, u32[]{:S(2)}, u32[]{:S(2)}) collective-permute-start(bf16[64,1536]{1,0:T(8,128)(2,1)S(1)} %get-tuple-element.244), channel_id=1, source_target_pairs={{0,32},{1,40},{2,48},{3,56},{4,0},{5,8},{6,16},{7,24},{8,33},{9,41... | collective-permute-start | bytes 589832 | tf_op jit(solution)/shard_map/ppermute | solution.py:678
  63.9 8.2 %collective-permute-done.5.refs_1_ = bf16[128,1536]{1,0:T(8,128)(2,1)S(1)} collective-permute-done((bf16[128,1536]{1,0:T(8,128)(2,1)S(1)}, bf16[128,1536]{1,0:T(8,128)(2,1)S(1)}, u32[]{:S(2)}, u32[]{:S(2)}) %collective-permute-start.5) | collective-permute-done | bytes 393248 | tf_op jit(solution)/shard_map/ppermute | solution.py:709
  99.3 9.0 %attend.2 = (f32[128,1536]{1,0:T(8,128)S(1)}, f32[128,1536]{1,0:T(8,128)S(1)}, f32[128,1536]{1,0:T(8,128)S(1)}, bf16[128,1536]{1,0:T(8,128)(2,1)S(1)}, bf16[512,...) custom-call(s32[1]{0:T(128)} %collective-permute-done.4.length.refs_2_.refs_1_, ...), custom_call_target="tpu_custom_call" | custom-call | flops 3000000000 | bytes 6000000 | tf_op jit(solution)/shard_map/attend/pallas_call | solution.py:380
  121.4 6.9 collective-permute-start.34
  138.2 11.2 %collective-permute-done.16.refs_1_ = bf16[128,1536]{1,0:T(8,128)(2,1)S(1)} collective-permute-done((bf16[128,1536]{1,0:T(8,128)(2,1)S(1)}, bf16[128,1536]{1,0:T(8,128)(2,1)S(1)}, u32[]{:S(2)}, u32[]{:S(2)}) %collective-permute-start.16) | collective-permute-done | bytes 393248 | tf_op jit(solution)/shard_map/ppermute | solution.py:709
  156.4 9.3 %feed_forward.2 = (f32[128,1536]{1,0:T(8,128)S(1)}, f32[128,1536]{1,0:T(8,128)S(1)}, f32[128,1536]{1,0:T(8,128)S(1)}, bf16[128,1536]{1,0:T(8,128)(2,1)S(1)}, f32...) custom-call(bf16[128,1536]{1,0:T(8,128)(2,1)S(1)} %multiply_convert_fusion.2.refs_0_, ...), custom_call_target="tpu_custom_call" | custom-call | flops 4899999744 | bytes 18000000 | tf_op jit(solution)/shard_map/feed_forward/pallas_call | solution.py:138
  179.4 7.5 %collective-permute-done.44 = bf16[192,3072]{1,0:T(8,128)(2,1)} collective-permute-done((bf16[192,3072]{1,0:T(8,128)(2,1)S(1)}, bf16[192,3072]{1,0:T(8,128)(2,1)}, u32[]{:S(2)}, u32[]{:S(2)}) %collective-permute-start.44) | collective-permute-done | bytes 1179680 | tf_op jit(solution)/shard_map/ppermute | solution.py:791
  210.0 7.6 %collective-permute-start.35 = (bf16[512,384]{1,0:T(8,128)(2,1)S(1)}, bf16[512,384]{1,0:T(8,128)(2,1)S(1)}, u32[]{:S(2)}, u32[]{:S(2)}) collective-permute-start(bf16[512,384]{1,0:T(8,128)(2,1)S(1)} %get-tuple-element.128.refs_4_.refs_8_), channel_id=1, source_target_pairs={{0,8},{8,0},{1,9},{9,1},{2,10},{10,2},{3,11},{11,3},{4,12},{12,4},... | collective-permute-start | bytes 1179656 | tf_op jit(solution)/shard_map/ppermute | solution.py:862
  226.2 9.1 %attend.3 = (f32[128,1536]{1,0:T(8,128)S(1)}, f32[128,1536]{1,0:T(8,128)S(1)}, f32[128,1536]{1,0:T(8,128)S(1)}, bf16[128,1536]{1,0:T(8,128)(2,1)S(1)}, bf16[512,...) custom-call(bf16[64,1536]{1,0:T(8,128)(2,1)S(1)} %collective-permute-done.26.refs_0_.refs_3_.refs_8_, ...), custom_call_target="tpu_custom_call" | custom-call | flops 3000000000 | bytes 6000000 | tf_op jit(solution)/shard_map/attend/pallas_call | solution.py:380
  246.8 7.2 collective-permute-done.37
  259.6 7.2 collective-permute-done.40.refs_1_
  276.8 9.2 %feed_forward.3 = (f32[128,1536]{1,0:T(8,128)S(1)}, f32[128,1536]{1,0:T(8,128)S(1)}, f32[128,1536]{1,0:T(8,128)S(1)}, bf16[128,1536]{1,0:T(8,128)(2,1)S(1)}, f32...) custom-call(bf16[128,1536]{1,0:T(8,128)(2,1)S(1)} %multiply_convert_fusion.refs_0_, ...), custom_call_target="tpu_custom_call" | custom-call | flops 4899999744 | bytes 18000000 | tf_op jit(solution)/shard_map/feed_forward/pallas_call | solution.py:138
  291.8 13.6 %feed_backward.2 = (f32[128,1536]{1,0:T(8,128)S(1)}, bf16[128,1536]{1,0:T(8,128)(2,1)}, bf16[128,1536]{1,0:T(8,128)(2,1)}, bf16[128,1536]{1,0:T(8,128)(2,1)}, bf...) custom-call(bf16[128,1536]{1,0:T(8,128)(2,1)S(1)} %pad_maximum_fusion.9.refs_0_.refs_5_, ...), custom_call_target="tpu_custom_call" | custom-call | flops 4899999744 | bytes 20000000 | tf_op jit(solution)/shard_map/feed_backward/pallas_call | solution.py:191
  309.0 11.6 %feed_weights.2 = bf16[8,192,3072]{2,1,0:T(8,128)(2,1)} custom-call(bf16[128,1536]{1,0:T(8,128)(2,1)S(1)} %multiply_convert_fusion.refs_0_, bf16[128,1536]{1,0:T(8,128)(2,1)S(1)} %copy-done.41, bf16[128,1536]{1,0:T(8,128)(2,1)S(1)} %copy-done.44, bf16[64,1536]{1,0:T(8,128)(2,1)S(1)} %collective-permute-done.42.refs_3_, bf16[64,1536]{1,0:T(8,128)(2,1)S(1)} %copy-done.86, ...), custom_call_target="tpu_custom_call" | custom-call | flops 4899999744 | bytes 18000000 | tf_op jit(solution)/shard_map/feed_weights/pallas_call | solution.py:244
  350.9 13.3 %attend_backward.2 = (bf16[512,384]{1,0:T(8,128)(2,1)S(1)}, f32[512,384]{1,0:T(8,128)}, bf16[512,384]{1,0:T(8,128)(2,1)S(1)}) custom-call(bf16[128,1536]{1,0:T(8,128)(2,1)S(1)} %get-tuple-element.241.refs_0_, s32[1]{0:T(128)} %collective-permute-done.4.length.refs_2_.refs_1_, bf16[128,1536]{1,0:T(8,128)(2,1)} %copy-done.29, bf16[128,1536]{1,0:T(8,128)(2,1)} %copy-done.49, ...), custom_call_target="tpu_custom_call" | custom-call | flops 6000000000 | bytes 6000000 | tf_op jit(solution)/shard_map/attend_backward/pallas_call | solution.py:455
  364.2 9.2 %collective-permute-start.56 = (bf16[512,384]{1,0:T(8,128)(2,1)S(1)}, bf16[512,384]{1,0:T(8,128)(2,1)S(1)}, u32[]{:S(2)}, u32[]{:S(2)}) collective-permute-start(bf16[512,384]{1,0:T(8,128)(2,1)S(1)} %get-tuple-element.151), channel_id=1, source_target_pairs={{0,8},{8,0},{1,9},{9,1},{2,10},{10,2},{3,11},{11,3},{4,12},{12,4},... | collective-permute-start | bytes 1179656 | tf_op jit(solution)/shard_map/ppermute | solution.py:902
  391.5 7.2 collective-permute-done.58
  408.3 7.7 %collective-permute-done.60.refs_2_.refs_6_ = bf16[128,1536]{1,0:T(8,128)(2,1)S(1)} collective-permute-done((bf16[128,1536]{1,0:T(8,128)(2,1)S(1)}, bf16[128,1536]{1,0:T(8,128)(2,1)S(1)}, u32[]{:S(2)}, u32[]{:S(2)}) %collective-permute-start.60) | collective-permute-done | bytes 393248 | tf_op jit(solution)/shard_map/ppermute | solution.py:709
  425.2 13.8 %feed_backward.3 = (f32[128,1536]{1,0:T(8,128)S(1)}, bf16[128,1536]{1,0:T(8,128)(2,1)}, bf16[128,1536]{1,0:T(8,128)(2,1)}, bf16[128,1536]{1,0:T(8,128)(2,1)}, bf...) custom-call(bf16[1,192,3072]{2,1,0:T(8,128)(2,1)S(1)} %copy-done.8, ...), custom_call_target="tpu_custom_call" | custom-call | flops 4899999744 | bytes 20000000 | tf_op jit(solution)/shard_map/feed_backward/pallas_call | solution.py:191
  444.0 11.6 %feed_weights.3 = bf16[8,192,3072]{2,1,0:T(8,128)(2,1)} custom-call(bf16[128,1536]{1,0:T(8,128)(2,1)S(1)} %copy-done.16, bf16[128,1536]{1,0:T(8,128)(2,1)S(1)} %copy-done.34, bf16[128,1536]{1,0:T(8,128)(2,1)S(1)} %copy-done.36, bf16[64,1536]{1,0:T(8,128)(2,1)S(1)} %copy-done.77, bf16[64,1536]{1,0:T(8,128)(2,1)S(1)} %copy-done.79, ...), custom_call_target="tpu_custom_call" | custom-call | flops 4899999744 | bytes 18000000 | tf_op jit(solution)/shard_map/feed_weights/pallas_call | solution.py:244
  481.0 15.5 %collective-permute-done.68 = bf16[96,4224]{1,0:T(8,128)(2,1)S(1)} collective-permute-done((bf16[96,4224]{1,0:T(8,128)(2,1)S(1)}, bf16[96,4224]{1,0:T(8,128)(2,1)S(1)}, u32[]{:S(2)}, u32[]{:S(2)}) %collective-permute-start.68) | collective-permute-done | bytes 811040 | tf_op jit(solution)/shard_map/ppermute | solution.py:753
  506.2 13.4 %attend_backward.3 = (bf16[512,384]{1,0:T(8,128)(2,1)S(1)}, f32[512,384]{1,0:T(8,128)}, bf16[512,384]{1,0:T(8,128)(2,1)S(1)}) custom-call(bf16[96,4224]{1,0:T(8,128)(2,1)} %copy-done.116, s32[1]{0:T(128)} %collective-permute-done.4.length.refs_2_.refs_1_, bf16[128,1536]{1,0:T(8,128)(2,1)S(1)} %get-tuple-element.170.refs_2_.refs_1_, ...), custom_call_target="tpu_custom_call" | custom-call | flops 6000000000 | bytes 6000000 | tf_op jit(solution)/shard_map/attend_backward/pallas_call | solution.py:455
  539.3 6.7 collective-permute-done.76
  564.6 18.1 %collective-permute-done.83 = bf16[96,3072]{1,0:T(8,128)(2,1)S(1)} collective-permute-done((bf16[96,3072]{1,0:T(8,128)(2,1)S(1)}, bf16[96,3072]{1,0:T(8,128)(2,1)S(1)}, u32[]{:S(2)}, u32[]{:S(2)}) %collective-permute-start.83) | collective-permute-done | bytes 589856 | tf_op jit(solution)/shard_map/ppermute | solution.py:753
  592.0 15.8 %collective-permute-done.84 = bf16[96,3072]{1,0:T(8,128)(2,1)S(1)} collective-permute-done((bf16[96,3072]{1,0:T(8,128)(2,1)S(1)}, bf16[96,3072]{1,0:T(8,128)(2,1)S(1)}, u32[]{:S(2)}, u32[]{:S(2)}) %collective-permute-start.84) | collective-permute-done | bytes 589856 | tf_op jit(solution)/shard_map/ppermute | solution.py:757
  621.3 6.8 collective-permute-done.80
  635.6 9.9 %collective-permute-done.81 = bf16[64,1536]{1,0:T(8,128)(2,1)S(1)} collective-permute-done((bf16[64,1536]{1,0:T(8,128)(2,1)S(1)}, bf16[64,1536]{1,0:T(8,128)(2,1)S(1)}, u32[]{:S(2)}, u32[]{:S(2)}) %collective-permute-start.81) | collective-permute-done | bytes 196640 | tf_op jit(solution)/shard_map/ppermute | solution.py:685
  649.2 19.0 %all-gather.23.cloned.1.call-done = bf16[768,4224]{1,0:T(8,128)(2,1)} async-done(((bf16[96,4224]{1,0:T(8,128)(2,1)}), bf16[768,4224]{1,0:T(8,128)(2,1)}) %all-gather.23.cloned.1.call-update) | async-done | bytes 6488080 | tf_op jit(solution)/shard_map/all_gather | solution.py:934
  668.2 7.4 %unpack.3 = (f32[192,1536]{1,0:T(8,128)}, f32[192,768]{1,0:T(8,128)}, f32[192,768]{1,0:T(8,128)}, f32[192,1536]{1,0:T(8,128)}, f32[192,4096]{1,0:T(8,128)}, /*in...) custom-call(bf16[4,2,96,4224]{3,2,1,0:T(8,128)(2,1)} %bitcast.81), custom_call_target="tpu_custom_call" | custom-call | flops 1000000 | bytes 30000000 | tf_op jit(solution)/shard_map/unpack/pallas_call | solution.py:577
  675.6 36.5 %all-gather.21.cloned.1.call-done = bf16[768,4352]{1,0:T(8,128)(2,1)} async-done(((bf16[96,4352]{1,0:T(8,128)(2,1)}), bf16[768,4352]{1,0:T(8,128)(2,1)}) %all-gather.21.cloned.1.call-update) | async-done | bytes 6684688 | tf_op jit(solution)/shard_map/all_gather | solution.py:939
  712.1 7.5 %unpack.2 = (f32[192,1536]{1,0:T(8,128)}, f32[192,768]{1,0:T(8,128)}, f32[192,768]{1,0:T(8,128)}, f32[192,1536]{1,0:T(8,128)}, f32[192,4096]{1,0:T(8,128)}, /*in...) custom-call(bf16[4,2,96,4352]{3,2,1,0:T(8,128)(2,1)} %bitcast.79), custom_call_target="tpu_custom_call" | custom-call | flops 1000000 | bytes 30000000 | tf_op jit(solution)/shard_map/unpack/pallas_call | solution.py:577
  (707 shorter events, 356.6 us)
Async XLA Ops:
  7.2 77.4 %all-gather.13.cloned.1.call-start = ((), (), s32[]{:S(2)}) async-start(), calls=%async_computation.8 | async-start | bytes 4423680 | tf_op jit(solution)/shard_map/all_gather | solution.py:808
  26.3 130.0 %all-gather.15.cloned.1.call-start = ((), (), s32[]{:S(2)}) async-start(), calls=%async_computation.9 | async-start | bytes 10616832 | tf_op jit(solution)/shard_map/all_gather | solution.py:808
  26.7 24.7 %collective-permute-start = (bf16[64,1536]{1,0:T(8,128)(2,1)S(1)}, bf16[64,1536]{1,0:T(8,128)(2,1)S(1)}, u32[]{:S(2)}, u32[]{:S(2)}) collective-permute-start(bf16[64,1536]{1,0:T(8,128)(2,1)S(1)} %get-tuple-element.242), channel_id=1, source_target_pairs={{0,0},{1,8},{2,16},{3,24},{4,32},{5,40},{6,48},{7,56},{8,1},{9,9},... | collective-permute-start | bytes 589832 | tf_op jit(solution)/shard_map/ppermute | solution.py:678
  33.3 18.7 %collective-permute-start.1 = (bf16[64,1536]{1,0:T(8,128)(2,1)S(1)}, bf16[64,1536]{1,0:T(8,128)(2,1)S(1)}, u32[]{:S(2)}, u32[]{:S(2)}) collective-permute-start(bf16[64,1536]{1,0:T(8,128)(2,1)S(1)} %get-tuple-element.245), channel_id=1, source_target_pairs={{0,16},{1,24},{2,32},{3,40},{4,48},{5,56},{6,0},{7,8},{8,17},{9,25... | collective-permute-start | bytes 589832 | tf_op jit(solution)/shard_map/ppermute | solution.py:678
  34.7 24.5 %collective-permute-start.2 = (bf16[64,1536]{1,0:T(8,128)(2,1)S(1)}, bf16[64,1536]{1,0:T(8,128)(2,1)S(1)}, u32[]{:S(2)}, u32[]{:S(2)}) collective-permute-start(bf16[64,1536]{1,0:T(8,128)(2,1)S(1)} %get-tuple-element.244), channel_id=1, source_target_pairs={{0,32},{1,40},{2,48},{3,56},{4,0},{5,8},{6,16},{7,24},{8,33},{9,41... | collective-permute-start | bytes 589832 | tf_op jit(solution)/shard_map/ppermute | solution.py:678
  50.1 25.1 %collective-permute-start.20 = (bf16[192,3072]{1,0:T(8,128)(2,1)S(1)}, bf16[192,3072]{1,0:T(8,128)(2,1)S(1)}, u32[]{:S(2)}, u32[]{:S(2)}) collective-permute-start(bf16[192,3072]{1,0:T(8,128)(2,1)S(1)} %pack_feed.2), channel_id=1, source_target_pairs={{0,1},{2,3},{4,5},{6,7},{9,8},{11,10},{13,12},{15,14},{16,17},{18,... | collective-permute-start | bytes 3538952 | tf_op jit(solution)/shard_map/ppermute | solution.py:791
  80.3 124.3 %all-gather.17.cloned.1.call-start = ((), (), s32[]{:S(2)}) async-start(), calls=%async_computation.10 | async-start | bytes 3981312 | tf_op jit(solution)/shard_map/all_gather | solution.py:808
  130.6 18.8 %collective-permute-start.16 = (bf16[128,1536]{1,0:T(8,128)(2,1)S(1)}, bf16[128,1536]{1,0:T(8,128)(2,1)S(1)}, u32[]{:S(2)}, u32[]{:S(2)}) collective-permute-start(bf16[128,1536]{1,0:T(8,128)(2,1)S(1)} %multiply_convert_fusion.2.refs_0_), channel_id=1, source_target_pairs={{0,16},{16,32},{32,48},{48,0},{1,17},{17,33},{33,49},{49,1},{2,18}... | collective-permute-start | bytes 1179656 | tf_op jit(solution)/shard_map/ppermute | solution.py:709
  130.7 18.8 %collective-permute-start.17 = (bf16[128,1536]{1,0:T(8,128)(2,1)S(1)}, bf16[128,1536]{1,0:T(8,128)(2,1)S(1)}, u32[]{:S(2)}, u32[]{:S(2)}) collective-permute-start(bf16[128,1536]{1,0:T(8,128)(2,1)S(1)} %multiply_convert_fusion.2.refs_0_), channel_id=1, source_target_pairs={{0,48},{16,0},{32,16},{48,32},{1,49},{17,1},{33,17},{49,33},{2,50}... | collective-permute-start | bytes 1179656 | tf_op jit(solution)/shard_map/ppermute | solution.py:710
  149.5 124.3 %all-gather.19.cloned.1.call-start = ((), (), s32[]{:S(2)}) async-start(), calls=%async_computation.11 | async-start | bytes 10616832 | tf_op jit(solution)/shard_map/all_gather | solution.py:808
  197.5 208.0 %reduce-scatter.5.cloned.1.call-start = ((), (), s32[]{:S(2)}) async-start(), calls=%async_computation.4 | async-start | bytes 10616832 | tf_op jit(solution)/shard_map/reduce_scatter | solution.py:911
  288.6 34.1 %collective-permute-start.45 = (bf16[64,1536]{1,0:T(8,128)(2,1)}, bf16[64,1536]{1,0:T(8,128)(2,1)}, u32[]{:S(2)}, u32[]{:S(2)}) collective-permute-start(bf16[64,1536]{1,0:T(8,128)(2,1)} %get-tuple-element.254), channel_id=1, source_target_pairs={{0,16},{16,32},{32,48},{48,0},{1,17},{17,33},{33,49},{49,1},{2,18}... | collective-permute-start | bytes 589832 | tf_op jit(solution)/shard_map/ppermute | solution.py:718
  288.7 36.2 %collective-permute-start.47 = (bf16[64,1536]{1,0:T(8,128)(2,1)}, bf16[64,1536]{1,0:T(8,128)(2,1)}, u32[]{:S(2)}, u32[]{:S(2)}) collective-permute-start(bf16[64,1536]{1,0:T(8,128)(2,1)} %get-tuple-element.255), channel_id=1, source_target_pairs={{0,48},{16,0},{32,16},{48,32},{1,49},{17,1},{33,17},{49,33},{2,50}... | collective-permute-start | bytes 589832 | tf_op jit(solution)/shard_map/ppermute | solution.py:719
  306.3 21.7 %collective-permute-start.49 = (bf16[128,1536]{1,0:T(8,128)(2,1)}, bf16[128,1536]{1,0:T(8,128)(2,1)}, u32[]{:S(2)}, u32[]{:S(2)}) collective-permute-start(bf16[128,1536]{1,0:T(8,128)(2,1)} %get-tuple-element.141), channel_id=1, source_target_pairs={{0,16},{16,32},{32,48},{48,0},{1,17},{17,33},{33,49},{49,1},{2,18}... | collective-permute-start | bytes 1179656 | tf_op jit(solution)/shard_map/ppermute | solution.py:728
  306.3 21.7 %collective-permute-start.50 = (bf16[128,1536]{1,0:T(8,128)(2,1)}, bf16[128,1536]{1,0:T(8,128)(2,1)}, u32[]{:S(2)}, u32[]{:S(2)}) collective-permute-start(bf16[128,1536]{1,0:T(8,128)(2,1)} %get-tuple-element.142), channel_id=1, source_target_pairs={{0,48},{16,0},{32,16},{48,32},{1,49},{17,1},{33,17},{49,33},{2,50}... | collective-permute-start | bytes 1179656 | tf_op jit(solution)/shard_map/ppermute | solution.py:729
  309.0 19.1 %collective-permute-start.51 = (bf16[128,1536]{1,0:T(8,128)(2,1)}, bf16[128,1536]{1,0:T(8,128)(2,1)}, u32[]{:S(2)}, u32[]{:S(2)}) collective-permute-start(bf16[128,1536]{1,0:T(8,128)(2,1)} %get-tuple-element.143), channel_id=1, source_target_pairs={{0,32},{16,48},{32,0},{48,16},{1,33},{17,49},{33,1},{49,17},{2,34}... | collective-permute-start | bytes 1179656 | tf_op jit(solution)/shard_map/ppermute | solution.py:730
  333.7 127.3 %reduce-scatter.7.cloned.1.call-start = ((), (), s32[]{:S(2)}) async-start(), calls=%async_computation.5 | async-start | bytes 3981312 | tf_op jit(solution)/shard_map/reduce_scatter | solution.py:911
  379.2 19.5 %collective-permute-start.58 = (bf16[128,1536]{1,0:T(8,128)(2,1)}, bf16[128,1536]{1,0:T(8,128)(2,1)}, u32[]{:S(2)}, u32[]{:S(2)}) collective-permute-start(bf16[128,1536]{1,0:T(8,128)(2,1)} %get-tuple-element.154), channel_id=1, source_target_pairs={{0,48},{16,0},{32,16},{48,32},{1,49},{17,1},{33,17},{49,33},{2,50}... | collective-permute-start | bytes 1179656 | tf_op jit(solution)/shard_map/ppermute | solution.py:729
  382.0 18.8 %collective-permute-start.59 = (bf16[128,1536]{1,0:T(8,128)(2,1)S(1)}, bf16[128,1536]{1,0:T(8,128)(2,1)}, u32[]{:S(2)}, u32[]{:S(2)}) collective-permute-start(bf16[128,1536]{1,0:T(8,128)(2,1)S(1)} %get-tuple-element.155), channel_id=1, source_target_pairs={{0,32},{16,48},{32,0},{48,16},{1,33},{17,49},{33,1},{49,17},{2,34}... | collective-permute-start | bytes 1179656 | tf_op jit(solution)/shard_map/ppermute | solution.py:730
  405.6 145.6 %reduce-scatter.9.cloned.1.call-start = ((), (), s32[]{:S(2)}) async-start(), calls=%async_computation.6 | async-start | bytes 10616832 | tf_op jit(solution)/shard_map/reduce_scatter | solution.py:911
  461.0 148.4 %reduce-scatter.11.cloned.1.call-start = ((), (), s32[]{:S(2)}) async-start(), calls=%async_computation.7 | async-start | bytes 4423680 | tf_op jit(solution)/shard_map/reduce_scatter | solution.py:911
  473.1 23.3 %collective-permute-start.68 = (bf16[96,4224]{1,0:T(8,128)(2,1)S(1)}, bf16[96,4224]{1,0:T(8,128)(2,1)S(1)}, u32[]{:S(2)}, u32[]{:S(2)}) collective-permute-start(bf16[96,4224]{1,0:T(8,128)(2,1)S(1)} %bitcast_select_fusion), channel_id=1, source_target_pairs={{0,1},{1,0},{2,3},{3,2},{4,5},{5,4},{6,7},{7,6},{8,9},{9,8},{10,11... | collective-permute-start | bytes 2433032 | tf_op jit(solution)/shard_map/ppermute | solution.py:753
  478.3 19.7 %collective-permute-start.70 = (bf16[128,1536]{1,0:T(8,128)(2,1)S(1)}, bf16[128,1536]{1,0:T(8,128)(2,1)S(1)}, u32[]{:S(2)}, u32[]{:S(2)}) collective-permute-start(bf16[128,1536]{1,0:T(8,128)(2,1)S(1)} %get-tuple-element.170.refs_2_.refs_1_), channel_id=1, source_target_pairs={{0,16},{16,32},{32,48},{48,0},{1,17},{17,33},{33,49},{49,1},{2,18}... | collective-permute-start | bytes 1179656 | tf_op jit(solution)/shard_map/ppermute | solution.py:709
  479.2 19.8 %collective-permute-start.71 = (bf16[128,1536]{1,0:T(8,128)(2,1)S(1)}, bf16[128,1536]{1,0:T(8,128)(2,1)S(1)}, u32[]{:S(2)}, u32[]{:S(2)}) collective-permute-start(bf16[128,1536]{1,0:T(8,128)(2,1)S(1)} %get-tuple-element.170.refs_2_.refs_1_), channel_id=1, source_target_pairs={{0,48},{16,0},{32,16},{48,32},{1,49},{17,1},{33,17},{49,33},{2,50}... | collective-permute-start | bytes 1179656 | tf_op jit(solution)/shard_map/ppermute | solution.py:710
  497.9 22.3 %collective-permute-start.69 = (bf16[96,4224]{1,0:T(8,128)(2,1)S(1)}, bf16[96,4224]{1,0:T(8,128)(2,1)S(1)}, u32[]{:S(2)}, u32[]{:S(2)}) collective-permute-start(bf16[96,4224]{1,0:T(8,128)(2,1)S(1)} %add_convert_fusion.1.refs_0_), channel_id=1, source_target_pairs={{0,64},{64,0},{1,65},{65,1},{2,66},{66,2},{3,67},{67,3},{4,68},{68... | collective-permute-start | bytes 2433032 | tf_op jit(solution)/shard_map/ppermute | solution.py:757
  526.2 19.8 %collective-permute-start.76 = (bf16[128,1536]{1,0:T(8,128)(2,1)}, bf16[128,1536]{1,0:T(8,128)(2,1)}, u32[]{:S(2)}, u32[]{:S(2)}) collective-permute-start(bf16[128,1536]{1,0:T(8,128)(2,1)} %get-tuple-element.177), channel_id=1, source_target_pairs={{0,48},{16,0},{32,16},{48,32},{1,49},{17,1},{33,17},{49,33},{2,50}... | collective-permute-start | bytes 1179656 | tf_op jit(solution)/shard_map/ppermute | solution.py:729
  529.2 18.8 %collective-permute-start.77 = (bf16[128,1536]{1,0:T(8,128)(2,1)}, bf16[128,1536]{1,0:T(8,128)(2,1)}, u32[]{:S(2)}, u32[]{:S(2)}) collective-permute-start(bf16[128,1536]{1,0:T(8,128)(2,1)} %get-tuple-element.178), channel_id=1, source_target_pairs={{0,32},{16,48},{32,0},{48,16},{1,33},{17,49},{33,1},{49,17},{2,34}... | collective-permute-start | bytes 1179656 | tf_op jit(solution)/shard_map/ppermute | solution.py:730
  554.7 113.5 %all-gather.23.cloned.1.call-start = ((), (), s32[]{:S(2)}) async-start(), calls=%async_computation.13 | async-start | bytes 7299072 | tf_op jit(solution)/shard_map/all_gather | solution.py:934
  559.0 23.7 %collective-permute-start.83 = (bf16[96,3072]{1,0:T(8,128)(2,1)S(1)}, bf16[96,3072]{1,0:T(8,128)(2,1)S(1)}, u32[]{:S(2)}, u32[]{:S(2)}) collective-permute-start(bf16[96,3072]{1,0:T(8,128)(2,1)S(1)} %bitcast_select_fusion.2), channel_id=1, source_target_pairs={{0,1},{1,0},{2,3},{3,2},{4,5},{5,4},{6,7},{7,6},{8,9},{9,8},{10,11... | collective-permute-start | bytes 1769480 | tf_op jit(solution)/shard_map/ppermute | solution.py:753
  561.5 23.8 %collective-permute-start.78 = (bf16[64,1536]{1,0:T(8,128)(2,1)S(1)}, bf16[64,1536]{1,0:T(8,128)(2,1)S(1)}, u32[]{:S(2)}, u32[]{:S(2)}) collective-permute-start(bf16[64,1536]{1,0:T(8,128)(2,1)S(1)} %pad_maximum_fusion.15), channel_id=1, source_target_pairs={{0,0},{8,1},{16,2},{24,3},{32,4},{40,5},{48,6},{56,7},{1,8},{9,9},... | collective-permute-start | bytes 589832 | tf_op jit(solution)/shard_map/ppermute | solution.py:685
  585.4 22.4 %collective-permute-start.84 = (bf16[96,3072]{1,0:T(8,128)(2,1)S(1)}, bf16[96,3072]{1,0:T(8,128)(2,1)S(1)}, u32[]{:S(2)}, u32[]{:S(2)}) collective-permute-start(bf16[96,3072]{1,0:T(8,128)(2,1)S(1)} %add_convert_fusion.3), channel_id=1, source_target_pairs={{0,64},{64,0},{1,65},{65,1},{2,66},{66,2},{3,67},{67,3},{4,68},{68... | collective-permute-start | bytes 1769480 | tf_op jit(solution)/shard_map/ppermute | solution.py:757
  610.5 101.6 %all-gather.21.cloned.1.call-start = ((), (), s32[]{:S(2)}) async-start(), calls=%async_computation.12 | async-start | bytes 7520256 | tf_op jit(solution)/shard_map/all_gather | solution.py:939
  (226 other events, 2076.1 us)
Sparse Core Ops, SparseCore 0:
  26.4 45.1 all-gather.12
  80.4 51.0 all-gather.14
  149.6 32.9 all-gather.16
  197.7 65.6 all-gather.18
  333.8 71.7 reduce-scatter.4
  407.8 37.6 reduce-scatter.6
  461.1 66.7 reduce-scatter.8
  554.8 54.2 reduce-scatter.10
  611.4 56.7 all-gather.22
  670.4 41.6 all-gather.20

commit v15 on v12

--- a/solution.py
+++ b/solution.py
@@ -759,9 +759,14 @@
     return jnp.concatenate([piece[:, :first], moved, piece[:, last:]], axis=1)
 
 
-def gain_rows(grads):
-    tall = grads.astype(BF16).T.reshape(8, 192, 4)
-    return jnp.pad(tall, ((0, 0), (0, 0), (0, 124)))
+def butterfly(values):
+    for axis, size in (("core", 2), ("x", 4), ("z", 4), ("yhi", 2), ("ylo", 2)):
+        step = 1
+        while step < size:
+            pairs = [(i, i ^ step) for i in range(size)]
+            values = values + lax.ppermute(values, axis, pairs)
+            step *= 2
+    return values
 
 
 def norm_back(grad, own_normed, state, gain):
@@ -917,23 +922,22 @@
     second = yhi_sum(jnp.concatenate([second_feed, second_attn], axis=2)[0], core, yhi)
     grad, attn_grad = attention_back(0, grad, ring_gather(low), (), (second,))
     low = grad.astype(BF16)
-    attn_grad = tie(attn_grad, first_feed, low)
-    attn_grad = jnp.concatenate([attn_grad, gain_rows(jnp.stack(gain_grads))], axis=2)
-    first_attn = scatter(attn_grad)
-    second_piece = cross(ylo_sum(second), 3072, first_attn)
-    feed_piece = ylo_sum(yhi_sum(first_feed[0], core, yhi))
+    first_attn = scatter(tie(attn_grad, first_feed))
+    second_piece = cross(ylo_sum(second), 3072, first_attn, low)
+    feed_piece = ylo_sum(yhi_sum(tie(first_feed, low)[0], core, yhi))
+    gain_sums = butterfly(jnp.stack(gain_grads))
     back = from_lines(interleave(last_rows, low), z)
     output, input_grad = separate(back)
     output, input_grad = output[None], input_grad.astype(F32)[None]
 
     every = lax.all_gather(second_piece, ("x", "core"), axis=0, tiled=False)
     results[10:14], results[15:18] = unpack_call(every.reshape(4, 2, 96, -1))
-    attn_piece = ylo_sum(yhi_sum(tie(first_attn, feed_piece)[0], core, yhi))
+    attn_piece = ylo_sum(yhi_sum(tie(first_attn, feed_piece, gain_sums)[0], core, yhi))
     first_piece = jnp.concatenate([feed_piece, cross(attn_piece, 0)], axis=1)
     every = lax.all_gather(first_piece, ("x", "core"), axis=0, tiled=False)
     every = every.reshape(4, 2, 96, -1)
     results[1:5], results[6:9] = unpack_call(every)
-    gain_sums = every[..., 4224:4228].astype(F32).sum(axis=0).reshape(192, 4).T
+    gain_sums = lax.dynamic_slice_in_dim(gain_sums, (2 * z + yhi) * 192, 192, axis=1)
     for index, slot in enumerate((0, 5, 9, 14)):
         results[slot] = gain_sums[index]
     return (output, input_grad, *results)

time: 738 us -> 732 us (level)
  starting transfers between devices: 201 us -> 213 us
  waiting for transfers between devices: 257 us -> 249 us
    ppermute x3, waiting for transfers between devices: 34.6 us -> 5.49 us  [ylo_sum(): return add_low(piece, lax.ppermute(piece, 'ylo', SWAP))]
    ppermute x0 -> x7, waiting for transfers between devices: none -> 14.8 us  [butterfly(): values = values + lax.ppermute(values, axis, pairs)]
    unnamed x325 -> x321, local copies, waits for them, and re-layouts: 40.4 us -> 37 us
  transfers between devices with their start and end apart: 100 -> 107, of which waited for: 47 -> 53; matrix products, arithmetic and copies ran while one was open for 7% -> 7% of each run, Pallas kernels for 18% -> 18%
where the time goes in v15:
time: 732 us; the launch traced here: 723 us
  waiting for transfers between devices  249 us (34%)
  starting transfers between devices  213 us (29%)
  Pallas kernels  145 us (20%)
  local copies, waits for them, and re-layouts  57.7 us (8%)
  other arithmetic  39.7 us (5%)
  between operations  17.8 us (2%)
    ppermute x8, waiting for transfers between devices, ring_gather(): from_left = lax.ppermute(block, 'x', RIGHT)  43.3 us
    unnamed x321, local copies, waits for them, and re-layouts  37 us
    reduce_scatter x4, waiting for transfers between devices, scatter(): return lax.psum_scatter(block, SPREAD, scatter_dimension=0, tiled=True)  30.2 us
    pallas_call x2, Pallas kernels, feed_backward_call(): pl.pallas_call(later(feed_backward_kernel, len(after)), grid=(4,), in_spe...  27.4 us
    pallas_call x2, Pallas kernels, attend_backward_call(): pl.pallas_call(later(functools.partial(attend_backward_kernel, window), l...  26.7 us
    ppermute x4, starting transfers between devices, from_lines(): lax.ppermute(block[part * k:part * (k + 1)], AXES, inverse(LINES[k]))  23.9 us
    ppermute x8, waiting for transfers between devices, ring_gather(): far_first = lax.ppermute(from_left[:half], 'x', RIGHT)  23.8 us
    pallas_call x2, Pallas kernels, feed_weights_call(): pl.pallas_call(feed_weights_kernel, grid=(12,), in_specs=PIECES + PIECES...  23.2 us
  transfers between devices with their start and end apart: 107, of which 53 were waited for; matrix products, arithmetic and copies ran while one was open for 7% of the time, Pallas kernels for 18%

profile of v15, /device:TPU:1, one launch (start us, length us, event | category | flops | bytes accessed | tf_op | source)
XLA Modules:
  0.0 722.6 jit_solution(15922018634290602492)
XLA Ops:
  26.7 6.6 collective-permute-start
  34.7 10.0 %collective-permute-start.2 = (bf16[64,1536]{1,0:T(8,128)(2,1)S(1)}, bf16[64,1536]{1,0:T(8,128)(2,1)S(1)}, u32[]{:S(2)}, u32[]{:S(2)}) collective-permute-start(bf16[64,1536]{1,0:T(8,128)(2,1)S(1)} %get-tuple-element.238), channel_id=1, source_target_pairs={{0,32},{1,40},{2,48},{3,56},{4,0},{5,8},{6,16},{7,24},{8,33},{9,41... | collective-permute-start | bytes 589832 | tf_op jit(solution)/shard_map/ppermute | solution.py:678
  63.9 8.2 %collective-permute-done.5.refs_1_ = bf16[128,1536]{1,0:T(8,128)(2,1)S(1)} collective-permute-done((bf16[128,1536]{1,0:T(8,128)(2,1)S(1)}, bf16[128,1536]{1,0:T(8,128)(2,1)S(1)}, u32[]{:S(2)}, u32[]{:S(2)}) %collective-permute-start.5) | collective-permute-done | bytes 393248 | tf_op jit(solution)/shard_map/ppermute | solution.py:703
  99.4 9.0 %attend.2 = (f32[128,1536]{1,0:T(8,128)S(1)}, f32[128,1536]{1,0:T(8,128)S(1)}, f32[128,1536]{1,0:T(8,128)S(1)}, bf16[128,1536]{1,0:T(8,128)(2,1)S(1)}, bf16[512,...) custom-call(s32[1]{0:T(128)} %collective-permute-done.4.length.refs_2_.refs_1_, ...), custom_call_target="tpu_custom_call" | custom-call | flops 3000000000 | bytes 6000000 | tf_op jit(solution)/shard_map/attend/pallas_call | solution.py:380
  121.4 6.9 collective-permute-start.34
  138.2 11.2 %collective-permute-done.16.refs_1_ = bf16[128,1536]{1,0:T(8,128)(2,1)S(1)} collective-permute-done((bf16[128,1536]{1,0:T(8,128)(2,1)S(1)}, bf16[128,1536]{1,0:T(8,128)(2,1)S(1)}, u32[]{:S(2)}, u32[]{:S(2)}) %collective-permute-start.16) | collective-permute-done | bytes 393248 | tf_op jit(solution)/shard_map/ppermute | solution.py:703
  156.3 9.3 %feed_forward.2 = (f32[128,1536]{1,0:T(8,128)S(1)}, f32[128,1536]{1,0:T(8,128)S(1)}, f32[128,1536]{1,0:T(8,128)S(1)}, bf16[128,1536]{1,0:T(8,128)(2,1)S(1)}, f32...) custom-call(bf16[128,1536]{1,0:T(8,128)(2,1)S(1)} %multiply_convert_fusion.2.refs_0_, ...), custom_call_target="tpu_custom_call" | custom-call | flops 4899999744 | bytes 18000000 | tf_op jit(solution)/shard_map/feed_forward/pallas_call | solution.py:138
  179.5 7.3 %collective-permute-done.44 = bf16[192,3072]{1,0:T(8,128)(2,1)} collective-permute-done((bf16[192,3072]{1,0:T(8,128)(2,1)S(1)}, bf16[192,3072]{1,0:T(8,128)(2,1)}, u32[]{:S(2)}, u32[]{:S(2)}) %collective-permute-start.44) | collective-permute-done | bytes 1179680 | tf_op jit(solution)/shard_map/ppermute | solution.py:790
  210.1 7.6 %collective-permute-start.35 = (bf16[512,384]{1,0:T(8,128)(2,1)S(1)}, bf16[512,384]{1,0:T(8,128)(2,1)S(1)}, u32[]{:S(2)}, u32[]{:S(2)}) collective-permute-start(bf16[512,384]{1,0:T(8,128)(2,1)S(1)} %get-tuple-element.125.refs_4_.refs_8_), channel_id=1, source_target_pairs={{0,8},{8,0},{1,9},{9,1},{2,10},{10,2},{3,11},{11,3},{4,12},{12,4},... | collective-permute-start | bytes 1179656 | tf_op jit(solution)/shard_map/ppermute | solution.py:861
  225.7 9.0 %attend.3 = (f32[128,1536]{1,0:T(8,128)S(1)}, f32[128,1536]{1,0:T(8,128)S(1)}, f32[128,1536]{1,0:T(8,128)S(1)}, bf16[128,1536]{1,0:T(8,128)(2,1)S(1)}, bf16[512,...) custom-call(bf16[64,1536]{1,0:T(8,128)(2,1)S(1)} %collective-permute-done.26.refs_0_.refs_3_.refs_8_, ...), custom_call_target="tpu_custom_call" | custom-call | flops 3000000000 | bytes 6000000 | tf_op jit(solution)/shard_map/attend/pallas_call | solution.py:380
  246.5 6.9 collective-permute-done.37
  259.5 6.8 collective-permute-done.40.refs_1_
  276.2 9.2 %feed_forward.3 = (f32[128,1536]{1,0:T(8,128)S(1)}, f32[128,1536]{1,0:T(8,128)S(1)}, f32[128,1536]{1,0:T(8,128)S(1)}, bf16[128,1536]{1,0:T(8,128)(2,1)S(1)}, f32...) custom-call(bf16[128,1536]{1,0:T(8,128)(2,1)S(1)} %multiply_convert_fusion.refs_0_, ...), custom_call_target="tpu_custom_call" | custom-call | flops 4899999744 | bytes 18000000 | tf_op jit(solution)/shard_map/feed_forward/pallas_call | solution.py:138
  291.2 13.6 %feed_backward.2 = (f32[128,1536]{1,0:T(8,128)S(1)}, bf16[128,1536]{1,0:T(8,128)(2,1)}, bf16[128,1536]{1,0:T(8,128)(2,1)}, bf16[128,1536]{1,0:T(8,128)(2,1)}, bf...) custom-call(bf16[128,1536]{1,0:T(8,128)(2,1)S(1)} %pad_maximum_fusion.9.refs_0_.refs_5_, ...), custom_call_target="tpu_custom_call" | custom-call | flops 4899999744 | bytes 20000000 | tf_op jit(solution)/shard_map/feed_backward/pallas_call | solution.py:191
  308.4 11.6 %feed_weights.2 = bf16[8,192,3072]{2,1,0:T(8,128)(2,1)} custom-call(bf16[128,1536]{1,0:T(8,128)(2,1)S(1)} %multiply_convert_fusion.refs_0_, bf16[128,1536]{1,0:T(8,128)(2,1)S(1)} %copy-done.41, bf16[128,1536]{1,0:T(8,128)(2,1)S(1)} %copy-done.44, bf16[64,1536]{1,0:T(8,128)(2,1)S(1)} %collective-permute-done.42.refs_3_, bf16[64,1536]{1,0:T(8,128)(2,1)S(1)} %copy-done.82, ...), custom_call_target="tpu_custom_call" | custom-call | flops 4899999744 | bytes 18000000 | tf_op jit(solution)/shard_map/feed_weights/pallas_call | solution.py:244
  350.9 13.2 %attend_backward.2 = (bf16[512,384]{1,0:T(8,128)(2,1)S(1)}, f32[512,384]{1,0:T(8,128)}, bf16[512,384]{1,0:T(8,128)(2,1)S(1)}) custom-call(bf16[128,1536]{1,0:T(8,128)(2,1)S(1)} %get-tuple-element.235.refs_0_, s32[1]{0:T(128)} %collective-permute-done.4.length.refs_2_.refs_1_, bf16[128,1536]{1,0:T(8,128)(2,1)} %copy-done.29, bf16[128,1536]{1,0:T(8,128)(2,1)} %copy-done.47, ...), custom_call_target="tpu_custom_call" | custom-call | flops 6000000000 | bytes 6000000 | tf_op jit(solution)/shard_map/attend_backward/pallas_call | solution.py:455
  364.2 9.5 %collective-permute-start.56 = (bf16[512,384]{1,0:T(8,128)(2,1)S(1)}, bf16[512,384]{1,0:T(8,128)(2,1)S(1)}, u32[]{:S(2)}, u32[]{:S(2)}) collective-permute-start(bf16[512,384]{1,0:T(8,128)(2,1)S(1)} %get-tuple-element.148), channel_id=1, source_target_pairs={{0,8},{8,0},{1,9},{9,1},{2,10},{10,2},{3,11},{11,3},{4,12},{12,4},... | collective-permute-start | bytes 1179656 | tf_op jit(solution)/shard_map/ppermute | solution.py:901
  391.7 7.2 collective-permute-done.58
  409.5 7.7 %collective-permute-done.60.refs_2_.refs_6_ = bf16[128,1536]{1,0:T(8,128)(2,1)S(1)} collective-permute-done((bf16[128,1536]{1,0:T(8,128)(2,1)S(1)}, bf16[128,1536]{1,0:T(8,128)(2,1)S(1)}, u32[]{:S(2)}, u32[]{:S(2)}) %collective-permute-start.60) | collective-permute-done | bytes 393248 | tf_op jit(solution)/shard_map/ppermute | solution.py:703
  426.3 13.8 %feed_backward.3 = (f32[128,1536]{1,0:T(8,128)S(1)}, bf16[128,1536]{1,0:T(8,128)(2,1)}, bf16[128,1536]{1,0:T(8,128)(2,1)}, bf16[128,1536]{1,0:T(8,128)(2,1)}, bf...) custom-call(bf16[1,192,3072]{2,1,0:T(8,128)(2,1)S(1)} %copy-done.8, ...), custom_call_target="tpu_custom_call" | custom-call | flops 4899999744 | bytes 20000000 | tf_op jit(solution)/shard_map/feed_backward/pallas_call | solution.py:191
  445.2 11.6 %feed_weights.3 = bf16[8,192,3072]{2,1,0:T(8,128)(2,1)} custom-call(bf16[128,1536]{1,0:T(8,128)(2,1)S(1)} %copy-done.16, bf16[128,1536]{1,0:T(8,128)(2,1)S(1)} %copy-done.34, bf16[128,1536]{1,0:T(8,128)(2,1)S(1)} %copy-done.36, bf16[64,1536]{1,0:T(8,128)(2,1)S(1)} %copy-done.73, bf16[64,1536]{1,0:T(8,128)(2,1)S(1)} %copy-done.75, ...), custom_call_target="tpu_custom_call" | custom-call | flops 4899999744 | bytes 18000000 | tf_op jit(solution)/shard_map/feed_weights/pallas_call | solution.py:244
  489.5 13.5 %attend_backward.3 = (bf16[512,384]{1,0:T(8,128)(2,1)S(1)}, f32[512,384]{1,0:T(8,128)}, bf16[512,384]{1,0:T(8,128)(2,1)S(1)}) custom-call(s32[1]{0:T(128)} %collective-permute-done.4.length.refs_2_.refs_1_, bf16[128,1536]{1,0:T(8,128)(2,1)S(1)} %get-tuple-element.167.refs_0_.refs_1_, bf16[128,1536]{1,0:T(8,128)(2,1)} %copy-done.45, ...), custom_call_target="tpu_custom_call" | custom-call | flops 6000000000 | bytes 6000000 | tf_op jit(solution)/shard_map/attend_backward/pallas_call | solution.py:455
  513.5 15.2 %reduce-scatter.9.cloned.1.call-done = bf16[1,192,3072]{2,1,0:T(8,128)(2,1)} async-done(((bf16[8,192,3072]{2,1,0:T(8,128)(2,1)}), bf16[1,192,3072]{2,1,0:T(8,128)(2,1)}) %reduce-scatter.9.cloned.1.call-update) | async-done | bytes 1179664 | tf_op jit(solution)/shard_map/reduce_scatter | solution.py:910
  539.4 9.3 %collective-permute-done.76 = bf16[128,1536]{1,0:T(8,128)(2,1)} collective-permute-done((bf16[128,1536]{1,0:T(8,128)(2,1)S(1)}, bf16[128,1536]{1,0:T(8,128)(2,1)}, u32[]{:S(2)}, u32[]{:S(2)}) %collective-permute-start.76) | collective-permute-done | bytes 393248 | tf_op jit(solution)/shard_map/ppermute | solution.py:724
  552.9 12.9 %reduce-scatter.11.cloned.1.call-done = bf16[1,192,1152]{2,1,0:T(8,128)(2,1)} async-done(((bf16[8,192,1152]{2,1,0:T(8,128)(2,1)}), bf16[1,192,1152]{2,1,0:T(8,128)(2,1)}) %reduce-scatter.11.cloned.1.call-update) | async-done | bytes 442384 | tf_op jit(solution)/shard_map/reduce_scatter | solution.py:910
  578.4 10.8 %collective-permute-done.89 = bf16[96,3072]{1,0:T(8,128)(2,1)S(1)} collective-permute-done((bf16[96,3072]{1,0:T(8,128)(2,1)S(1)}, bf16[96,3072]{1,0:T(8,128)(2,1)S(1)}, u32[]{:S(2)}, u32[]{:S(2)}) %collective-permute-start.89) | collective-permute-done | bytes 589856 | tf_op jit(solution)/shard_map/ppermute | solution.py:747
  634.5 10.3 %collective-permute-start.80 = (bf16[64,1536]{1,0:T(8,128)(2,1)S(1)}, bf16[64,1536]{1,0:T(8,128)(2,1)S(1)}, u32[]{:S(2)}, u32[]{:S(2)}) collective-permute-start(bf16[64,1536]{1,0:T(8,128)(2,1)S(1)} %pad_maximum_fusion.18), channel_id=1, source_target_pairs={{48,0},{56,1},{0,2},{8,3},{16,4},{24,5},{32,6},{40,7},{49,8},{57,9... | collective-permute-start | bytes 589832 | tf_op jit(solution)/shard_map/ppermute | solution.py:686
  648.1 6.7 collective-permute-start.77
  659.1 11.7 %collective-permute-done.77 = bf16[64,1536]{1,0:T(8,128)(2,1)S(1)} collective-permute-done((bf16[64,1536]{1,0:T(8,128)(2,1)S(1)}, bf16[64,1536]{1,0:T(8,128)(2,1)S(1)}, u32[]{:S(2)}, u32[]{:S(2)}) %collective-permute-start.77) | collective-permute-done | bytes 196640 | tf_op jit(solution)/shard_map/ppermute | solution.py:686
  678.6 7.4 %unpack.3 = (f32[192,1536]{1,0:T(8,128)}, f32[192,768]{1,0:T(8,128)}, f32[192,768]{1,0:T(8,128)}, f32[192,1536]{1,0:T(8,128)}, f32[192,4096]{1,0:T(8,128)}, /*in...) custom-call(bf16[4,2,96,4224]{3,2,1,0:T(8,128)(2,1)} %bitcast.74), custom_call_target="tpu_custom_call" | custom-call | flops 1000000 | bytes 30000000 | tf_op jit(solution)/shard_map/unpack/pallas_call | solution.py:577
  686.0 22.1 %all-gather.21.cloned.1.call-done = bf16[768,4224]{1,0:T(8,128)(2,1)} async-done(((bf16[96,4224]{1,0:T(8,128)(2,1)}), bf16[768,4224]{1,0:T(8,128)(2,1)}) %all-gather.21.cloned.1.call-update) | async-done | bytes 6488080 | tf_op jit(solution)/shard_map/all_gather | solution.py:937
  708.1 7.5 %unpack.2 = (f32[192,1536]{1,0:T(8,128)}, f32[192,768]{1,0:T(8,128)}, f32[192,768]{1,0:T(8,128)}, f32[192,1536]{1,0:T(8,128)}, f32[192,4096]{1,0:T(8,128)}, /*in...) custom-call(bf16[4,2,96,4224]{3,2,1,0:T(8,128)(2,1)} %bitcast.75), custom_call_target="tpu_custom_call" | custom-call | flops 1000000 | bytes 30000000 | tf_op jit(solution)/shard_map/unpack/pallas_call | solution.py:577
  (713 shorter events, 381.0 us)
Async XLA Ops:
  7.2 77.5 %all-gather.13.cloned.1.call-start = ((), (), s32[]{:S(2)}) async-start(), calls=%async_computation.8 | async-start | bytes 4423680 | tf_op jit(solution)/shard_map/all_gather | solution.py:807
  26.3 129.9 %all-gather.15.cloned.1.call-start = ((), (), s32[]{:S(2)}) async-start(), calls=%async_computation.9 | async-start | bytes 10616832 | tf_op jit(solution)/shard_map/all_gather | solution.py:807
  26.7 24.7 %collective-permute-start = (bf16[64,1536]{1,0:T(8,128)(2,1)S(1)}, bf16[64,1536]{1,0:T(8,128)(2,1)S(1)}, u32[]{:S(2)}, u32[]{:S(2)}) collective-permute-start(bf16[64,1536]{1,0:T(8,128)(2,1)S(1)} %get-tuple-element.236), channel_id=1, source_target_pairs={{0,0},{1,8},{2,16},{3,24},{4,32},{5,40},{6,48},{7,56},{8,1},{9,9},... | collective-permute-start | bytes 589832 | tf_op jit(solution)/shard_map/ppermute | solution.py:678
  33.3 18.7 %collective-permute-start.1 = (bf16[64,1536]{1,0:T(8,128)(2,1)S(1)}, bf16[64,1536]{1,0:T(8,128)(2,1)S(1)}, u32[]{:S(2)}, u32[]{:S(2)}) collective-permute-start(bf16[64,1536]{1,0:T(8,128)(2,1)S(1)} %get-tuple-element.239), channel_id=1, source_target_pairs={{0,16},{1,24},{2,32},{3,40},{4,48},{5,56},{6,0},{7,8},{8,17},{9,25... | collective-permute-start | bytes 589832 | tf_op jit(solution)/shard_map/ppermute | solution.py:678
  34.7 24.5 %collective-permute-start.2 = (bf16[64,1536]{1,0:T(8,128)(2,1)S(1)}, bf16[64,1536]{1,0:T(8,128)(2,1)S(1)}, u32[]{:S(2)}, u32[]{:S(2)}) collective-permute-start(bf16[64,1536]{1,0:T(8,128)(2,1)S(1)} %get-tuple-element.238), channel_id=1, source_target_pairs={{0,32},{1,40},{2,48},{3,56},{4,0},{5,8},{6,16},{7,24},{8,33},{9,41... | collective-permute-start | bytes 589832 | tf_op jit(solution)/shard_map/ppermute | solution.py:678
  50.1 25.1 %collective-permute-start.20 = (bf16[192,3072]{1,0:T(8,128)(2,1)S(1)}, bf16[192,3072]{1,0:T(8,128)(2,1)S(1)}, u32[]{:S(2)}, u32[]{:S(2)}) collective-permute-start(bf16[192,3072]{1,0:T(8,128)(2,1)S(1)} %pack_feed.2), channel_id=1, source_target_pairs={{0,1},{2,3},{4,5},{6,7},{9,8},{11,10},{13,12},{15,14},{16,17},{18,... | collective-permute-start | bytes 3538952 | tf_op jit(solution)/shard_map/ppermute | solution.py:790
  80.3 124.0 %all-gather.17.cloned.1.call-start = ((), (), s32[]{:S(2)}) async-start(), calls=%async_computation.10 | async-start | bytes 3981312 | tf_op jit(solution)/shard_map/all_gather | solution.py:807
  130.7 18.8 %collective-permute-start.16 = (bf16[128,1536]{1,0:T(8,128)(2,1)S(1)}, bf16[128,1536]{1,0:T(8,128)(2,1)S(1)}, u32[]{:S(2)}, u32[]{:S(2)}) collective-permute-start(bf16[128,1536]{1,0:T(8,128)(2,1)S(1)} %multiply_convert_fusion.2.refs_0_), channel_id=1, source_target_pairs={{0,16},{16,32},{32,48},{48,0},{1,17},{17,33},{33,49},{49,1},{2,18}... | collective-permute-start | bytes 1179656 | tf_op jit(solution)/shard_map/ppermute | solution.py:703
  130.7 18.8 %collective-permute-start.17 = (bf16[128,1536]{1,0:T(8,128)(2,1)S(1)}, bf16[128,1536]{1,0:T(8,128)(2,1)S(1)}, u32[]{:S(2)}, u32[]{:S(2)}) collective-permute-start(bf16[128,1536]{1,0:T(8,128)(2,1)S(1)} %multiply_convert_fusion.2.refs_0_), channel_id=1, source_target_pairs={{0,48},{16,0},{32,16},{48,32},{1,49},{17,1},{33,17},{49,33},{2,50}... | collective-permute-start | bytes 1179656 | tf_op jit(solution)/shard_map/ppermute | solution.py:704
  149.5 123.8 %all-gather.19.cloned.1.call-start = ((), (), s32[]{:S(2)}) async-start(), calls=%async_computation.11 | async-start | bytes 10616832 | tf_op jit(solution)/shard_map/all_gather | solution.py:807
  168.3 18.5 %collective-permute-start.44 = (bf16[192,3072]{1,0:T(8,128)(2,1)S(1)}, bf16[192,3072]{1,0:T(8,128)(2,1)}, u32[]{:S(2)}, u32[]{:S(2)}) collective-permute-start(bf16[192,3072]{1,0:T(8,128)(2,1)S(1)} %pack_feed.3), channel_id=1, source_target_pairs={{0,1},{2,3},{4,5},{6,7},{9,8},{11,10},{13,12},{15,14},{16,17},{18,... | collective-permute-start | bytes 3538952 | tf_op jit(solution)/shard_map/ppermute | solution.py:790
  197.3 209.4 %reduce-scatter.5.cloned.1.call-start = ((), (), s32[]{:S(2)}) async-start(), calls=%async_computation.4 | async-start | bytes 10616832 | tf_op jit(solution)/shard_map/reduce_scatter | solution.py:910
  288.1 34.1 %collective-permute-start.45 = (bf16[64,1536]{1,0:T(8,128)(2,1)}, bf16[64,1536]{1,0:T(8,128)(2,1)}, u32[]{:S(2)}, u32[]{:S(2)}) collective-permute-start(bf16[64,1536]{1,0:T(8,128)(2,1)} %get-tuple-element.248), channel_id=1, source_target_pairs={{0,16},{16,32},{32,48},{48,0},{1,17},{17,33},{33,49},{49,1},{2,18}... | collective-permute-start | bytes 589832 | tf_op jit(solution)/shard_map/ppermute | solution.py:712
  288.2 36.2 %collective-permute-start.47 = (bf16[64,1536]{1,0:T(8,128)(2,1)}, bf16[64,1536]{1,0:T(8,128)(2,1)}, u32[]{:S(2)}, u32[]{:S(2)}) collective-permute-start(bf16[64,1536]{1,0:T(8,128)(2,1)} %get-tuple-element.249), channel_id=1, source_target_pairs={{0,48},{16,0},{32,16},{48,32},{1,49},{17,1},{33,17},{49,33},{2,50}... | collective-permute-start | bytes 589832 | tf_op jit(solution)/shard_map/ppermute | solution.py:713
  305.7 22.0 %collective-permute-start.49 = (bf16[128,1536]{1,0:T(8,128)(2,1)}, bf16[128,1536]{1,0:T(8,128)(2,1)}, u32[]{:S(2)}, u32[]{:S(2)}) collective-permute-start(bf16[128,1536]{1,0:T(8,128)(2,1)} %get-tuple-element.138), channel_id=1, source_target_pairs={{0,16},{16,32},{32,48},{48,0},{1,17},{17,33},{33,49},{49,1},{2,18}... | collective-permute-start | bytes 1179656 | tf_op jit(solution)/shard_map/ppermute | solution.py:722
  305.7 22.0 %collective-permute-start.50 = (bf16[128,1536]{1,0:T(8,128)(2,1)}, bf16[128,1536]{1,0:T(8,128)(2,1)}, u32[]{:S(2)}, u32[]{:S(2)}) collective-permute-start(bf16[128,1536]{1,0:T(8,128)(2,1)} %get-tuple-element.139), channel_id=1, source_target_pairs={{0,48},{16,0},{32,16},{48,32},{1,49},{17,1},{33,17},{49,33},{2,50}... | collective-permute-start | bytes 1179656 | tf_op jit(solution)/shard_map/ppermute | solution.py:723
  308.4 19.3 %collective-permute-start.51 = (bf16[128,1536]{1,0:T(8,128)(2,1)}, bf16[128,1536]{1,0:T(8,128)(2,1)}, u32[]{:S(2)}, u32[]{:S(2)}) collective-permute-start(bf16[128,1536]{1,0:T(8,128)(2,1)} %get-tuple-element.140), channel_id=1, source_target_pairs={{0,32},{16,48},{32,0},{48,16},{1,33},{17,49},{33,1},{49,17},{2,34}... | collective-permute-start | bytes 1179656 | tf_op jit(solution)/shard_map/ppermute | solution.py:724
  333.3 128.8 %reduce-scatter.7.cloned.1.call-start = ((), (), s32[]{:S(2)}) async-start(), calls=%async_computation.5 | async-start | bytes 3981312 | tf_op jit(solution)/shard_map/reduce_scatter | solution.py:910
  379.3 19.6 %collective-permute-start.58 = (bf16[128,1536]{1,0:T(8,128)(2,1)}, bf16[128,1536]{1,0:T(8,128)(2,1)}, u32[]{:S(2)}, u32[]{:S(2)}) collective-permute-start(bf16[128,1536]{1,0:T(8,128)(2,1)} %get-tuple-element.151), channel_id=1, source_target_pairs={{0,48},{16,0},{32,16},{48,32},{1,49},{17,1},{33,17},{49,33},{2,50}... | collective-permute-start | bytes 1179656 | tf_op jit(solution)/shard_map/ppermute | solution.py:723
  382.2 18.8 %collective-permute-start.59 = (bf16[128,1536]{1,0:T(8,128)(2,1)S(1)}, bf16[128,1536]{1,0:T(8,128)(2,1)}, u32[]{:S(2)}, u32[]{:S(2)}) collective-permute-start(bf16[128,1536]{1,0:T(8,128)(2,1)S(1)} %get-tuple-element.152), channel_id=1, source_target_pairs={{0,32},{16,48},{32,0},{48,16},{1,33},{17,49},{33,1},{49,17},{2,34}... | collective-permute-start | bytes 1179656 | tf_op jit(solution)/shard_map/ppermute | solution.py:724
  406.7 122.0 %reduce-scatter.9.cloned.1.call-start = ((), (), s32[]{:S(2)}) async-start(), calls=%async_computation.6 | async-start | bytes 10616832 | tf_op jit(solution)/shard_map/reduce_scatter | solution.py:910
  462.2 103.6 %reduce-scatter.11.cloned.1.call-start = ((), (), s32[]{:S(2)}) async-start(), calls=%async_computation.7 | async-start | bytes 3981312 | tf_op jit(solution)/shard_map/reduce_scatter | solution.py:910
  475.4 29.4 %collective-permute-start.68 = (bf16[96,4224]{1,0:T(8,128)(2,1)}, bf16[96,4224]{1,0:T(8,128)(2,1)S(1)}, u32[]{:S(2)}, u32[]{:S(2)}) collective-permute-start(bf16[96,4224]{1,0:T(8,128)(2,1)} %bitcast_select_fusion), channel_id=1, source_target_pairs={{0,1},{1,0},{2,3},{3,2},{4,5},{5,4},{6,7},{7,6},{8,9},{9,8},{10,11... | collective-permute-start | bytes 2433032 | tf_op jit(solution)/shard_map/ppermute | solution.py:747
  528.8 149.8 %all-gather.23.cloned.1.call-start = ((), (), s32[]{:S(2)}) async-start(), calls=%async_computation.13 | async-start | bytes 7299072 | tf_op jit(solution)/shard_map/all_gather | solution.py:933
  531.6 17.2 %collective-permute-start.76 = (bf16[128,1536]{1,0:T(8,128)(2,1)S(1)}, bf16[128,1536]{1,0:T(8,128)(2,1)}, u32[]{:S(2)}, u32[]{:S(2)}) collective-permute-start(bf16[128,1536]{1,0:T(8,128)(2,1)S(1)} %get-tuple-element.175), channel_id=1, source_target_pairs={{0,32},{16,48},{32,0},{48,16},{1,33},{17,49},{33,1},{49,17},{2,34}... | collective-permute-start | bytes 1179656 | tf_op jit(solution)/shard_map/ppermute | solution.py:724
  533.0 17.4 %collective-permute-start.95 = (bf16[96,4224]{1,0:T(8,128)(2,1)S(1)}, bf16[96,4224]{1,0:T(8,128)(2,1)}, u32[]{:S(2)}, u32[]{:S(2)}) collective-permute-start(bf16[96,4224]{1,0:T(8,128)(2,1)S(1)} %add_convert_fusion.1.refs_0_), channel_id=1, source_target_pairs={{0,64},{64,0},{1,65},{65,1},{2,66},{66,2},{3,67},{67,3},{4,68},{68... | collective-permute-start | bytes 2433032 | tf_op jit(solution)/shard_map/ppermute | solution.py:751
  566.8 141.3 %all-gather.21.cloned.1.call-start = ((), (), s32[]{:S(2)}) async-start(), calls=%async_computation.12 | async-start | bytes 7299072 | tf_op jit(solution)/shard_map/all_gather | solution.py:937
  589.5 21.2 %collective-permute-start.90 = (bf16[96,3072]{1,0:T(8,128)(2,1)S(1)}, bf16[96,3072]{1,0:T(8,128)(2,1)S(1)}, u32[]{:S(2)}, u32[]{:S(2)}) collective-permute-start(bf16[96,3072]{1,0:T(8,128)(2,1)S(1)} %add_convert_fusion.3), channel_id=1, source_target_pairs={{0,64},{64,0},{1,65},{65,1},{2,66},{66,2},{3,67},{67,3},{4,68},{68... | collective-permute-start | bytes 1769480 | tf_op jit(solution)/shard_map/ppermute | solution.py:751
  634.5 42.3 %collective-permute-start.80 = (bf16[64,1536]{1,0:T(8,128)(2,1)S(1)}, bf16[64,1536]{1,0:T(8,128)(2,1)S(1)}, u32[]{:S(2)}, u32[]{:S(2)}) collective-permute-start(bf16[64,1536]{1,0:T(8,128)(2,1)S(1)} %pad_maximum_fusion.18), channel_id=1, source_target_pairs={{48,0},{56,1},{0,2},{8,3},{16,4},{24,5},{32,6},{40,7},{49,8},{57,9... | collective-permute-start | bytes 589832 | tf_op jit(solution)/shard_map/ppermute | solution.py:686
  644.8 31.9 %collective-permute-start.79 = (bf16[64,1536]{1,0:T(8,128)(2,1)S(1)}, bf16[64,1536]{1,0:T(8,128)(2,1)S(1)}, u32[]{:S(2)}, u32[]{:S(2)}) collective-permute-start(bf16[64,1536]{1,0:T(8,128)(2,1)S(1)} %pad_maximum_fusion.17), channel_id=1, source_target_pairs={{32,0},{40,1},{48,2},{56,3},{0,4},{8,5},{16,6},{24,7},{33,8},{41,9... | collective-permute-start | bytes 589832 | tf_op jit(solution)/shard_map/ppermute | solution.py:686
  648.1 22.8 %collective-permute-start.77 = (bf16[64,1536]{1,0:T(8,128)(2,1)S(1)}, bf16[64,1536]{1,0:T(8,128)(2,1)S(1)}, u32[]{:S(2)}, u32[]{:S(2)}) collective-permute-start(bf16[64,1536]{1,0:T(8,128)(2,1)S(1)} %pad_maximum_fusion.15), channel_id=1, source_target_pairs={{0,0},{8,1},{16,2},{24,3},{32,4},{40,5},{48,6},{56,7},{1,8},{9,9},... | collective-permute-start | bytes 589832 | tf_op jit(solution)/shard_map/ppermute | solution.py:686
  654.8 21.9 %collective-permute-start.78 = (bf16[64,1536]{1,0:T(8,128)(2,1)S(1)}, bf16[64,1536]{1,0:T(8,128)(2,1)S(1)}, u32[]{:S(2)}, u32[]{:S(2)}) collective-permute-start(bf16[64,1536]{1,0:T(8,128)(2,1)S(1)} %pad_maximum_fusion.16), channel_id=1, source_target_pairs={{16,0},{24,1},{32,2},{40,3},{48,4},{56,5},{0,6},{8,7},{17,8},{25,9... | collective-permute-start | bytes 589832 | tf_op jit(solution)/shard_map/ppermute | solution.py:686
  (228 other events, 1993.0 us)
Sparse Core Ops, SparseCore 0:
  26.4 45.1 all-gather.12
  80.4 51.0 all-gather.14
  149.6 33.0 all-gather.16
  197.4 66.1 all-gather.18
  333.4 73.2 reduce-scatter.4
  409.0 37.2 reduce-scatter.6
  462.3 66.3 reduce-scatter.8
  531.3 34.4 reduce-scatter.10
  568.1 45.1 all-gather.22
  634.5 73.5 all-gather.20

commit v16 on v15

--- a/solution.py
+++ b/solution.py
@@ -679,12 +679,18 @@
     return out
 
 
-def from_lines(block, z):
+def send_home(block):
     part = block.shape[0] // 4
-    out = jnp.zeros_like(block)
+    return [
+        lax.ppermute(block[part * k : part * (k + 1)], AXES, inverse(LINES[k])) for k in range(4)
+    ]
+
+
+def place_home(parts, z):
+    rows = parts[0].shape[0]
+    out = jnp.zeros((4 * rows,) + parts[0].shape[1:], parts[0].dtype)
     for k in range(4):
-        piece = lax.ppermute(block[part * k : part * (k + 1)], AXES, inverse(LINES[k]))
-        out = lax.dynamic_update_slice_in_dim(out, piece, ((z + k) % 4) * part, axis=0)
+        out = lax.dynamic_update_slice_in_dim(out, parts[k], ((z + k) % 4) * rows, axis=0)
     return out
 
 
@@ -924,15 +930,17 @@
     low = grad.astype(BF16)
     first_attn = scatter(tie(attn_grad, first_feed))
     second_piece = cross(ylo_sum(second), 3072, first_attn, low)
-    feed_piece = ylo_sum(yhi_sum(tie(first_feed, low)[0], core, yhi))
+    back = send_home(interleave(last_rows, low))
+    feed_piece = tie(yhi_sum(tie(first_feed, low)[0], core, yhi), back[0])
+    feed_piece = tie(ylo_sum(feed_piece), back[1])
     gain_sums = butterfly(jnp.stack(gain_grads))
-    back = from_lines(interleave(last_rows, low), z)
-    output, input_grad = separate(back)
+    output, input_grad = separate(place_home(back, z))
     output, input_grad = output[None], input_grad.astype(F32)[None]
 
     every = lax.all_gather(second_piece, ("x", "core"), axis=0, tiled=False)
     results[10:14], results[15:18] = unpack_call(every.reshape(4, 2, 96, -1))
-    attn_piece = ylo_sum(yhi_sum(tie(first_attn, feed_piece, gain_sums)[0], core, yhi))
+    attn_piece = yhi_sum(tie(first_attn, feed_piece, gain_sums)[0], core, yhi)
+    attn_piece = tie(ylo_sum(tie(attn_piece, back[2])), back[3])
     first_piece = jnp.concatenate([feed_piece, cross(attn_piece, 0)], axis=1)
     every = lax.all_gather(first_piece, ("x", "core"), axis=0, tiled=False)
     every = every.reshape(4, 2, 96, -1)

time: 732 us -> 746 us (1.019)
  waiting for transfers between devices: 249 us -> 274 us
  starting transfers between devices: 213 us -> 201 us
    all_gather x1, waiting for transfers between devices: 22.1 us -> 46.2 us  [body(): every = lax.all_gather(first_piece, ('x', 'core'), axis=0, tiled=False)]
  transfers between devices with their start and end apart: 107 -> 107, of which waited for: 53 -> 52; matrix products, arithmetic and copies ran while one was open for 7% -> 7% of each run, Pallas kernels for 18% -> 17%
where the time goes in v16:
time: 746 us; the launch traced here: 736 us
  waiting for transfers between devices  274 us (37%)
  starting transfers between devices  201 us (27%)
  Pallas kernels  145 us (19%)
  local copies, waits for them, and re-layouts  58.2 us (8%)
  other arithmetic  39.7 us (5%)
  between operations  17.8 us (2%)
    all_gather x1, waiting for transfers between devices, body(): every = lax.all_gather(first_piece, ('x', 'core'), axis=0, tiled=False)  46.2 us
    ppermute x8, waiting for transfers between devices, ring_gather(): from_left = lax.ppermute(block, 'x', RIGHT)  43.3 us
    unnamed x321, local copies, waits for them, and re-layouts  37.4 us
    reduce_scatter x4, waiting for transfers between devices, scatter(): return lax.psum_scatter(block, SPREAD, scatter_dimension=0, tiled=True)  30.2 us
    pallas_call x2, Pallas kernels, feed_backward_call(): pl.pallas_call(later(feed_backward_kernel, len(after)), grid=(4,), in_spe...  27.4 us
    pallas_call x2, Pallas kernels, attend_backward_call(): pl.pallas_call(later(functools.partial(attend_backward_kernel, window), l...  26.7 us
    ppermute x8, waiting for transfers between devices, ring_gather(): far_first = lax.ppermute(from_left[:half], 'x', RIGHT)  23.8 us
    pallas_call x2, Pallas kernels, feed_weights_call(): pl.pallas_call(feed_weights_kernel, grid=(12,), in_specs=PIECES + PIECES...  23.2 us
  transfers between devices with their start and end apart: 107, of which 52 were waited for; matrix products, arithmetic and copies ran while one was open for 7% of the time, Pallas kernels for 17%

profile of v16, /device:TPU:1, one launch (start us, length us, event | category | flops | bytes accessed | tf_op | source)
XLA Modules:
  0.0 736.0 jit_solution(6335606929735735606)
XLA Ops:
  26.7 6.6 collective-permute-start
  34.7 10.0 %collective-permute-start.2 = (bf16[64,1536]{1,0:T(8,128)(2,1)S(1)}, bf16[64,1536]{1,0:T(8,128)(2,1)S(1)}, u32[]{:S(2)}, u32[]{:S(2)}) collective-permute-start(bf16[64,1536]{1,0:T(8,128)(2,1)S(1)} %get-tuple-element.246), channel_id=1, source_target_pairs={{0,32},{1,40},{2,48},{3,56},{4,0},{5,8},{6,16},{7,24},{8,33},{9,41... | collective-permute-start | bytes 589832 | tf_op jit(solution)/shard_map/ppermute | solution.py:678
  63.9 8.2 %collective-permute-done.5.refs_1_ = bf16[128,1536]{1,0:T(8,128)(2,1)S(1)} collective-permute-done((bf16[128,1536]{1,0:T(8,128)(2,1)S(1)}, bf16[128,1536]{1,0:T(8,128)(2,1)S(1)}, u32[]{:S(2)}, u32[]{:S(2)}) %collective-permute-start.5) | collective-permute-done | bytes 393248 | tf_op jit(solution)/shard_map/ppermute | solution.py:709
  99.4 9.0 %attend.2 = (f32[128,1536]{1,0:T(8,128)S(1)}, f32[128,1536]{1,0:T(8,128)S(1)}, f32[128,1536]{1,0:T(8,128)S(1)}, bf16[128,1536]{1,0:T(8,128)(2,1)S(1)}, bf16[512,...) custom-call(s32[1]{0:T(128)} %collective-permute-done.4.length.refs_2_.refs_1_, ...), custom_call_target="tpu_custom_call" | custom-call | flops 3000000000 | bytes 6000000 | tf_op jit(solution)/shard_map/attend/pallas_call | solution.py:380
  121.4 6.9 collective-permute-start.34
  138.2 11.2 %collective-permute-done.16.refs_1_ = bf16[128,1536]{1,0:T(8,128)(2,1)S(1)} collective-permute-done((bf16[128,1536]{1,0:T(8,128)(2,1)S(1)}, bf16[128,1536]{1,0:T(8,128)(2,1)S(1)}, u32[]{:S(2)}, u32[]{:S(2)}) %collective-permute-start.16) | collective-permute-done | bytes 393248 | tf_op jit(solution)/shard_map/ppermute | solution.py:709
  156.3 9.3 %feed_forward.2 = (f32[128,1536]{1,0:T(8,128)S(1)}, f32[128,1536]{1,0:T(8,128)S(1)}, f32[128,1536]{1,0:T(8,128)S(1)}, bf16[128,1536]{1,0:T(8,128)(2,1)S(1)}, f32...) custom-call(bf16[128,1536]{1,0:T(8,128)(2,1)S(1)} %multiply_convert_fusion.2.refs_0_, ...), custom_call_target="tpu_custom_call" | custom-call | flops 4899999744 | bytes 18000000 | tf_op jit(solution)/shard_map/feed_forward/pallas_call | solution.py:138
  179.5 7.3 collective-permute-done.44
  210.1 7.6 %collective-permute-start.35 = (bf16[512,384]{1,0:T(8,128)(2,1)S(1)}, bf16[512,384]{1,0:T(8,128)(2,1)S(1)}, u32[]{:S(2)}, u32[]{:S(2)}) collective-permute-start(bf16[512,384]{1,0:T(8,128)(2,1)S(1)} %get-tuple-element.129.refs_4_.refs_8_), channel_id=1, source_target_pairs={{0,8},{8,0},{1,9},{9,1},{2,10},{10,2},{3,11},{11,3},{4,12},{12,4},... | collective-permute-start | bytes 1179656 | tf_op jit(solution)/shard_map/ppermute | solution.py:867
  225.7 9.0 %attend.3 = (f32[128,1536]{1,0:T(8,128)S(1)}, f32[128,1536]{1,0:T(8,128)S(1)}, f32[128,1536]{1,0:T(8,128)S(1)}, bf16[128,1536]{1,0:T(8,128)(2,1)S(1)}, bf16[512,...) custom-call(bf16[64,1536]{1,0:T(8,128)(2,1)S(1)} %collective-permute-done.26.refs_0_.refs_3_.refs_8_, ...), custom_call_target="tpu_custom_call" | custom-call | flops 3000000000 | bytes 6000000 | tf_op jit(solution)/shard_map/attend/pallas_call | solution.py:380
  246.5 6.9 collective-permute-done.37
  259.5 6.8 collective-permute-done.40.refs_1_
  276.2 9.2 %feed_forward.3 = (f32[128,1536]{1,0:T(8,128)S(1)}, f32[128,1536]{1,0:T(8,128)S(1)}, f32[128,1536]{1,0:T(8,128)S(1)}, bf16[128,1536]{1,0:T(8,128)(2,1)S(1)}, f32...) custom-call(bf16[128,1536]{1,0:T(8,128)(2,1)S(1)} %multiply_convert_fusion.refs_0_, ...), custom_call_target="tpu_custom_call" | custom-call | flops 4899999744 | bytes 18000000 | tf_op jit(solution)/shard_map/feed_forward/pallas_call | solution.py:138
  291.2 13.6 %feed_backward.2 = (f32[128,1536]{1,0:T(8,128)S(1)}, bf16[128,1536]{1,0:T(8,128)(2,1)}, bf16[128,1536]{1,0:T(8,128)(2,1)}, bf16[128,1536]{1,0:T(8,128)(2,1)}, bf...) custom-call(bf16[128,1536]{1,0:T(8,128)(2,1)S(1)} %pad_maximum_fusion.9.refs_0_.refs_5_, ...), custom_call_target="tpu_custom_call" | custom-call | flops 4899999744 | bytes 20000000 | tf_op jit(solution)/shard_map/feed_backward/pallas_call | solution.py:191
  308.4 11.6 %feed_weights.2 = bf16[8,192,3072]{2,1,0:T(8,128)(2,1)} custom-call(bf16[128,1536]{1,0:T(8,128)(2,1)S(1)} %multiply_convert_fusion.refs_0_, bf16[128,1536]{1,0:T(8,128)(2,1)S(1)} %copy-done.41, bf16[128,1536]{1,0:T(8,128)(2,1)S(1)} %copy-done.44, bf16[64,1536]{1,0:T(8,128)(2,1)S(1)} %collective-permute-done.42.refs_3_, bf16[64,1536]{1,0:T(8,128)(2,1)S(1)} %copy-done.82, ...), custom_call_target="tpu_custom_call" | custom-call | flops 4899999744 | bytes 18000000 | tf_op jit(solution)/shard_map/feed_weights/pallas_call | solution.py:244
  350.9 13.2 %attend_backward.2 = (bf16[512,384]{1,0:T(8,128)(2,1)S(1)}, f32[512,384]{1,0:T(8,128)}, bf16[512,384]{1,0:T(8,128)(2,1)S(1)}) custom-call(bf16[128,1536]{1,0:T(8,128)(2,1)S(1)} %get-tuple-element.243.refs_0_, s32[1]{0:T(128)} %collective-permute-done.4.length.refs_2_.refs_1_, bf16[128,1536]{1,0:T(8,128)(2,1)} %copy-done.29, bf16[128,1536]{1,0:T(8,128)(2,1)} %copy-done.47, ...), custom_call_target="tpu_custom_call" | custom-call | flops 6000000000 | bytes 6000000 | tf_op jit(solution)/shard_map/attend_backward/pallas_call | solution.py:455
  364.2 9.5 %collective-permute-start.56 = (bf16[512,384]{1,0:T(8,128)(2,1)S(1)}, bf16[512,384]{1,0:T(8,128)(2,1)S(1)}, u32[]{:S(2)}, u32[]{:S(2)}) collective-permute-start(bf16[512,384]{1,0:T(8,128)(2,1)S(1)} %get-tuple-element.152), channel_id=1, source_target_pairs={{0,8},{8,0},{1,9},{9,1},{2,10},{10,2},{3,11},{11,3},{4,12},{12,4},... | collective-permute-start | bytes 1179656 | tf_op jit(solution)/shard_map/ppermute | solution.py:907
  391.7 7.2 collective-permute-done.58
  409.5 7.7 %collective-permute-done.60.refs_2_.refs_6_ = bf16[128,1536]{1,0:T(8,128)(2,1)S(1)} collective-permute-done((bf16[128,1536]{1,0:T(8,128)(2,1)S(1)}, bf16[128,1536]{1,0:T(8,128)(2,1)S(1)}, u32[]{:S(2)}, u32[]{:S(2)}) %collective-permute-start.60) | collective-permute-done | bytes 393248 | tf_op jit(solution)/shard_map/ppermute | solution.py:709
  426.3 13.8 %feed_backward.3 = (f32[128,1536]{1,0:T(8,128)S(1)}, bf16[128,1536]{1,0:T(8,128)(2,1)}, bf16[128,1536]{1,0:T(8,128)(2,1)}, bf16[128,1536]{1,0:T(8,128)(2,1)}, bf...) custom-call(bf16[1,192,3072]{2,1,0:T(8,128)(2,1)S(1)} %copy-done.8, ...), custom_call_target="tpu_custom_call" | custom-call | flops 4899999744 | bytes 20000000 | tf_op jit(solution)/shard_map/feed_backward/pallas_call | solution.py:191
  445.2 11.6 %feed_weights.3 = bf16[8,192,3072]{2,1,0:T(8,128)(2,1)} custom-call(bf16[128,1536]{1,0:T(8,128)(2,1)S(1)} %copy-done.16, bf16[128,1536]{1,0:T(8,128)(2,1)S(1)} %copy-done.34, bf16[128,1536]{1,0:T(8,128)(2,1)S(1)} %copy-done.36, bf16[64,1536]{1,0:T(8,128)(2,1)S(1)} %copy-done.73, bf16[64,1536]{1,0:T(8,128)(2,1)S(1)} %copy-done.75, ...), custom_call_target="tpu_custom_call" | custom-call | flops 4899999744 | bytes 18000000 | tf_op jit(solution)/shard_map/feed_weights/pallas_call | solution.py:244
  489.5 13.5 %attend_backward.3 = (bf16[512,384]{1,0:T(8,128)(2,1)S(1)}, f32[512,384]{1,0:T(8,128)}, bf16[512,384]{1,0:T(8,128)(2,1)S(1)}) custom-call(s32[1]{0:T(128)} %collective-permute-done.4.length.refs_2_.refs_1_, bf16[128,1536]{1,0:T(8,128)(2,1)S(1)} %get-tuple-element.171.refs_0_.refs_1_, bf16[128,1536]{1,0:T(8,128)(2,1)} %copy-done.45, ...), custom_call_target="tpu_custom_call" | custom-call | flops 6000000000 | bytes 6000000 | tf_op jit(solution)/shard_map/attend_backward/pallas_call | solution.py:455
  513.5 15.2 %reduce-scatter.9.cloned.1.call-done = bf16[1,192,3072]{2,1,0:T(8,128)(2,1)} async-done(((bf16[8,192,3072]{2,1,0:T(8,128)(2,1)}), bf16[1,192,3072]{2,1,0:T(8,128)(2,1)}) %reduce-scatter.9.cloned.1.call-update) | async-done | bytes 1179664 | tf_op jit(solution)/shard_map/reduce_scatter | solution.py:916
  539.4 9.3 %collective-permute-done.76 = bf16[128,1536]{1,0:T(8,128)(2,1)} collective-permute-done((bf16[128,1536]{1,0:T(8,128)(2,1)S(1)}, bf16[128,1536]{1,0:T(8,128)(2,1)}, u32[]{:S(2)}, u32[]{:S(2)}) %collective-permute-start.76) | collective-permute-done | bytes 393248 | tf_op jit(solution)/shard_map/ppermute | solution.py:730
  552.9 12.9 %reduce-scatter.11.cloned.1.call-done = bf16[1,192,1152]{2,1,0:T(8,128)(2,1)} async-done(((bf16[8,192,1152]{2,1,0:T(8,128)(2,1)}), bf16[1,192,1152]{2,1,0:T(8,128)(2,1)}) %reduce-scatter.11.cloned.1.call-update) | async-done | bytes 442384 | tf_op jit(solution)/shard_map/reduce_scatter | solution.py:916
  579.3 18.0 %collective-permute-done.89 = bf16[96,3072]{1,0:T(8,128)(2,1)S(1)} collective-permute-done((bf16[96,3072]{1,0:T(8,128)(2,1)S(1)}, bf16[96,3072]{1,0:T(8,128)(2,1)S(1)}, u32[]{:S(2)}, u32[]{:S(2)}) %collective-permute-start.89) | collective-permute-done | bytes 589856 | tf_op jit(solution)/shard_map/ppermute | solution.py:753
  630.3 6.6 collective-permute-start.92
  643.3 7.4 %collective-permute-done.79 = bf16[64,1536]{1,0:T(8,128)(2,1)S(1)} collective-permute-done((bf16[64,1536]{1,0:T(8,128)(2,1)S(1)}, bf16[64,1536]{1,0:T(8,128)(2,1)S(1)}, u32[]{:S(2)}, u32[]{:S(2)}) %collective-permute-start.79) | collective-permute-done | bytes 196640 | tf_op jit(solution)/shard_map/ppermute | solution.py:685
  656.8 6.7 collective-permute-done.80
  667.8 7.4 %unpack.3 = (f32[192,1536]{1,0:T(8,128)}, f32[192,768]{1,0:T(8,128)}, f32[192,768]{1,0:T(8,128)}, f32[192,1536]{1,0:T(8,128)}, f32[192,4096]{1,0:T(8,128)}, /*in...) custom-call(bf16[4,2,96,4224]{3,2,1,0:T(8,128)(2,1)} %bitcast.74), custom_call_target="tpu_custom_call" | custom-call | flops 1000000 | bytes 30000000 | tf_op jit(solution)/shard_map/unpack/pallas_call | solution.py:577
  675.3 46.2 %all-gather.21.cloned.1.call-done = bf16[768,4224]{1,0:T(8,128)(2,1)} async-done(((bf16[96,4224]{1,0:T(8,128)(2,1)}), bf16[768,4224]{1,0:T(8,128)(2,1)}) %all-gather.21.cloned.1.call-update) | async-done | bytes 6488080 | tf_op jit(solution)/shard_map/all_gather | solution.py:945
  721.5 7.5 %unpack.2 = (f32[192,1536]{1,0:T(8,128)}, f32[192,768]{1,0:T(8,128)}, f32[192,768]{1,0:T(8,128)}, f32[192,1536]{1,0:T(8,128)}, f32[192,4096]{1,0:T(8,128)}, /*in...) custom-call(bf16[4,2,96,4224]{3,2,1,0:T(8,128)(2,1)} %bitcast.75), custom_call_target="tpu_custom_call" | custom-call | flops 1000000 | bytes 30000000 | tf_op jit(solution)/shard_map/unpack/pallas_call | solution.py:577
  (713 shorter events, 371.1 us)
Async XLA Ops:
  7.2 77.5 %all-gather.13.cloned.1.call-start = ((), (), s32[]{:S(2)}) async-start(), calls=%async_computation.8 | async-start | bytes 4423680 | tf_op jit(solution)/shard_map/all_gather | solution.py:813
  26.3 129.9 %all-gather.15.cloned.1.call-start = ((), (), s32[]{:S(2)}) async-start(), calls=%async_computation.9 | async-start | bytes 10616832 | tf_op jit(solution)/shard_map/all_gather | solution.py:813
  26.7 24.7 %collective-permute-start = (bf16[64,1536]{1,0:T(8,128)(2,1)S(1)}, bf16[64,1536]{1,0:T(8,128)(2,1)S(1)}, u32[]{:S(2)}, u32[]{:S(2)}) collective-permute-start(bf16[64,1536]{1,0:T(8,128)(2,1)S(1)} %get-tuple-element.244), channel_id=1, source_target_pairs={{0,0},{1,8},{2,16},{3,24},{4,32},{5,40},{6,48},{7,56},{8,1},{9,9},... | collective-permute-start | bytes 589832 | tf_op jit(solution)/shard_map/ppermute | solution.py:678
  33.3 18.7 %collective-permute-start.1 = (bf16[64,1536]{1,0:T(8,128)(2,1)S(1)}, bf16[64,1536]{1,0:T(8,128)(2,1)S(1)}, u32[]{:S(2)}, u32[]{:S(2)}) collective-permute-start(bf16[64,1536]{1,0:T(8,128)(2,1)S(1)} %get-tuple-element.247), channel_id=1, source_target_pairs={{0,16},{1,24},{2,32},{3,40},{4,48},{5,56},{6,0},{7,8},{8,17},{9,25... | collective-permute-start | bytes 589832 | tf_op jit(solution)/shard_map/ppermute | solution.py:678
  34.7 24.5 %collective-permute-start.2 = (bf16[64,1536]{1,0:T(8,128)(2,1)S(1)}, bf16[64,1536]{1,0:T(8,128)(2,1)S(1)}, u32[]{:S(2)}, u32[]{:S(2)}) collective-permute-start(bf16[64,1536]{1,0:T(8,128)(2,1)S(1)} %get-tuple-element.246), channel_id=1, source_target_pairs={{0,32},{1,40},{2,48},{3,56},{4,0},{5,8},{6,16},{7,24},{8,33},{9,41... | collective-permute-start | bytes 589832 | tf_op jit(solution)/shard_map/ppermute | solution.py:678
  50.1 25.1 %collective-permute-start.20 = (bf16[192,3072]{1,0:T(8,128)(2,1)S(1)}, bf16[192,3072]{1,0:T(8,128)(2,1)S(1)}, u32[]{:S(2)}, u32[]{:S(2)}) collective-permute-start(bf16[192,3072]{1,0:T(8,128)(2,1)S(1)} %pack_feed.2), channel_id=1, source_target_pairs={{0,1},{2,3},{4,5},{6,7},{9,8},{11,10},{13,12},{15,14},{16,17},{18,... | collective-permute-start | bytes 3538952 | tf_op jit(solution)/shard_map/ppermute | solution.py:796
  80.3 124.0 %all-gather.17.cloned.1.call-start = ((), (), s32[]{:S(2)}) async-start(), calls=%async_computation.10 | async-start | bytes 3981312 | tf_op jit(solution)/shard_map/all_gather | solution.py:813
  130.7 18.8 %collective-permute-start.16 = (bf16[128,1536]{1,0:T(8,128)(2,1)S(1)}, bf16[128,1536]{1,0:T(8,128)(2,1)S(1)}, u32[]{:S(2)}, u32[]{:S(2)}) collective-permute-start(bf16[128,1536]{1,0:T(8,128)(2,1)S(1)} %multiply_convert_fusion.2.refs_0_), channel_id=1, source_target_pairs={{0,16},{16,32},{32,48},{48,0},{1,17},{17,33},{33,49},{49,1},{2,18}... | collective-permute-start | bytes 1179656 | tf_op jit(solution)/shard_map/ppermute | solution.py:709
  130.7 18.8 %collective-permute-start.17 = (bf16[128,1536]{1,0:T(8,128)(2,1)S(1)}, bf16[128,1536]{1,0:T(8,128)(2,1)S(1)}, u32[]{:S(2)}, u32[]{:S(2)}) collective-permute-start(bf16[128,1536]{1,0:T(8,128)(2,1)S(1)} %multiply_convert_fusion.2.refs_0_), channel_id=1, source_target_pairs={{0,48},{16,0},{32,16},{48,32},{1,49},{17,1},{33,17},{49,33},{2,50}... | collective-permute-start | bytes 1179656 | tf_op jit(solution)/shard_map/ppermute | solution.py:710
  149.5 123.8 %all-gather.19.cloned.1.call-start = ((), (), s32[]{:S(2)}) async-start(), calls=%async_computation.11 | async-start | bytes 10616832 | tf_op jit(solution)/shard_map/all_gather | solution.py:813
  168.3 18.5 %collective-permute-start.44 = (bf16[192,3072]{1,0:T(8,128)(2,1)S(1)}, bf16[192,3072]{1,0:T(8,128)(2,1)}, u32[]{:S(2)}, u32[]{:S(2)}) collective-permute-start(bf16[192,3072]{1,0:T(8,128)(2,1)S(1)} %pack_feed.3), channel_id=1, source_target_pairs={{0,1},{2,3},{4,5},{6,7},{9,8},{11,10},{13,12},{15,14},{16,17},{18,... | collective-permute-start | bytes 3538952 | tf_op jit(solution)/shard_map/ppermute | solution.py:796
  197.3 209.4 %reduce-scatter.5.cloned.1.call-start = ((), (), s32[]{:S(2)}) async-start(), calls=%async_computation.4 | async-start | bytes 10616832 | tf_op jit(solution)/shard_map/reduce_scatter | solution.py:916
  201.6 17.2 %collective-permute-start.27 = (bf16[128,1536]{1,0:T(8,128)(2,1)S(1)}, bf16[128,1536]{1,0:T(8,128)(2,1)S(1)}, u32[]{:S(2)}, u32[]{:S(2)}) collective-permute-start(bf16[128,1536]{1,0:T(8,128)(2,1)S(1)} %pad_maximum_fusion.9.refs_0_.refs_5_), channel_id=1, source_target_pairs={{0,48},{16,0},{32,16},{48,32},{1,49},{17,1},{33,17},{49,33},{2,50}... | collective-permute-start | bytes 1179656 | tf_op jit(solution)/shard_map/ppermute | solution.py:710
  288.1 34.1 %collective-permute-start.45 = (bf16[64,1536]{1,0:T(8,128)(2,1)}, bf16[64,1536]{1,0:T(8,128)(2,1)}, u32[]{:S(2)}, u32[]{:S(2)}) collective-permute-start(bf16[64,1536]{1,0:T(8,128)(2,1)} %get-tuple-element.256), channel_id=1, source_target_pairs={{0,16},{16,32},{32,48},{48,0},{1,17},{17,33},{33,49},{49,1},{2,18}... | collective-permute-start | bytes 589832 | tf_op jit(solution)/shard_map/ppermute | solution.py:718
  288.2 36.2 %collective-permute-start.47 = (bf16[64,1536]{1,0:T(8,128)(2,1)}, bf16[64,1536]{1,0:T(8,128)(2,1)}, u32[]{:S(2)}, u32[]{:S(2)}) collective-permute-start(bf16[64,1536]{1,0:T(8,128)(2,1)} %get-tuple-element.257), channel_id=1, source_target_pairs={{0,48},{16,0},{32,16},{48,32},{1,49},{17,1},{33,17},{49,33},{2,50}... | collective-permute-start | bytes 589832 | tf_op jit(solution)/shard_map/ppermute | solution.py:719
  305.7 22.0 %collective-permute-start.49 = (bf16[128,1536]{1,0:T(8,128)(2,1)}, bf16[128,1536]{1,0:T(8,128)(2,1)}, u32[]{:S(2)}, u32[]{:S(2)}) collective-permute-start(bf16[128,1536]{1,0:T(8,128)(2,1)} %get-tuple-element.142), channel_id=1, source_target_pairs={{0,16},{16,32},{32,48},{48,0},{1,17},{17,33},{33,49},{49,1},{2,18}... | collective-permute-start | bytes 1179656 | tf_op jit(solution)/shard_map/ppermute | solution.py:728
  305.7 22.0 %collective-permute-start.50 = (bf16[128,1536]{1,0:T(8,128)(2,1)}, bf16[128,1536]{1,0:T(8,128)(2,1)}, u32[]{:S(2)}, u32[]{:S(2)}) collective-permute-start(bf16[128,1536]{1,0:T(8,128)(2,1)} %get-tuple-element.143), channel_id=1, source_target_pairs={{0,48},{16,0},{32,16},{48,32},{1,49},{17,1},{33,17},{49,33},{2,50}... | collective-permute-start | bytes 1179656 | tf_op jit(solution)/shard_map/ppermute | solution.py:729
  308.4 19.3 %collective-permute-start.51 = (bf16[128,1536]{1,0:T(8,128)(2,1)}, bf16[128,1536]{1,0:T(8,128)(2,1)}, u32[]{:S(2)}, u32[]{:S(2)}) collective-permute-start(bf16[128,1536]{1,0:T(8,128)(2,1)} %get-tuple-element.144), channel_id=1, source_target_pairs={{0,32},{16,48},{32,0},{48,16},{1,33},{17,49},{33,1},{49,17},{2,34}... | collective-permute-start | bytes 1179656 | tf_op jit(solution)/shard_map/ppermute | solution.py:730
  333.3 128.8 %reduce-scatter.7.cloned.1.call-start = ((), (), s32[]{:S(2)}) async-start(), calls=%async_computation.5 | async-start | bytes 3981312 | tf_op jit(solution)/shard_map/reduce_scatter | solution.py:916
  379.3 19.6 %collective-permute-start.58 = (bf16[128,1536]{1,0:T(8,128)(2,1)}, bf16[128,1536]{1,0:T(8,128)(2,1)}, u32[]{:S(2)}, u32[]{:S(2)}) collective-permute-start(bf16[128,1536]{1,0:T(8,128)(2,1)} %get-tuple-element.155), channel_id=1, source_target_pairs={{0,48},{16,0},{32,16},{48,32},{1,49},{17,1},{33,17},{49,33},{2,50}... | collective-permute-start | bytes 1179656 | tf_op jit(solution)/shard_map/ppermute | solution.py:729
  382.2 18.8 %collective-permute-start.59 = (bf16[128,1536]{1,0:T(8,128)(2,1)S(1)}, bf16[128,1536]{1,0:T(8,128)(2,1)}, u32[]{:S(2)}, u32[]{:S(2)}) collective-permute-start(bf16[128,1536]{1,0:T(8,128)(2,1)S(1)} %get-tuple-element.156), channel_id=1, source_target_pairs={{0,32},{16,48},{32,0},{48,16},{1,33},{17,49},{33,1},{49,17},{2,34}... | collective-permute-start | bytes 1179656 | tf_op jit(solution)/shard_map/ppermute | solution.py:730
  406.7 122.0 %reduce-scatter.9.cloned.1.call-start = ((), (), s32[]{:S(2)}) async-start(), calls=%async_computation.6 | async-start | bytes 10616832 | tf_op jit(solution)/shard_map/reduce_scatter | solution.py:916
  462.2 103.6 %reduce-scatter.11.cloned.1.call-start = ((), (), s32[]{:S(2)}) async-start(), calls=%async_computation.7 | async-start | bytes 3981312 | tf_op jit(solution)/shard_map/reduce_scatter | solution.py:916
  475.4 29.4 %collective-permute-start.68 = (bf16[96,4224]{1,0:T(8,128)(2,1)}, bf16[96,4224]{1,0:T(8,128)(2,1)S(1)}, u32[]{:S(2)}, u32[]{:S(2)}) collective-permute-start(bf16[96,4224]{1,0:T(8,128)(2,1)} %bitcast_select_fusion), channel_id=1, source_target_pairs={{0,1},{1,0},{2,3},{3,2},{4,5},{5,4},{6,7},{7,6},{8,9},{9,8},{10,11... | collective-permute-start | bytes 2433032 | tf_op jit(solution)/shard_map/ppermute | solution.py:753
  528.8 139.1 %all-gather.23.cloned.1.call-start = ((), (), s32[]{:S(2)}) async-start(), calls=%async_computation.13 | async-start | bytes 7299072 | tf_op jit(solution)/shard_map/all_gather | solution.py:940
  531.6 17.2 %collective-permute-start.76 = (bf16[128,1536]{1,0:T(8,128)(2,1)S(1)}, bf16[128,1536]{1,0:T(8,128)(2,1)}, u32[]{:S(2)}, u32[]{:S(2)}) collective-permute-start(bf16[128,1536]{1,0:T(8,128)(2,1)S(1)} %get-tuple-element.179), channel_id=1, source_target_pairs={{0,32},{16,48},{32,0},{48,16},{1,33},{17,49},{33,1},{49,17},{2,34}... | collective-permute-start | bytes 1179656 | tf_op jit(solution)/shard_map/ppermute | solution.py:730
  533.0 17.4 %collective-permute-start.95 = (bf16[96,4224]{1,0:T(8,128)(2,1)S(1)}, bf16[96,4224]{1,0:T(8,128)(2,1)}, u32[]{:S(2)}, u32[]{:S(2)}) collective-permute-start(bf16[96,4224]{1,0:T(8,128)(2,1)S(1)} %add_convert_fusion.1.refs_0_), channel_id=1, source_target_pairs={{0,64},{64,0},{1,65},{65,1},{2,66},{66,2},{3,67},{67,3},{4,68},{68... | collective-permute-start | bytes 2433032 | tf_op jit(solution)/shard_map/ppermute | solution.py:757
  566.8 154.7 %all-gather.21.cloned.1.call-start = ((), (), s32[]{:S(2)}) async-start(), calls=%async_computation.12 | async-start | bytes 7299072 | tf_op jit(solution)/shard_map/all_gather | solution.py:945
  573.7 23.7 %collective-permute-start.89 = (bf16[96,3072]{1,0:T(8,128)(2,1)S(1)}, bf16[96,3072]{1,0:T(8,128)(2,1)S(1)}, u32[]{:S(2)}, u32[]{:S(2)}) collective-permute-start(bf16[96,3072]{1,0:T(8,128)(2,1)S(1)} %bitcast_select_fusion.2), channel_id=1, source_target_pairs={{0,1},{1,0},{2,3},{3,2},{4,5},{5,4},{6,7},{7,6},{8,9},{9,8},{10,11... | collective-permute-start | bytes 1769480 | tf_op jit(solution)/shard_map/ppermute | solution.py:753
  576.5 23.5 %collective-permute-start.77 = (bf16[64,1536]{1,0:T(8,128)(2,1)S(1)}, bf16[64,1536]{1,0:T(8,128)(2,1)S(1)}, u32[]{:S(2)}, u32[]{:S(2)}) collective-permute-start(bf16[64,1536]{1,0:T(8,128)(2,1)S(1)} %pad_maximum_fusion.15), channel_id=1, source_target_pairs={{0,0},{8,1},{16,2},{24,3},{32,4},{40,5},{48,6},{56,7},{1,8},{9,9},... | collective-permute-start | bytes 589832 | tf_op jit(solution)/shard_map/ppermute | solution.py:685
  579.2 24.0 %collective-permute-start.82 = (f32[4,1536]{1,0:T(4,128)S(1)}, f32[4,1536]{1,0:T(4,128)S(1)}, u32[]{:S(2)}, u32[]{:S(2)}) collective-permute-start(f32[4,1536]{1,0:T(4,128)S(1)} %fusion.23), channel_id=1, source_target_pairs={{0,16},{16,0},{32,48},{48,32},{1,17},{17,1},{33,49},{49,33},{2,18}... | collective-permute-start | bytes 73736 | tf_op jit(solution)/shard_map/ppermute | solution.py:773
  600.0 25.0 %collective-permute-start.90 = (bf16[96,3072]{1,0:T(8,128)(2,1)S(1)}, bf16[96,3072]{1,0:T(8,128)(2,1)S(1)}, u32[]{:S(2)}, u32[]{:S(2)}) collective-permute-start(bf16[96,3072]{1,0:T(8,128)(2,1)S(1)} %add_convert_fusion.3), channel_id=1, source_target_pairs={{0,64},{64,0},{1,65},{65,1},{2,66},{66,2},{3,67},{67,3},{4,68},{68... | collective-permute-start | bytes 1769480 | tf_op jit(solution)/shard_map/ppermute | solution.py:757
  (228 other events, 1990.8 us)
Sparse Core Ops, SparseCore 0:
  26.4 45.1 all-gather.12
  80.4 51.0 all-gather.14
  149.6 33.0 all-gather.16
  197.4 66.1 all-gather.18
  333.4 73.2 reduce-scatter.4
  409.0 37.2 reduce-scatter.6
  462.3 66.3 reduce-scatter.8
  531.3 34.4 reduce-scatter.10
  568.1 50.6 all-gather.22
  665.3 56.1 all-gather.20
